TPU v7x, 32 devices: a whole 2x2x4 slice. The times are simulated.
32 devices in a mesh: section: 2 (over x), dp: 4 (over y, core), shard: 4 (over z).
Axes of the slice: x: 2, y: 2, z: 4, core: 2. Of those that a mesh axis runs over, the one named last changes fastest.
Arguments:
- token_ids: int32 [2, 16, 256], P(None, ('dp', 'shard')), may hold values from 0 to 30527
- targets: int32 [2, 16, 256], P(None, ('dp', 'shard')), may hold values from 0 to 30527
- segment_ids: int32 [2, 16, 256], P(None, ('dp', 'shard')), may hold values from 0 to 7, never falling along the last dimension, each value on 1 to 128 neighbouring positions
- word_table: bfloat16 [30528, 768], P('shard'), may hold values from -0.59765625 to 0.59765625
- pos_table: bfloat16 [512, 768], P('shard'), may hold values from -0.59765625 to 0.59765625
- embed_gain: bfloat16 [768], P('shard'), may hold values from 0.5 to 1.5
- embed_shift: bfloat16 [768], P('shard'), may hold values from -1.1953125 to 1.1953125
- qkv_weight: bfloat16 [2, 3, 4, 192, 192], P('section', None, None, 'shard'), may hold values from -0.4375 to 0.4375
- out_weight: bfloat16 [2, 768, 768], P('section', 'shard'), may hold values from -0.875 to 0.875
- ffn_in: bfloat16 [2, 4, 192, 768], P('section', None, 'shard'), may hold values from -0.4375 to 0.4375
- ffn_out: bfloat16 [2, 4, 768, 192], P('section', None, 'shard'), may hold values from -0.21875 to 0.21875
- layer_gains: bfloat16 [2, 2, 768], P('section', None, 'shard'), may hold values from 0.5 to 1.5
- layer_biases: bfloat16 [2, 9, 768], P('section', None, 'shard'), may hold values from -1.1953125 to 1.1953125
Outputs:
- layer_outputs: bfloat16 [2, 2, 16, 256, 768], P('section', None, ('dp', 'shard'))
- input_grads: float32 [2, 2, 16, 256, 768], P('section', None, ('dp', 'shard'))
- word_grad: float32 [30528, 768], P('shard', ('section', 'dp'))
- pos_grad: float32 [512, 768], P('shard')
- embed_gain_grad: float32 [768], P('shard')
- embed_shift_grad: float32 [768], P('shard')
- qkv_grad: float32 [2, 3, 4, 192, 192], P('section', None, None, 'shard')
- out_grad: float32 [2, 768, 768], P('section', 'shard')
- ffn_in_grad: float32 [2, 4, 192, 768], P('section', None, 'shard')
- ffn_out_grad: float32 [2, 4, 768, 192], P('section', None, 'shard')
- gains_grad: float32 [2, 2, 768], P('section', None, 'shard')
- biases_grad: float32 [2, 9, 768], P('section', None, 'shard')
Inputs may be any that keep to these rules, and one draw needn't show every extreme that they name: `targets`: token ids. `segment_ids`: within each row of 256 positions the document number never falls; each document has 1 to 128 positions, and one has exactly 128.
All inputs are finite; a program needn't handle non-finite values.
Results may differ from a plain program's by a relative error of at most 0.018.
Values may be sent and summed in bfloat16 or wider, within the bound.
No kernel may reach another device: no remote copies, remote signals or barrier semaphores. Data moves between devices by JAX's collectives and lax.ppermute only.
A program may use at most 320 MiB of HBM per device.

v0:
```python
from functools import partial
import math

import jax
import jax.numpy as jnp
from jax import lax
from jax.sharding import PartitionSpec as P

HEADS = 12


EPSILON = 1e-06
MASKED = -1000000000.0


def shifted_2(block, axis, distance):
    devices = range(lax.axis_size(axis))
    route = [(i - distance, i) for i in devices if i - distance in devices]
    return lax.ppermute(block, axis, route)


def joined(value, axis, join):
    pieces = jax.tree.map(lambda part: lax.all_gather(part, axis), value)
    head = jax.tree.map(lambda part: part[0], pieces)
    tail = jax.tree.map(lambda part: part[1:], pieces)
    subtotal, _ = lax.scan(lambda subtotal, piece: (join(subtotal, piece), None), head, tail)
    return subtotal


def passed_along(shard, axis, by):
    size = lax.axis_size(axis)
    return lax.ppermute(shard, axis, [(i, (i + by) % size) for i in range(size)])


def layer_norm(inputs, gain_row, shift_row):
    centered = inputs - jnp.mean(inputs, axis=-1, keepdims=True)
    variance = jnp.mean(centered * centered, axis=-1, keepdims=True)
    return centered * lax.rsqrt(variance + EPSILON) * gain_row + shift_row


def norm_back(inputs, gain_row, shift_row, out_grad):
    _, pullback = jax.vjp(layer_norm, inputs, gain_row, shift_row)
    return pullback(out_grad)


def grouped(inputs, weight):
    seq_len = inputs.shape[0]
    group_count = weight.shape[0]
    split = inputs.reshape(seq_len, group_count, -1)
    return jnp.einsum("sgi,gio->sgo", split, weight, preferred_element_type=jnp.float32).reshape(
        seq_len, -1
    )


def places(segments):
    seq_len = segments.shape[0]
    same_doc = segments[:, None] == segments[None, :]
    order = jnp.arange(seq_len, dtype=jnp.int32)
    before = order[None, :] < order[:, None]
    return (jnp.sum((same_doc & before).astype(jnp.int32), axis=1), same_doc)


def unpack(gathered):
    w_qkv, w_out, w_in, w_back, norm_gains, biases, pos_full, egain, eshift = gathered
    layer_weights = (
        w_qkv[0],
        w_out[0],
        w_in[0],
        w_back[0],
        norm_gains[0].astype(jnp.float32),
        biases[0].astype(jnp.float32),
    )
    return (layer_weights, pos_full, egain.astype(jnp.float32), eshift.astype(jnp.float32))


def layer_forward(layer_in, same_doc, weights):
    w_qkv, w_out, w_in, w_back, norm_gains, biases = weights
    seq_len, model_width = layer_in.shape
    group_count = w_qkv.shape[1]
    head_size = model_width // HEADS
    score_scale = 1.0 / math.sqrt(head_size)
    input_low = layer_in.astype(jnp.bfloat16)
    projected = jnp.einsum(
        "sgi,cgio->csgo",
        input_low.reshape(seq_len, group_count, -1),
        w_qkv,
        preferred_element_type=jnp.float32,
    ).reshape(3, seq_len, model_width)
    queries = projected[0].astype(jnp.bfloat16)
    key_low = projected[1].astype(jnp.bfloat16)
    value_low = (projected[2] + biases[0]).astype(jnp.bfloat16)
    q_heads = queries.reshape(seq_len, HEADS, head_size)
    k_heads = key_low.reshape(seq_len, HEADS, head_size)
    v_heads = value_low.reshape(seq_len, HEADS, head_size)
    scores = (
        jnp.einsum("qhd,khd->hqk", q_heads, k_heads, preferred_element_type=jnp.float32)
        * score_scale
    )
    scores = jnp.where(same_doc[None], scores, MASKED)
    row_max = jnp.max(scores, axis=-1, keepdims=True)
    exp_scores = jnp.exp(scores - row_max)
    attn_probs = exp_scores / jnp.sum(exp_scores, axis=-1, keepdims=True)
    probs_low = attn_probs.astype(jnp.bfloat16)
    attended = (
        jnp.einsum("hqk,khd->qhd", probs_low, v_heads, preferred_element_type=jnp.float32)
        .reshape(seq_len, model_width)
        .astype(jnp.bfloat16)
    )
    middle_in = layer_in + (
        jnp.dot(attended, w_out, preferred_element_type=jnp.float32) + biases[1]
    )
    middle = layer_norm(middle_in, norm_gains[0], biases[2])
    middle_low = middle.astype(jnp.bfloat16)
    pre_gelu = grouped(middle_low, w_in) + biases[3:7].reshape(-1)
    activated = jax.nn.gelu(pre_gelu, approximate=False).astype(jnp.bfloat16)
    final_in = middle + (grouped(activated, w_back) + biases[7])
    layer_out = layer_norm(final_in, norm_gains[1], biases[8])
    state = (
        layer_in,
        input_low,
        q_heads,
        k_heads,
        v_heads,
        attn_probs,
        probs_low,
        attended,
        middle_in,
        middle_low,
        pre_gelu,
        activated,
        final_in,
    )
    return (layer_out, state)


def layer_backward(state, out_grad, weights):
    w_qkv, w_out, w_in, w_back, norm_gains, biases = weights
    (
        layer_in,
        input_low,
        q_heads,
        k_heads,
        v_heads,
        attn_probs,
        probs_low,
        attended,
        middle_in,
        middle_low,
        pre_gelu,
        activated,
        final_in,
    ) = state
    seq_len, model_width = layer_in.shape
    group_count = w_qkv.shape[1]
    head_size = model_width // HEADS
    score_scale = 1.0 / math.sqrt(head_size)
    final_grad, gain_two, shift_two = norm_back(final_in, norm_gains[1], biases[8], out_grad)
    ffn_grad = final_grad.astype(jnp.bfloat16).reshape(seq_len, group_count, -1)
    grad_back = jnp.einsum(
        "sgf,sgo->gfo",
        activated.reshape(seq_len, group_count, -1),
        ffn_grad,
        preferred_element_type=jnp.float32,
    )
    act_grad = jnp.einsum(
        "sgo,gfo->sgf", ffn_grad, w_back, preferred_element_type=jnp.float32
    ).reshape(seq_len, -1)
    _, gelu_pull = jax.vjp(partial(jax.nn.gelu, approximate=False), pre_gelu)
    gelu_grad = gelu_pull(act_grad)[0].astype(jnp.bfloat16)
    gelu_split = gelu_grad.reshape(seq_len, group_count, -1)
    grad_in = jnp.einsum(
        "sgi,sgf->gif",
        middle_low.reshape(seq_len, group_count, -1),
        gelu_split,
        preferred_element_type=jnp.float32,
    )
    middle_grad = final_grad + jnp.einsum(
        "sgf,gif->sgi", gelu_split, w_in, preferred_element_type=jnp.float32
    ).reshape(seq_len, model_width)
    residual_grad, gain_one, shift_one = norm_back(middle_in, norm_gains[0], biases[2], middle_grad)
    branch_grad = residual_grad.astype(jnp.bfloat16)
    grad_out = jnp.einsum("sd,se->de", attended, branch_grad, preferred_element_type=jnp.float32)
    attended_grad = jnp.einsum(
        "se,de->sd", branch_grad, w_out, preferred_element_type=jnp.float32
    ).astype(jnp.bfloat16)
    heads_grad = attended_grad.reshape(seq_len, HEADS, head_size)
    probs_grad = jnp.einsum("qhd,khd->hqk", heads_grad, v_heads, preferred_element_type=jnp.float32)
    scores_grad = (
        attn_probs * (probs_grad - jnp.sum(attn_probs * probs_grad, axis=-1, keepdims=True))
    ).astype(jnp.bfloat16)
    query_grad = (
        jnp.einsum("hqk,khd->qhd", scores_grad, k_heads, preferred_element_type=jnp.float32)
        * score_scale
    )
    key_grad = (
        jnp.einsum("hqk,qhd->khd", scores_grad, q_heads, preferred_element_type=jnp.float32)
        * score_scale
    )
    value_grad = jnp.einsum(
        "hqk,qhd->khd", probs_low, heads_grad, preferred_element_type=jnp.float32
    )
    proj_grad = (
        jnp.stack([query_grad, key_grad, value_grad])
        .astype(jnp.bfloat16)
        .reshape(3, seq_len, group_count, -1)
    )
    grad_qkv = jnp.einsum(
        "sgi,csgo->cgio",
        input_low.reshape(seq_len, group_count, -1),
        proj_grad,
        preferred_element_type=jnp.float32,
    )
    input_grad = residual_grad + jnp.einsum(
        "csgo,cgio->sgi", proj_grad, w_qkv, preferred_element_type=jnp.float32
    ).reshape(seq_len, model_width)
    value_sum = jnp.sum(proj_grad[2], axis=0, dtype=jnp.float32).reshape(1, model_width)
    bias_grad = jnp.concatenate(
        [
            value_sum,
            jnp.sum(branch_grad, axis=0, dtype=jnp.float32)[None],
            shift_one[None],
            jnp.sum(gelu_grad, axis=0, dtype=jnp.float32).reshape(-1, model_width),
            jnp.sum(ffn_grad, axis=0, dtype=jnp.float32).reshape(1, model_width),
            shift_two[None],
        ]
    )
    gain_grad = jnp.stack([gain_one, gain_two])
    return (input_grad, (grad_qkv, grad_out, grad_in, grad_back, gain_grad, bias_grad))


def head_stats(head_rows, word_part):
    row_count, model_width = head_rows.shape
    block_rows = min(row_count, 512)

    def per_block(rows_block):
        logits = jnp.einsum("rd,vd->rv", rows_block, word_part, preferred_element_type=jnp.float32)
        block_max = jnp.max(logits, axis=1)
        return (block_max, jnp.sum(jnp.exp(logits - block_max[:, None]), axis=1))

    maxima, totals = lax.map(per_block, head_rows.reshape(-1, block_rows, model_width))
    return (maxima.reshape(-1), totals.reshape(-1))


def head_back(head_rows, head_targets, log_total, word_part, columns):
    row_count, model_width = head_rows.shape
    block_rows = min(row_count, 512)

    def per_block(running, pieces):
        rows_block, target_block, total_block = pieces
        logits = jnp.einsum("rd,vd->rv", rows_block, word_part, preferred_element_type=jnp.float32)
        onehot = (columns[None, :] == target_block[:, None]).astype(jnp.float32)
        slope_low = (jnp.exp(logits - total_block[:, None]) - onehot).astype(jnp.bfloat16)
        running = running + jnp.einsum(
            "rv,rd->vd", slope_low, rows_block, preferred_element_type=jnp.float32
        )
        return (running, slope_low)

    start_grad = jnp.zeros(word_part.shape, jnp.float32)
    table_add, slopes = lax.scan(
        per_block,
        start_grad,
        (
            head_rows.reshape(-1, block_rows, model_width),
            head_targets.reshape(-1, block_rows),
            log_total.reshape(-1, block_rows),
        ),
    )
    return (table_add, slopes.reshape(row_count, -1))


def combine(earlier, later):
    joint_max = jnp.maximum(earlier[0], later[0])
    joint_total = earlier[1] * jnp.exp(earlier[0] - joint_max) + later[1] * jnp.exp(
        later[0] - joint_max
    )
    return (joint_max, joint_total)


def body(
    token_ids,
    targets,
    segment_ids,
    word_table,
    pos_table,
    embed_gain,
    embed_shift,
    qkv_weight,
    out_weight,
    ffn_in,
    ffn_out,
    layer_gains,
    layer_biases,
):
    micro_count = token_ids.shape[0]
    seq_len = token_ids.shape[2]
    vocab_part, model_width = word_table.shape
    section_index = lax.axis_index("section")
    is_first = section_index == 0
    is_last = section_index == lax.axis_size("section") - 1
    first_scale = is_first.astype(jnp.float32)
    offset = lax.axis_index("shard") * vocab_part
    columns = offset + jnp.arange(vocab_part, dtype=jnp.int32)
    id_rows, target_rows = (
        lax.all_gather(token_ids, "shard", axis=1, tiled=True),
        lax.all_gather(targets, "shard", axis=1, tiled=True),
    )
    segment_info = [places(segment_ids[micro_index, 0]) for micro_index in range(micro_count)]
    gathered = (
        lax.all_gather(qkv_weight, "shard", axis=3, tiled=True),
        lax.all_gather(out_weight, "shard", axis=1, tiled=True),
        lax.all_gather(ffn_in, "shard", axis=2, tiled=True),
        lax.all_gather(ffn_out, "shard", axis=2, tiled=True),
        lax.all_gather(layer_gains, "shard", axis=2, tiled=True),
        lax.all_gather(layer_biases, "shard", axis=2, tiled=True),
        lax.all_gather(pos_table, "shard", axis=0, tiled=True),
        lax.all_gather(embed_gain, "shard", axis=0, tiled=True),
        lax.all_gather(embed_shift, "shard", axis=0, tiled=True),
    )
    layer_weights, pos_full, norm_gain, norm_shift = unpack(gathered)
    zero_rows = jnp.zeros((seq_len, model_width), jnp.float32)

    def local_ids(micro_index):
        flat_ids = id_rows[micro_index].reshape(-1)
        shifted = flat_ids - offset
        inside = ((shifted >= 0) & (shifted < vocab_part)).astype(jnp.float32)
        return (jnp.clip(shifted, 0, vocab_part - 1), inside)

    received = jnp.zeros((seq_len, model_width), jnp.bfloat16)
    kept_inputs = []
    kept_docs = []
    kept_sums = []
    layer_lows = []
    head_grads = []
    table_grad = jnp.zeros((vocab_part, model_width), jnp.float32)
    for step_index in range(micro_count + 1):
        early = min(step_index, micro_count - 1)
        late = max(step_index - 1, 0)
        if step_index < micro_count:
            clipped, inside = local_ids(step_index)
            picked = jnp.take(word_table, clipped, axis=0).astype(jnp.float32) * inside[:, None]
            word_rows = lax.psum_scatter(
                picked.astype(jnp.bfloat16), "shard", scatter_dimension=0, tiled=True
            ).astype(jnp.float32)
            embed_sum = word_rows + jnp.take(pos_full, segment_info[step_index][0], axis=0).astype(
                jnp.float32
            )
            embedded = layer_norm(embed_sum, norm_gain, norm_shift)
        else:
            embed_sum = zero_rows
            embedded = zero_rows
        layer_in = jnp.where(is_first, embedded, received.astype(jnp.float32))
        same_doc = jnp.where(is_first, segment_info[early][1], segment_info[late][1])
        layer_out, _ = layer_forward(layer_in, same_doc, layer_weights)
        out_low = layer_out.astype(jnp.bfloat16)
        if step_index < micro_count:
            received = shifted_2(out_low, "section", 1)
        if step_index >= 1:
            head_rows = lax.all_gather(out_low, "shard", axis=0, tiled=True)
            head_targets = target_rows[step_index - 1].reshape(-1)
            row_total = head_rows.shape[0]
            stats = lax.cond(
                is_last,
                lambda: head_stats(head_rows, word_table),
                lambda: (jnp.zeros((row_total,), jnp.float32), jnp.ones((row_total,), jnp.float32)),
            )
            joint_max, joint_total = joined((stats[0], stats[1]), "shard", combine)
            log_total = joint_max + jnp.log(joint_total)
            table_add, slopes = lax.cond(
                is_last,
                lambda: head_back(head_rows, head_targets, log_total, word_table, columns),
                lambda: (
                    jnp.zeros((vocab_part, model_width), jnp.float32),
                    jnp.zeros((row_total, vocab_part), jnp.bfloat16),
                ),
            )
            table_grad = table_grad + table_add

            def project(row_start, row_count, slopes=slopes):
                return lax.cond(
                    is_last,
                    lambda: jnp.dot(slopes, word_table, preferred_element_type=jnp.float32),
                    lambda: jnp.zeros((row_count, model_width), jnp.float32),
                )

            head_grads.append(
                lax.psum_scatter(
                    project(jnp.int32(0), seq_len * lax.axis_size("shard")).astype(jnp.bfloat16),
                    "shard",
                    scatter_dimension=0,
                    tiled=True,
                ).astype(jnp.float32)
            )
        kept_inputs.append(layer_in)
        kept_docs.append(same_doc)
        kept_sums.append(embed_sum)
        layer_lows.append(out_low)
    layer_weights, pos_full, norm_gain, norm_shift = unpack(
        (
            lax.all_gather(qkv_weight, "shard", axis=3, tiled=True),
            lax.all_gather(out_weight, "shard", axis=1, tiled=True),
            lax.all_gather(ffn_in, "shard", axis=2, tiled=True),
            lax.all_gather(ffn_out, "shard", axis=2, tiled=True),
            lax.all_gather(layer_gains, "shard", axis=2, tiled=True),
            lax.all_gather(layer_biases, "shard", axis=2, tiled=True),
            lax.all_gather(pos_table, "shard", axis=0, tiled=True),
            lax.all_gather(embed_gain, "shard", axis=0, tiled=True),
            lax.all_gather(embed_shift, "shard", axis=0, tiled=True),
        )
    )
    received_grad = jnp.zeros((seq_len, model_width), jnp.bfloat16)
    accum = jax.tree.map(lambda weight: jnp.zeros(weight.shape, jnp.float32), layer_weights)
    pos_grad = jnp.zeros(pos_full.shape, jnp.float32)
    gain_acc = jnp.zeros((model_width,), jnp.float32)
    shift_acc = jnp.zeros((model_width,), jnp.float32)
    step_grads = []
    for step_index in range(micro_count + 1):
        early_in = kept_inputs[step_index - 1] if step_index >= 1 else zero_rows
        late_in = kept_inputs[step_index + 1] if step_index + 1 <= micro_count else zero_rows
        early_doc = kept_docs[step_index - 1] if step_index >= 1 else kept_docs[0]
        late_doc = kept_docs[step_index + 1] if step_index + 1 <= micro_count else kept_docs[0]
        layer_in = jnp.where(is_first, early_in, late_in)
        same_doc = jnp.where(is_first, early_doc, late_doc)
        from_head = head_grads[step_index] if step_index < micro_count else zero_rows
        out_grad = jnp.where(is_first, received_grad.astype(jnp.float32), from_head)
        _, state = layer_forward(layer_in, same_doc, layer_weights)
        input_grad, step_weight_grads = layer_backward(state, out_grad, layer_weights)
        accum = jax.tree.map(lambda total_now, added: total_now + added, accum, step_weight_grads)
        step_grads.append(input_grad)
        if step_index < micro_count:
            received_grad = shifted_2(input_grad.astype(jnp.bfloat16), "section", -1)
        if step_index >= 1:
            sum_grad, gain_add, shift_add = norm_back(
                kept_sums[step_index - 1], norm_gain, norm_shift, input_grad * first_scale
            )
            pos_grad = pos_grad + jax.ops.segment_sum(
                sum_grad, segment_info[step_index - 1][0], num_segments=pos_full.shape[0]
            )
            gain_acc = gain_acc + gain_add
            shift_acc = shift_acc + shift_add
            rows_grad = lax.all_gather(
                sum_grad.astype(jnp.bfloat16), "shard", axis=0, tiled=True
            ).astype(sum_grad.dtype)
            clipped, inside = local_ids(step_index - 1)
            table_grad = table_grad + jax.ops.segment_sum(
                rows_grad * inside[:, None], clipped, num_segments=vocab_part
            )
    reduced = (
        lax.psum_scatter(
            accum[0][None].astype(jnp.bfloat16), "shard", scatter_dimension=3, tiled=True
        ).astype(jnp.float32),
        lax.psum_scatter(
            accum[1][None].astype(jnp.bfloat16), "shard", scatter_dimension=1, tiled=True
        ).astype(jnp.float32),
        lax.psum_scatter(
            accum[2][None].astype(jnp.bfloat16), "shard", scatter_dimension=2, tiled=True
        ).astype(jnp.float32),
        lax.psum_scatter(
            accum[3][None].astype(jnp.bfloat16), "shard", scatter_dimension=2, tiled=True
        ).astype(jnp.float32),
        lax.psum_scatter(
            accum[4][None].astype(jnp.bfloat16), "shard", scatter_dimension=2, tiled=True
        ).astype(jnp.float32),
        lax.psum_scatter(
            accum[5][None].astype(jnp.bfloat16), "shard", scatter_dimension=2, tiled=True
        ).astype(jnp.float32),
        lax.psum_scatter(
            pos_grad.astype(jnp.bfloat16), "shard", scatter_dimension=0, tiled=True
        ).astype(jnp.float32),
        lax.psum_scatter(
            gain_acc.astype(jnp.bfloat16), "shard", scatter_dimension=0, tiled=True
        ).astype(jnp.float32),
        lax.psum_scatter(
            shift_acc.astype(jnp.bfloat16), "shard", scatter_dimension=0, tiled=True
        ).astype(jnp.float32),
    )
    summed = (
        lax.psum(reduced[0].astype(jnp.bfloat16), "dp").astype(jnp.float32),
        lax.psum(reduced[1].astype(jnp.bfloat16), "dp").astype(jnp.float32),
        lax.psum(reduced[2].astype(jnp.bfloat16), "dp").astype(jnp.float32),
        lax.psum(reduced[3].astype(jnp.bfloat16), "dp").astype(jnp.float32),
        lax.psum(reduced[4].astype(jnp.bfloat16), "dp").astype(jnp.float32),
        lax.psum(reduced[5].astype(jnp.bfloat16), "dp").astype(jnp.float32),
        lax.psum(reduced[6].astype(jnp.bfloat16), "dp").astype(jnp.float32),
        lax.psum(reduced[7].astype(jnp.bfloat16), "dp").astype(jnp.float32),
        lax.psum(reduced[8].astype(jnp.bfloat16), "dp").astype(jnp.float32),
    )
    half_width = model_width // 2
    pos_piece = summed[6]
    gain_piece = summed[7]
    shift_piece = summed[8]
    full_grad = table_grad + passed_along(table_grad.astype(jnp.bfloat16), "section", 1).astype(
        table_grad.dtype
    )
    own_half = lax.dynamic_slice_in_dim(full_grad, section_index * half_width, half_width, 1)
    word_grad = lax.psum_scatter(
        own_half.astype(jnp.bfloat16), "dp", scatter_dimension=1, tiled=True
    ).astype(jnp.float32)
    pos_out = summed[6] + passed_along(pos_piece.astype(jnp.bfloat16), "section", 1).astype(
        pos_piece.dtype
    )
    gain_out = summed[7] + passed_along(gain_piece.astype(jnp.bfloat16), "section", 1).astype(
        gain_piece.dtype
    )
    shift_out = summed[8] + passed_along(shift_piece.astype(jnp.bfloat16), "section", 1).astype(
        shift_piece.dtype
    )
    out_shape = (1, micro_count, 1, seq_len, model_width)
    layer_outputs = jnp.stack(
        [
            jnp.where(is_first, layer_lows[micro_index], layer_lows[micro_index + 1])
            for micro_index in range(micro_count)
        ]
    ).reshape(out_shape)
    input_grads = jnp.stack(
        [
            jnp.where(is_first, step_grads[micro_index + 1], step_grads[micro_index])
            for micro_index in range(micro_count)
        ]
    ).reshape(out_shape)
    return (
        layer_outputs,
        input_grads,
        word_grad,
        pos_out,
        gain_out,
        shift_out,
        summed[0],
        summed[1],
        summed[2],
        summed[3],
        summed[4],
        summed[5],
    )


def solution(mesh):
    placed = (
        P(None, ("dp", "shard"), None),
        P(None, ("dp", "shard"), None),
        P(None, ("dp", "shard"), None),
        P("shard", None),
        P("shard", None),
        P("shard"),
        P("shard"),
        P("section", None, None, "shard", None),
        P("section", "shard", None),
        P("section", None, "shard", None),
        P("section", None, "shard", None),
        P("section", None, "shard"),
        P("section", None, "shard"),
    )
    return jax.shard_map(
        body,
        mesh=mesh,
        in_specs=placed,
        out_specs=(
            P("section", None, ("dp", "shard"), None, None),
            P("section", None, ("dp", "shard"), None, None),
            P("shard", ("section", "dp")),
            P("shard", None),
            P("shard"),
            P("shard"),
            P("section", None, None, "shard", None),
            P("section", "shard", None),
            P("section", None, "shard", None),
            P("section", None, "shard", None),
            P("section", None, "shard"),
            P("section", None, "shard"),
        ),
        check_vma=False,
    )
```

profile of v0, /device:TPU:0, one launch (start us, length us, event | category | flops | bytes accessed | tf_op | source)
XLA Modules:
  0.0 1413.6 jit_solution(6123283547579311281)
XLA Ops:
  10.0 13.5 all_gather.76
  49.9 17.1 %all_gather.81 = bf16[1,9,768]{1,0,2:T(2,128)(2,1)S(1)} all-gather(bf16[1,9,192]{1,0,2:T(2,128)(2,1)S(1)} %copy.252), channel_id=1, replica_groups=mesh['section'=2,'dp'=4,'shard'=4] {'shard'}, dimensions={2}, use_global_device_ids=true | all-gather | bytes 17280 | tf_op jit(solution)/shard_map/all_gather | solution.py:314
  70.8 27.7 %all_gather.77 = bf16[512,768]{1,0:T(8,128)(2,1)S(1)} all-gather(bf16[128,768]{1,0:T(8,128)(2,1)S(1)} %copy-done.162), channel_id=1, replica_groups=mesh['section'=2,'dp'=4,'shard'=4] {'shard'}, dimensions={0}, use_global_device_ids=true | all-gather | bytes 983040 | tf_op jit(solution)/shard_map/all_gather | solution.py:315
  100.4 11.7 all-reduce.6
  112.8 33.9 %all_gather.80 = bf16[1,3,4,192,192]{4,2,1,0,3:T(4,128)(2,1)S(1)} all-gather(bf16[1,3,4,48,192]{4,2,1,0,3:T(4,128)(2,1)S(1)} %copy.250), channel_id=1, replica_groups=mesh['section'=2,'dp'=4,'shard'=4] {'shard'}, dimensions={3}, use_global_device_ids=true | all-gather | bytes 1105920 | tf_op jit(solution)/shard_map/all_gather | solution.py:309
  148.7 12.3 slice_reduce_fusion
  162.6 16.8 %all_gather.83 = bf16[1,2,768]{1,0,2:T(2,128)(2,1)S(1)} all-gather(bf16[1,2,192]{1,0,2:T(2,128)(2,1)S(1)} %copy.254), channel_id=1, replica_groups=mesh['section'=2,'dp'=4,'shard'=4] {'shard'}, dimensions={2}, use_global_device_ids=true | all-gather | bytes 3840 | tf_op jit(solution)/shard_map/all_gather | solution.py:313
  210.4 10.5 fusion.190
  283.3 16.3 %fusion.69 = (bf16[256,4,768]{2,0,1:T(8,128)(2,1)S(1)}, f32[256,4,768]{2,0,1:T(8,128)}, bf16[256,4,768]{2,0,1:T(8,128)(2,1)}, f32[256,4,768]{2,0,1:T(8,128)}, f32[4,256,768]{2,1,0:T(8,128)}) fusion(f32[4,768]{1,0:T(4,128)S(1)} %copy-done.254, f32[4,256,768]{2,1,0:T(8,128)S(1)} %fusion.214, bf16[256,4,192]{0,2,1:T(8,128)(2,1)S(1)} %bitcast.1032, ...), kind=kOutput, calls=%fused_computation.125 | convolution fusion | flops 405798912 | bytes 17313792 | tf_op jit(solution)/shard_map/sgi,gio->sgo/dot_general | solution.py:50
  325.2 11.9 all_gather.87
  363.5 13.1 all-gather
  376.6 13.1 all-gather.1
  390.0 16.3 %conditional.7 = (f32[7632,768]{1,0:T(8,128)}, bf16[1024,7632]{1,0:T(8,128)(2,1)}) conditional(s32[]{:T(128)} %convert_element_type.650, () %tuple.79, (bf16[1024,768]{1,0:T(8,128)(2,1)}, s32[2,4,256]{2,0,1:T(2,128)S(1)}, f32[1024]{0:T(1024)S(1)}, f32[1024]{0:T(1024)S(1)}, bf16[7632,768]{1,0:T(8,128)(2,1)}, /*index=5*/s32[7632]{0:T(1024)}) %tuple.83), branch_computations={%region_34.37_spmd, %region_35.40_spmd} | conditional | flops 12035359744 | bytes 121283840 | solution.py:368
  427.8 144.5 %reduce-scatter.24.cloned.1.call-done = bf16[256,768]{1,0:T(8,128)(2,1)} async-done(((bf16[1024,768]{1,0:T(8,128)(2,1)}), bf16[256,768]{1,0:T(8,128)(2,1)}) %reduce-scatter.24.cloned.1.call-update) | async-done | bytes 393232 | tf_op jit(solution)/shard_map/reduce_scatter | solution.py:386
  627.7 33.1 %all-gather.20.cloned.1.call-done = bf16[1024,768]{1,0:T(8,128)(2,1)} async-done(((bf16[256,768]{1,0:T(8,128)(2,1)}), bf16[1024,768]{1,0:T(8,128)(2,1)}) %all-gather.20.cloned.1.call-update) | async-done | bytes 1572880 | tf_op jit(solution)/shard_map/all_gather | solution.py:358
  661.1 13.1 all-gather.2
  674.2 13.1 all-gather.3
  687.5 15.9 %conditional.10 = (f32[7632,768]{1,0:T(8,128)}, bf16[1024,7632]{1,0:T(8,128)(2,1)}) conditional(s32[]{:T(128)} %convert_element_type.650, () %tuple.86, (bf16[1024,768]{1,0:T(8,128)(2,1)}, s32[2,4,256]{2,0,1:T(2,128)S(1)}, f32[1024]{0:T(1024)S(1)}, f32[1024]{0:T(1024)S(1)}, bf16[7632,768]{1,0:T(8,128)(2,1)}, /*index=5*/s32[7632]{0:T(1024)}) %tuple.373), branch_computations={%region_60.63_spmd, %region_61.66_spmd} | conditional | flops 12035359744 | bytes 121283840 | solution.py:368
  716.5 135.7 %collective-permute-done.2 = bf16[256,768]{1,0:T(8,128)(2,1)S(1)} collective-permute-done((bf16[256,768]{1,0:T(8,128)(2,1)S(1)}, bf16[256,768]{1,0:T(8,128)(2,1)S(1)}, u32[]{:S(2)}, u32[]{:S(2)}) %collective-permute-start.2) | collective-permute-done | bytes 393248 | tf_op jit(solution)/shard_map/ppermute | solution.py:19
  852.2 16.0 %reduce-scatter.26.cloned.1.call-done = bf16[256,768]{1,0:T(8,128)(2,1)} async-done(((bf16[1024,768]{1,0:T(8,128)(2,1)}), bf16[256,768]{1,0:T(8,128)(2,1)}) %reduce-scatter.26.cloned.1.call-update) | async-done | bytes 393232 | tf_op jit(solution)/shard_map/reduce_scatter | solution.py:386
  955.9 24.4 %add.744 = f32[7632,768]{1,0:T(8,128)} add(f32[7632,768]{1,0:T(8,128)} %get-tuple-element.302, f32[7632,768]{1,0:T(8,128)} %get-tuple-element.303) | non-fusion elementwise | flops 5861376 | bytes 70336512 | tf_op jit(solution)/shard_map/add | solution.py:376
  990.9 36.4 %all-gather.24.cloned.1.call-done = bf16[1024,768]{1,0:T(8,128)(2,1)} async-done(((bf16[256,768]{1,0:T(8,128)(2,1)}), bf16[1024,768]{1,0:T(8,128)(2,1)}) %all-gather.24.cloned.1.call-update) | async-done | bytes 1572880 | tf_op jit(solution)/shard_map/all_gather | solution.py:440
  1030.7 29.8 %scatter_custom_fusion = f32[7632,768]{1,0:T(8,128)} fusion(f32[7632,768]{1,0:T(8,128)} %add.744, s32[2048]{0:T(1024)S(1)} %bitcast.1139, f32[1024,768]{1,0:T(8,128)} %convert_multiply_fusion, f32[]{:T(128)} %constant.236.clone.1, f32[1024,768]{1,0:T(8,128)S(1)} %convert_multiply_fusion.1), kind=kCustom, calls=%fused_computation.55 | custom fusion | flops 3145728 | bytes 29737472 | tf_op jit(solution)/shard_map/add | solution.py:444
  1060.4 12.8 convert_element_type.709
  1115.7 17.9 %all-reduce.12.cloned.1.call-done = bf16[1,3,4,192,192]{4,2,1,0,3:T(4,128)(2,1)} async-done(((bf16[1,3,4,192,192]{4,2,1,0,3:T(4,128)(2,1)}), bf16[1,3,4,192,192]{4,2,1,0,3:T(4,128)(2,1)}) %all-reduce.12.cloned.1.call-update) | async-done | bytes 884752
  1135.4 29.3 %reduce-scatter.36.cloned.1.call-done = bf16[192,768]{1,0:T(8,128)(2,1)} async-done(((bf16[768,768]{1,0:T(8,128)(2,1)}), bf16[192,768]{1,0:T(8,128)(2,1)}) %reduce-scatter.36.cloned.1.call-update) | async-done | bytes 294928
  1167.0 22.4 %reduce-scatter.28.cloned.1.call-done = bf16[128,768]{1,0:T(8,128)(2,1)} async-done(((bf16[512,768]{1,0:T(8,128)(2,1)}), bf16[128,768]{1,0:T(8,128)(2,1)}) %reduce-scatter.28.cloned.1.call-update) | async-done | bytes 196624 | tf_op jit(solution)/shard_map/reduce_scatter | solution.py:466
  1189.4 31.2 %reduce-scatter.32.cloned.1.call-done = bf16[1,4,48,768]{3,2,1,0:T(8,128)(2,1)} async-done(((bf16[1,4,192,768]{3,2,1,0:T(8,128)(2,1)}), bf16[1,4,48,768]{3,2,1,0:T(8,128)(2,1)}) %reduce-scatter.32.cloned.1.call-update) | async-done | bytes 294928 | tf_op jit(solution)/shard_map/reduce_scatter | solution.py:454
  1220.6 30.7 %reduce-scatter.30.cloned.1.call-done = bf16[1,192,768]{2,1,0:T(8,128)(2,1)} async-done(((bf16[1,768,768]{2,1,0:T(8,128)(2,1)}), bf16[1,192,768]{2,1,0:T(8,128)(2,1)}) %reduce-scatter.30.cloned.1.call-update) | async-done | bytes 294928 | tf_op jit(solution)/shard_map/reduce_scatter | solution.py:451
  1251.4 75.9 %collective-permute-done.4 = bf16[7632,768]{1,0:T(8,128)(2,1)} collective-permute-done((bf16[7632,768]{1,0:T(8,128)(2,1)}, bf16[7632,768]{1,0:T(8,128)(2,1)}, u32[]{:S(2)}, u32[]{:S(2)}) %collective-permute-start.4) | collective-permute-done | bytes 11722784 | tf_op jit(solution)/shard_map/ppermute | solution.py:32
  1360.2 10.6 all-reduce.7
  1385.5 15.2 %reduce-scatter.34.cloned.1.call-done = bf16[96,7632]{1,0:T(8,128)(2,1)} async-done(((bf16[384,7632]{1,0:T(8,128)(2,1)}), bf16[96,7632]{1,0:T(8,128)(2,1)}) %reduce-scatter.34.cloned.1.call-update) | async-done | bytes 1465360
  (1025 shorter events, 502.7 us)
Async XLA Ops:
  7.2 181.3 %all-gather.16.cloned.1.call-start = ((), (), s32[]{:S(2)}) async-start(), calls=%async_computation.14 | async-start | bytes 1966080 | tf_op jit(solution)/shard_map/all_gather | solution.py:312
  9.3 182.1 %reduce-scatter.20.cloned.1.call-start = ((), (), s32[]{:S(2)}) async-start(), calls=%async_computation.11 | async-start | bytes 1966080 | tf_op jit(solution)/shard_map/reduce_scatter | solution.py:341
  35.7 170.6 %all-gather.12.cloned.1.call-start = ((), (), s32[]{:S(2)}) async-start(), calls=%async_computation.12 | async-start | bytes 1474560 | tf_op jit(solution)/shard_map/all_gather | solution.py:310
  36.4 174.0 %all-gather.14.cloned.1.call-start = ((), (), s32[]{:S(2)}) async-start(), calls=%async_computation.13 | async-start | bytes 1474560 | tf_op jit(solution)/shard_map/all_gather | solution.py:311
  37.0 193.0 %reduce-scatter.22.cloned.1.call-start = ((), (), s32[]{:S(2)}) async-start(), calls=%async_computation.15 | async-start | bytes 1966080 | tf_op jit(solution)/shard_map/reduce_scatter | solution.py:341
  49.1 314.4 %all-gather.18.cloned.1.call-start = ((), (), s32[]{:S(2)}) async-start(), calls=%async_computation.16 | async-start | bytes 1966080 | tf_op jit(solution)/shard_map/all_gather | solution.py:358
  112.0 235.9 %copy-start.158 = (f32[768]{0:T(1024)}, f32[768]{0:T(1024)S(1)}, u32[]{:S(2)}) copy-start(f32[768]{0:T(1024)S(1)} %convert_element_type.604) | copy-start | bytes 9220
  147.7 203.2 %copy-start = (bf16[1,3,4,192,192]{3,4,1,2,0:T(8,128)(2,1)}, bf16[1,3,4,192,192]{3,4,1,2,0:T(8,128)(2,1)S(1)}, u32[]{:S(2)}) copy-start(bf16[1,3,4,192,192]{3,4,1,2,0:T(8,128)(2,1)S(1)} %copy.251) | copy-start | bytes 2654212
  225.2 9.2 collective-permute-start
  325.1 247.2 %reduce-scatter.24.cloned.1.call-start = ((), (), s32[]{:S(2)}) async-start(), calls=%async_computation.17 | async-start | bytes 1966080 | tf_op jit(solution)/shard_map/reduce_scatter | solution.py:386
  337.7 10.2 collective-permute-start.1
  407.6 253.2 %all-gather.20.cloned.1.call-start = ((), (), s32[]{:S(2)}) async-start(), calls=%async_computation.18 | async-start | bytes 1966080 | tf_op jit(solution)/shard_map/all_gather | solution.py:358
  418.1 201.0 %copy-start.12 = (f32[256,768]{1,0:T(8,128)}, f32[256,768]{1,0:T(8,128)S(1)}, u32[]{:S(2)}) copy-start(f32[256,768]{1,0:T(8,128)S(1)} %get-tuple-element.699) | copy-start | bytes 2359300
  418.1 170.2 %copy-start.194 = (f32[256]{0:T(256)}, f32[256]{0:T(256)S(1)}, u32[]{:S(2)}) copy-start(f32[256]{0:T(256)S(1)} %broadcast_multiply_fusion.3) | copy-start | bytes 3076
  624.7 243.6 %reduce-scatter.26.cloned.1.call-start = ((), (), s32[]{:S(2)}) async-start(), calls=%async_computation.19 | async-start | bytes 1966080 | tf_op jit(solution)/shard_map/reduce_scatter | solution.py:386
  704.9 284.1 %all-gather.22.cloned.1.call-start = ((), (), s32[]{:S(2)}) async-start(), calls=%async_computation.20 | async-start | bytes 1966080 | tf_op jit(solution)/shard_map/all_gather | solution.py:440
  714.7 137.6 %collective-permute-start.2 = (bf16[256,768]{1,0:T(8,128)(2,1)S(1)}, bf16[256,768]{1,0:T(8,128)(2,1)S(1)}, u32[]{:S(2)}, u32[]{:S(2)}) collective-permute-start(bf16[256,768]{1,0:T(8,128)(2,1)S(1)} %fusion.304), channel_id=1, source_target_pairs={{16,0},{17,1},{18,2},{19,3},{20,4},{21,5},{22,6},{23,7},{24,8},{25... | collective-permute-start | bytes 1179656 | tf_op jit(solution)/shard_map/ppermute | solution.py:19
  904.2 12.6 collective-permute-start.3
  953.5 73.7 %all-gather.24.cloned.1.call-start = ((), (), s32[]{:S(2)}) async-start(), calls=%async_computation.21 | async-start | bytes 1966080 | tf_op jit(solution)/shard_map/all_gather | solution.py:440
  955.6 178.0 %all-reduce.12.cloned.1.call-start = ((), (), s32[]{:S(2)}) async-start(), calls=%async_computation.29 | async-start | bytes 2359296
  1073.3 253.9 %collective-permute-start.4 = (bf16[7632,768]{1,0:T(8,128)(2,1)}, bf16[7632,768]{1,0:T(8,128)(2,1)}, u32[]{:S(2)}, u32[]{:S(2)}) collective-permute-start(bf16[7632,768]{1,0:T(8,128)(2,1)} %convert_element_type.709), channel_id=1, source_target_pairs={{0,16},{16,0},{1,17},{17,1},{2,18},{18,2},{3,19},{19,3},{4,20},{20... | collective-permute-start | bytes 35168264 | tf_op jit(solution)/shard_map/ppermute | solution.py:32
  1079.4 85.2 %reduce-scatter.36.cloned.1.call-start = ((), (), s32[]{:S(2)}) async-start(), calls=%async_computation.26 | async-start | bytes 1474560
  1088.9 100.5 %reduce-scatter.28.cloned.1.call-start = ((), (), s32[]{:S(2)}) async-start(), calls=%async_computation.22 | async-start | bytes 983040 | tf_op jit(solution)/shard_map/reduce_scatter | solution.py:466
  1099.6 121.0 %reduce-scatter.32.cloned.1.call-start = ((), (), s32[]{:S(2)}) async-start(), calls=%async_computation.24 | async-start | bytes 1474560 | tf_op jit(solution)/shard_map/reduce_scatter | solution.py:454
  1104.3 147.0 %reduce-scatter.30.cloned.1.call-start = ((), (), s32[]{:S(2)}) async-start(), calls=%async_computation.23 | async-start | bytes 1474560 | tf_op jit(solution)/shard_map/reduce_scatter | solution.py:451
  1108.0 249.4 %reduce-scatter.38.cloned.1.call-start = ((), (), s32[]{:S(2)}) async-start(), calls=%async_computation.27 | async-start | bytes 245760
  1113.2 245.3 %reduce-scatter.40.cloned.1.call-start = ((), (), s32[]{:S(2)}) async-start(), calls=%async_computation.28 | async-start | bytes 245760
  1115.7 260.2 %all-reduce.14.cloned.1.call-start = ((), (), s32[]{:S(2)}) async-start(), calls=%async_computation.30 | async-start | bytes 2949120 | tf_op jit(solution)/shard_map/psum | solution.py:477
  1251.3 149.4 %reduce-scatter.34.cloned.1.call-start = ((), (), s32[]{:S(2)}) async-start(), calls=%async_computation.25 | async-start | bytes 7372800
  1370.8 4.5 collective-permute-start.7
  1373.7 3.8 collective-permute-start.6
  1375.9 8.8 collective-permute-start.5
  (296 other events, 3533.7 us)
Sparse Core Ops, SparseCore 0:
  10.2 39.7 all-gather.15
  52.9 47.9 reduce-scatter.19
  102.4 43.4 all-gather.11
  147.3 34.7 all-gather.13
  184.8 34.1 reduce-scatter.21
  325.3 38.1 all-gather.17
  407.8 164.4 reduce-scatter.23
  624.8 36.0 all-gather.19
  705.1 163.1 reduce-scatter.25
  953.7 35.3 all-gather.21
  991.2 35.9 all-gather.23
  1079.5 53.9 all-reduce.11
  1135.9 28.7 reduce-scatter.35
  1167.4 21.9 reduce-scatter.27
  1192.2 28.4 reduce-scatter.31
  1223.4 27.8 reduce-scatter.29
  1254.0 18.0 reduce-scatter.37
  1274.9 17.5 reduce-scatter.39
  1296.3 40.1 all-reduce.13
  1345.7 54.9 reduce-scatter.33
where the time goes:
time: 1420 us; the launch traced here: 1410 us
  waiting for transfers between devices  621 us (44%)
  blocking collectives  205 us (14%)
  local copies, waits for them, and re-layouts  189 us (13%)
  other arithmetic  182 us (13%)
  matrix products  168 us (12%)
  starting transfers between devices  25.9 us (2%)
  between operations  20.7 us (1%)
    reduce_scatter x2, waiting for transfers between devices, body(): lax.psum_scatter(project(jnp.int32(0), seq_len * lax.axis_size('shard'))....  160 us
    ppermute x4, waiting for transfers between devices, shifted_2(): return lax.ppermute(block, axis, route)  152 us
    ppermute x4, waiting for transfers between devices, passed_along(): lax.ppermute(shard, axis, [(i, (i + by) % size) for i in range(size)])  75.9 us
    unnamed x25, waiting for transfers between devices  63.9 us
    dot_general x9, matrix products, grouped(): jnp.einsum('sgi,gio->sgo', split, weight, preferred_element_type=jnp.floa...  61.2 us
    unnamed x646, local copies, waits for them, and re-layouts  60.1 us
    all_gather x4, blocking collectives, joined(): pieces = jax.tree.map(lambda part: lax.all_gather(part, axis), value)  52.5 us
    all_gather x2, waiting for transfers between devices, body(): lax.all_gather(sum_grad.astype(jnp.bfloat16), 'shard', axis=0, tiled=True)  45.1 us
  transfers between devices with their start and end apart: 28, of which 17 were waited for; matrix products, arithmetic and copies ran while one was open for 16% of the time, Pallas kernels for 0%

commit v1 on v0

v1 whole, which is shorter than its diff:
```python
import math

import jax
import jax.numpy as jnp
from jax import lax
from jax.experimental import pallas as pl
from jax.experimental.pallas import tpu as pltpu
from jax.sharding import PartitionSpec as P

HEADS = 12
EPSILON = 1e-06
MASKED = -1000000000.0
F32 = jnp.float32
BF16 = jnp.bfloat16
MIB = 1 << 20


def nn(a, b):
    return jnp.dot(a, b, preferred_element_type=F32)


def nt(a, b):
    return lax.dot_general(a, b, (((1,), (1,)), ((), ())), preferred_element_type=F32)


def tn(a, b):
    return lax.dot_general(a, b, (((0,), (0,)), ((), ())), preferred_element_type=F32)


def iota(shape, axis):
    return lax.broadcasted_iota(jnp.int32, shape, axis)


def group_of(index, width, count):
    total = jnp.zeros(index.shape, jnp.int32)
    for step in range(1, count):
        total = total + (index >= step * width).astype(jnp.int32)
    return total


def normed(value):
    centered = value - jnp.mean(value, axis=-1, keepdims=True)
    scale = lax.rsqrt(jnp.mean(centered * centered, axis=-1, keepdims=True) + EPSILON)
    return centered * scale, scale


def norm_back(grad, unit, scale, gain):
    inner = grad * gain
    first = jnp.mean(inner, axis=-1, keepdims=True)
    second = jnp.mean(inner * unit, axis=-1, keepdims=True)
    return scale * (inner - first - unit * second)


def col_sum(value):
    return jnp.sum(value, axis=0, keepdims=True)


def call(kernel, outs, ins, specs=None, scratch=(), limit=56, flops=0, moved=0, grid=None, out_specs=None, name=None):
    vmem = pl.BlockSpec(memory_space=pltpu.VMEM)
    extra = {} if grid is None else {"grid": grid}
    return pl.pallas_call(
        kernel,
        out_shape=outs,
        in_specs=[vmem if s is None else s for s in (specs or [None] * len(ins))],
        out_specs=out_specs if out_specs is not None else [vmem] * len(outs),
        scratch_shapes=list(scratch),
        compiler_params=pltpu.CompilerParams(vmem_limit_bytes=limit * MIB),
        cost_estimate=pl.CostEstimate(flops=flops, bytes_accessed=moved, transcendentals=0),
        name=name,
        **extra,
    )(*ins)


def like(shape, dtype):
    return jax.ShapeDtypeStruct(shape, dtype)


def turned(block, axis, by):
    size = lax.axis_size(axis)
    return lax.ppermute(block, axis, [(i, (i + by) % size) for i in range(size)])


def crossed(block, axis, bit):
    return lax.ppermute(block, axis, [(i, i ^ bit) for i in range(lax.axis_size(axis))])


def ring_gather(block, axis):
    half = block.shape[0] // 2
    before = turned(block, axis, 1)
    after = turned(block, axis, -1)
    return before, after, turned(before[:half], axis, 1), turned(after[half:], axis, -1)


class Sizes:
    def __init__(self, qkv, out, shards, pos_rows):
        _, _, groups, part, width = qkv
        self.shards, self.groups, self.gw, self.gi = shards, groups, width, part
        self.d = out[2]
        self.ds = out[1]
        self.gf = self.d // shards
        self.at_qkv = self.ds
        self.at_small = self.ds + 3 * part
        self.at_out = groups * part
        self.rows = self.at_out + self.gf
        self.extra = pos_rows // 2 + 16


def pack_weights(z, qkv, out, fin, fout, gains, biases, egain, eshift):
    def kernel(qkv_ref, out_ref, fin_ref, fout_ref, gain_ref, bias_ref, eg_ref, es_ref, o_ref):
        core = lax.axis_index("dp") % 2
        shard = lax.axis_index("shard")

        def spread(pieces):
            return jnp.concatenate([piece.astype(F32) for piece in pieces], axis=1)

        @pl.when(core == 0)
        def _():
            o_ref[0 : z.ds] = out_ref[...]
            for c in range(3):
                row = z.at_qkv + c * z.gi
                o_ref[row : row + z.gi] = spread([qkv_ref[c, g] for g in range(z.groups)]).astype(BF16)
            tall = jnp.concatenate(
                [gain_ref[...].astype(F32), bias_ref[...].astype(F32), eg_ref[...].astype(F32), es_ref[...].astype(F32), jnp.zeros((3, z.ds), F32)],
                axis=0,
            )
            wide = jnp.concatenate([tall] * z.shards, axis=1)
            lane = group_of(iota(wide.shape, 1), z.ds, z.shards)
            o_ref[z.at_small : z.at_small + 16] = jnp.where(lane == shard, wide, 0.0).astype(BF16)
            o_ref[z.at_small + 16 : z.rows] = jnp.zeros((z.rows - z.at_small - 16, z.d), BF16)

        @pl.when(core == 1)
        def _():
            o_ref[0 : z.at_out] = fin_ref[...].reshape(z.at_out, z.d)
            o_ref[z.at_out : z.rows] = spread([fout_ref[g] for g in range(z.groups)]).astype(BF16)

    return call(kernel, [like((z.rows, z.d), BF16)], (qkv, out, fin, fout, gains, biases, egain, eshift), name="pack")[0]


def piece_specs():
    return [pl.BlockSpec(memory_space=pl.ANY)] * 10


def piece_copies(z, refs, w_ref, sems):
    core = lax.axis_index("dp") % 2
    shard = lax.axis_index("shard")
    half = z.rows // 2
    copies = []
    for side in range(2):
        own, before, after, far_a, far_b = refs[5 * side : 5 * side + 5]
        place = core if side == 0 else 1 - core
        for ref, by, row, many in ((own, 0, 0, z.rows), (before, 3, 0, z.rows), (after, 1, 0, z.rows), (far_a, 2, 0, half), (far_b, 2, half, half)):
            index = (shard + by) % z.shards
            copies.append(
                pltpu.make_async_copy(ref, w_ref.at[place, index, pl.ds(row, many)], sems.at[len(copies)])
            )
    return copies


class Weights:
    def __init__(self, z, w_ref):
        self.z, self.w = z, w_ref

    def out(self):
        z = self.z
        return self.w[0, :, 0 : z.ds, :].reshape(z.d, z.d)

    def small(self):
        z = self.z
        return sum(self.w[0, h, z.at_small : z.at_small + 16, :].astype(F32) for h in range(z.shards))

    def proj(self, c):
        z = self.z
        row = z.at_qkv + c * z.gi
        dense = self.w[0, :, row : row + z.gi, :].reshape(z.gw, z.d)
        tall = jnp.concatenate([dense] * z.groups, axis=0)
        keep = group_of(iota(tall.shape, 0), z.gw, z.groups) == group_of(iota(tall.shape, 1), z.gw, z.groups)
        return jnp.where(keep, tall, jnp.zeros_like(tall))

    def fin(self, g):
        z = self.z
        dense = self.w[1, :, g * z.gi : (g + 1) * z.gi, :].reshape(z.gw, z.d)
        blank = jnp.zeros_like(dense)
        return jnp.concatenate([dense, blank] if g % 2 == 0 else [blank, dense], axis=0)

    def fout(self, g):
        z = self.z
        at = (g // 2) * 2 * z.gw
        pair = self.w[1, :, z.at_out : z.rows, at : at + 2 * z.gw].reshape(z.d, 2 * z.gw)
        keep = (iota(pair.shape, 1) >= z.gw) == (g % 2 == 1)
        return jnp.where(keep, pair, jnp.zeros_like(pair))


def embed_parts(picked, inside, seg_col, seg_row, pos_table):
    count, seq = seg_row.shape
    width = picked.shape[1]
    half = seq // 2
    rows = pos_table.shape[0]

    def kernel(p_ref, i_ref, c_ref, r_ref, t_ref, c0, c1, c2a, c2b, c3):
        start = lax.axis_index("shard") * rows
        for k in range(count):
            span = slice(k * seq, (k + 1) * seq)
            same = c_ref[span] == r_ref[k : k + 1]
            earlier = iota((seq, seq), 1) < iota((seq, seq), 0)
            place = jnp.sum(jnp.where(same & earlier, 1.0, 0.0), axis=1, keepdims=True).astype(jnp.int32) - start
            spot = (iota((seq, rows), 1) == place).astype(BF16)
            word = jnp.where(i_ref[span] > 0, p_ref[span].astype(F32), 0.0)
            total = (word + nn(spot, t_ref[...])).astype(BF16)
            if k == 2:
                c2a[...] = total[:half]
                c2b[...] = total[half:]
            else:
                (c0, c1, None, c3)[k][...] = total

    full, part = like((seq, width), BF16), like((half, width), BF16)
    return call(kernel, [full, full, part, part, full], (picked, inside, seg_col, seg_row, pos_table), name="embed_parts")


def layer_forward(z, pieces, seg_col, seg_row, first, words=None, layer_in=None):
    seq = seg_col.shape[0]
    d, wide = z.d, z.groups * z.d
    names = ["out", "q", "k", "v", "p", "att", "n1", "mid", "act", "slope", "n2", "stats"]
    shapes = [
        like((seq, d), BF16),
        like((seq, d), BF16),
        like((seq, d), BF16),
        like((seq, d), BF16),
        like((HEADS, seq, seq), BF16),
        like((seq, d), BF16),
        like((seq, d), F32),
        like((seq, d), BF16),
        like((seq, wide), BF16),
        like((seq, wide), BF16),
        like((seq, d), F32),
        like((seq, 128), F32),
    ]
    if first:
        names += ["x", "n0"]
        shapes += [like((seq, d), BF16), like((seq, d), F32)]
    head = d // HEADS
    inputs = list(words) if first else [layer_in]

    def kernel(*refs):
        piece_refs, refs = refs[:10], refs[10:]
        col_ref, row_ref, refs = refs[0], refs[1], refs[2:]
        in_refs, refs = refs[: len(inputs)], refs[len(inputs) :]
        o = dict(zip(names, refs))
        w_ref, sems = refs[len(names)], refs[len(names) + 1]
        copies = piece_copies(z, piece_refs, w_ref, sems)
        for copy in copies:
            copy.start()
        for copy in copies:
            copy.wait()
        w = Weights(z, w_ref)
        small = w.small()
        if first:
            embed_sum = sum(ref[...].astype(F32) for ref in in_refs)
            unit, r0 = normed(embed_sum)
            o["n0"][...] = unit
            x = unit * small[11:12] + small[12:13]
            x_low = x.astype(BF16)
            o["x"][...] = x_low
        else:
            r0 = jnp.zeros((seq, 1), F32)
            x_low = in_refs[0][...]
            x = x_low.astype(F32)
        q = (nn(x_low, w.proj(0)).astype(BF16).astype(F32) * (1.0 / math.sqrt(head))).astype(BF16)
        k = nn(x_low, w.proj(1)).astype(BF16)
        v = (nn(x_low, w.proj(2)) + small[2:3]).astype(BF16)
        o["q"][...], o["k"][...], o["v"][...] = q, k, v
        same = col_ref[...] == row_ref[...]
        second = iota((seq, 128), 1) >= head
        tiles = []
        for t in range(d // 128):
            lanes = slice(t * 128, (t + 1) * 128)
            q_t, k_t, v_t = q[:, lanes], k[:, lanes], v[:, lanes]
            results = []
            for j in range(2):
                picked = jnp.where(second == (j == 1), q_t, jnp.zeros_like(q_t))
                scores = jnp.where(same, nt(picked, k_t), MASKED)
                scores = jnp.exp(scores - jnp.max(scores, axis=-1, keepdims=True))
                probs = (scores * (1.0 / jnp.sum(scores, axis=-1, keepdims=True))).astype(BF16)
                o["p"][2 * t + j] = probs
                results.append(nn(probs, v_t))
            tiles.append(jnp.where(second, results[1], results[0]).astype(BF16))
        attended = jnp.concatenate(tiles, axis=1)
        o["att"][...] = attended
        unit, r1 = normed(x + (nn(attended, w.out()) + small[3:4]))
        o["n1"][...] = unit
        middle = unit * small[0:1] + small[4:5]
        middle_low = middle.astype(BF16)
        o["mid"][...] = middle_low
        back = [None] * (z.groups // 2)
        for g in range(z.groups):
            pair = slice((g // 2) * 2 * z.gw, (g // 2 + 1) * 2 * z.gw)
            span = slice(g * d, (g + 1) * d)
            pre = nn(middle_low[:, pair], w.fin(g)) + small[5 + g : 6 + g]
            half = 0.5 + 0.5 * lax.erf(pre * math.sqrt(0.5))
            slope = half + pre * (jnp.exp(-0.5 * pre * pre) * (1.0 / math.sqrt(2.0 * math.pi)))
            active = (pre * half).astype(BF16)
            o["act"][:, span] = active
            o["slope"][:, span] = slope.astype(BF16)
            added = nn(active, w.fout(g))
            back[g // 2] = added if back[g // 2] is None else back[g // 2] + added
        unit, r2 = normed(middle + (jnp.concatenate(back, axis=1) + small[9:10]))
        o["n2"][...] = unit
        o["out"][...] = (unit * small[1:2] + small[10:11]).astype(BF16)
        lane = iota((seq, 128), 1)
        o["stats"][...] = jnp.where(lane == 0, r0, jnp.where(lane == 1, r1, r2))

    outs = call(
        kernel,
        shapes,
        (*pieces, seg_col, seg_row, *inputs),
        specs=piece_specs() + [None] * (2 + len(inputs)),
        scratch=[pltpu.VMEM((2, z.shards, z.rows, d), BF16), pltpu.SemaphoreType.DMA((10,))],
        flops=3 * 10**9,
        moved=16 * MIB,
        name="layer_first" if first else "layer_second",
    )
    return dict(zip(names, outs))


def layer_backward(z, pieces, state, out_grad, first, seg_col=None, seg_row=None, pos_rows=0):
    seq, d = state["q"].shape
    wide = z.groups * d
    head = d // HEADS
    keys = ["x", "q", "k", "v", "p", "att", "n1", "mid", "act", "slope", "n2", "stats"] + (["n0"] if first else [])
    inputs = [state[key] for key in keys] + [out_grad] + ([seg_col, seg_row] if first else [])
    rows = z.rows + (z.extra if first else 0)
    outs = [like((seq, d), F32), like((2, z.shards, rows, d), BF16)]
    if first:
        outs.append(like((d, seq), BF16))

    def kernel(*refs):
        piece_refs, refs = refs[:10], refs[10:]
        s = dict(zip(keys, refs))
        refs = refs[len(keys) :]
        dy_ref, refs = refs[0], refs[1:]
        if first:
            col_ref, row_ref, refs = refs[0], refs[1], refs[2:]
        dx_ref, g_ref = refs[0], refs[1]
        de_ref = refs[2] if first else None
        w_ref, sems = refs[len(outs)], refs[len(outs) + 1]
        core = lax.axis_index("dp") % 2
        keep0 = core
        keep1 = 1 - core
        copies = piece_copies(z, piece_refs, w_ref, sems)
        for copy in copies:
            copy.start()
        for copy in copies:
            copy.wait()
        w = Weights(z, w_ref)
        small = w.small()
        stats = s["stats"][...]
        r0, r1, r2 = stats[:, 0:1], stats[:, 1:2], stats[:, 2:3]
        dy = dy_ref[...].astype(F32)
        n2 = s["n2"][...]
        gain_two, shift_two = col_sum(dy * n2), col_sum(dy)
        d_final = norm_back(dy, n2, r2, small[1:2])
        d_ffn = d_final.astype(BF16)
        ffn_shift = col_sum(d_ffn.astype(F32))
        middle_t = s["mid"][...].T
        pre_shift = []
        pair_back = [None] * (z.groups // 2)
        for p in range(z.groups // 2):
            lanes = slice(p * 2 * z.gw, (p + 1) * 2 * z.gw)
            out_pair = d_ffn[:, lanes]
            back_pair = []
            for g in (2 * p, 2 * p + 1):
                span = slice(g * d, (g + 1) * d)
                d_pre = (nt(out_pair, w.fout(g)) * s["slope"][:, span].astype(F32)).astype(BF16)
                pre_shift.append(col_sum(d_pre.astype(F32)))
                back_pair.append(tn(s["act"][:, span], out_pair))
                grad_in = nn(middle_t[g * z.gw : (g + 1) * z.gw], d_pre)
                g_ref[keep1, :, g * z.gi : (g + 1) * z.gi, :] = grad_in.astype(BF16).reshape(z.shards, z.gi, d)
                added = nt(d_pre, w.fin(g))
                pair_back[p] = added if pair_back[p] is None else pair_back[p] + added
            odd = iota(back_pair[0].shape, 1) >= z.gw
            both = jnp.where(odd, back_pair[1], back_pair[0]).astype(BF16)
            g_ref[keep1, :, z.at_out : z.rows, lanes] = both.reshape(z.shards, z.gf, 2 * z.gw)
        d_middle = d_final + jnp.concatenate(pair_back, axis=1)
        n1 = s["n1"][...]
        gain_one, shift_one = col_sum(d_middle * n1), col_sum(d_middle)
        d_mid = norm_back(d_middle, n1, r1, small[0:1])
        d_branch = d_mid.astype(BF16)
        branch_shift = col_sum(d_branch.astype(F32))
        attended = s["att"][...]
        g_ref[keep0, :, 0 : z.ds, :] = tn(attended, d_branch).astype(BF16).reshape(z.shards, z.ds, d)
        d_att = nt(d_branch, w.out()).astype(BF16)
        second = iota((seq, 128), 1) >= head
        scale = 1.0 / math.sqrt(head)
        dq, dk, dv = [], [], []
        for t in range(d // 128):
            lanes = slice(t * 128, (t + 1) * 128)
            q_t, k_t, v_t, a_t = s["q"][:, lanes], s["k"][:, lanes], s["v"][:, lanes], d_att[:, lanes]
            parts = []
            for j in range(2):
                a_j = jnp.where(second == (j == 1), a_t, jnp.zeros_like(a_t))
                probs_low = s["p"][2 * t + j]
                probs = probs_low.astype(F32)
                d_probs = nt(a_j, v_t)
                inner = jnp.sum(probs * d_probs, axis=-1, keepdims=True)
                d_scores = (probs * (d_probs - inner)).astype(BF16)
                parts.append((nn(d_scores, k_t), tn(d_scores, q_t), tn(probs_low, a_t)))
            dq.append((jnp.where(second, parts[1][0], parts[0][0]) * scale).astype(BF16))
            dk.append(jnp.where(second, parts[1][1], parts[0][1]).astype(BF16))
            dv.append(jnp.where(second, parts[1][2], parts[0][2]).astype(BF16))
        value_shift = col_sum(jnp.concatenate(dv, axis=1).astype(F32))
        x_t = s["x"][...].T
        d_in = d_mid
        for c, parts in enumerate((dq, dk, dv)):
            d_c = jnp.concatenate(parts, axis=1)
            full = nn(x_t, d_c)
            lane = group_of(iota((z.gw, d), 1), z.gw, z.groups)
            grad = full[0 : z.gw]
            for g in range(1, z.groups):
                grad = jnp.where(lane == g, full[g * z.gw : (g + 1) * z.gw], grad)
            row = z.at_qkv + c * z.gi
            g_ref[keep0, :, row : row + z.gi, :] = grad.astype(BF16).reshape(z.shards, z.gi, d)
            d_in = d_in + nt(d_c, w.proj(c))
        dx_ref[...] = d_in
        small_grads = jnp.concatenate(
            [gain_one, gain_two, value_shift, branch_shift, shift_one, *pre_shift, ffn_shift, shift_two, jnp.zeros((5, d), F32)], axis=0
        ).astype(BF16)
        blank = jnp.zeros((z.rows - z.at_small - 16, d), BF16)
        for h in range(z.shards):
            g_ref[keep0, h, z.at_small : z.at_small + 16, :] = small_grads
            g_ref[keep0, h, z.at_small + 16 : z.rows, :] = blank
        if first:
            n0 = s["n0"][...]
            embed_grads = jnp.concatenate([col_sum(d_in * n0), col_sum(d_in), jnp.zeros((14, d), F32)], axis=0).astype(BF16)
            d_embed = norm_back(d_in, n0, r0, small[11:12])
            d_embed_low = d_embed.astype(BF16)
            de_ref[...] = d_embed.T.astype(BF16)
            same = col_ref[...] == row_ref[...]
            later = iota((seq, seq), 0) < iota((seq, seq), 1)
            place = jnp.sum(jnp.where(same & later, 1.0, 0.0), axis=0, keepdims=True).astype(jnp.int32)
            spot = (iota((pos_rows, seq), 0) == place).astype(BF16)
            pos_grad = nn(spot, d_embed_low).astype(BF16)
            half = pos_rows // 2
            for side, place in enumerate((keep0, keep1)):
                for h in range(z.shards):
                    part = pos_grad[side * half : (side + 1) * half]
                    g_ref[place, h, z.rows : z.rows + half, :] = part if h == 0 else jnp.zeros_like(part)
                    g_ref[place, h, z.rows + half : z.rows + half + 16, :] = embed_grads

    return call(
        kernel,
        outs,
        (*pieces, *inputs),
        specs=piece_specs() + [None] * len(inputs),
        scratch=[pltpu.VMEM((2, z.shards, z.rows, d), BF16), pltpu.SemaphoreType.DMA((10,))],
        flops=8 * 10**9,
        moved=20 * MIB,
        limit=60,
        name="layer_first_back" if first else "layer_second_back",
    )


def head_forward(rows, table):
    count, d = rows.shape
    vocab = table.shape[0]
    tiles = 6
    block = vocab // tiles
    chunk = 256

    def kernel(x_ref, w_ref, ctx_ref, lse_ref, m_ref, s_ref, acc_ref):
        step = pl.program_id(0)

        @pl.when(step == 0)
        def _():
            m_ref[...] = jnp.full(m_ref.shape, -1e30, F32)
            s_ref[...] = jnp.zeros(s_ref.shape, F32)
            acc_ref[...] = jnp.zeros(acc_ref.shape, F32)

        w = w_ref[...]
        for r in range(count // chunk):
            span = slice(r * chunk, (r + 1) * chunk)
            logits = nt(x_ref[span], w)
            old = m_ref[span]
            new = jnp.maximum(old, jnp.max(logits, axis=-1, keepdims=True))
            keep = jnp.exp(old - new)
            part = jnp.exp(logits - new)
            s_ref[span] = s_ref[span] * keep + jnp.sum(part, axis=-1, keepdims=True)
            acc_ref[span] = acc_ref[span] * keep + nn(part.astype(BF16), w)
            m_ref[span] = new

        @pl.when(step == tiles - 1)
        def _():
            total = s_ref[...]
            ctx_ref[...] = acc_ref[...] * (1.0 / total)
            lse = m_ref[...] + jnp.log(total)
            lse_ref[...] = jnp.broadcast_to(lse, (count, 128)).T[0:8]

    fixed = lambda i: (0, 0)
    return call(
        kernel,
        [like((count, d), F32), like((8, count), F32)],
        (rows, table),
        specs=[pl.BlockSpec((count, d), fixed), pl.BlockSpec((block, d), lambda i: (i, 0))],
        out_specs=[pl.BlockSpec((count, d), fixed), pl.BlockSpec((8, count), fixed)],
        scratch=[pltpu.VMEM((count, 1), F32), pltpu.VMEM((count, 1), F32), pltpu.VMEM((count, d), F32)],
        grid=(tiles,),
        flops=4 * count * vocab * d,
        moved=20 * MIB,
        name="head_forward",
    )


def head_combine(seq, ctx, picked, inside, lses):
    count, d = ctx.shape
    shards = count // seq

    def kernel(ctx_ref, p_ref, i_ref, a_ref, b_ref, c_ref, e_ref, out_ref, lse_ref):
        shard = lax.axis_index("shard")
        parts = (a_ref, b_ref, c_ref, e_ref)
        for k in range(shards):
            rows = [parts[m][:, ((k - m) % shards) * seq : ((k - m) % shards + 1) * seq] for m in range(shards)]
            top = rows[0]
            for row in rows[1:]:
                top = jnp.maximum(top, row)
            total = top + jnp.log(sum(jnp.exp(row - top) for row in rows))
            whole = jnp.broadcast_to(total[0:1], (128, seq)).T
            own = jnp.broadcast_to(rows[0][0:1], (128, seq)).T
            span = slice(k * seq, (k + 1) * seq)
            lse_ref[span] = whole[:, 0:1]
            weight = jnp.exp(own[:, 0:1] - whole[:, 0:1])
            hit = jnp.where(i_ref[span] > 0, p_ref[span].astype(F32), 0.0)
            target = pl.multiple_of(((shard + k) % shards) * seq, seq)
            out_ref[pl.ds(target, seq), :] = (ctx_ref[span] * weight - hit).astype(BF16)

    return call(kernel, [like((count, d), BF16), like((count, 1), F32)], (ctx, picked, inside, *lses), moved=9 * MIB, name="head_combine")


def head_table(rows, table, lse, targets):
    count, d = rows.shape
    vocab = table.shape[0]
    block = 1280
    tiles = pl.cdiv(vocab, block)
    chunk = 256

    def kernel(x_ref, w_ref, lse_ref, t_ref, o_ref, xt_ref, p_ref):
        step = pl.program_id(0)

        @pl.when(step == 0)
        def _():
            xt_ref[...] = x_ref[...].T

        w = w_ref[...]
        for r in range(count // chunk):
            span = slice(r * chunk, (r + 1) * chunk)
            logits = nt(x_ref[span], w)
            hit = iota(logits.shape, 1) == t_ref[span] - step * block
            p_ref[span] = (jnp.exp(logits - lse_ref[span]) - jnp.where(hit, 1.0, 0.0)).astype(BF16)
        o_ref[...] = nn(xt_ref[...], p_ref[...]).astype(BF16)

    fixed = lambda i: (0, 0)
    return call(
        kernel,
        [like((d, vocab), BF16)],
        (rows, table, lse, targets),
        specs=[
            pl.BlockSpec((count, d), fixed),
            pl.BlockSpec((block, d), lambda i: (i, 0)),
            pl.BlockSpec((count, 1), fixed),
            pl.BlockSpec((count, 1), fixed),
        ],
        out_specs=[pl.BlockSpec((d, block), lambda i: (0, i))],
        scratch=[pltpu.VMEM((d, count), BF16), pltpu.VMEM((count, block), BF16)],
        grid=(tiles,),
        flops=4 * count * vocab * d,
        moved=30 * MIB,
        name="head_table",
    )[0]


def list_tokens(ids, vocab):
    count = ids.shape[1]

    def kernel(ids_ref, token_ref, row_ref, many_ref):
        start = lax.axis_index("shard") * vocab

        def step(i, many):
            local = ids_ref[0, i] - start
            token_ref[0, many] = i
            row_ref[0, many] = local
            return many + ((local >= 0) & (local < vocab)).astype(jnp.int32)

        many_ref[0, 0] = lax.fori_loop(0, count, step, jnp.int32(0), unroll=8)

    smem = pl.BlockSpec(memory_space=pltpu.SMEM)
    return call(
        kernel,
        [like((1, count), jnp.int32), like((1, count), jnp.int32), like((1, 1), jnp.int32)],
        (ids,),
        specs=[smem],
        out_specs=[smem] * 3,
        name="list_tokens",
    )


def table_grad(dense, grads, tokens, rows, many):
    width, vocab = dense.shape
    shards, _, per = grads.shape
    count = shards * per
    ways = 4

    def kernel(d_ref, g_ref, t_ref, r_ref, n_ref, o_ref, flat_ref, *acc):
        for h in range(shards):
            for at in range(0, per, 512):
                span = slice(at, min(at + 512, per))
                flat_ref[h * per + span.start : h * per + span.stop] = g_ref[h, :, span].astype(F32).T
        for ref in acc:
            ref[...] = jnp.zeros(ref.shape, F32)
        many = n_ref[0, 0]
        rounds = many // ways

        def step(i, carry):
            for way, ref in enumerate(acc):
                at = i * ways + way
                row, token = r_ref[0, at], t_ref[0, at]
                ref[pl.ds(row, 1), :] += flat_ref[pl.ds(token, 1), :]
            return carry

        lax.fori_loop(0, rounds, step, jnp.int32(0))

        def rest(at, carry):
            row, token = r_ref[0, at], t_ref[0, at]
            acc[0][pl.ds(row, 1), :] += flat_ref[pl.ds(token, 1), :]
            return carry

        lax.fori_loop(rounds * ways, many, rest, jnp.int32(0))
        o_ref[...] = d_ref[...].astype(F32).T + sum(ref[...] for ref in acc)

    smem = pl.BlockSpec(memory_space=pltpu.SMEM)
    return call(
        kernel,
        [like((vocab, width), F32)],
        (dense, grads, tokens, rows, many),
        specs=[None, None, smem, smem, smem],
        scratch=[pltpu.VMEM((count, width), F32)] + [pltpu.VMEM((vocab, width), F32)] * ways,
        limit=60,
        name="table_grad",
    )[0]


def unpack_grads(z, sums, pos_rows, extra_at):
    half = pos_rows // 2

    def kernel(a_ref, b_ref, qkv_ref, out_ref, fin_ref, fout_ref, gain_ref, bias_ref, pos_ref, eg_ref, es_ref):
        core = lax.axis_index("dp") % 2
        shard = lax.axis_index("shard")

        def own_lanes(value):
            total = jnp.zeros((value.shape[0], z.ds), F32)
            for h in range(z.shards):
                total = total + jnp.where(shard == h, value[:, h * z.ds : (h + 1) * z.ds], 0.0)
            return total

        def halves(zero_ref, one_ref):
            out_ref[...] = zero_ref[0 : z.ds].astype(F32)
            for c in range(3):
                row = z.at_qkv + c * z.gi
                part = zero_ref[row : row + z.gi].astype(F32)
                for g in range(z.groups):
                    qkv_ref[c, g] = part[:, g * z.gw : (g + 1) * z.gw]
            small = own_lanes(zero_ref[z.at_small : z.at_small + 16].astype(F32))
            gain_ref[...] = small[0:2]
            bias_ref[...] = small[2:11]
            fin_ref[...] = one_ref[0 : z.at_out].astype(F32).reshape(z.groups, z.gi, z.d)
            part = one_ref[z.at_out : z.rows].astype(F32)
            for g in range(z.groups):
                fout_ref[g] = part[:, g * z.gw : (g + 1) * z.gw]
            pos_ref[0:half] = zero_ref[z.rows : z.rows + half].astype(F32)
            pos_ref[half:pos_rows] = one_ref[z.rows : z.rows + half].astype(F32)
            small = own_lanes(zero_ref[z.rows + half : z.rows + half + 16].astype(F32))
            eg_ref[...] = small[0:1]
            es_ref[...] = small[1:2]

        @pl.when(core == 0)
        def _():
            halves(a_ref, b_ref)

        @pl.when(core == 1)
        def _():
            halves(b_ref, a_ref)

    return call(
        kernel,
        [
            like((3, z.groups, z.gi, z.gw), F32),
            like((z.ds, z.d), F32),
            like((z.groups, z.gi, z.d), F32),
            like((z.groups, z.gf, z.gw), F32),
            like((2, z.ds), F32),
            like((9, z.ds), F32),
            like((pos_rows, z.d), F32),
            like((1, z.ds), F32),
            like((1, z.ds), F32),
        ],
        sums,
        name="unpack",
    )


def body(token_ids, targets, segment_ids, word_table, pos_table, embed_gain, embed_shift, qkv_weight, out_weight, ffn_in, ffn_out, layer_gains, layer_biases):
    micro, _, seq = token_ids.shape
    vocab, d = word_table.shape
    pos_rows = pos_table.shape[0]
    shards = lax.axis_size("shard")
    dp = lax.axis_size("dp")
    both = ("section", "dp")
    section = lax.axis_index("section")
    first = section == 0
    z = Sizes(qkv_weight.shape, out_weight.shape, shards, pos_rows)
    offset = lax.axis_index("shard") * vocab

    mine = lax.dynamic_index_in_dim(jnp.stack([token_ids[:, 0], targets[:, 0], segment_ids[:, 0]], axis=1), section, 0, keepdims=False)
    ids_by = jnp.stack([mine, turned(mine, "shard", -1), turned(mine, "shard", 2), turned(mine, "shard", 1)])
    token_by, target_by, seg_by = ids_by[:, 0], ids_by[:, 1], ids_by[:, 2]
    seg_row, seg_col = mine[2:3], mine[2].reshape(seq, 1)

    def local(ids):
        shifted = ids.reshape(-1) - offset
        inside = ((shifted >= 0) & (shifted < vocab)).astype(jnp.int32)
        return jnp.clip(shifted, 0, vocab - 1), inside.reshape(-1, 1), shifted.reshape(-1, 1)

    packed = pack_weights(
        z, qkv_weight[0], out_weight[0], ffn_in[0], ffn_out[0], layer_gains[0], layer_biases[0], embed_gain.reshape(1, -1), embed_shift.reshape(1, -1)
    )
    other = crossed(packed, "section", 1)
    layers = []
    for l in range(2):
        own = jnp.where(section == l, packed, other)
        pieces = (own, *ring_gather(own, "shard"))
        layers.append((*pieces, *(crossed(piece, "dp", 1) for piece in pieces)))

    clipped, inside, _ = local(token_by)
    picked = jnp.take(word_table, clipped, axis=0)
    c0, c1, c2a, c2b, c3 = embed_parts(picked, inside, seg_by.reshape(-1, 1), seg_by, pos_table)
    half = seq // 2
    c1 = jnp.concatenate([c1[:half] + turned(c2a, "shard", 1), c1[half:]], axis=0)
    c3 = jnp.concatenate([c3[:half], c3[half:] + turned(c2b, "shard", -1)], axis=0)
    words = (c0, turned(c1, "shard", 1), turned(c3, "shard", -1))

    one = layer_forward(z, layers[0], seg_col, seg_row, True, words=words)
    two = layer_forward(z, layers[1], seg_col, seg_row, False, layer_in=one["out"])
    two["x"] = one["out"]

    before, after, far_a, far_b = ring_gather(two["out"], "shard")
    head_rows = jnp.concatenate([two["out"], after, far_a, far_b, before], axis=0)
    target_clip, target_in, target_local = local(target_by)
    target_rows = jnp.take(word_table, target_clip, axis=0)
    ctx, lse = head_forward(head_rows, word_table)
    lses = (lse, turned(lse, "shard", -1), turned(lse, "shard", 2), turned(lse, "shard", 1))
    parts, whole_lse = head_combine(seq, ctx, target_rows, target_in, lses)
    out_grad = lax.psum_scatter(parts, "shard", scatter_dimension=0, tiled=True)
    dense = head_table(head_rows, word_table, whole_lse, target_local)
    dense = lax.psum_scatter(dense, both, scatter_dimension=0, tiled=True)

    def shared(grads):
        kept = grads[0] + crossed(grads[1], "dp", 1)
        return lax.psum_scatter(kept, "shard", scatter_dimension=0, tiled=True)[0]

    in_two, grads_two = layer_backward(z, layers[1], two, out_grad, False)
    in_one, grads_one, d_embed = layer_backward(z, layers[0], one, in_two.astype(BF16), True, seg_col, seg_row, pos_rows)
    sum_two = shared(grads_two)
    sum_one = shared(grads_one)
    one_layer, one_extra = sum_one[: z.rows], sum_one[z.rows :]
    keep = jnp.concatenate([jnp.where(first, one_layer, sum_two), one_extra], axis=0)
    send = jnp.concatenate([jnp.where(first, sum_two, one_layer), one_extra], axis=0)
    total = keep + crossed(send, "section", 1)
    bit = 2
    while bit < dp:
        total = total + crossed(total, "dp", bit)
        bit *= 2
    unpacked = unpack_grads(z, (total, crossed(total, "dp", 1)), pos_rows, z.rows)

    all_ids = lax.all_gather(token_ids[:, 0], ("shard", "dp"), axis=0)
    all_ids = all_ids.reshape(shards, dp, micro, seq).transpose(0, 2, 1, 3).reshape(1, -1)
    tokens, rows, many = list_tokens(all_ids, vocab)
    columns = lax.all_to_all(d_embed, both, split_axis=0, concat_axis=1, tiled=True)
    columns = lax.all_gather(columns, "shard")
    word_grad = table_grad(dense, columns, tokens, rows, many)

    def by_micro(layer_one, layer_two, moved, dtype):
        own = jnp.where(first, layer_one, layer_two)
        sent = jnp.where(first, layer_two, layer_one).astype(moved)
        came = crossed(sent, "section", 1).astype(dtype)
        return jnp.stack([jnp.where(first, own, came), jnp.where(first, came, own)]).reshape(1, micro, 1, seq, d)

    layer_outputs = by_micro(one["out"], two["out"], BF16, BF16)
    input_grads = by_micro(in_one, in_two, BF16, F32)
    qkv_g, out_g, fin_g, fout_g, gain_g, bias_g, pos_g, eg_g, es_g = unpacked
    return (
        layer_outputs,
        input_grads,
        word_grad,
        pos_g,
        eg_g.reshape(-1),
        es_g.reshape(-1),
        qkv_g[None],
        out_g[None],
        fin_g[None],
        fout_g[None],
        gain_g[None],
        bias_g[None],
    )


def solution(mesh):
    rows = P(None, ("dp", "shard"), None)
    weights = (
        P("section", None, None, "shard", None),
        P("section", "shard", None),
        P("section", None, "shard", None),
        P("section", None, "shard", None),
        P("section", None, "shard"),
        P("section", None, "shard"),
    )
    states = P("section", None, ("dp", "shard"), None, None)
    return jax.shard_map(
        body,
        mesh=mesh,
        in_specs=(rows, rows, rows, P("shard", None), P("shard", None), P("shard"), P("shard"), *weights),
        out_specs=(states, states, P("shard", ("section", "dp")), P("shard", None), P("shard"), P("shard"), *weights),
        check_vma=False,
    )
```

time: 1420 us -> 625 us (0.44)
  waiting for transfers between devices: 621 us -> 254 us
  Pallas kernels: 0 us -> 201 us
  matrix products: 168 us -> 0 us
  blocking collectives: 205 us -> 38.9 us
  other arithmetic: 182 us -> 20.1 us
  local copies, waits for them, and re-layouts: 189 us -> 46.8 us
  starting transfers between devices: 25.9 us -> 44.1 us
    pallas_call x0 -> x12, Pallas kernels: none -> 201 us  [call(): pl.pallas_call(kernel, out_shape=outs, in_specs=[vmem if s is None else s...]
    all_gather x10 -> x1, blocking collectives: 173 us -> 27.4 us  [body(): all_ids = lax.all_gather(token_ids[:, 0], ('shard', 'dp'), axis=0)]
    dot_general x63 -> x0, matrix products: 143 us -> none  [the longest x9 61.2 us: grouped(): jnp.einsum('sgi,gio->sgo', split, weight, preferred_element_type=jnp.floa...]
    reduce_scatter x7 -> x4, waiting for transfers between devices: 245 us -> 107 us  [the longest x2 49.2 us: shared(): return lax.psum_scatter(kept, 'shard', scatter_dimension=0, tiled=True)[0]]
    all_gather x7 -> x1, waiting for transfers between devices: 84.8 us -> 0.01 us  [body(): columns = lax.all_gather(columns, 'shard')]
    ppermute x8 -> x40, waiting for transfers between devices: 228 us -> 146 us  [the longest x22 105 us: turned(): lax.ppermute(block, axis, [(i, (i + by) % size) for i in range(size)])]
    unnamed x25 -> x5, waiting for transfers between devices: 63.9 us -> 0.08 us
    reduce_sum x41 -> x0, other arithmetic: 50.3 us -> none  [the longest x11 19.5 us: layer_norm(): centered = inputs - jnp.mean(inputs, axis=-1, keepdims=True)]
  transfers between devices with their start and end apart: 28 -> 45, of which waited for: 17 -> 20; matrix products, arithmetic and copies ran while one was open for 16% -> 8% of each run, Pallas kernels for 0% -> 14%
where the time goes in v1:
time: 625 us; the launch traced here: 619 us
  waiting for transfers between devices  254 us (41%)
  Pallas kernels  201 us (32%)
  local copies, waits for them, and re-layouts  46.8 us (7%)
  starting transfers between devices  44.1 us (7%)
  blocking collectives  38.9 us (6%)
  other arithmetic  20.1 us (3%)
  between operations  14.9 us (2%)
    pallas_call x12, Pallas kernels, call(): pl.pallas_call(kernel, out_shape=outs, in_specs=[vmem if s is None else s...  201 us
    ppermute x22, waiting for transfers between devices, turned(): lax.ppermute(block, axis, [(i, (i + by) % size) for i in range(size)])  105 us
    reduce_scatter x2, waiting for transfers between devices, shared(): return lax.psum_scatter(kept, 'shard', scatter_dimension=0, tiled=True)[0]  49.2 us
    ppermute x18, waiting for transfers between devices, crossed(): lax.ppermute(block, axis, [(i, i ^ bit) for i in range(lax.axis_size(axis...  40.7 us
    ppermute x22, starting transfers between devices, turned(): lax.ppermute(block, axis, [(i, (i + by) % size) for i in range(size)])  33.8 us
    reduce_scatter x1, waiting for transfers between devices, body(): out_grad = lax.psum_scatter(parts, 'shard', scatter_dimension=0, tiled=True)  33.1 us
    all_gather x1, blocking collectives, body(): all_ids = lax.all_gather(token_ids[:, 0], ('shard', 'dp'), axis=0)  27.4 us
    reduce_scatter x1, waiting for transfers between devices, body(): dense = lax.psum_scatter(dense, both, scatter_dimension=0, tiled=True)  25.1 us
  transfers between devices with their start and end apart: 45, of which 20 were waited for; matrix products, arithmetic and copies ran while one was open for 8% of the time, Pallas kernels for 14%

profile of v1, /device:TPU:0, one launch (start us, length us, event | category | flops | bytes accessed | tf_op | source)
XLA Modules:
  0.0 618.9 jit_solution(4601763483978647587)
XLA Ops:
  9.3 4.1 collective-permute-start.11
  22.3 10.3 %gather_fusion = bf16[1024,768]{1,0:T(8,128)(2,1)S(1)} fusion(bf16[7632,768]{1,0:T(8,128)(2,1)} %w_ref.3, s32[1024]{0:T(1024)S(1)} %get-tuple-element.198), kind=kCustom, calls=%fused_computation.clone | custom fusion | bytes 3149824 | tf_op jit(solution)/shard_map/jit(_take)/gather | solution.py:740
  36.0 4.1 embed_parts.1
  44.0 5.9 collective-permute-done.13
  57.2 20.6 %collective-permute-done.14.refs_13_ = bf16[256,768]{1,0:T(8,128)(2,1)} collective-permute-done((bf16[256,768]{1,0:T(8,128)(2,1)S(1)}, bf16[256,768]{1,0:T(8,128)(2,1)}, u32[]{:S(2)}, u32[]{:S(2)}) %collective-permute-start.14) | collective-permute-done | bytes 393248 | tf_op jit(solution)/shard_map/ppermute | solution.py:80
  78.2 40.8 %collective-permute-done.16.refs_14_ = bf16[256,768]{1,0:T(8,128)(2,1)S(1)} collective-permute-done((bf16[256,768]{1,0:T(8,128)(2,1)S(1)}, bf16[256,768]{1,0:T(8,128)(2,1)S(1)}, u32[]{:S(2)}, u32[]{:S(2)}) %collective-permute-start.16) | collective-permute-done | bytes 393248 | tf_op jit(solution)/shard_map/ppermute | solution.py:80
  125.3 5.7 collective-permute-done.19.refs_3_
  131.2 5.9 collective-permute-done.3.refs_3_
  137.1 4.9 collective-permute-done.4.refs_4_
  141.9 6.3 %collective-permute-done.20.refs_4_ = bf16[192,768]{1,0:T(8,128)(2,1)} collective-permute-done((bf16[192,768]{1,0:T(8,128)(2,1)S(1)}, bf16[192,768]{1,0:T(8,128)(2,1)}, u32[]{:S(2)}, u32[]{:S(2)}) %collective-permute-start.20) | collective-permute-done | bytes 294944 | tf_op jit(solution)/shard_map/ppermute | solution.py:80
  150.8 13.2 %layer_first.1 = (bf16[256,768]{1,0:T(8,128)(2,1)}, bf16[256,768]{1,0:T(8,128)(2,1)}, bf16[256,768]{1,0:T(8,128)(2,1)}, bf16[256,768]{1,0:T(8,128)(2,1)}, bf16[1...) custom-call(bf16[384,768]{1,0:T(8,128)(2,1)} %copy-done.10, ...), custom_call_target="tpu_custom_call" | custom-call | flops 3000000000 | bytes 16777216 | tf_op jit(solution)/shard_map/layer_first/pallas_call | solution.py:61
  164.1 12.2 %layer_second.1 = (bf16[256,768]{1,0:T(8,128)(2,1)}, bf16[256,768]{1,0:T(8,128)(2,1)}, bf16[256,768]{1,0:T(8,128)(2,1)}, bf16[256,768]{1,0:T(8,128)(2,1)}, bf16[...) custom-call(bf16[384,768]{1,0:T(8,128)(2,1)} %copy-done.11, ...), custom_call_target="tpu_custom_call" | custom-call | flops 3000000000 | bytes 16777216 | tf_op jit(solution)/shard_map/layer_second/pallas_call | solution.py:61
  177.0 10.4 %gather_fusion.1 = bf16[1024,768]{1,0:T(8,128)(2,1)S(1)} fusion(bf16[7632,768]{1,0:T(8,128)(2,1)} %w_ref.3, s32[1024]{0:T(1024)S(1)} %get-tuple-element.199), kind=kCustom, calls=%fused_computation.1.clone | custom fusion | bytes 3149824 | tf_op jit(solution)/shard_map/jit(_take)/gather | solution.py:754
  193.3 6.9 %collective-permute-done.27 = bf16[256,768]{1,0:T(8,128)(2,1)S(1)} collective-permute-done((bf16[256,768]{1,0:T(8,128)(2,1)S(1)}, bf16[256,768]{1,0:T(8,128)(2,1)S(1)}, u32[]{:S(2)}, u32[]{:S(2)}) %collective-permute-start.27) | collective-permute-done | bytes 393248 | tf_op jit(solution)/shard_map/ppermute | solution.py:80
  200.3 4.3 collective-permute-start.30
  209.7 44.0 %head_forward.1 = (f32[1024,768]{1,0:T(8,128)}, f32[8,1024]{1,0:T(8,128)}) custom-call(bf16[1024,768]{1,0:T(8,128)(2,1)} %copy-done.19, bf16[7632,768]{1,0:T(8,128)(2,1)} %w_ref.3), custom_call_target="tpu_custom_call" | custom-call | flops 24008196096 | bytes 20971520 | tf_op jit(solution)/shard_map/head_forward/pallas_call | solution.py:61
  263.9 4.5 head_combine.1
  268.7 33.1 %reduce-scatter.5.cloned.1.call-done.refs_22_ = bf16[256,768]{1,0:T(8,128)(2,1)} async-done(((bf16[1024,768]{1,0:T(8,128)(2,1)}), bf16[256,768]{1,0:T(8,128)(2,1)}) %reduce-scatter.5.cloned.1.call-update) | async-done | bytes 393232 | tf_op jit(solution)/shard_map/reduce_scatter | solution.py:758
  301.8 18.8 %layer_second_back.1 = (f32[256,768]{1,0:T(8,128)}, bf16[2,4,384,768]{3,2,1,0:T(8,128)(2,1)}) custom-call(bf16[384,768]{1,0:T(8,128)(2,1)} %copy-done.11, bf16[384,768]{1,0:T(8,128)(2,1)} %copy-done.17, bf16[384,768]{1,0:T(8,128)(2,1)} %copy-done.18, bf16[192,768]{1,0:T(8,128)(2,1)} %collective-permute-done.19.refs_3_, ...), custom_call_target="tpu_custom_call" | custom-call | flops 8000000000 | bytes 20971520 | tf_op jit(solution)/shard_map/layer_second_back/pallas_call | solution.py:61
  322.5 20.3 %layer_first_back.1 = (f32[256,768]{1,0:T(8,128)}, bf16[2,4,464,768]{3,2,1,0:T(8,128)(2,1)}, bf16[768,256]{1,0:T(8,128)(2,1)}) custom-call(bf16[384,768]{1,0:T(8,128)(2,1)} %copy-done.10, bf16[384,768]{1,0:T(8,128)(2,1)} %copy-done.15, bf16[384,768]{1,0:T(8,128)(2,1)} %copy-done.16, bf16[192,768]{1,0:T(8,128)(2,1)} %copy-done.28, ...), custom_call_target="tpu_custom_call" | custom-call | flops 8000000000 | bytes 20971520 | tf_op jit(solution)/shard_map/layer_first_back/pallas_call | solution.py:61
  345.1 5.2 collective-permute-done.35
  354.2 4.4 collective-permute-done.36
  363.0 11.5 %all_to_all.16 = bf16[8,96,256]{2,1,0:T(8,128)(2,1)S(1)} all-to-all(bf16[8,96,256]{2,1,0:T(8,128)(2,1)S(1)} %bitcast.88), channel_id=1, replica_groups=mesh['section'=2,'dp'=4,'shard'=4] {'section','dp'}, dimensions={0} | all-to-all | bytes 786432 | tf_op jit(solution)/shard_map/all_to_all | solution.py:783
  376.0 31.2 %head_table.1 = bf16[768,7632]{1,0:T(8,128)(2,1)} custom-call(bf16[1024,768]{1,0:T(8,128)(2,1)} %copy-done.19, bf16[7632,768]{1,0:T(8,128)(2,1)} %w_ref.3, f32[1024,1]{1,0:T(8,128)} %get-tuple-element.101.lse_ref, s32[1024,1]{1,0:T(8,128)} %bitcast.84), custom_call_target="tpu_custom_call" | custom-call | flops 24008196096 | bytes 31457280 | tf_op jit(solution)/shard_map/head_table/pallas_call | solution.py:61
  408.1 49.2 %reduce-scatter.11.cloned.1.call-done = bf16[1,384,768]{2,1,0:T(8,128)(2,1)} async-done(((bf16[4,384,768]{2,1,0:T(8,128)(2,1)}), bf16[1,384,768]{2,1,0:T(8,128)(2,1)}) %reduce-scatter.11.cloned.1.call-update) | async-done | bytes 589840 | tf_op jit(solution)/shard_map/reduce_scatter | solution.py:764
  460.2 16.1 %collective-permute-done.37 = bf16[464,768]{1,0:T(8,128)(2,1)S(1)} collective-permute-done((bf16[464,768]{1,0:T(8,128)(2,1)S(1)}, bf16[464,768]{1,0:T(8,128)(2,1)S(1)}, u32[]{:S(2)}, u32[]{:S(2)}) %collective-permute-start.37) | collective-permute-done | bytes 712736 | tf_op jit(solution)/shard_map/ppermute | solution.py:84
  479.5 27.4 %all-gather = s32[32,1,256]{2,1,0:T(1,128)S(1)} all-gather(s32[2,1,256]{2,1,0:T(1,128)S(1)} %copy-done.23), channel_id=2, replica_groups=mesh['section'=2,'dp'=4,'shard'=4] {'shard','dp'}, dimensions={0}, use_global_device_ids=true | all-gather | bytes 34816 | tf_op jit(solution)/shard_map/all_gather | solution.py:780
  507.7 34.6 %list_tokens.1 = (s32[1,8192]{1,0:T(1,128)}, s32[1,8192]{1,0:T(1,128)}, s32[1,1]{1,0:T(1,128)}) custom-call(s32[1,8192]{1,0:T(1,128)} %reshape.142.ids_ref), custom_call_target="tpu_custom_call" | custom-call | tf_op jit(solution)/shard_map/list_tokens/pallas_call | solution.py:61
  547.6 15.0 %collective-permute-done.34 = bf16[256,768]{1,0:T(8,128)(2,1)S(1)} collective-permute-done((bf16[256,768]{1,0:T(8,128)(2,1)S(1)}, bf16[256,768]{1,0:T(8,128)(2,1)S(1)}, u32[]{:S(2)}, u32[]{:S(2)}) %collective-permute-start.34) | collective-permute-done | bytes 393248 | tf_op jit(solution)/shard_map/ppermute | solution.py:84
  569.5 25.1 %reduce-scatter.7.cloned.1.call-done.d_ref = bf16[96,7632]{1,0:T(8,128)(2,1)} async-done(((bf16[768,7632]{1,0:T(8,128)(2,1)}), bf16[96,7632]{1,0:T(8,128)(2,1)}) %reduce-scatter.7.cloned.1.call-update) | async-done | bytes 1465360 | tf_op jit(solution)/shard_map/reduce_scatter | solution.py:760
  594.6 12.2 %table_grad.1 = f32[7632,96]{1,0:T(8,128)} custom-call(bf16[96,7632]{1,0:T(8,128)(2,1)} %reduce-scatter.7.cloned.1.call-done.d_ref, bf16[4,96,2048]{2,1,0:T(8,128)(2,1)} %all-gather.3.cloned.1.call-done.g_ref, s32[1,8192]{1,0:T(1,128)} %get-tuple-element.103.t_ref, s32[1,8192]{1,0:T(1,128)} %get-tuple-element.104.r_ref, s32[1,1]{1,0:T(1,128)} %get-tuple-element.105.n_ref), custom_call_target="tpu_custom_call" | custom-call | tf_op jit(solution)/shard_map/table_grad/pallas_call | solution.py:61
  606.8 5.1 copy.112
  (211 shorter events, 90.7 us)
Async XLA Ops:
  7.2 294.6 %reduce-scatter.5.cloned.1.call-start = ((), (), s32[]{:S(2)}) async-start(), calls=%async_computation.5 | async-start | bytes 1966080 | tf_op jit(solution)/shard_map/reduce_scatter | solution.py:758
  20.1 30.8 %collective-permute-start = (bf16[384,768]{1,0:T(8,128)(2,1)}, bf16[384,768]{1,0:T(8,128)(2,1)S(1)}, u32[]{:S(2)}, u32[]{:S(2)}) collective-permute-start(bf16[384,768]{1,0:T(8,128)(2,1)} %pack.1), channel_id=1, source_target_pairs={{0,16},{16,0},{1,17},{17,1},{2,18},{18,2},{3,19},{19,3},{4,20},{20... | collective-permute-start | bytes 1769480 | tf_op jit(solution)/shard_map/ppermute | solution.py:84
  41.7 13.7 %collective-permute-start.15 = (bf16[128,768]{1,0:T(8,128)(2,1)}, bf16[128,768]{1,0:T(8,128)(2,1)S(1)}, u32[]{:S(2)}, u32[]{:S(2)}) collective-permute-start(bf16[128,768]{1,0:T(8,128)(2,1)} %get-tuple-element.69), channel_id=1, source_target_pairs={{0,3},{1,0},{2,1},{3,2},{4,7},{5,4},{6,5},{7,6},{8,11},{9,8},{10,9... | collective-permute-start | bytes 589832 | tf_op jit(solution)/shard_map/ppermute | solution.py:80
  51.1 26.8 %collective-permute-start.17 = (bf16[384,768]{1,0:T(8,128)(2,1)S(1)}, bf16[384,768]{1,0:T(8,128)(2,1)S(1)}, u32[]{:S(2)}, u32[]{:S(2)}) collective-permute-start(bf16[384,768]{1,0:T(8,128)(2,1)S(1)} %get-tuple-element.184.refs_0_), channel_id=1, source_target_pairs={{0,1},{1,2},{2,3},{3,0},{4,5},{5,6},{6,7},{7,4},{8,9},{9,10},{10,1... | collective-permute-start | bytes 1769480 | tf_op jit(solution)/shard_map/ppermute | solution.py:80
  51.2 26.7 %collective-permute-start.14 = (bf16[256,768]{1,0:T(8,128)(2,1)S(1)}, bf16[256,768]{1,0:T(8,128)(2,1)}, u32[]{:S(2)}, u32[]{:S(2)}) collective-permute-start(bf16[256,768]{1,0:T(8,128)(2,1)S(1)} %pad_maximum_fusion.2), channel_id=1, source_target_pairs={{0,1},{1,2},{2,3},{3,0},{4,5},{5,6},{6,7},{7,4},{8,9},{9,10},{10,1... | collective-permute-start | bytes 1179656 | tf_op jit(solution)/shard_map/ppermute | solution.py:80
  51.5 68.4 %collective-permute-start.1 = (bf16[384,768]{1,0:T(8,128)(2,1)S(1)}, bf16[384,768]{1,0:T(8,128)(2,1)S(1)}, u32[]{:S(2)}, u32[]{:S(2)}) collective-permute-start(bf16[384,768]{1,0:T(8,128)(2,1)S(1)} %get-tuple-element.183.refs_0_), channel_id=1, source_target_pairs={{0,1},{1,2},{2,3},{3,0},{4,5},{5,6},{6,7},{7,4},{8,9},{9,10},{10,1... | collective-permute-start | bytes 1769480 | tf_op jit(solution)/shard_map/ppermute | solution.py:80
  54.5 65.5 %collective-permute-start.2 = (bf16[384,768]{1,0:T(8,128)(2,1)S(1)}, bf16[384,768]{1,0:T(8,128)(2,1)S(1)}, u32[]{:S(2)}, u32[]{:S(2)}) collective-permute-start(bf16[384,768]{1,0:T(8,128)(2,1)S(1)} %get-tuple-element.183.refs_0_), channel_id=1, source_target_pairs={{0,3},{1,0},{2,1},{3,2},{4,7},{5,4},{6,5},{7,6},{8,11},{9,8},{10,9... | collective-permute-start | bytes 1769480 | tf_op jit(solution)/shard_map/ppermute | solution.py:80
  55.4 65.1 %collective-permute-start.18 = (bf16[384,768]{1,0:T(8,128)(2,1)S(1)}, bf16[384,768]{1,0:T(8,128)(2,1)S(1)}, u32[]{:S(2)}, u32[]{:S(2)}) collective-permute-start(bf16[384,768]{1,0:T(8,128)(2,1)S(1)} %get-tuple-element.184.refs_0_), channel_id=1, source_target_pairs={{0,3},{1,0},{2,1},{3,2},{4,7},{5,4},{6,5},{7,6},{8,11},{9,8},{10,9... | collective-permute-start | bytes 1769480 | tf_op jit(solution)/shard_map/ppermute | solution.py:80
  77.8 43.5 %collective-permute-start.5 = (bf16[384,768]{1,0:T(8,128)(2,1)S(1)}, bf16[384,768]{1,0:T(8,128)(2,1)S(1)}, u32[]{:S(2)}, u32[]{:S(2)}) collective-permute-start(bf16[384,768]{1,0:T(8,128)(2,1)S(1)} %get-tuple-element.183.refs_0_), channel_id=1, source_target_pairs={{0,4},{4,0},{8,12},{12,8},{1,5},{5,1},{9,13},{13,9},{2,6},{6,2},{1... | collective-permute-start | bytes 1769480 | tf_op jit(solution)/shard_map/ppermute | solution.py:84
  77.9 41.1 %collective-permute-start.16 = (bf16[256,768]{1,0:T(8,128)(2,1)S(1)}, bf16[256,768]{1,0:T(8,128)(2,1)S(1)}, u32[]{:S(2)}, u32[]{:S(2)}) collective-permute-start(bf16[256,768]{1,0:T(8,128)(2,1)S(1)} %pad_maximum_fusion.3), channel_id=1, source_target_pairs={{0,3},{1,0},{2,1},{3,2},{4,7},{5,4},{6,5},{7,6},{8,11},{9,8},{10,9... | collective-permute-start | bytes 1179656 | tf_op jit(solution)/shard_map/ppermute | solution.py:80
  119.9 28.4 %collective-permute-start.6 = (bf16[384,768]{1,0:T(8,128)(2,1)S(1)}, bf16[384,768]{1,0:T(8,128)(2,1)S(1)}, u32[]{:S(2)}, u32[]{:S(2)}) collective-permute-start(bf16[384,768]{1,0:T(8,128)(2,1)S(1)} %collective-permute-done.1.refs_1_), channel_id=1, source_target_pairs={{0,4},{4,0},{8,12},{12,8},{1,5},{5,1},{9,13},{13,9},{2,6},{6,2},{1... | collective-permute-start | bytes 1769480 | tf_op jit(solution)/shard_map/ppermute | solution.py:84
  120.0 28.8 %collective-permute-start.7 = (bf16[384,768]{1,0:T(8,128)(2,1)S(1)}, bf16[384,768]{1,0:T(8,128)(2,1)S(1)}, u32[]{:S(2)}, u32[]{:S(2)}) collective-permute-start(bf16[384,768]{1,0:T(8,128)(2,1)S(1)} %collective-permute-done.2.refs_2_), channel_id=1, source_target_pairs={{0,4},{4,0},{8,12},{12,8},{1,5},{5,1},{9,13},{13,9},{2,6},{6,2},{1... | collective-permute-start | bytes 1769480 | tf_op jit(solution)/shard_map/ppermute | solution.py:84
  120.6 16.5 %collective-permute-start.3 = (bf16[192,768]{1,0:T(8,128)(2,1)S(1)}, bf16[192,768]{1,0:T(8,128)(2,1)S(1)}, u32[]{:S(2)}, u32[]{:S(2)}) collective-permute-start(bf16[192,768]{1,0:T(8,128)(2,1)S(1)} %slice.94), channel_id=1, source_target_pairs={{0,1},{1,2},{2,3},{3,0},{4,5},{5,6},{6,7},{7,4},{8,9},{9,10},{10,1... | collective-permute-start | bytes 884744 | tf_op jit(solution)/shard_map/ppermute | solution.py:80
  122.1 19.8 %collective-permute-start.4 = (bf16[192,768]{1,0:T(8,128)(2,1)S(1)}, bf16[192,768]{1,0:T(8,128)(2,1)S(1)}, u32[]{:S(2)}, u32[]{:S(2)}) collective-permute-start(bf16[192,768]{1,0:T(8,128)(2,1)S(1)} %slice.95), channel_id=1, source_target_pairs={{0,3},{1,0},{2,1},{3,2},{4,7},{5,4},{6,5},{7,6},{8,11},{9,8},{10,9... | collective-permute-start | bytes 884744 | tf_op jit(solution)/shard_map/ppermute | solution.py:80
  131.0 17.3 %collective-permute-start.20 = (bf16[192,768]{1,0:T(8,128)(2,1)S(1)}, bf16[192,768]{1,0:T(8,128)(2,1)}, u32[]{:S(2)}, u32[]{:S(2)}) collective-permute-start(bf16[192,768]{1,0:T(8,128)(2,1)S(1)} %slice.100), channel_id=1, source_target_pairs={{0,3},{1,0},{2,1},{3,2},{4,7},{5,4},{6,5},{7,6},{8,11},{9,8},{10,9... | collective-permute-start | bytes 884744 | tf_op jit(solution)/shard_map/ppermute | solution.py:80
  148.3 15.8 %collective-permute-start.21 = (bf16[384,768]{1,0:T(8,128)(2,1)S(1)}, bf16[384,768]{1,0:T(8,128)(2,1)}, u32[]{:S(2)}, u32[]{:S(2)}) collective-permute-start(bf16[384,768]{1,0:T(8,128)(2,1)S(1)} %get-tuple-element.184.refs_0_), channel_id=1, source_target_pairs={{0,4},{4,0},{8,12},{12,8},{1,5},{5,1},{9,13},{13,9},{2,6},{6,2},{1... | collective-permute-start | bytes 1769480 | tf_op jit(solution)/shard_map/ppermute | solution.py:84
  148.3 15.8 %collective-permute-start.22 = (bf16[384,768]{1,0:T(8,128)(2,1)S(1)}, bf16[384,768]{1,0:T(8,128)(2,1)}, u32[]{:S(2)}, u32[]{:S(2)}) collective-permute-start(bf16[384,768]{1,0:T(8,128)(2,1)S(1)} %collective-permute-done.17.refs_1_), channel_id=1, source_target_pairs={{0,4},{4,0},{8,12},{12,8},{1,5},{5,1},{9,13},{13,9},{2,6},{6,2},{1... | collective-permute-start | bytes 1769480 | tf_op jit(solution)/shard_map/ppermute | solution.py:84
  148.8 15.3 %collective-permute-start.23 = (bf16[384,768]{1,0:T(8,128)(2,1)S(1)}, bf16[384,768]{1,0:T(8,128)(2,1)}, u32[]{:S(2)}, u32[]{:S(2)}) collective-permute-start(bf16[384,768]{1,0:T(8,128)(2,1)S(1)} %collective-permute-done.18.refs_2_), channel_id=1, source_target_pairs={{0,4},{4,0},{8,12},{12,8},{1,5},{5,1},{9,13},{13,9},{2,6},{6,2},{1... | collective-permute-start | bytes 1769480 | tf_op jit(solution)/shard_map/ppermute | solution.py:84
  148.9 15.2 %collective-permute-start.24 = (bf16[192,768]{1,0:T(8,128)(2,1)}, bf16[192,768]{1,0:T(8,128)(2,1)}, u32[]{:S(2)}, u32[]{:S(2)}) collective-permute-start(bf16[192,768]{1,0:T(8,128)(2,1)} %collective-permute-done.19.refs_3_), channel_id=1, source_target_pairs={{0,4},{4,0},{8,12},{12,8},{1,5},{5,1},{9,13},{13,9},{2,6},{6,2},{1... | collective-permute-start | bytes 884744 | tf_op jit(solution)/shard_map/ppermute | solution.py:84
  149.3 14.8 %collective-permute-start.25 = (bf16[192,768]{1,0:T(8,128)(2,1)}, bf16[192,768]{1,0:T(8,128)(2,1)}, u32[]{:S(2)}, u32[]{:S(2)}) collective-permute-start(bf16[192,768]{1,0:T(8,128)(2,1)} %collective-permute-done.20.refs_4_), channel_id=1, source_target_pairs={{0,4},{4,0},{8,12},{12,8},{1,5},{5,1},{9,13},{13,9},{2,6},{6,2},{1... | collective-permute-start | bytes 884744 | tf_op jit(solution)/shard_map/ppermute | solution.py:84
  176.3 16.0 %collective-permute-start.28 = (bf16[256,768]{1,0:T(8,128)(2,1)}, bf16[256,768]{1,0:T(8,128)(2,1)S(1)}, u32[]{:S(2)}, u32[]{:S(2)}) collective-permute-start(bf16[256,768]{1,0:T(8,128)(2,1)} %get-tuple-element.71), channel_id=1, source_target_pairs={{0,1},{1,2},{2,3},{3,0},{4,5},{5,6},{6,7},{7,4},{8,9},{9,10},{10,1... | collective-permute-start | bytes 1179656 | tf_op jit(solution)/shard_map/ppermute | solution.py:80
  187.4 12.8 %collective-permute-start.27 = (bf16[256,768]{1,0:T(8,128)(2,1)S(1)}, bf16[256,768]{1,0:T(8,128)(2,1)S(1)}, u32[]{:S(2)}, u32[]{:S(2)}) collective-permute-start(bf16[256,768]{1,0:T(8,128)(2,1)S(1)} %copy-done.8), channel_id=1, source_target_pairs={{0,3},{1,0},{2,1},{3,2},{4,7},{5,4},{6,5},{7,6},{8,11},{9,8},{10,9... | collective-permute-start | bytes 1179656 | tf_op jit(solution)/shard_map/ppermute | solution.py:80
  192.4 12.4 %collective-permute-start.29 = (bf16[128,768]{1,0:T(8,128)(2,1)S(1)}, bf16[128,768]{1,0:T(8,128)(2,1)S(1)}, u32[]{:S(2)}, u32[]{:S(2)}) collective-permute-start(bf16[128,768]{1,0:T(8,128)(2,1)S(1)} %slice.101), channel_id=1, source_target_pairs={{0,1},{1,2},{2,3},{3,0},{4,5},{5,6},{6,7},{7,4},{8,9},{9,10},{10,1... | collective-permute-start | bytes 589832 | tf_op jit(solution)/shard_map/ppermute | solution.py:80
  268.5 138.7 %reduce-scatter.9.cloned.1.call-start = ((), (), s32[]{:S(2)}) async-start(), calls=%async_computation.8 | async-start | bytes 3563520 | tf_op jit(solution)/shard_map/reduce_scatter | solution.py:764
  352.2 105.1 %reduce-scatter.11.cloned.1.call-start = ((), (), s32[]{:S(2)}) async-start(), calls=%async_computation.9 | async-start | bytes 2949120 | tf_op jit(solution)/shard_map/reduce_scatter | solution.py:764
  362.0 207.5 %all-gather.3.cloned.1.call-start = ((), (), s32[]{:S(2)}) async-start(), calls=%async_computation.7 | async-start | bytes 1966080 | tf_op jit(solution)/shard_map/all_gather | solution.py:784
  375.7 219.0 %reduce-scatter.7.cloned.1.call-start = ((), (), s32[]{:S(2)}) async-start(), calls=%async_computation.6 | async-start | bytes 13271040 | tf_op jit(solution)/shard_map/reduce_scatter | solution.py:760
  458.7 17.6 %collective-permute-start.37 = (bf16[464,768]{1,0:T(8,128)(2,1)S(1)}, bf16[464,768]{1,0:T(8,128)(2,1)S(1)}, u32[]{:S(2)}, u32[]{:S(2)}) collective-permute-start(bf16[464,768]{1,0:T(8,128)(2,1)S(1)} %pad_maximum_fusion), channel_id=1, source_target_pairs={{0,16},{16,0},{1,17},{17,1},{2,18},{18,2},{3,19},{19,3},{4,20},{20... | collective-permute-start | bytes 2138120 | tf_op jit(solution)/shard_map/ppermute | solution.py:84
  476.5 67.4 %collective-permute-start.38 = (bf16[464,768]{1,0:T(8,128)(2,1)S(1)}, bf16[464,768]{1,0:T(8,128)(2,1)}, u32[]{:S(2)}, u32[]{:S(2)}) collective-permute-start(bf16[464,768]{1,0:T(8,128)(2,1)S(1)} %fusion.2), channel_id=1, source_target_pairs={{0,8},{4,12},{8,0},{12,4},{1,9},{5,13},{9,1},{13,5},{2,10},{6,14},... | collective-permute-start | bytes 2138120 | tf_op jit(solution)/shard_map/ppermute | solution.py:84
  478.0 67.3 %collective-permute-start.26 = (bf16[256,768]{1,0:T(8,128)(2,1)S(1)}, bf16[256,768]{1,0:T(8,128)(2,1)}, u32[]{:S(2)}, u32[]{:S(2)}) collective-permute-start(bf16[256,768]{1,0:T(8,128)(2,1)S(1)} %copy-done.13), channel_id=1, source_target_pairs={{0,16},{16,0},{1,17},{17,1},{2,18},{18,2},{3,19},{19,3},{4,20},{20... | collective-permute-start | bytes 1179656 | tf_op jit(solution)/shard_map/ppermute | solution.py:84
  542.4 20.2 %collective-permute-start.34 = (bf16[256,768]{1,0:T(8,128)(2,1)S(1)}, bf16[256,768]{1,0:T(8,128)(2,1)S(1)}, u32[]{:S(2)}, u32[]{:S(2)}) collective-permute-start(bf16[256,768]{1,0:T(8,128)(2,1)S(1)} %select_convert_fusion), channel_id=1, source_target_pairs={{0,16},{16,0},{1,17},{17,1},{2,18},{18,2},{3,19},{19,3},{4,20},{20... | collective-permute-start | bytes 1179656 | tf_op jit(solution)/shard_map/ppermute | solution.py:84
  545.2 18.8 %collective-permute-start.39 = (bf16[464,768]{1,0:T(8,128)(2,1)S(1)}, bf16[464,768]{1,0:T(8,128)(2,1)S(1)}, u32[]{:S(2)}, u32[]{:S(2)}) collective-permute-start(bf16[464,768]{1,0:T(8,128)(2,1)S(1)} %add.42.a_ref), channel_id=1, source_target_pairs={{0,4},{4,0},{8,12},{12,8},{1,5},{5,1},{9,13},{13,9},{2,6},{6,2},{1... | collective-permute-start | bytes 2138120 | tf_op jit(solution)/shard_map/ppermute | solution.py:84
  (45 other events, 776.3 us)
Sparse Core Ops, SparseCore 0:
  268.6 33.1 reduce-scatter.4
  352.3 54.6 reduce-scatter.8
  409.4 47.8 reduce-scatter.10
  458.8 36.6 all-gather.2
  499.3 95.3 reduce-scatter.6

commit v2 on v1

v2 whole, which is shorter than its diff:
```python
import math

import jax
import jax.numpy as jnp
from jax import lax
from jax.experimental import pallas as pl
from jax.experimental.pallas import tpu as pltpu
from jax.sharding import PartitionSpec as P

HEADS = 12
EPSILON = 1e-06
MASKED = -1000000000.0
F32 = jnp.float32
BF16 = jnp.bfloat16
MIB = 1 << 20


def nn(a, b):
    return jnp.dot(a, b, preferred_element_type=F32)


def nt(a, b):
    return lax.dot_general(a, b, (((1,), (1,)), ((), ())), preferred_element_type=F32)


def tn(a, b):
    return lax.dot_general(a, b, (((0,), (0,)), ((), ())), preferred_element_type=F32)


def iota(shape, axis):
    return lax.broadcasted_iota(jnp.int32, shape, axis)


def group_of(index, width, count):
    total = jnp.zeros(index.shape, jnp.int32)
    for step in range(1, count):
        total = total + (index >= step * width).astype(jnp.int32)
    return total


def normed(value):
    centered = value - jnp.mean(value, axis=-1, keepdims=True)
    scale = lax.rsqrt(jnp.mean(centered * centered, axis=-1, keepdims=True) + EPSILON)
    return centered * scale, scale


def norm_back(grad, unit, scale, gain):
    inner = grad * gain
    first = jnp.mean(inner, axis=-1, keepdims=True)
    second = jnp.mean(inner * unit, axis=-1, keepdims=True)
    return scale * (inner - first - unit * second)


def col_sum(value):
    return jnp.sum(value, axis=0, keepdims=True)


def upright(row, count):
    return jnp.broadcast_to(row.astype(F32), (128, count)).T[:, 0:1]


def call(kernel, outs, ins, specs=None, scratch=(), limit=56, flops=0, moved=0, grid=None, out_specs=None, name=None):
    vmem = pl.BlockSpec(memory_space=pltpu.VMEM)
    extra = {} if grid is None else {"grid": grid}
    return pl.pallas_call(
        kernel,
        out_shape=outs,
        in_specs=[vmem if s is None else s for s in (specs or [None] * len(ins))],
        out_specs=out_specs if out_specs is not None else [vmem] * len(outs),
        scratch_shapes=list(scratch),
        compiler_params=pltpu.CompilerParams(vmem_limit_bytes=limit * MIB),
        cost_estimate=pl.CostEstimate(flops=0, bytes_accessed=0, transcendentals=0),
        name=name,
        **extra,
    )(*ins)


def like(shape, dtype):
    return jax.ShapeDtypeStruct(shape, dtype)


def turned(block, axis, by):
    size = lax.axis_size(axis)
    return lax.ppermute(block, axis, [(i, (i + by) % size) for i in range(size)])


def crossed(block, axis, bit):
    return lax.ppermute(block, axis, [(i, i ^ bit) for i in range(lax.axis_size(axis))])


def after(value, first):
    return lax.optimization_barrier((value, first))[0]


def scatter_first(c0, c1, c2a, c2b, c3, axis):
    half = c2a.shape[0]
    right, left = turned(c2a, axis, 1), turned(c2b, axis, -1)
    return c0, jnp.concatenate([c1[:half] + right, c1[half:]], axis=0), jnp.concatenate([c3[:half], c3[half:] + left], axis=0)


def scatter_second(c0, c1, c3, axis):
    return c0, turned(c1, axis, 1), turned(c3, axis, -1)


def side_of(bit):
    return (lax.axis_index("dp") // bit) % 2


def gather_first(block, axis):
    return turned(block, axis, 1), turned(block, axis, -1)


def gather_second(before, later, axis):
    half = before.shape[0] // 2
    return turned(before[:half], axis, 1), turned(later[half:], axis, -1)


def ring_gather(block, axis):
    first = gather_first(block, axis)
    return (*first, *gather_second(*first, axis))


class Sizes:
    def __init__(self, qkv, out, shards, pos_rows):
        _, _, groups, part, width = qkv
        self.shards, self.groups, self.gw, self.gi = shards, groups, width, part
        self.d = out[2]
        self.part = out[1]
        self.at_small = 3 * part
        self.rows = 2 * self.part
        self.pos = pos_rows // 4
        self.extra = self.pos + 16


def pack_weights(z, qkv, out, fin, fout, small):
    def kernel(qkv_ref, out_ref, fin_ref, fout_ref, small_ref, o_ref, own_ref):
        shard = lax.axis_index("shard")

        def spread(pieces):
            return jnp.concatenate([piece.astype(F32) for piece in pieces], axis=1).astype(BF16)

        o_ref[0, 0] = out_ref[...]
        o_ref[0, 1] = fin_ref[...].reshape(z.part, z.d)
        for c in range(3):
            o_ref[1, 0, c * z.gi : (c + 1) * z.gi] = spread([qkv_ref[c, g] for g in range(z.groups)])
        tall = jnp.concatenate([small_ref[...].astype(F32), jnp.zeros((16 - small_ref.shape[0], z.part), F32)], axis=0)
        wide = jnp.concatenate([tall] * z.shards, axis=1)
        lane = group_of(iota(wide.shape, 1), z.part, z.shards)
        o_ref[1, 0, z.at_small : z.at_small + 16] = jnp.where(lane == shard, wide, 0.0).astype(BF16)
        o_ref[1, 0, z.at_small + 16 : z.part] = jnp.zeros((z.part - z.at_small - 16, z.d), BF16)
        o_ref[1, 1] = spread([fout_ref[g] for g in range(z.groups)])
        own_ref[...] = o_ref[side_of(1), side_of(2)]

    return call(kernel, [like((2, 2, z.part, z.d), BF16), like((z.part, z.d), BF16)], (qkv, out, fin, fout, small), name="pack")


class Pieces:
    def __init__(self, z, local, mine, others, layer):
        self.z, self.layer = z, layer
        self.arrays = (local, *mine, *others)
        self.specs = [pl.BlockSpec(memory_space=pl.ANY)] * len(self.arrays)
        self.scratch = [pltpu.VMEM((2, z.shards, z.rows, z.d), BF16), pltpu.SemaphoreType.DMA((2, 2, 4))]

    def start(self, refs, w_ref, sems, parts):
        z = self.z
        core, y = side_of(1), side_of(2)
        shard = lax.axis_index("shard")
        own_layer = lax.axis_index("section") == self.layer
        local, mine, others = refs[0], refs[1:9], refs[9:21]
        waits = {}
        for part in parts:
            copies = []
            for side in range(2):
                place = core if side == 0 else 1 - core
                for n, by in enumerate((0, 3, 1, 2)):
                    target = w_ref.at[place, (shard + by) % z.shards, pl.ds(part * z.part, z.part)]
                    sem = sems.at[part, side, n]
                    rows = pl.ds((n - 1) * z.part, z.part)
                    choices = []
                    for across in range(2):
                        here = (y == part) if across == 0 else (y != part)
                        at = 2 * across + side
                        if n == 0:
                            own, other = local.at[place, part], others[3 * at]
                        elif n < 3:
                            own, other = mine[2 * at].at[rows], others[3 * at + 1].at[rows]
                        else:
                            own, other = mine[2 * at + 1], others[3 * at + 2]
                        choices.append((jnp.logical_and(here, own_layer), own))
                        choices.append((jnp.logical_and(here, jnp.logical_not(own_layer)), other))
                    for here, source in choices:
                        copy = pltpu.make_async_copy(source, target, sem)
                        pl.when(here)(copy.start)
                    copies.append(pltpu.make_async_copy(choices[1][1], target, sem))
            waits[part] = copies
        return waits


def wait_all(copies):
    for copy in copies:
        copy.wait()


class Loads:
    def __init__(self, arrays):
        self.names = list(arrays)
        self.arrays = list(arrays.values())
        self.specs = [pl.BlockSpec(memory_space=pl.ANY)] * len(self.arrays)
        self.scratch = [pltpu.VMEM(a.shape, a.dtype) for a in self.arrays] + [pltpu.SemaphoreType.DMA((len(self.arrays),))]

    def start(self, refs, scratch):
        self.buffers = dict(zip(self.names, scratch))
        self.copies = {
            name: pltpu.make_async_copy(ref, buffer, scratch[-1].at[n])
            for n, (name, ref, buffer) in enumerate(zip(self.names, refs, scratch))
        }
        for copy in self.copies.values():
            copy.start()

    def __getitem__(self, name):
        copy = self.copies.pop(name, None)
        if copy is not None:
            copy.wait()
        return self.buffers[name]


class Stores:
    def __init__(self, shapes, split=()):
        self.names = list(shapes)
        self.shapes = list(shapes.values())
        self.split = split
        self.specs = [pl.BlockSpec(memory_space=pl.ANY)] * len(self.shapes)
        count = sum(a.shape[0] if name in split else 1 for name, a in shapes.items())
        self.scratch = [pltpu.VMEM(a.shape, a.dtype) for a in self.shapes] + [pltpu.SemaphoreType.DMA((count,))]

    def bind(self, refs, scratch):
        self.refs = dict(zip(self.names, refs))
        self.buffers = dict(zip(self.names, scratch))
        self.sems = scratch[-1]
        self.copies = []

    def put(self, name, value, index=None):
        source, target = self.buffers[name], self.refs[name]
        if index is not None:
            source, target = source.at[index], target.at[index]
        source[...] = value.astype(source.dtype)
        copy = pltpu.make_async_copy(source, target, self.sems.at[len(self.copies)])
        copy.start()
        self.copies.append(copy)

    def finish(self):
        wait_all(self.copies)


class Weights:
    def __init__(self, z, w_ref):
        self.z, self.w = z, w_ref

    def out(self):
        z = self.z
        return self.w[0, :, 0 : z.part, :].reshape(z.d, z.d)

    def small(self):
        z = self.z
        return sum(self.w[1, h, z.at_small : z.at_small + 16, :].astype(F32) for h in range(z.shards))

    def proj(self, c):
        z = self.z
        dense = self.w[1, :, c * z.gi : (c + 1) * z.gi, :].reshape(z.gw, z.d)
        tall = jnp.concatenate([dense] * z.groups, axis=0)
        keep = group_of(iota(tall.shape, 0), z.gw, z.groups) == group_of(iota(tall.shape, 1), z.gw, z.groups)
        return jnp.where(keep, tall, jnp.zeros_like(tall))

    def fin(self, g):
        z = self.z
        row = z.part + g * z.gi
        dense = self.w[0, :, row : row + z.gi, :].reshape(z.gw, z.d)
        blank = jnp.zeros_like(dense)
        return jnp.concatenate([dense, blank] if g % 2 == 0 else [blank, dense], axis=0)

    def fout(self, g):
        z = self.z
        at = (g // 2) * 2 * z.gw
        pair = self.w[1, :, z.part : z.rows, at : at + 2 * z.gw].reshape(z.d, 2 * z.gw)
        keep = (iota(pair.shape, 1) >= z.gw) == (g % 2 == 1)
        return jnp.where(keep, pair, jnp.zeros_like(pair))


def embed_parts(picked, ids_by, pos_table, vocab):
    count, _, seq = ids_by.shape
    width = picked.shape[1]
    half = seq // 2
    rows = pos_table.shape[0]

    def kernel(p_ref, i_ref, t_ref, c0, c1, c2a, c2b, c3):
        shard = lax.axis_index("shard")
        for k in range(count):
            span = slice(k * seq, (k + 1) * seq)
            token, seg_row = i_ref[k, 0:1], i_ref[k, 2:3]
            seg_col = upright(seg_row, seq)
            same = seg_col == seg_row.astype(F32)
            earlier = iota((seq, seq), 1) < iota((seq, seq), 0)
            place = jnp.sum(jnp.where(same & earlier, 1.0, 0.0), axis=1, keepdims=True).astype(jnp.int32) - shard * rows
            spot = (iota((seq, rows), 1) == place).astype(BF16)
            local = token - shard * vocab
            inside = upright(jnp.where((local >= 0) & (local < vocab), 1.0, 0.0), seq)
            word = jnp.where(inside > 0.5, p_ref[span].astype(F32), 0.0)
            total = (word + nn(spot, t_ref[...])).astype(BF16)
            if k == 2:
                c2a[...] = total[:half]
                c2b[...] = total[half:]
            else:
                (c0, c1, None, c3)[k][...] = total

    full, part = like((seq, width), BF16), like((half, width), BF16)
    return call(kernel, [full, full, part, part, full], (picked, ids_by, pos_table), moved=4 * MIB, name="embed_parts")


def layer_forward(z, pieces, seg_row, first, words=None, layer_in=None):
    seq = seg_row.shape[1]
    d = z.d
    flat, whole = like((seq, d), BF16), like((seq, d), F32)
    shapes = {"q": flat, "k": flat, "v": flat, "p": like((HEADS, seq, seq), BF16), "att": flat, "n1": whole, "mid": flat}
    shapes.update({"act": like((z.groups, seq, d), BF16), "slope": like((z.groups, seq, d), BF16)})
    shapes.update({"n2": whole, "stats": like((seq, 128), F32), "small": like((16, d), F32), "out": flat})
    if first:
        shapes.update({"x": flat, "n0": whole})
    stores = Stores(shapes, split=("p", "act", "slope"))
    head = d // HEADS
    inputs = list(words) if first else [layer_in]

    def kernel(*refs):
        piece_refs, refs = refs[: len(pieces.arrays)], refs[len(pieces.arrays) :]
        row_ref, refs = refs[0], refs[1:]
        in_refs, refs = refs[: len(inputs)], refs[len(inputs) :]
        out_refs, refs = refs[: len(shapes)], refs[len(shapes) :]
        w_ref, sems, *buffers = refs
        waits = pieces.start(piece_refs, w_ref, sems, (0, 1))
        stores.bind(out_refs, buffers)
        put = stores.put
        w = Weights(z, w_ref)
        if first:
            unit, r0 = normed(sum(ref[...].astype(F32) for ref in in_refs))
            put("n0", unit)
        wait_all(waits[0])
        small = w.small()
        put("small", small)
        if first:
            x = unit * small[11:12] + small[12:13]
            x_low = x.astype(BF16)
            put("x", x_low)
        else:
            r0 = jnp.zeros((seq, 1), F32)
            x_low = in_refs[0][...]
            x = x_low.astype(F32)
        q = (nn(x_low, w.proj(0)).astype(BF16).astype(F32) * (1.0 / math.sqrt(head))).astype(BF16)
        k = nn(x_low, w.proj(1)).astype(BF16)
        v = (nn(x_low, w.proj(2)) + small[2:3]).astype(BF16)
        put("q", q)
        put("k", k)
        put("v", v)
        same = upright(row_ref[...], seq) == row_ref[...].astype(F32)
        second = iota((seq, 128), 1) >= head
        tiles = []
        for t in range(d // 128):
            lanes = slice(t * 128, (t + 1) * 128)
            q_t, k_t, v_t = q[:, lanes], k[:, lanes], v[:, lanes]
            results = []
            for j in range(2):
                picked = jnp.where(second == (j == 1), q_t, jnp.zeros_like(q_t))
                scores = jnp.where(same, nt(picked, k_t), MASKED)
                scores = jnp.exp(scores - jnp.max(scores, axis=-1, keepdims=True))
                probs = (scores * (1.0 / jnp.sum(scores, axis=-1, keepdims=True))).astype(BF16)
                put("p", probs, 2 * t + j)
                results.append(nn(probs, v_t))
            tiles.append(jnp.where(second, results[1], results[0]).astype(BF16))
        attended = jnp.concatenate(tiles, axis=1)
        put("att", attended)
        unit, r1 = normed(x + (nn(attended, w.out()) + small[3:4]))
        put("n1", unit)
        middle = unit * small[0:1] + small[4:5]
        middle_low = middle.astype(BF16)
        put("mid", middle_low)
        wait_all(waits[1])
        back = [None] * (z.groups // 2)
        for g in range(z.groups):
            pair = slice((g // 2) * 2 * z.gw, (g // 2 + 1) * 2 * z.gw)
            pre = nn(middle_low[:, pair], w.fin(g)) + small[5 + g : 6 + g]
            half = 0.5 + 0.5 * lax.erf(pre * math.sqrt(0.5))
            slope = half + pre * (jnp.exp(-0.5 * pre * pre) * (1.0 / math.sqrt(2.0 * math.pi)))
            active = (pre * half).astype(BF16)
            put("act", active, g)
            put("slope", slope, g)
            added = nn(active, w.fout(g))
            back[g // 2] = added if back[g // 2] is None else back[g // 2] + added
        unit, r2 = normed(middle + (jnp.concatenate(back, axis=1) + small[9:10]))
        put("n2", unit)
        put("out", unit * small[1:2] + small[10:11])
        lane = iota((seq, 128), 1)
        put("stats", jnp.where(lane == 0, r0, jnp.where(lane == 1, r1, r2)))
        stores.finish()

    outs = call(
        kernel,
        stores.shapes,
        (*pieces.arrays, seg_row, *inputs),
        specs=pieces.specs + [None] * (1 + len(inputs)),
        out_specs=stores.specs,
        scratch=pieces.scratch + stores.scratch,
        flops=3 * 10**9,
        moved=16 * MIB,
        name="layer_first" if first else "layer_second",
    )
    return dict(zip(stores.names, outs))


def send_halves(z, g_ref, keep_ref, send_ref, sems):
    core = lax.axis_index("dp") % 2
    shard = lax.axis_index("shard")
    copies = []
    for k in range(z.shards):
        to = (shard + k) % z.shards
        copies.append(pltpu.make_async_copy(g_ref.at[1 - core, to], send_ref.at[k], sems.at[2 * k]))
        copies.append(pltpu.make_async_copy(g_ref.at[core, to], keep_ref.at[k], sems.at[2 * k + 1]))
    for copy in copies:
        copy.start()
    return copies


def ffn_backward(z, pieces, state, out_grad):
    seq, d = out_grad.shape
    loads = Loads({"dy": out_grad, **{key: state[key] for key in ("n2", "stats", "small", "mid", "act", "slope")}})
    outs = [like((seq, d), F32), like((16, d), F32)] + [like((z.shards, z.part, d), BF16)] * 2

    def kernel(*refs):
        piece_refs, refs = refs[: len(pieces.arrays)], refs[len(pieces.arrays) :]
        load_refs, refs = refs[: len(loads.names)], refs[len(loads.names) :]
        dm_ref, small_ref, keep_ref, send_ref, w_ref, sems, g_ref, out_sems, *buffers = refs
        loads.start(load_refs, buffers)
        waits = pieces.start(piece_refs, w_ref, sems, (1,))
        w = Weights(z, w_ref)
        dy = loads["dy"][...].astype(F32)
        n2 = loads["n2"][...]
        scale = loads["stats"][:, 2:3]
        small = loads["small"][...]
        gain_two, shift_two = col_sum(dy * n2), col_sum(dy)
        d_final = norm_back(dy, n2, scale, small[1:2])
        d_ffn = d_final.astype(BF16)
        ffn_shift = col_sum(d_ffn.astype(F32))
        middle_t = loads["mid"][...].T
        act, slope = loads["act"], loads["slope"]
        wait_all(waits[1])
        pre_shift = []
        pair_back = [None] * (z.groups // 2)
        for p in range(z.groups // 2):
            lanes = slice(p * 2 * z.gw, (p + 1) * 2 * z.gw)
            out_pair = d_ffn[:, lanes]
            back_pair = []
            for g in (2 * p, 2 * p + 1):
                d_pre = (nt(out_pair, w.fout(g)) * slope[g].astype(F32)).astype(BF16)
                pre_shift.append(col_sum(d_pre.astype(F32)))
                back_pair.append(tn(act[g], out_pair))
                grad_in = nn(middle_t[g * z.gw : (g + 1) * z.gw], d_pre)
                g_ref[0, :, g * z.gi : (g + 1) * z.gi, :] = grad_in.astype(BF16).reshape(z.shards, z.gi, d)
                added = nt(d_pre, w.fin(g))
                pair_back[p] = added if pair_back[p] is None else pair_back[p] + added
            odd = iota(back_pair[0].shape, 1) >= z.gw
            both = jnp.where(odd, back_pair[1], back_pair[0]).astype(BF16)
            g_ref[1, :, :, lanes] = both.reshape(z.shards, z.part, 2 * z.gw)
        copies = send_halves(z, g_ref, keep_ref, send_ref, out_sems)
        dm_ref[...] = d_final + jnp.concatenate(pair_back, axis=1)
        blank = jnp.zeros((1, d), F32)
        small_ref[...] = jnp.concatenate(
            [blank, gain_two, blank, blank, blank, *pre_shift, ffn_shift, shift_two, jnp.zeros((5, d), F32)], axis=0
        )
        wait_all(copies)

    anywhere = pl.BlockSpec(memory_space=pl.ANY)
    return call(
        kernel,
        outs,
        (*pieces.arrays, *loads.arrays),
        specs=pieces.specs + loads.specs,
        out_specs=[pl.BlockSpec(memory_space=pltpu.VMEM)] * 2 + [anywhere] * 2,
        scratch=pieces.scratch + [pltpu.VMEM((2, z.shards, z.part, d), BF16), pltpu.SemaphoreType.DMA((2 * z.shards,))] + loads.scratch,
        flops=8 * 10**9,
        moved=16 * MIB,
        name="ffn_back",
    )


def attention_backward(z, pieces, state, d_middle, small_in, first, seg_row=None, pos_rows=0):
    seq, d = d_middle.shape
    head = d // HEADS
    keys = ["n1", "stats", "small", "att", "q", "k", "v", "p", "x"] + (["n0"] if first else [])
    loads = Loads({"dm": d_middle, **{key: state[key] for key in keys}, "grads": small_in, **({"seg": seg_row} if first else {})})
    rows = z.part + (2 * z.extra if first else 0)
    outs = [like((seq, d), F32), like((seq, d), BF16)] + [like((z.shards, rows, d), BF16)] * 2
    blocks = 2 * lax.axis_size("dp")
    if first:
        outs.append(like((blocks, d // blocks, seq), BF16))

    def kernel(*refs):
        piece_refs, refs = refs[: len(pieces.arrays)], refs[len(pieces.arrays) :]
        load_refs, refs = refs[: len(loads.names)], refs[len(loads.names) :]
        dx_ref, low_ref, keep_ref, send_ref = refs[:4]
        de_ref = refs[4] if first else None
        w_ref, sems, g_ref, out_sems, *buffers = refs[len(outs) :]
        loads.start(load_refs, buffers)
        waits = pieces.start(piece_refs, w_ref, sems, (0,))
        w = Weights(z, w_ref)
        d_middle = loads["dm"][...]
        n1 = loads["n1"][...]
        stats = loads["stats"][...]
        r0, r1 = stats[:, 0:1], stats[:, 1:2]
        small = loads["small"][...]
        gain_one, shift_one = col_sum(d_middle * n1), col_sum(d_middle)
        d_mid = norm_back(d_middle, n1, r1, small[0:1])
        d_branch = d_mid.astype(BF16)
        branch_shift = col_sum(d_branch.astype(F32))
        g_ref[0, :, 0 : z.part, :] = tn(loads["att"][...], d_branch).astype(BF16).reshape(z.shards, z.part, d)
        wait_all(waits[0])
        d_att = nt(d_branch, w.out()).astype(BF16)
        second = iota((seq, 128), 1) >= head
        scale = 1.0 / math.sqrt(head)
        q_ref, k_ref, v_ref, p_ref = (loads[key] for key in ("q", "k", "v", "p"))
        dq, dk, dv = [], [], []
        for t in range(d // 128):
            lanes = slice(t * 128, (t + 1) * 128)
            q_t, k_t, v_t, a_t = q_ref[:, lanes], k_ref[:, lanes], v_ref[:, lanes], d_att[:, lanes]
            parts = []
            for j in range(2):
                a_j = jnp.where(second == (j == 1), a_t, jnp.zeros_like(a_t))
                probs_low = p_ref[2 * t + j]
                probs = probs_low.astype(F32)
                d_probs = nt(a_j, v_t)
                inner = jnp.sum(probs * d_probs, axis=-1, keepdims=True)
                d_scores = (probs * (d_probs - inner)).astype(BF16)
                parts.append((nn(d_scores, k_t), tn(d_scores, q_t), tn(probs_low, a_t)))
            dq.append((jnp.where(second, parts[1][0], parts[0][0]) * scale).astype(BF16))
            dk.append(jnp.where(second, parts[1][1], parts[0][1]).astype(BF16))
            dv.append(jnp.where(second, parts[1][2], parts[0][2]).astype(BF16))
        value_shift = col_sum(jnp.concatenate(dv, axis=1).astype(F32))
        x_t = loads["x"][...].T
        d_in = d_mid
        for c, parts in enumerate((dq, dk, dv)):
            d_c = jnp.concatenate(parts, axis=1)
            full = nn(x_t, d_c)
            lane = group_of(iota((z.gw, d), 1), z.gw, z.groups)
            grad = full[0 : z.gw]
            for g in range(1, z.groups):
                grad = jnp.where(lane == g, full[g * z.gw : (g + 1) * z.gw], grad)
            g_ref[1, :, c * z.gi : (c + 1) * z.gi, :] = grad.astype(BF16).reshape(z.shards, z.gi, d)
            d_in = d_in + nt(d_c, w.proj(c))
        blank = jnp.zeros((1, d), F32)
        small_grads = jnp.concatenate([gain_one, blank, value_shift, branch_shift, shift_one, jnp.zeros((11, d), F32)], axis=0)
        small_grads = (small_grads + loads["grads"][...]).astype(BF16)
        spare = jnp.zeros((z.part - z.at_small - 16, d), BF16)
        for h in range(z.shards):
            g_ref[1, h, z.at_small : z.at_small + 16, :] = small_grads
            g_ref[1, h, z.at_small + 16 : z.part, :] = spare
        if first:
            n0 = loads["n0"][...]
            embed_grads = jnp.concatenate([col_sum(d_in * n0), col_sum(d_in), jnp.zeros((14, d), F32)], axis=0).astype(BF16)
            d_embed = norm_back(d_in, n0, r0, small[11:12])
            d_embed_t = d_embed.T
            bits = blocks.bit_length() - 1
            me = lax.axis_index("section") * (blocks // 2) + lax.axis_index("dp")
            for b in range(blocks):
                to = me ^ b
                place = sum(((to >> bit) & 1) << (bits - 1 - bit) for bit in range(bits))
                de_ref[place] = d_embed_t[b * (d // blocks) : (b + 1) * (d // blocks)].astype(BF16)
            seg = loads["seg"][...]
            same = upright(seg, seq) == seg.astype(F32)
            later = iota((seq, seq), 0) < iota((seq, seq), 1)
            place = jnp.sum(jnp.where(same & later, 1.0, 0.0), axis=0, keepdims=True).astype(jnp.int32)
            spot = (iota((pos_rows, seq), 0) == place).astype(BF16)
            pos_grad = nn(spot, d_embed.astype(BF16)).astype(BF16)
            for side in range(2):
                for h in range(z.shards):
                    for y in range(2):
                        row = z.part + y * z.extra
                        part = pos_grad[(2 * side + y) * z.pos : (2 * side + y + 1) * z.pos]
                        g_ref[side, h, row : row + z.pos, :] = part if h == 0 else jnp.zeros_like(part)
                        g_ref[side, h, row + z.pos : row + z.extra, :] = embed_grads
        copies = send_halves(z, g_ref, keep_ref, send_ref, out_sems)
        dx_ref[...] = d_in
        low_ref[...] = d_in.astype(BF16)
        wait_all(copies)

    anywhere = pl.BlockSpec(memory_space=pl.ANY)
    vmem = pl.BlockSpec(memory_space=pltpu.VMEM)
    return call(
        kernel,
        outs,
        (*pieces.arrays, *loads.arrays),
        specs=pieces.specs + loads.specs,
        out_specs=[vmem, vmem, anywhere, anywhere] + [vmem] * (len(outs) - 4),
        scratch=pieces.scratch + [pltpu.VMEM((2, z.shards, rows, d), BF16), pltpu.SemaphoreType.DMA((2 * z.shards,))] + loads.scratch,
        flops=8 * 10**9,
        moved=16 * MIB,
        name="att_back",
    )


def add_cores_split(keep, came):
    shards, part, d = keep[0].shape

    def kernel(a_ref, f_ref, b_ref, e_ref, c0, c1, c2a, c2b, c3):
        for k, ref in ((0, c0), (1, c1), (3, c3)):
            ref[:part] = a_ref[k] + b_ref[k]
            ref[part:] = f_ref[k] + e_ref[k]
        c2a[...] = a_ref[2] + b_ref[2]
        c2b[...] = f_ref[2] + e_ref[2]

    full, half = like((2 * part, d), BF16), like((part, d), BF16)
    return call(kernel, [full, full, half, half, full], (*keep, *came), name="add_cores_split")


def halves_by_y(z, terms):
    def kernel(a_ref, b_ref, c_ref, keep_ref, send_ref):
        y = side_of(2)
        for ref, part in ((keep_ref, y), (send_ref, 1 - y)):
            span = pl.ds(pl.multiple_of(part * z.part, z.part), z.part)
            ref[...] = (a_ref[span].astype(F32) + b_ref[span].astype(F32) + c_ref[span].astype(F32)).astype(BF16)

    return call(kernel, [like((z.part, z.d), BF16)] * 2, terms, name="halves_by_y")


def add_core(z, keep_a, came_a, keep_f, came_f):
    extra = (keep_a.shape[1] - z.part) // 2
    rows = z.part + extra

    def kernel(a_ref, b_ref, c_ref, e_ref, keep_ref, send_ref):
        y = side_of(2)

        def place(ref, part):
            if part == 0:
                ref[:, : z.part] = a_ref[:, : z.part] + b_ref[:, : z.part]
            else:
                ref[:, : z.part] = c_ref[...] + e_ref[...]
            if extra:
                span = slice(z.part + part * extra, z.part + (part + 1) * extra)
                ref[:, z.part :] = a_ref[:, span] + b_ref[:, span]

        @pl.when(y == 0)
        def _():
            place(keep_ref, 0)
            place(send_ref, 1)

        @pl.when(y == 1)
        def _():
            place(keep_ref, 1)
            place(send_ref, 0)

    return call(kernel, [like((z.shards, rows, z.d), BF16)] * 2, (keep_a, came_a, keep_f, came_f), moved=2 * MIB, name="add_core")


def add_split(kept, came):
    _, rows, d = kept.shape
    half = rows // 32 * 16

    def kernel(a_ref, b_ref, c0, c1, c2a, c2b, c3):
        for k, ref in ((0, c0), (1, c1), (3, c3)):
            ref[...] = a_ref[k] + b_ref[k]
        c2a[...] = a_ref[2, :half] + b_ref[2, :half]
        c2b[...] = a_ref[2, half:] + b_ref[2, half:]

    full = like((rows, d), BF16)
    outs = [full, full, like((half, d), BF16), like((rows - half, d), BF16), full]
    return call(kernel, outs, (kept, came), moved=2 * MIB, name="add_split")


def head_forward(pieces, table):
    count = sum(piece.shape[0] for piece in pieces)
    vocab, d = table.shape
    tiles = 6
    block = vocab // tiles
    chunk = 256
    many = len(pieces)

    def kernel(*refs):
        piece_refs, (w_ref, ctx_ref, lse_ref, x_ref, m_ref, s_ref, acc_ref) = refs[:many], refs[many:]
        step = pl.program_id(0)

        @pl.when(step == 0)
        def _():
            at = 0
            for ref in piece_refs:
                x_ref[at : at + ref.shape[0]] = ref[...]
                at += ref.shape[0]
            m_ref[...] = jnp.full(m_ref.shape, -1e30, F32)
            s_ref[...] = jnp.zeros(s_ref.shape, F32)
            acc_ref[...] = jnp.zeros(acc_ref.shape, F32)

        w = w_ref[...]
        for r in range(count // chunk):
            span = slice(r * chunk, (r + 1) * chunk)
            logits = nt(x_ref[span], w)
            old = m_ref[span]
            new = jnp.maximum(old, jnp.max(logits, axis=-1, keepdims=True))
            keep = jnp.exp(old - new)
            part = jnp.exp(logits - new)
            s_ref[span] = s_ref[span] * keep + jnp.sum(part, axis=-1, keepdims=True)
            acc_ref[span] = acc_ref[span] * keep + nn(part.astype(BF16), w)
            m_ref[span] = new

        @pl.when(step == tiles - 1)
        def _():
            total = s_ref[...]
            ctx_ref[...] = acc_ref[...] * (1.0 / total)
            lse = m_ref[...] + jnp.log(total)
            lse_ref[...] = jnp.broadcast_to(lse, (count, 128)).T[0:8]

    fixed = lambda i: (0, 0)
    return call(
        kernel,
        [like((count, d), F32), like((8, count), F32)],
        (*pieces, table),
        specs=[pl.BlockSpec(piece.shape, fixed) for piece in pieces] + [pl.BlockSpec((block, d), lambda i: (i, 0))],
        out_specs=[pl.BlockSpec((count, d), fixed), pl.BlockSpec((8, count), fixed)],
        scratch=[pltpu.VMEM((count, d), BF16), pltpu.VMEM((count, 1), F32), pltpu.VMEM((count, 1), F32), pltpu.VMEM((count, d), F32)],
        grid=(tiles,),
        flops=8 * count * vocab * d,
        moved=14 * MIB,
        name="head_forward",
    )


def head_combine(seq, ctxs, picked, ids_by, lses, vocab):
    shards = ids_by.shape[0]
    d = picked.shape[1]

    def kernel(own_ref, rest_ref, p_ref, i_ref, a_ref, b_ref, c_ref, e_ref, out_ref, lse_ref):
        shard = lax.axis_index("shard")
        parts = (a_ref, b_ref, c_ref, e_ref)
        for k in range(shards):
            rows = [parts[m][:, ((k - m) % shards) * seq : ((k - m) % shards + 1) * seq] for m in range(shards)]
            top = rows[0]
            for row in rows[1:]:
                top = jnp.maximum(top, row)
            total = top + jnp.log(sum(jnp.exp(row - top) for row in rows))
            whole = upright(total, seq)
            span = slice(k * seq, (k + 1) * seq)
            lse_ref[span] = whole
            weight = upright(jnp.exp(rows[0] - total), seq)
            local = i_ref[k, 1:2] - shard * vocab
            inside = upright(jnp.where((local >= 0) & (local < vocab), 1.0, 0.0), seq)
            hit = jnp.where(inside > 0.5, p_ref[span].astype(F32), 0.0)
            ctx = own_ref[...] if k == 0 else rest_ref[(k - 1) * seq : k * seq]
            target = pl.multiple_of(((shard + k) % shards) * seq, seq)
            out_ref[pl.ds(target, seq), :] = (ctx * weight - hit).astype(BF16)

    return call(
        kernel,
        [like((shards * seq, d), BF16), like((shards * seq, 1), F32)],
        (*ctxs, picked, ids_by, *lses),
        moved=7 * MIB,
        name="head_combine",
    )


def head_table(pieces, table, lse, ids_by, first_tile, tiles, block):
    count = sum(piece.shape[0] for piece in pieces)
    shards, _, seq = ids_by.shape
    vocab, d = table.shape
    width = min(vocab - first_tile * block, tiles * block)
    chunk = 256
    many = len(pieces)

    def kernel(*refs):
        piece_refs, (w_ref, lse_ref, i_ref, o_ref, x_ref, xt_ref, t_ref, p_ref) = refs[:many], refs[many:]
        step = pl.program_id(0)

        @pl.when(step == 0)
        def _():
            at = 0
            for ref in piece_refs:
                x_ref[at : at + ref.shape[0]] = ref[...]
                at += ref.shape[0]
            xt_ref[...] = x_ref[...].T
            start = lax.axis_index("shard") * vocab + first_tile * block
            for k in range(shards):
                t_ref[k * seq : (k + 1) * seq] = upright(i_ref[k, 1:2] - start, seq).astype(jnp.int32)

        w = w_ref[...]
        for r in range(count // chunk):
            span = slice(r * chunk, (r + 1) * chunk)
            logits = nt(x_ref[span], w)
            hit = iota(logits.shape, 1) == t_ref[span] - step * block
            p_ref[span] = (jnp.exp(logits - lse_ref[span]) - jnp.where(hit, 1.0, 0.0)).astype(BF16)
        o_ref[...] = nn(xt_ref[...], p_ref[...]).astype(BF16)

    fixed = lambda i: (0, 0)
    return call(
        kernel,
        [like((d, width), BF16)],
        (*pieces, table, lse, ids_by),
        specs=[pl.BlockSpec(piece.shape, fixed) for piece in pieces]
        + [
            pl.BlockSpec((block, d), lambda i: (i + first_tile, 0)),
            pl.BlockSpec((count, 1), fixed),
            pl.BlockSpec(ids_by.shape, lambda i: (0, 0, 0)),
        ],
        out_specs=[pl.BlockSpec((d, block), lambda i: (0, i))],
        scratch=[pltpu.VMEM((count, d), BF16), pltpu.VMEM((d, count), BF16), pltpu.VMEM((count, 1), jnp.int32), pltpu.VMEM((count, block), BF16)],
        grid=(tiles,),
        flops=6 * count * width * d,
        moved=8 * MIB,
        name="head_table",
    )[0]


def list_tokens(ids, vocab):
    count = ids.shape[1]
    unit = 1 << (vocab - 1).bit_length()

    def kernel(ids_ref, list_ref):
        start = lax.axis_index("shard") * vocab

        def step(i, many):
            local = ids_ref[0, i] - start
            list_ref[0, many] = i * unit + local
            return many + ((local >= 0) & (local < vocab)).astype(jnp.int32)

        list_ref[0, count] = lax.fori_loop(0, count, step, jnp.int32(0), unroll=8)

    smem = pl.BlockSpec(memory_space=pltpu.SMEM)
    return call(kernel, [like((1, count + 128), jnp.int32)], (ids,), specs=[smem], out_specs=[smem], name="list_tokens")[0]


def table_grad(denses, pieces, lists, vocab):
    width = denses[0].shape[0]
    many_parts = len(denses)
    own = pieces[0]
    sources, _, seq = own.shape
    shards = 4
    count = shards * sources * seq
    unit = 1 << (vocab - 1).bit_length()
    ways = 4
    listed = shards * seq

    def kernel(*refs):
        d_refs, refs = refs[:many_parts], refs[many_parts:]
        own_ref, before_ref, after_ref, far_a_ref, far_b_ref, l_ref, o_ref, flat_ref, *acc = refs
        def rows_of(k, j):
            if k == 2:
                half = sources // 2
                return far_a_ref[j] if j < half else far_b_ref[j - half]
            return (own_ref, after_ref, None, before_ref)[k][j]

        for k in range(shards):
            for j in range(sources):
                at = (j * shards + k) * seq
                flat_ref[at : at + seq] = rows_of(k, j).astype(F32).T
        for ref in acc:
            ref[...] = jnp.zeros(ref.shape, F32)

        def add(ref, j, at):
            packed = l_ref[j, at]
            row = packed & (unit - 1)
            token = lax.shift_right_logical(packed, unit.bit_length() - 1) + j * listed
            ref[pl.ds(row, 1), :] += flat_ref[pl.ds(token, 1), :]

        def source(j, carry):
            many = l_ref[j, listed]
            rounds = many // ways

            def step(i, carry):
                for way, ref in enumerate(acc):
                    add(ref, j, i * ways + way)
                return carry

            def rest(at, carry):
                add(acc[0], j, at)
                return carry

            lax.fori_loop(0, rounds, step, jnp.int32(0))
            lax.fori_loop(rounds * ways, many, rest, jnp.int32(0))
            return carry

        lax.fori_loop(0, sources, source, jnp.int32(0))
        at = 0
        for ref in d_refs:
            span = slice(at, at + ref.shape[1])
            o_ref[:, span] = ref[...].astype(F32) + sum(part[span] for part in acc).T
            at = span.stop

    smem = pl.BlockSpec(memory_space=pltpu.SMEM)
    return call(
        kernel,
        [like((width, vocab), F32)],
        (*denses, *pieces, lists),
        specs=[None] * (5 + many_parts) + [smem],
        scratch=[pltpu.VMEM((count, width), F32)] + [pltpu.VMEM((vocab, width), F32)] * ways,
        limit=60,
        name="table_grad",
    )[0]


def unpack_grads(z, blocks):
    rows = z.part + z.extra

    def kernel(own_ref, y_ref, core_ref, both_ref, qkv_ref, out_ref, fin_ref, fout_ref, gain_ref, bias_ref, pos_ref, eg_ref, es_ref, all_ref):
        core, y = side_of(1), side_of(2)
        shard = lax.axis_index("shard")
        all_ref[core, y] = own_ref[...]
        all_ref[core, 1 - y] = y_ref[...]
        all_ref[1 - core, y] = core_ref[...]
        all_ref[1 - core, 1 - y] = both_ref[...]

        def own_lanes(value):
            total = jnp.zeros((value.shape[0], z.part), F32)
            for h in range(z.shards):
                total = total + jnp.where(shard == h, value[:, h * z.part : (h + 1) * z.part], 0.0)
            return total

        out_ref[...] = all_ref[0, 0, : z.part].astype(F32)
        fin_ref[...] = all_ref[0, 1, : z.part].astype(F32).reshape(z.groups, z.gi, z.d)
        for c in range(3):
            part = all_ref[1, 0, c * z.gi : (c + 1) * z.gi].astype(F32)
            for g in range(z.groups):
                qkv_ref[c, g] = part[:, g * z.gw : (g + 1) * z.gw]
        part = all_ref[1, 1, : z.part].astype(F32)
        for g in range(z.groups):
            fout_ref[g] = part[:, g * z.gw : (g + 1) * z.gw]
        small = own_lanes(all_ref[1, 0, z.at_small : z.at_small + 16].astype(F32))
        gain_ref[...] = small[0:2]
        bias_ref[...] = small[2:11]
        for n in range(4):
            pos_ref[n * z.pos : (n + 1) * z.pos] = all_ref[n // 2, n % 2, z.part : z.part + z.pos].astype(F32)
        small = own_lanes(all_ref[0, 0, z.part + z.pos : rows].astype(F32))
        eg_ref[...] = small[0:1]
        es_ref[...] = small[1:2]

    return call(
        kernel,
        [
            like((3, z.groups, z.gi, z.gw), F32),
            like((z.part, z.d), F32),
            like((z.groups, z.gi, z.d), F32),
            like((z.groups, z.part, z.gw), F32),
            like((2, z.part), F32),
            like((9, z.part), F32),
            like((4 * z.pos, z.d), F32),
            like((1, z.part), F32),
            like((1, z.part), F32),
        ],
        blocks,
        scratch=[pltpu.VMEM((2, 2, rows, z.d), BF16)],
        name="unpack",
    )


def body(token_ids, targets, segment_ids, word_table, pos_table, embed_gain, embed_shift, qkv_weight, out_weight, ffn_in, ffn_out, layer_gains, layer_biases):
    micro, _, seq = token_ids.shape
    vocab, d = word_table.shape
    pos_rows = pos_table.shape[0]
    shards = lax.axis_size("shard")
    dp = lax.axis_size("dp")
    both = ("section", "dp")
    section = lax.axis_index("section")
    first = section == 0
    z = Sizes(qkv_weight.shape, out_weight.shape, shards, pos_rows)
    offset = lax.axis_index("shard") * vocab

    mine = lax.dynamic_index_in_dim(jnp.stack([token_ids[:, 0], targets[:, 0], segment_ids[:, 0]], axis=1), section, 0, keepdims=False)
    ids_by = jnp.stack([mine, turned(mine, "shard", -1), turned(mine, "shard", 2), turned(mine, "shard", 1)])
    seg_row = mine[2:3]

    def rows_of(ids):
        return word_table.at[jnp.clip(ids.reshape(-1) - offset, 0, vocab - 1)].get(mode="promise_in_bounds")

    small = jnp.concatenate([layer_gains[0], layer_biases[0], embed_gain[None], embed_shift[None]], axis=0)
    local, packed = pack_weights(z, qkv_weight[0], out_weight[0], ffn_in[0], ffn_out[0], small)
    cross_own = crossed(packed, "section", 1)
    near = gather_first(packed, "shard")
    picked = rows_of(ids_by[:, 0])
    near, cross_own, pos_table = after((near, cross_own, pos_table), (near, cross_own))
    word_parts = embed_parts(picked, ids_by, pos_table, vocab)
    near, cross_own = after((near, cross_own), word_parts)
    near_rows = jnp.concatenate(near, axis=0)
    near_y = crossed(near_rows, "dp", 2)
    cross_near = crossed(near_rows, "section", 1)
    cross_own_y = crossed(cross_own, "dp", 2)
    word_parts = scatter_first(*word_parts, "shard")
    far = gather_second(*near, "shard")
    far, word_parts = after((far, word_parts), (far, word_parts, cross_own_y))
    far = jnp.concatenate(far, axis=0)
    words = scatter_second(*word_parts, "shard")
    cross_far = crossed(far, "section", 1)
    far_y = crossed(far, "dp", 2)
    cross_near_y = crossed(cross_near, "dp", 2)
    target_rows = rows_of(after(ids_by[:, 1], (near_y, cross_near)))
    cross_far, words = after((cross_far, words), target_rows)
    cross_far_y = crossed(cross_far, "dp", 2)
    mine = (near_rows, far)
    mine_y = (near_y, far_y)
    others = (cross_own, cross_near, cross_far)
    others_y = (cross_own_y, cross_near_y, cross_far_y)
    mine = (*mine, *(crossed(b, "dp", 1) for b in mine), *mine_y, *(crossed(b, "dp", 1) for b in mine_y))
    others = (*others, *(crossed(b, "dp", 1) for b in others), *others_y, *(crossed(b, "dp", 1) for b in others_y))
    weights_one, weights_two = (Pieces(z, local, mine, others, layer) for layer in range(2))
    one = layer_forward(z, weights_one, seg_row, True, words=words)
    two = layer_forward(z, weights_two, seg_row, False, layer_in=one["out"])
    two["x"] = one["out"]

    ring_first = gather_first(two["out"], "shard")
    ctx_own, lse_own = head_forward([two["out"]], word_table)
    before, later = after(ring_first, ctx_own)
    far_a, far_b = gather_second(before, later, "shard")
    ctx_rest, lse_rest = head_forward([later, far_a, far_b, before], word_table)
    lse = jnp.concatenate([lse_own[0:1], lse_rest[0:1]], axis=1)
    lists = list_tokens(after(ids_by[:, 0].reshape(1, -1), lse), vocab)
    lses = (lse, turned(lse, "shard", -1), turned(lse, "shard", 2), turned(lse, "shard", 1))
    lses = after(lses, lists)
    parts, whole_lse = head_combine(seq, (ctx_own, ctx_rest), target_rows, ids_by, lses, vocab)
    out_grad = lax.psum_scatter(parts, "shard", scatter_dimension=0, tiled=True)
    dense = head_table([two["out"], later, far_a, far_b, before], word_table, whole_lse, ids_by, 0, 6, 1280)

    bit = 1
    while bit < dp:
        lists = jnp.concatenate([lists, crossed(lists, "dp", bit)], axis=0)
        bit *= 2
    lists = jnp.concatenate([lists, crossed(lists, "section", 1)], axis=0)
    out_grad = after(out_grad, (dense, lists))
    dense = lax.psum_scatter(dense, both, scatter_dimension=0, tiled=True)

    d_middle, small_grads, keep_f, send_f = ffn_backward(z, weights_two, two, out_grad)
    in_two, in_low, keep_a, send_a = attention_backward(z, weights_two, two, d_middle, small_grads, False)
    came_f, came_a = crossed(send_f, "dp", 1), crossed(send_a, "dp", 1)
    d_middle, small_grads, keep_one_f, send_one_f = ffn_backward(z, weights_one, one, in_low)
    keep_f, came_f, keep_a, came_a = after((keep_f, came_f, keep_a, came_a), d_middle)
    split_two = add_cores_split((keep_a, keep_f), (came_a, came_f))
    d_middle = after(d_middle, split_two)
    terms_two = scatter_first(*split_two, "shard")
    came_one_f = crossed(send_one_f, "dp", 1)
    in_one, in_one_low, keep_one_a, send_one_a, d_embed = attention_backward(z, weights_one, one, d_middle, small_grads, True, seg_row, pos_rows)
    keep_one_f, came_one_f = after((keep_one_f, came_one_f), d_embed)
    send_one_a, d_embed = after((send_one_a, d_embed), terms_two)
    came_one_a = crossed(send_one_a, "dp", 1)
    columns = d_embed[None]
    steps = [("dp", 1 << n) for n in range(dp.bit_length() - 1)] + [("section", 1)]
    for n, (axis, bit) in enumerate(steps):
        middle = columns.shape[1] // 2
        columns = jnp.concatenate([columns[:, :middle], crossed(columns[:, middle:], axis, bit)], axis=0)
        if n == 0:
            came_one_a = after(came_one_a, columns)
    columns = columns[:, 0]
    stay_one, leave_one = add_core(z, keep_one_a, came_one_a, keep_one_f, came_one_f)
    came_one = crossed(leave_one, "dp", 2)
    terms_two = scatter_second(*terms_two, "shard")
    terms_two, columns = after((terms_two, columns), (stay_one, columns))
    stay_two, leave_two = halves_by_y(z, terms_two)
    ring_columns = gather_first(after(columns, stay_two), "shard")
    stay_one = after(stay_one, stay_two)
    split_one = add_split(stay_one, came_one)
    terms_one = scatter_first(*split_one, "shard")
    sum_two = stay_two + crossed(leave_two, "dp", 2)
    ring_columns = after(ring_columns, terms_one)
    sum_one = sum(scatter_second(*terms_one, "shard"))
    layer_one, extra = sum_one[: z.part], sum_one[z.part :]
    keep = jnp.concatenate([jnp.where(first, layer_one, sum_two), extra], axis=0)
    send = jnp.concatenate([jnp.where(first, sum_two, layer_one), extra], axis=0)
    total = keep + crossed(send, "section", 1)
    far_columns = gather_second(*after(ring_columns, sum_one), "shard")
    bit = 4
    while bit < dp:
        total = total + crossed(total, "dp", bit)
        bit *= 2
    total_y = crossed(total, "dp", 2)
    unpacked = unpack_grads(z, (total, total_y, crossed(total, "dp", 1), crossed(total_y, "dp", 1)))

    word_grad = table_grad([dense], (columns, *ring_columns, *far_columns), lists, vocab).T

    def by_micro(layer_one, layer_two, moved, dtype):
        own = jnp.where(first, layer_one, layer_two)
        sent = jnp.where(first, layer_two, layer_one).astype(moved)
        came = crossed(sent, "section", 1).astype(dtype)
        return jnp.stack([jnp.where(first, own, came), jnp.where(first, came, own)]).reshape(1, micro, 1, seq, d)

    layer_outputs = by_micro(one["out"], two["out"], BF16, BF16)
    input_grads = by_micro(in_one, in_two, BF16, F32)
    qkv_g, out_g, fin_g, fout_g, gain_g, bias_g, pos_g, eg_g, es_g = unpacked
    return (
        layer_outputs,
        input_grads,
        word_grad,
        pos_g,
        eg_g.reshape(-1),
        es_g.reshape(-1),
        qkv_g[None],
        out_g[None],
        fin_g[None],
        fout_g[None],
        gain_g[None],
        bias_g[None],
    )


def solution(mesh):
    rows = P(None, ("dp", "shard"), None)
    weights = (
        P("section", None, None, "shard", None),
        P("section", "shard", None),
        P("section", None, "shard", None),
        P("section", None, "shard", None),
        P("section", None, "shard"),
        P("section", None, "shard"),
    )
    states = P("section", None, ("dp", "shard"), None, None)
    return jax.shard_map(
        body,
        mesh=mesh,
        in_specs=(rows, rows, rows, P("shard", None), P("shard", None), P("shard"), P("shard"), *weights),
        out_specs=(states, states, P("shard", ("section", "dp")), P("shard", None), P("shard"), P("shard"), *weights),
        check_vma=False,
    )
```

time: 625 us -> 475 us (0.76)
  waiting for transfers between devices: 254 us -> 126 us
  blocking collectives: 38.9 us -> 0 us
  starting transfers between devices: 44.1 us -> 76.2 us
  other arithmetic: 20.1 us -> 7.56 us
    ppermute x22 -> x30, waiting for transfers between devices: 105 us -> 41.6 us  [turned(): lax.ppermute(block, axis, [(i, (i + by) % size) for i in range(size)])]
    reduce_scatter x2 -> x0, waiting for transfers between devices: 49.2 us -> none  [shared(): return lax.psum_scatter(kept, 'shard', scatter_dimension=0, tiled=True)[0]]
    ppermute x18 -> x36, waiting for transfers between devices: 40.7 us -> 84.8 us  [crossed(): lax.ppermute(block, axis, [(i, i ^ bit) for i in range(lax.axis_size(axis...]
    reduce_scatter x1, waiting for transfers between devices: 33.1 us -> 0.01 us  [body(): out_grad = lax.psum_scatter(parts, 'shard', scatter_dimension=0, tiled=True)]
    all_gather x1 -> x0, blocking collectives: 27.4 us -> none  [body(): all_ids = lax.all_gather(token_ids[:, 0], ('shard', 'dp'), axis=0)]
    reduce_scatter x1, waiting for transfers between devices: 25.1 us -> 0.02 us  [body(): dense = lax.psum_scatter(dense, both, scatter_dimension=0, tiled=True)]
    ppermute x22 -> x30, starting transfers between devices: 33.8 us -> 50.6 us  [turned(): lax.ppermute(block, axis, [(i, (i + by) % size) for i in range(size)])]
    ppermute x18 -> x36, starting transfers between devices: 9.64 us -> 25.6 us  [crossed(): lax.ppermute(block, axis, [(i, i ^ bit) for i in range(lax.axis_size(axis...]
  transfers between devices with their start and end apart: 45 -> 68, of which waited for: 20 -> 30; matrix products, arithmetic and copies ran while one was open for 8% -> 8% of each run, Pallas kernels for 14% -> 26%
where the time goes in v2:
time: 475 us; the launch traced here: 468 us
  Pallas kernels  197 us (41%)
  waiting for transfers between devices  126 us (27%)
  starting transfers between devices  76.2 us (16%)
  local copies, waits for them, and re-layouts  44.6 us (9%)
  between operations  15.4 us (3%)
  other arithmetic  7.56 us (2%)
    pallas_call x19, Pallas kernels, call(): pl.pallas_call(kernel, out_shape=outs, in_specs=[vmem if s is None else s...  197 us
    ppermute x36, waiting for transfers between devices, crossed(): lax.ppermute(block, axis, [(i, i ^ bit) for i in range(lax.axis_size(axis...  84.8 us
    ppermute x30, starting transfers between devices, turned(): lax.ppermute(block, axis, [(i, (i + by) % size) for i in range(size)])  50.6 us
    ppermute x30, waiting for transfers between devices, turned(): lax.ppermute(block, axis, [(i, (i + by) % size) for i in range(size)])  41.6 us
    ppermute x36, starting transfers between devices, crossed(): lax.ppermute(block, axis, [(i, i ^ bit) for i in range(lax.axis_size(axis...  25.6 us
    gather x2, local copies, waits for them, and re-layouts, rows_of(): word_table.at[jnp.clip(ids.reshape(-1) - offset, 0, vocab - 1)]  23 us
    unnamed x119, local copies, waits for them, and re-layouts  14.9 us
  transfers between devices with their start and end apart: 68, of which 30 were waited for; matrix products, arithmetic and copies ran while one was open for 8% of the time, Pallas kernels for 26%

profile of v2, /device:TPU:0, one launch (start us, length us, event | category | flops | bytes accessed | tf_op | source)
XLA Modules:
  0.0 467.6 jit_solution(10198915960833481045)
XLA Ops:
  8.0 5.1 %collective-permute-start.3 = (s32[3,256]{1,0:T(4,128)S(1)}, s32[3,256]{1,0:T(4,128)S(1)}, u32[]{:S(2)}, u32[]{:S(2)}) collective-permute-start(s32[3,256]{1,0:T(4,128)S(1)} %bitcast.58), channel_id=1, source_target_pairs={{0,3},{1,0},{2,1},{3,2},{4,7},{5,4},{6,5},{7,6},{8,11},{9,8},{10,9... | collective-permute-start | bytes 9224 | tf_op jit(solution)/shard_map/ppermute | solution.py:84
  25.2 11.4 %gather_fusion = bf16[1024,768]{1,0:T(8,128)(2,1)} fusion(bf16[7632,768]{1,0:T(8,128)(2,1)} %refs_5_.1, s32[1024]{0:T(1024)S(1)} %broadcast_clamp_fusion.1), kind=kCustom, calls=%fused_computation | custom fusion | bytes 3149824 | tf_op jit(solution)/shard_map/gather | solution.py:972
  36.6 3.9 embed_parts.1
  47.2 5.6 %collective-permute-done.8 = bf16[128,768]{1,0:T(8,128)(2,1)S(1)} collective-permute-done((bf16[128,768]{1,0:T(8,128)(2,1)}, bf16[128,768]{1,0:T(8,128)(2,1)S(1)}, u32[]{:S(2)}, u32[]{:S(2)}) %collective-permute-start.8) | collective-permute-done | bytes 196640 | tf_op jit(solution)/shard_map/ppermute | solution.py:84
  57.9 3.6 collective-permute-done.10.refs_15_
  75.5 4.2 collective-permute-done.20.refs_24_
  79.7 11.6 %gather_fusion.1 = bf16[1024,768]{1,0:T(8,128)(2,1)} fusion(bf16[7632,768]{1,0:T(8,128)(2,1)} %refs_5_.1, s32[1024]{0:T(1024)S(1)} %broadcast_clamp_fusion), kind=kCustom, calls=%fused_computation.1 | custom fusion | bytes 3149824 | tf_op jit(solution)/shard_map/gather | solution.py:972
  95.0 6.7 %collective-permute-done.25.refs_17_ = bf16[192,768]{1,0:T(8,128)(2,1)S(1)} collective-permute-done((bf16[192,768]{1,0:T(8,128)(2,1)}, bf16[192,768]{1,0:T(8,128)(2,1)S(1)}, u32[]{:S(2)}, u32[]{:S(2)}) %collective-permute-start.25) | collective-permute-done | bytes 294944 | tf_op jit(solution)/shard_map/ppermute | solution.py:88
  104.4 11.1 %layer_first.1 = (bf16[256,768]{1,0:T(8,128)(2,1)}, bf16[256,768]{1,0:T(8,128)(2,1)}, bf16[256,768]{1,0:T(8,128)(2,1)}, bf16[12,256,256]{2,1,0:T(8,128)(2,1)}, b...) custom-call(bf16[2,2,192,768]{3,2,1,0:T(8,128)(2,1)} %get-tuple-elem, ...), custom_call_target="tpu_custom_call" | custom-call | tf_op jit(solution)/shard_map/layer_first/pallas_call | solution.py:65
  115.5 11.1 %layer_second.1 = (bf16[256,768]{1,0:T(8,128)(2,1)}, bf16[256,768]{1,0:T(8,128)(2,1)}, bf16[256,768]{1,0:T(8,128)(2,1)}, bf16[12,256,256]{2,1,0:T(8,128)(2,1)}, ...) custom-call(bf16[2,2,192,768]{3,2,1,0:T(8,128)(2,1)} %get-tuple-elem, ...), custom_call_target="tpu_custom_call" | custom-call | tf_op jit(solution)/shard_map/layer_second/pallas_call | solution.py:65
  130.4 14.6 %head_forward.2 = (f32[256,768]{1,0:T(8,128)}, f32[8,256]{1,0:T(8,128)}) custom-call(bf16[256,768]{1,0:T(8,128)(2,1)} %get-tuple-element.162.refs_0_, bf16[7632,768]{1,0:T(8,128)(2,1)} %refs_5_.1), custom_call_target="tpu_custom_call" | custom-call | tf_op jit(solution)/shard_map/head_forward/pallas_call | solution.py:65
  151.7 5.1 %collective-permute-done.32.refs_1_.refs_2_ = bf16[128,768]{1,0:T(8,128)(2,1)S(1)} collective-permute-done((bf16[128,768]{1,0:T(8,128)(2,1)S(1)}, bf16[128,768]{1,0:T(8,128)(2,1)S(1)}, u32[]{:S(2)}, u32[]{:S(2)}) %collective-permute-start.32) | collective-permute-done | bytes 196640 | tf_op jit(solution)/shard_map/ppermute | solution.py:84
  159.4 33.3 %head_forward.3 = (f32[768,768]{1,0:T(8,128)}, f32[8,768]{1,0:T(8,128)}) custom-call(bf16[256,768]{1,0:T(8,128)(2,1)} %copy-done.19, bf16[128,768]{1,0:T(8,128)(2,1)} %copy-done.29, bf16[128,768]{1,0:T(8,128)(2,1)} %copy-done.30, bf16[256,768]{1,0:T(8,128)(2,1)} %copy-done.18, bf16[7632,768]{1,0:T(8,128)(2,1)} %refs_5_.1), custom_call_target="tpu_custom_call" | custom-call | tf_op jit(solution)/shard_map/head_forward/pallas_call | solution.py:65
  197.5 5.2 %list_tokens.1 = s32[1,1152]{1,0:T(1,128)} custom-call(s32[1,1024]{1,0:T(1,128)} %bitcast.66), custom_call_target="tpu_custom_call" | custom-call | tf_op jit(solution)/shard_map/list_tokens/pallas_call | solution.py:65
  203.3 4.5 head_combine.1
  207.9 31.4 %head_table.1 = bf16[768,7632]{1,0:T(8,128)(2,1)} custom-call(bf16[256,768]{1,0:T(8,128)(2,1)} %get-tuple-element.162.refs_0_, bf16[256,768]{1,0:T(8,128)(2,1)} %copy-done.19, bf16[128,768]{1,0:T(8,128)(2,1)} %copy-done.29, bf16[128,768]{1,0:T(8,128)(2,1)} %copy-done.30, bf16[256,768]{1,0:T(8,128)(2,1)} %copy-done.18, bf16[7632,768]{1,0:T(8,128)(2,1)} %refs_5_.1, ...), custom_call_target="tpu_custom_call" | custom-call | tf_op jit(solution)/shard_map/head_table/pallas_call | solution.py:65
  249.4 8.9 %ffn_back.2 = (f32[256,768]{1,0:T(8,128)}, f32[16,768]{1,0:T(8,128)}, bf16[4,192,768]{2,1,0:T(8,128)(2,1)}, bf16[4,192,768]{2,1,0:T(8,128)(2,1)}) custom-call(bf16[2,2,192,768]{3,2,1,0:T(8,128)(2,1)} %get-tuple-element.137.refs_0_, bf16[384,768]{1,0:T(8,128)(2,1)} %copy-done, bf16[192,768]{1,0:T(8,128)(2,1)} %constant_dynamic-update-slice_fusion.2.refs_2_, ...), custom_call_target="tpu_custom_call" | custom-call | tf_op jit(solution)/shard_map/ffn_back/pallas_call | solution.py:65
  258.4 15.2 %att_back.2 = (f32[256,768]{1,0:T(8,128)}, bf16[256,768]{1,0:T(8,128)(2,1)}, bf16[4,192,768]{2,1,0:T(8,128)(2,1)}, bf16[4,192,768]{2,1,0:T(8,128)(2,1)}) custom-call(bf16[2,2,192,768]{3,2,1,0:T(8,128)(2,1)} %get-tuple-element.137.refs_0_, bf16[384,768]{1,0:T(8,128)(2,1)} %copy-done, bf16[192,768]{1,0:T(8,128)(2,1)} %constant_dynamic-update-slice_fusion.2.refs_2_, ...), custom_call_target="tpu_custom_call" | custom-call | tf_op jit(solution)/shard_map/att_back/pallas_call | solution.py:65
  274.1 8.8 %ffn_back.3 = (f32[256,768]{1,0:T(8,128)}, f32[16,768]{1,0:T(8,128)}, bf16[4,192,768]{2,1,0:T(8,128)(2,1)}, bf16[4,192,768]{2,1,0:T(8,128)(2,1)}) custom-call(bf16[2,2,192,768]{3,2,1,0:T(8,128)(2,1)} %get-tuple-element.137.refs_0_, bf16[384,768]{1,0:T(8,128)(2,1)} %copy-done, bf16[192,768]{1,0:T(8,128)(2,1)} %constant_dynamic-update-slice_fusion.2.refs_2_, ...), custom_call_target="tpu_custom_call" | custom-call | tf_op jit(solution)/shard_map/ffn_back/pallas_call | solution.py:65
  284.4 4.1 add_cores_split.1
  290.9 14.8 %att_back.3 = (f32[256,768]{1,0:T(8,128)}, bf16[256,768]{1,0:T(8,128)(2,1)}, bf16[4,288,768]{2,1,0:T(8,128)(2,1)}, bf16[4,288,768]{2,1,0:T(8,128)(2,1)}, bf16[8,96,256]{2,1,0:T(8,128)(2,1)}) custom-call(bf16[2,2,192,768]{3,2,1,0:T(8,128)(2,1)} %get-tuple-element.137.refs_0_, bf16[384,768]{1,0:T(8,128)(2,1)} %copy-done, ...), custom_call_target="tpu_custom_call" | custom-call | tf_op jit(solution)/shard_map/att_back/pallas_call | solution.py:65
  308.0 4.9 %collective-permute-done.51.e_ref = bf16[4,192,768]{2,1,0:T(8,128)(2,1)S(1)} collective-permute-done((bf16[4,192,768]{2,1,0:T(8,128)(2,1)S(1)}, bf16[4,192,768]{2,1,0:T(8,128)(2,1)S(1)}, u32[]{:S(2)}, u32[]{:S(2)}) %collective-permute-start.51) | collective-permute-done | bytes 1179680 | tf_op jit(solution)/shard_map/ppermute | solution.py:88
  314.5 5.4 %add_core.1 = (bf16[4,240,768]{2,1,0:T(8,128)(2,1)}, bf16[4,240,768]{2,1,0:T(8,128)(2,1)}) custom-call(bf16[4,288,768]{2,1,0:T(8,128)(2,1)} %get-tuple-element.227.a_ref, bf16[4,288,768]{2,1,0:T(8,128)(2,1)} %copy-done.20, bf16[4,192,768]{2,1,0:T(8,128)(2,1)} %get-tuple-element.232.c_ref, bf16[4,192,768]{2,1,0:T(8,128)(2,1)} %copy-done.26), custom_call_target="tpu_custom_call" | custom-call | tf_op jit(solution)/shard_map/add_core/pallas_call | solution.py:65
  323.6 3.8 collective-permute-start.46
  327.4 41.4 %collective-permute-done.48 = bf16[2,2,96,256]{3,2,0,1:T(8,128)(2,1)S(1)} collective-permute-done((bf16[2,2,96,256]{3,2,0,1:T(8,128)(2,1)S(1)}, bf16[2,2,96,256]{3,2,0,1:T(8,128)(2,1)S(1)}, u32[]{:S(2)}, u32[]{:S(2)}) %collective-permute-start.48) | collective-permute-done | bytes 196640 | tf_op jit(solution)/shard_map/ppermute | solution.py:88
  370.4 5.3 %collective-permute-done.49 = bf16[4,1,96,256]{3,2,0,1:T(8,128)(2,1)S(1)} collective-permute-done((bf16[4,1,96,256]{3,2,0,1:T(8,128)(2,1)S(1)}, bf16[4,1,96,256]{3,2,0,1:T(8,128)(2,1)S(1)}, u32[]{:S(2)}, u32[]{:S(2)}) %collective-permute-start.49) | collective-permute-done | bytes 196640 | tf_op jit(solution)/shard_map/ppermute | solution.py:88
  394.1 3.9 collective-permute-start.58
  398.7 7.9 %collective-permute-done.57 = bf16[240,768]{1,0:T(8,128)(2,1)S(1)} collective-permute-done((bf16[240,768]{1,0:T(8,128)(2,1)S(1)}, bf16[240,768]{1,0:T(8,128)(2,1)S(1)}, u32[]{:S(2)}, u32[]{:S(2)}) %collective-permute-start.57) | collective-permute-done | bytes 368672 | tf_op jit(solution)/shard_map/ppermute | solution.py:84
  406.6 3.9 collective-permute-done.58
  422.6 8.1 %collective-permute-done.29 = bf16[256,768]{1,0:T(8,128)(2,1)S(1)} collective-permute-done((bf16[256,768]{1,0:T(8,128)(2,1)S(1)}, bf16[256,768]{1,0:T(8,128)(2,1)S(1)}, u32[]{:S(2)}, u32[]{:S(2)}) %collective-permute-start.29) | collective-permute-done | bytes 393248 | tf_op jit(solution)/shard_map/ppermute | solution.py:88
  433.9 3.6 collective-permute-start.60
  446.3 14.0 %table_grad.1 = f32[96,7632]{1,0:T(8,128)} custom-call(bf16[96,7632]{1,0:T(8,128)(2,1)} %reduce-scatter.5.cloned.1.call-done.refs_0_, bf16[8,96,256]{2,1,0:T(8,128)(2,1)} %copy-done.21, bf16[8,96,256]{2,1,0:T(8,128)(2,1)} %copy-done.27, bf16[8,96,256]{2,1,0:T(8,128)(2,1)} %copy-done.28, bf16[4,96,256]{2,1,0:T(8,128)(2,1)} %copy-done.45, ...), custom_call_target="tpu_custom_call" | custom-call | tf_op jit(solution)/shard_map/table_grad/pallas_call | solution.py:65
  (300 shorter events, 129.9 us)
Async XLA Ops:
  7.2 242.3 %reduce-scatter.3.cloned.1.call-start = ((), (), s32[]{:S(2)}) async-start(), calls=%async_computation.2 | async-start | bytes 1966080 | tf_op jit(solution)/shard_map/reduce_scatter | solution.py:1018
  8.0 15.1 %collective-permute-start.3 = (s32[3,256]{1,0:T(4,128)S(1)}, s32[3,256]{1,0:T(4,128)S(1)}, u32[]{:S(2)}, u32[]{:S(2)}) collective-permute-start(s32[3,256]{1,0:T(4,128)S(1)} %bitcast.58), channel_id=1, source_target_pairs={{0,3},{1,0},{2,1},{3,2},{4,7},{5,4},{6,5},{7,6},{8,11},{9,8},{10,9... | collective-permute-start | bytes 9224 | tf_op jit(solution)/shard_map/ppermute | solution.py:84
  19.2 17.4 %collective-permute-start = (bf16[192,768]{1,0:T(8,128)(2,1)}, bf16[192,768]{1,0:T(8,128)(2,1)S(1)}, u32[]{:S(2)}, u32[]{:S(2)}) collective-permute-start(bf16[192,768]{1,0:T(8,128)(2,1)} %get-tuple-element.138), channel_id=1, source_target_pairs={{0,1},{1,2},{2,3},{3,0},{4,5},{5,6},{6,7},{7,4},{8,9},{9,10},{10,1... | collective-permute-start | bytes 884744 | tf_op jit(solution)/shard_map/ppermute | solution.py:84
  21.7 14.9 %collective-permute-start.1 = (bf16[192,768]{1,0:T(8,128)(2,1)}, bf16[192,768]{1,0:T(8,128)(2,1)S(1)}, u32[]{:S(2)}, u32[]{:S(2)}) collective-permute-start(bf16[192,768]{1,0:T(8,128)(2,1)} %get-tuple-element.138), channel_id=1, source_target_pairs={{0,3},{1,0},{2,1},{3,2},{4,7},{5,4},{6,5},{7,6},{8,11},{9,8},{10,9... | collective-permute-start | bytes 884744 | tf_op jit(solution)/shard_map/ppermute | solution.py:84
  23.1 13.6 %collective-permute-start.2 = (bf16[192,768]{1,0:T(8,128)(2,1)}, bf16[192,768]{1,0:T(8,128)(2,1)S(1)}, u32[]{:S(2)}, u32[]{:S(2)}) collective-permute-start(bf16[192,768]{1,0:T(8,128)(2,1)} %get-tuple-element.138), channel_id=1, source_target_pairs={{0,16},{16,0},{1,17},{17,1},{2,18},{18,2},{3,19},{19,3},{4,20},{20... | collective-permute-start | bytes 884744 | tf_op jit(solution)/shard_map/ppermute | solution.py:88
  41.9 24.8 %collective-permute-start.13 = (bf16[384,768]{1,0:T(8,128)(2,1)S(1)}, bf16[384,768]{1,0:T(8,128)(2,1)S(1)}, u32[]{:S(2)}, u32[]{:S(2)}) collective-permute-start(bf16[384,768]{1,0:T(8,128)(2,1)S(1)} %constant_dynamic-update-slice_fusion.refs_1_), channel_id=1, source_target_pairs={{0,8},{4,12},{8,0},{12,4},{1,9},{5,13},{9,1},{13,5},{2,10},{6,14},... | collective-permute-start | bytes 1769480 | tf_op jit(solution)/shard_map/ppermute | solution.py:88
  43.5 24.6 %collective-permute-start.17 = (bf16[384,768]{1,0:T(8,128)(2,1)S(1)}, bf16[384,768]{1,0:T(8,128)(2,1)S(1)}, u32[]{:S(2)}, u32[]{:S(2)}) collective-permute-start(bf16[384,768]{1,0:T(8,128)(2,1)S(1)} %constant_dynamic-update-slice_fusion.refs_1_), channel_id=1, source_target_pairs={{0,16},{16,0},{1,17},{17,1},{2,18},{18,2},{3,19},{19,3},{4,20},{20... | collective-permute-start | bytes 1769480 | tf_op jit(solution)/shard_map/ppermute | solution.py:88
  45.0 16.5 %collective-permute-start.10 = (bf16[192,768]{1,0:T(8,128)(2,1)S(1)}, bf16[192,768]{1,0:T(8,128)(2,1)}, u32[]{:S(2)}, u32[]{:S(2)}) collective-permute-start(bf16[192,768]{1,0:T(8,128)(2,1)S(1)} %collective-permute-done.2.refs_9_), channel_id=1, source_target_pairs={{0,8},{4,12},{8,0},{12,4},{1,9},{5,13},{9,1},{13,5},{2,10},{6,14},... | collective-permute-start | bytes 884744 | tf_op jit(solution)/shard_map/ppermute | solution.py:88
  54.4 13.8 %collective-permute-start.21 = (bf16[192,768]{1,0:T(8,128)(2,1)S(1)}, bf16[192,768]{1,0:T(8,128)(2,1)S(1)}, u32[]{:S(2)}, u32[]{:S(2)}) collective-permute-start(bf16[192,768]{1,0:T(8,128)(2,1)S(1)} %collective-permute-done.2.refs_9_), channel_id=1, source_target_pairs={{0,4},{4,0},{8,12},{12,8},{1,5},{5,1},{9,13},{13,9},{2,6},{6,2},{1... | collective-permute-start | bytes 884744 | tf_op jit(solution)/shard_map/ppermute | solution.py:88
  61.5 14.0 %collective-permute-start.19 = (bf16[256,768]{1,0:T(8,128)(2,1)S(1)}, bf16[256,768]{1,0:T(8,128)(2,1)}, u32[]{:S(2)}, u32[]{:S(2)}) collective-permute-start(bf16[256,768]{1,0:T(8,128)(2,1)S(1)} %get-tuple-element.154), channel_id=1, source_target_pairs={{0,1},{1,2},{2,3},{3,0},{4,5},{5,6},{6,7},{7,4},{8,9},{9,10},{10,1... | collective-permute-start | bytes 1179656 | tf_op jit(solution)/shard_map/ppermute | solution.py:84
  62.9 16.8 %collective-permute-start.20 = (bf16[256,768]{1,0:T(8,128)(2,1)S(1)}, bf16[256,768]{1,0:T(8,128)(2,1)}, u32[]{:S(2)}, u32[]{:S(2)}) collective-permute-start(bf16[256,768]{1,0:T(8,128)(2,1)S(1)} %get-tuple-element.155), channel_id=1, source_target_pairs={{0,3},{1,0},{2,1},{3,2},{4,7},{5,4},{6,5},{7,6},{8,11},{9,8},{10,9... | collective-permute-start | bytes 1179656 | tf_op jit(solution)/shard_map/ppermute | solution.py:84
  68.1 23.8 %collective-permute-start.11 = (bf16[384,768]{1,0:T(8,128)(2,1)S(1)}, bf16[384,768]{1,0:T(8,128)(2,1)S(1)}, u32[]{:S(2)}, u32[]{:S(2)}) collective-permute-start(bf16[384,768]{1,0:T(8,128)(2,1)S(1)} %constant_dynamic-update-slice_fusion.refs_1_), channel_id=1, source_target_pairs={{0,4},{4,0},{8,12},{12,8},{1,5},{5,1},{9,13},{13,9},{2,6},{6,2},{1... | collective-permute-start | bytes 1769480 | tf_op jit(solution)/shard_map/ppermute | solution.py:88
  69.1 24.9 %collective-permute-start.24 = (bf16[384,768]{1,0:T(8,128)(2,1)S(1)}, bf16[384,768]{1,0:T(8,128)(2,1)S(1)}, u32[]{:S(2)}, u32[]{:S(2)}) collective-permute-start(bf16[384,768]{1,0:T(8,128)(2,1)S(1)} %collective-permute-done.17.refs_10_), channel_id=1, source_target_pairs={{0,8},{4,12},{8,0},{12,4},{1,9},{5,13},{9,1},{13,5},{2,10},{6,14},... | collective-permute-start | bytes 1769480 | tf_op jit(solution)/shard_map/ppermute | solution.py:88
  73.8 17.6 %collective-permute-start.14 = (bf16[192,768]{1,0:T(8,128)(2,1)}, bf16[192,768]{1,0:T(8,128)(2,1)}, u32[]{:S(2)}, u32[]{:S(2)}) collective-permute-start(bf16[192,768]{1,0:T(8,128)(2,1)} %constant_dynamic-update-slice_fusion.2.refs_2_), channel_id=1, source_target_pairs={{0,8},{4,12},{8,0},{12,4},{1,9},{5,13},{9,1},{13,5},{2,10},{6,14},... | collective-permute-start | bytes 884744 | tf_op jit(solution)/shard_map/ppermute | solution.py:88
  75.5 16.4 %collective-permute-start.12 = (bf16[192,768]{1,0:T(8,128)(2,1)}, bf16[192,768]{1,0:T(8,128)(2,1)}, u32[]{:S(2)}, u32[]{:S(2)}) collective-permute-start(bf16[192,768]{1,0:T(8,128)(2,1)} %constant_dynamic-update-slice_fusion.2.refs_2_), channel_id=1, source_target_pairs={{0,4},{4,0},{8,12},{12,8},{1,5},{5,1},{9,13},{13,9},{2,6},{6,2},{1... | collective-permute-start | bytes 884744 | tf_op jit(solution)/shard_map/ppermute | solution.py:88
  79.7 12.7 %collective-permute-start.26 = (bf16[192,768]{1,0:T(8,128)(2,1)}, bf16[192,768]{1,0:T(8,128)(2,1)}, u32[]{:S(2)}, u32[]{:S(2)}) collective-permute-start(bf16[192,768]{1,0:T(8,128)(2,1)} %collective-permute-done.10.refs_15_), channel_id=1, source_target_pairs={{0,4},{4,0},{8,12},{12,8},{1,5},{5,1},{9,13},{13,9},{2,6},{6,2},{1... | collective-permute-start | bytes 884744 | tf_op jit(solution)/shard_map/ppermute | solution.py:88
  126.6 18.5 %collective-permute-start.30 = (bf16[256,768]{1,0:T(8,128)(2,1)}, bf16[256,768]{1,0:T(8,128)(2,1)S(1)}, u32[]{:S(2)}, u32[]{:S(2)}) collective-permute-start(bf16[256,768]{1,0:T(8,128)(2,1)} %get-tuple-element.162.refs_0_), channel_id=1, source_target_pairs={{0,1},{1,2},{2,3},{3,0},{4,5},{5,6},{6,7},{7,4},{8,9},{9,10},{10,1... | collective-permute-start | bytes 1179656 | tf_op jit(solution)/shard_map/ppermute | solution.py:84
  127.2 19.9 %collective-permute-start.31 = (bf16[256,768]{1,0:T(8,128)(2,1)}, bf16[256,768]{1,0:T(8,128)(2,1)S(1)}, u32[]{:S(2)}, u32[]{:S(2)}) collective-permute-start(bf16[256,768]{1,0:T(8,128)(2,1)} %get-tuple-element.162.refs_0_), channel_id=1, source_target_pairs={{0,3},{1,0},{2,1},{3,2},{4,7},{5,4},{6,5},{7,6},{8,11},{9,8},{10,9... | collective-permute-start | bytes 1179656 | tf_op jit(solution)/shard_map/ppermute | solution.py:84
  207.8 237.8 %reduce-scatter.5.cloned.1.call-start = ((), (), s32[]{:S(2)}) async-start(), calls=%async_computation.3 | async-start | bytes 13271040 | tf_op jit(solution)/shard_map/reduce_scatter | solution.py:1027
  288.5 17.2 %collective-permute-start.45 = (bf16[192,768]{1,0:T(8,128)(2,1)}, bf16[192,768]{1,0:T(8,128)(2,1)S(1)}, u32[]{:S(2)}, u32[]{:S(2)}) collective-permute-start(bf16[192,768]{1,0:T(8,128)(2,1)} %get-tuple-element.210), channel_id=1, source_target_pairs={{0,3},{1,0},{2,1},{3,2},{4,7},{5,4},{6,5},{7,6},{8,11},{9,8},{10,9... | collective-permute-start | bytes 884744 | tf_op jit(solution)/shard_map/ppermute | solution.py:84
  290.9 15.0 %collective-permute-start.43 = (bf16[192,768]{1,0:T(8,128)(2,1)}, bf16[192,768]{1,0:T(8,128)(2,1)S(1)}, u32[]{:S(2)}, u32[]{:S(2)}) collective-permute-start(bf16[192,768]{1,0:T(8,128)(2,1)} %get-tuple-element.209), channel_id=1, source_target_pairs={{0,1},{1,2},{2,3},{3,0},{4,5},{5,6},{6,7},{7,4},{8,9},{9,10},{10,1... | collective-permute-start | bytes 884744 | tf_op jit(solution)/shard_map/ppermute | solution.py:84
  319.9 59.2 %collective-permute-start.54 = (bf16[4,240,768]{2,1,0:T(8,128)(2,1)}, bf16[4,240,768]{2,1,0:T(8,128)(2,1)S(1)}, u32[]{:S(2)}, u32[]{:S(2)}) collective-permute-start(bf16[4,240,768]{2,1,0:T(8,128)(2,1)} %get-tuple-element.242), channel_id=1, source_target_pairs={{0,8},{4,12},{8,0},{12,4},{1,9},{5,13},{9,1},{13,5},{2,10},{6,14},... | collective-permute-start | bytes 4423688 | tf_op jit(solution)/shard_map/ppermute | solution.py:88
  323.4 45.4 %collective-permute-start.48 = (bf16[2,2,96,256]{3,2,0,1:T(8,128)(2,1)S(1)}, bf16[2,2,96,256]{3,2,0,1:T(8,128)(2,1)S(1)}, u32[]{:S(2)}, u32[]{:S(2)}) collective-permute-start(bf16[2,2,96,256]{3,2,0,1:T(8,128)(2,1)S(1)} %get-tuple-element.287), channel_id=1, source_target_pairs={{0,8},{4,12},{8,0},{12,4},{1,9},{5,13},{9,1},{13,5},{2,10},{6,14},... | collective-permute-start | bytes 589832 | tf_op jit(solution)/shard_map/ppermute | solution.py:88
  323.6 52.1 %collective-permute-start.46 = (bf16[384,768]{1,0:T(8,128)(2,1)S(1)}, bf16[384,768]{1,0:T(8,128)(2,1)S(1)}, u32[]{:S(2)}, u32[]{:S(2)}) collective-permute-start(bf16[384,768]{1,0:T(8,128)(2,1)S(1)} %pad_maximum_fusion.1), channel_id=1, source_target_pairs={{0,3},{1,0},{2,1},{3,2},{4,7},{5,4},{6,5},{7,6},{8,11},{9,8},{10,9... | collective-permute-start | bytes 1769480 | tf_op jit(solution)/shard_map/ppermute | solution.py:84
  327.4 48.3 %collective-permute-start.44 = (bf16[384,768]{1,0:T(8,128)(2,1)S(1)}, bf16[384,768]{1,0:T(8,128)(2,1)S(1)}, u32[]{:S(2)}, u32[]{:S(2)}) collective-permute-start(bf16[384,768]{1,0:T(8,128)(2,1)S(1)} %pad_maximum_fusion), channel_id=1, source_target_pairs={{0,1},{1,2},{2,3},{3,0},{4,5},{5,6},{6,7},{7,4},{8,9},{9,10},{10,1... | collective-permute-start | bytes 1769480 | tf_op jit(solution)/shard_map/ppermute | solution.py:84
  393.4 13.1 %collective-permute-start.57 = (bf16[240,768]{1,0:T(8,128)(2,1)S(1)}, bf16[240,768]{1,0:T(8,128)(2,1)S(1)}, u32[]{:S(2)}, u32[]{:S(2)}) collective-permute-start(bf16[240,768]{1,0:T(8,128)(2,1)S(1)} %pad_maximum_fusion.7), channel_id=1, source_target_pairs={{0,1},{1,2},{2,3},{3,0},{4,5},{5,6},{6,7},{7,4},{8,9},{9,10},{10,1... | collective-permute-start | bytes 1105928 | tf_op jit(solution)/shard_map/ppermute | solution.py:84
  394.1 16.4 %collective-permute-start.58 = (bf16[240,768]{1,0:T(8,128)(2,1)S(1)}, bf16[240,768]{1,0:T(8,128)(2,1)S(1)}, u32[]{:S(2)}, u32[]{:S(2)}) collective-permute-start(bf16[240,768]{1,0:T(8,128)(2,1)S(1)} %pad_maximum_fusion.8), channel_id=1, source_target_pairs={{0,3},{1,0},{2,1},{3,2},{4,7},{5,4},{6,5},{7,6},{8,11},{9,8},{10,9... | collective-permute-start | bytes 1105928 | tf_op jit(solution)/shard_map/ppermute | solution.py:84
  412.4 18.3 %collective-permute-start.29 = (bf16[256,768]{1,0:T(8,128)(2,1)S(1)}, bf16[256,768]{1,0:T(8,128)(2,1)S(1)}, u32[]{:S(2)}, u32[]{:S(2)}) collective-permute-start(bf16[256,768]{1,0:T(8,128)(2,1)S(1)} %broadcast_select_fusion.1), channel_id=1, source_target_pairs={{0,16},{16,0},{1,17},{17,1},{2,18},{18,2},{3,19},{19,3},{4,20},{20... | collective-permute-start | bytes 1179656 | tf_op jit(solution)/shard_map/ppermute | solution.py:88
  413.3 24.8 %collective-permute-start.42 = (bf16[256,768]{1,0:T(8,128)(2,1)S(1)}, bf16[256,768]{1,0:T(8,128)(2,1)S(1)}, u32[]{:S(2)}, u32[]{:S(2)}) collective-permute-start(bf16[256,768]{1,0:T(8,128)(2,1)S(1)} %select_convert_fusion), channel_id=1, source_target_pairs={{0,16},{16,0},{1,17},{17,1},{2,18},{18,2},{3,19},{19,3},{4,20},{20... | collective-permute-start | bytes 1179656 | tf_op jit(solution)/shard_map/ppermute | solution.py:88
  414.6 17.1 %collective-permute-start.52 = (bf16[8,96,256]{2,1,0:T(8,128)(2,1)S(1)}, bf16[8,96,256]{2,1,0:T(8,128)(2,1)S(1)}, u32[]{:S(2)}, u32[]{:S(2)}) collective-permute-start(bf16[8,96,256]{2,1,0:T(8,128)(2,1)S(1)} %maximum_bitcast_fusion.2.refs_1_), channel_id=1, source_target_pairs={{0,1},{1,2},{2,3},{3,0},{4,5},{5,6},{6,7},{7,4},{8,9},{9,10},{10,1... | collective-permute-start | bytes 1179656 | tf_op jit(solution)/shard_map/ppermute | solution.py:84
  415.2 18.4 %collective-permute-start.53 = (bf16[8,96,256]{2,1,0:T(8,128)(2,1)S(1)}, bf16[8,96,256]{2,1,0:T(8,128)(2,1)S(1)}, u32[]{:S(2)}, u32[]{:S(2)}) collective-permute-start(bf16[8,96,256]{2,1,0:T(8,128)(2,1)S(1)} %maximum_bitcast_fusion.2.refs_1_), channel_id=1, source_target_pairs={{0,3},{1,0},{2,1},{3,2},{4,7},{5,4},{6,5},{7,6},{8,11},{9,8},{10,9... | collective-permute-start | bytes 1179656 | tf_op jit(solution)/shard_map/ppermute | solution.py:84
  422.3 15.2 %collective-permute-start.63 = (bf16[240,768]{1,0:T(8,128)(2,1)S(1)}, bf16[240,768]{1,0:T(8,128)(2,1)S(1)}, u32[]{:S(2)}, u32[]{:S(2)}) collective-permute-start(bf16[240,768]{1,0:T(8,128)(2,1)S(1)} %fusion.2.own_ref), channel_id=1, source_target_pairs={{0,8},{4,12},{8,0},{12,4},{1,9},{5,13},{9,1},{13,5},{2,10},{6,14},... | collective-permute-start | bytes 1105928 | tf_op jit(solution)/shard_map/ppermute | solution.py:88
  (93 other events, 689.4 us)
Sparse Core Ops, SparseCore 0:
  208.0 36.0 reduce-scatter.2
  247.6 96.9 reduce-scatter.4

commit v3 on v2

--- a/solution.py
+++ b/solution.py
@@ -92,9 +92,9 @@
     return lax.optimization_barrier((value, first))[0]
 
 
-def scatter_first(c0, c1, c2a, c2b, c3, axis):
+def scatter_first(c0, c1, c2a, c2b, c3, axis, wait=()):
     half = c2a.shape[0]
-    right, left = turned(c2a, axis, 1), turned(c2b, axis, -1)
+    right, left = after((turned(c2a, axis, 1), turned(c2b, axis, -1)), wait)
     return c0, jnp.concatenate([c1[:half] + right, c1[half:]], axis=0), jnp.concatenate([c3[:half], c3[half:] + left], axis=0)
 
 
@@ -133,7 +133,7 @@
 
 
 def pack_weights(z, qkv, out, fin, fout, small):
-    def kernel(qkv_ref, out_ref, fin_ref, fout_ref, small_ref, o_ref, own_ref):
+    def kernel(qkv_ref, out_ref, fin_ref, fout_ref, small_ref, o_ref, pair_ref, own_ref):
         shard = lax.axis_index("shard")
 
         def spread(pieces):
@@ -149,15 +149,17 @@
         o_ref[1, 0, z.at_small : z.at_small + 16] = jnp.where(lane == shard, wide, 0.0).astype(BF16)
         o_ref[1, 0, z.at_small + 16 : z.part] = jnp.zeros((z.part - z.at_small - 16, z.d), BF16)
         o_ref[1, 1] = spread([fout_ref[g] for g in range(z.groups)])
+        pair_ref[...] = o_ref[side_of(1)]
         own_ref[...] = o_ref[side_of(1), side_of(2)]
 
-    return call(kernel, [like((2, 2, z.part, z.d), BF16), like((z.part, z.d), BF16)], (qkv, out, fin, fout, small), name="pack")
+    outs = [like((2, 2, z.part, z.d), BF16), like((2, z.part, z.d), BF16), like((z.part, z.d), BF16)]
+    return call(kernel, outs, (qkv, out, fin, fout, small), name="pack")
 
 
 class Pieces:
-    def __init__(self, z, local, mine, others, layer):
+    def __init__(self, z, local, mine, pairs, others, layer):
         self.z, self.layer = z, layer
-        self.arrays = (local, *mine, *others)
+        self.arrays = (local, *mine, *pairs, *others)
         self.specs = [pl.BlockSpec(memory_space=pl.ANY)] * len(self.arrays)
         self.scratch = [pltpu.VMEM((2, z.shards, z.rows, z.d), BF16), pltpu.SemaphoreType.DMA((2, 2, 4))]
 
@@ -166,7 +168,7 @@
         core, y = side_of(1), side_of(2)
         shard = lax.axis_index("shard")
         own_layer = lax.axis_index("section") == self.layer
-        local, mine, others = refs[0], refs[1:9], refs[9:21]
+        local, mine, pairs, others = refs[0], refs[1:9], refs[9:11], refs[11:19]
         waits = {}
         for part in parts:
             copies = []
@@ -181,11 +183,11 @@
                         here = (y == part) if across == 0 else (y != part)
                         at = 2 * across + side
                         if n == 0:
-                            own, other = local.at[place, part], others[3 * at]
+                            own, other = local.at[place, part], pairs[side].at[part]
                         elif n < 3:
-                            own, other = mine[2 * at].at[rows], others[3 * at + 1].at[rows]
+                            own, other = mine[2 * at].at[rows], others[2 * at].at[rows]
                         else:
-                            own, other = mine[2 * at + 1], others[3 * at + 2]
+                            own, other = mine[2 * at + 1], others[2 * at + 1]
                         choices.append((jnp.logical_and(here, own_layer), own))
                         choices.append((jnp.logical_and(here, jnp.logical_not(own_layer)), other))
                     for here, source in choices:
@@ -603,79 +605,31 @@
     )
 
 
-def add_cores_split(keep, came):
-    shards, part, d = keep[0].shape
+def add_cores_split(z, keep, came):
+    shards, high, d = keep[0].shape
+    rows = high + z.part
+    half = rows // 32 * 16
 
     def kernel(a_ref, f_ref, b_ref, e_ref, c0, c1, c2a, c2b, c3):
         for k, ref in ((0, c0), (1, c1), (3, c3)):
-            ref[:part] = a_ref[k] + b_ref[k]
-            ref[part:] = f_ref[k] + e_ref[k]
-        c2a[...] = a_ref[2] + b_ref[2]
-        c2b[...] = f_ref[2] + e_ref[2]
-
-    full, half = like((2 * part, d), BF16), like((part, d), BF16)
-    return call(kernel, [full, full, half, half, full], (*keep, *came), name="add_cores_split")
-
-
-def halves_by_y(z, terms):
-    def kernel(a_ref, b_ref, c_ref, keep_ref, send_ref):
-        y = side_of(2)
-        for ref, part in ((keep_ref, y), (send_ref, 1 - y)):
-            span = pl.ds(pl.multiple_of(part * z.part, z.part), z.part)
-            ref[...] = (a_ref[span].astype(F32) + b_ref[span].astype(F32) + c_ref[span].astype(F32)).astype(BF16)
-
-    return call(kernel, [like((z.part, z.d), BF16)] * 2, terms, name="halves_by_y")
-
-
-def add_core(z, keep_a, came_a, keep_f, came_f):
-    extra = (keep_a.shape[1] - z.part) // 2
-    rows = z.part + extra
-
-    def kernel(a_ref, b_ref, c_ref, e_ref, keep_ref, send_ref):
-        y = side_of(2)
-
-        def place(ref, part):
-            if part == 0:
-                ref[:, : z.part] = a_ref[:, : z.part] + b_ref[:, : z.part]
-            else:
-                ref[:, : z.part] = c_ref[...] + e_ref[...]
-            if extra:
-                span = slice(z.part + part * extra, z.part + (part + 1) * extra)
-                ref[:, z.part :] = a_ref[:, span] + b_ref[:, span]
-
-        @pl.when(y == 0)
-        def _():
-            place(keep_ref, 0)
-            place(send_ref, 1)
-
-        @pl.when(y == 1)
-        def _():
-            place(keep_ref, 1)
-            place(send_ref, 0)
-
-    return call(kernel, [like((z.shards, rows, z.d), BF16)] * 2, (keep_a, came_a, keep_f, came_f), moved=2 * MIB, name="add_core")
-
-
-def add_split(kept, came):
-    _, rows, d = kept.shape
-    half = rows // 32 * 16
-
-    def kernel(a_ref, b_ref, c0, c1, c2a, c2b, c3):
-        for k, ref in ((0, c0), (1, c1), (3, c3)):
-            ref[...] = a_ref[k] + b_ref[k]
+            ref[:high] = a_ref[k] + b_ref[k]
+            ref[high:] = f_ref[k] + e_ref[k]
         c2a[...] = a_ref[2, :half] + b_ref[2, :half]
-        c2b[...] = a_ref[2, half:] + b_ref[2, half:]
+        if half < high:
+            c2b[: high - half] = a_ref[2, half:] + b_ref[2, half:]
+        c2b[high - half :] = f_ref[2] + e_ref[2]
 
     full = like((rows, d), BF16)
     outs = [full, full, like((half, d), BF16), like((rows - half, d), BF16), full]
-    return call(kernel, outs, (kept, came), moved=2 * MIB, name="add_split")
+    return call(kernel, outs, (*keep, *came), name="add_cores_split")
 
 
 def head_forward(pieces, table):
     count = sum(piece.shape[0] for piece in pieces)
     vocab, d = table.shape
-    tiles = 6
+    tiles = 3
     block = vocab // tiles
+    part = block // 2
     chunk = 256
     many = len(pieces)
 
@@ -693,17 +647,24 @@
             s_ref[...] = jnp.zeros(s_ref.shape, F32)
             acc_ref[...] = jnp.zeros(acc_ref.shape, F32)
 
-        w = w_ref[...]
-        for r in range(count // chunk):
+        units = [(c, r) for c in range(2) for r in range(count // chunk)]
+
+        def logits_of(unit):
+            c, r = unit
+            return nt(x_ref[r * chunk : (r + 1) * chunk], w_ref[c * part : (c + 1) * part])
+
+        logits = logits_of(units[0])
+        for n, (c, r) in enumerate(units):
+            following = logits_of(units[n + 1]) if n + 1 < len(units) else None
             span = slice(r * chunk, (r + 1) * chunk)
-            logits = nt(x_ref[span], w)
             old = m_ref[span]
             new = jnp.maximum(old, jnp.max(logits, axis=-1, keepdims=True))
             keep = jnp.exp(old - new)
-            part = jnp.exp(logits - new)
-            s_ref[span] = s_ref[span] * keep + jnp.sum(part, axis=-1, keepdims=True)
-            acc_ref[span] = acc_ref[span] * keep + nn(part.astype(BF16), w)
+            weight = jnp.exp(logits - new)
+            s_ref[span] = s_ref[span] * keep + jnp.sum(weight, axis=-1, keepdims=True)
+            acc_ref[span] = acc_ref[span] * keep + nn(weight.astype(BF16), w_ref[c * part : (c + 1) * part])
             m_ref[span] = new
+            logits = following
 
         @pl.when(step == tiles - 1)
         def _():
@@ -731,7 +692,7 @@
     shards = ids_by.shape[0]
     d = picked.shape[1]
 
-    def kernel(own_ref, rest_ref, p_ref, i_ref, a_ref, b_ref, c_ref, e_ref, out_ref, lse_ref):
+    def kernel(x0_ref, x1_ref, x2_ref, x3_ref, p_ref, i_ref, a_ref, b_ref, c_ref, e_ref, out_ref, lse_ref):
         shard = lax.axis_index("shard")
         parts = (a_ref, b_ref, c_ref, e_ref)
         for k in range(shards):
@@ -747,7 +708,7 @@
             local = i_ref[k, 1:2] - shard * vocab
             inside = upright(jnp.where((local >= 0) & (local < vocab), 1.0, 0.0), seq)
             hit = jnp.where(inside > 0.5, p_ref[span].astype(F32), 0.0)
-            ctx = own_ref[...] if k == 0 else rest_ref[(k - 1) * seq : k * seq]
+            ctx = (x0_ref, x1_ref, x2_ref, x3_ref)[k][...]
             target = pl.multiple_of(((shard + k) % shards) * seq, seq)
             out_ref[pl.ds(target, seq), :] = (ctx * weight - hit).astype(BF16)
 
@@ -829,30 +790,21 @@
     return call(kernel, [like((1, count + 128), jnp.int32)], (ids,), specs=[smem], out_specs=[smem], name="list_tokens")[0]
 
 
-def table_grad(denses, pieces, lists, vocab):
-    width = denses[0].shape[0]
-    many_parts = len(denses)
-    own = pieces[0]
-    sources, _, seq = own.shape
+def table_grad(dense, pieces, lists, vocab):
+    width = dense.shape[0]
+    sources, _, seq = pieces[0].shape
     shards = 4
-    count = shards * sources * seq
+    listed = shards * seq
     unit = 1 << (vocab - 1).bit_length()
     ways = 4
-    listed = shards * seq
-
-    def kernel(*refs):
-        d_refs, refs = refs[:many_parts], refs[many_parts:]
-        own_ref, before_ref, after_ref, far_a_ref, far_b_ref, l_ref, o_ref, flat_ref, *acc = refs
-        def rows_of(k, j):
-            if k == 2:
-                half = sources // 2
-                return far_a_ref[j] if j < half else far_b_ref[j - half]
-            return (own_ref, after_ref, None, before_ref)[k][j]
-
-        for k in range(shards):
-            for j in range(sources):
-                at = (j * shards + k) * seq
-                flat_ref[at : at + seq] = rows_of(k, j).astype(F32).T
+
+    def kernel(d_ref, own_ref, later_ref, before_ref, far_a_ref, far_b_ref, l_ref, o_ref, flat_ref, *acc):
+        half = sources // 2
+        for j in range(sources):
+            far = far_a_ref[j] if j < half else far_b_ref[j - half]
+            for k, block in enumerate((own_ref[j], later_ref[j], before_ref[j], far)):
+                at = j * listed + k * seq
+                flat_ref[at : at + seq] = block.astype(F32).T
         for ref in acc:
             ref[...] = jnp.zeros(ref.shape, F32)
 
@@ -880,34 +832,28 @@
             return carry
 
         lax.fori_loop(0, sources, source, jnp.int32(0))
-        at = 0
-        for ref in d_refs:
-            span = slice(at, at + ref.shape[1])
-            o_ref[:, span] = ref[...].astype(F32) + sum(part[span] for part in acc).T
-            at = span.stop
+        o_ref[...] = d_ref[...].astype(F32) + sum(ref[...] for ref in acc).T
 
     smem = pl.BlockSpec(memory_space=pltpu.SMEM)
     return call(
         kernel,
         [like((width, vocab), F32)],
-        (*denses, *pieces, lists),
-        specs=[None] * (5 + many_parts) + [smem],
-        scratch=[pltpu.VMEM((count, width), F32)] + [pltpu.VMEM((vocab, width), F32)] * ways,
+        (dense, *pieces, lists),
+        specs=[None] * 6 + [smem],
+        scratch=[pltpu.VMEM((sources * listed, width), F32)] + [pltpu.VMEM((vocab, width), F32)] * ways,
         limit=60,
         name="table_grad",
     )[0]
 
 
-def unpack_grads(z, blocks):
-    rows = z.part + z.extra
-
-    def kernel(own_ref, y_ref, core_ref, both_ref, qkv_ref, out_ref, fin_ref, fout_ref, gain_ref, bias_ref, pos_ref, eg_ref, es_ref, all_ref):
-        core, y = side_of(1), side_of(2)
+def unpack_grads(z, own, other):
+    rows = z.rows + 2 * z.extra
+
+    def kernel(own_ref, other_ref, qkv_ref, out_ref, fin_ref, fout_ref, gain_ref, bias_ref, pos_ref, eg_ref, es_ref, all_ref):
+        core = side_of(1)
         shard = lax.axis_index("shard")
-        all_ref[core, y] = own_ref[...]
-        all_ref[core, 1 - y] = y_ref[...]
-        all_ref[1 - core, y] = core_ref[...]
-        all_ref[1 - core, 1 - y] = both_ref[...]
+        all_ref[core] = own_ref[...]
+        all_ref[1 - core] = other_ref[...]
 
         def own_lanes(value):
             total = jnp.zeros((value.shape[0], z.part), F32)
@@ -915,21 +861,22 @@
                 total = total + jnp.where(shard == h, value[:, h * z.part : (h + 1) * z.part], 0.0)
             return total
 
-        out_ref[...] = all_ref[0, 0, : z.part].astype(F32)
-        fin_ref[...] = all_ref[0, 1, : z.part].astype(F32).reshape(z.groups, z.gi, z.d)
+        out_ref[...] = all_ref[0, : z.part].astype(F32)
+        fin_ref[...] = all_ref[0, z.part : z.rows].astype(F32).reshape(z.groups, z.gi, z.d)
         for c in range(3):
-            part = all_ref[1, 0, c * z.gi : (c + 1) * z.gi].astype(F32)
+            part = all_ref[1, c * z.gi : (c + 1) * z.gi].astype(F32)
             for g in range(z.groups):
                 qkv_ref[c, g] = part[:, g * z.gw : (g + 1) * z.gw]
-        part = all_ref[1, 1, : z.part].astype(F32)
+        part = all_ref[1, z.part : z.rows].astype(F32)
         for g in range(z.groups):
             fout_ref[g] = part[:, g * z.gw : (g + 1) * z.gw]
-        small = own_lanes(all_ref[1, 0, z.at_small : z.at_small + 16].astype(F32))
+        small = own_lanes(all_ref[1, z.at_small : z.at_small + 16].astype(F32))
         gain_ref[...] = small[0:2]
         bias_ref[...] = small[2:11]
         for n in range(4):
-            pos_ref[n * z.pos : (n + 1) * z.pos] = all_ref[n // 2, n % 2, z.part : z.part + z.pos].astype(F32)
-        small = own_lanes(all_ref[0, 0, z.part + z.pos : rows].astype(F32))
+            row = z.rows + (n % 2) * z.extra
+            pos_ref[n * z.pos : (n + 1) * z.pos] = all_ref[n // 2, row : row + z.pos].astype(F32)
+        small = own_lanes(all_ref[0, z.rows + z.pos : z.rows + z.extra].astype(F32))
         eg_ref[...] = small[0:1]
         es_ref[...] = small[1:2]
 
@@ -946,8 +893,8 @@
             like((1, z.part), F32),
             like((1, z.part), F32),
         ],
-        blocks,
-        scratch=[pltpu.VMEM((2, 2, rows, z.d), BF16)],
+        (own, other),
+        scratch=[pltpu.VMEM((2, rows, z.d), BF16)],
         name="unpack",
     )
 
@@ -972,58 +919,64 @@
         return word_table.at[jnp.clip(ids.reshape(-1) - offset, 0, vocab - 1)].get(mode="promise_in_bounds")
 
     small = jnp.concatenate([layer_gains[0], layer_biases[0], embed_gain[None], embed_shift[None]], axis=0)
-    local, packed = pack_weights(z, qkv_weight[0], out_weight[0], ffn_in[0], ffn_out[0], small)
-    cross_own = crossed(packed, "section", 1)
+    local, pair, packed = pack_weights(z, qkv_weight[0], out_weight[0], ffn_in[0], ffn_out[0], small)
+    cross_pair = crossed(pair, "section", 1)
     near = gather_first(packed, "shard")
     picked = rows_of(ids_by[:, 0])
-    near, cross_own, pos_table = after((near, cross_own, pos_table), (near, cross_own))
+    near, pos_table = after((near, pos_table), near)
     word_parts = embed_parts(picked, ids_by, pos_table, vocab)
-    near, cross_own = after((near, cross_own), word_parts)
+    near = after(near, word_parts)
     near_rows = jnp.concatenate(near, axis=0)
     near_y = crossed(near_rows, "dp", 2)
     cross_near = crossed(near_rows, "section", 1)
-    cross_own_y = crossed(cross_own, "dp", 2)
-    word_parts = scatter_first(*word_parts, "shard")
-    far = gather_second(*near, "shard")
-    far, word_parts = after((far, word_parts), (far, word_parts, cross_own_y))
-    far = jnp.concatenate(far, axis=0)
-    words = scatter_second(*word_parts, "shard")
+    target_rows = rows_of(after(ids_by[:, 1], near_rows))
+    c0, c1, c2a, c2b, c3 = word_parts
+    half, quarter = seq // 2, z.part // 2
+    right = turned(jnp.concatenate([c2a, near[0][:quarter]], axis=0), "shard", 1)
+    left = turned(jnp.concatenate([c2b, near[1][quarter:]], axis=0), "shard", -1)
+    right, left = after((right, left), target_rows)
+    c1 = jnp.concatenate([c1[:half] + right[:half], c1[half:]], axis=0)
+    c3 = jnp.concatenate([c3[:half], c3[half:] + left[:half]], axis=0)
+    words = scatter_second(c0, c1, c3, "shard")
+    far = jnp.concatenate([right[half:], left[half:]], axis=0)
     cross_far = crossed(far, "section", 1)
-    far_y = crossed(far, "dp", 2)
-    cross_near_y = crossed(cross_near, "dp", 2)
-    target_rows = rows_of(after(ids_by[:, 1], (near_y, cross_near)))
-    cross_far, words = after((cross_far, words), target_rows)
+    both_y = crossed(jnp.concatenate([far, cross_near], axis=0), "dp", 2)
+    far_y, cross_near_y = both_y[: z.part], both_y[z.part :]
     cross_far_y = crossed(cross_far, "dp", 2)
     mine = (near_rows, far)
-    mine_y = (near_y, far_y)
-    others = (cross_own, cross_near, cross_far)
-    others_y = (cross_own_y, cross_near_y, cross_far_y)
-    mine = (*mine, *(crossed(b, "dp", 1) for b in mine), *mine_y, *(crossed(b, "dp", 1) for b in mine_y))
-    others = (*others, *(crossed(b, "dp", 1) for b in others), *others_y, *(crossed(b, "dp", 1) for b in others_y))
-    weights_one, weights_two = (Pieces(z, local, mine, others, layer) for layer in range(2))
+    mine = (*mine, *(crossed(b, "dp", 1) for b in mine), near_y, far_y, crossed(near_y, "dp", 1), crossed(far_y, "dp", 1))
+    others = (cross_near, cross_far)
+    others = (*others, *(crossed(b, "dp", 1) for b in others))
+    others = (*others, cross_near_y, cross_far_y, crossed(cross_near_y, "dp", 1), crossed(cross_far_y, "dp", 1))
+    pairs = (cross_pair, crossed(cross_pair, "dp", 1))
+    weights_one, weights_two = (Pieces(z, local, mine, pairs, others, layer) for layer in range(2))
     one = layer_forward(z, weights_one, seg_row, True, words=words)
     two = layer_forward(z, weights_two, seg_row, False, layer_in=one["out"])
     two["x"] = one["out"]
 
-    ring_first = gather_first(two["out"], "shard")
+    own_out = jnp.where(first, one["out"], two["out"])
+    came_out = crossed(jnp.where(first, two["out"], one["out"]), "section", 1)
+
+    before, later = gather_first(two["out"], "shard")
     ctx_own, lse_own = head_forward([two["out"]], word_table)
-    before, later = after(ring_first, ctx_own)
-    far_a, far_b = gather_second(before, later, "shard")
-    ctx_rest, lse_rest = head_forward([later, far_a, far_b, before], word_table)
-    lse = jnp.concatenate([lse_own[0:1], lse_rest[0:1]], axis=1)
-    lists = list_tokens(after(ids_by[:, 0].reshape(1, -1), lse), vocab)
+    before = after(before, ctx_own)
+    far_a = turned(before[: seq // 2], "shard", 1)
+    ctx_before, lse_before = head_forward([before], word_table)
+    later = after(later, ctx_before)
+    far_b = turned(later[seq // 2 :], "shard", -1)
+    ctx_later, lse_later = head_forward([later], word_table)
+    far_a, far_b = after((far_a, far_b), ctx_later)
+    ctx_far, lse_far = head_forward([far_a, far_b], word_table)
+    lse = jnp.concatenate([lse_own[0:1], lse_later[0:1], lse_far[0:1], lse_before[0:1]], axis=1)
+    listed = jnp.stack([ids_by[0, 0], ids_by[1, 0], ids_by[3, 0], ids_by[2, 0]]).reshape(1, -1)
+    lists = list_tokens(after(listed, lse), vocab)
     lses = (lse, turned(lse, "shard", -1), turned(lse, "shard", 2), turned(lse, "shard", 1))
-    lses = after(lses, lists)
-    parts, whole_lse = head_combine(seq, (ctx_own, ctx_rest), target_rows, ids_by, lses, vocab)
+    lses = after(lses, (lists, came_out))
+    parts, whole_lse = head_combine(seq, (ctx_own, ctx_later, ctx_far, ctx_before), target_rows, ids_by, lses, vocab)
     out_grad = lax.psum_scatter(parts, "shard", scatter_dimension=0, tiled=True)
     dense = head_table([two["out"], later, far_a, far_b, before], word_table, whole_lse, ids_by, 0, 6, 1280)
 
-    bit = 1
-    while bit < dp:
-        lists = jnp.concatenate([lists, crossed(lists, "dp", bit)], axis=0)
-        bit *= 2
-    lists = jnp.concatenate([lists, crossed(lists, "section", 1)], axis=0)
-    out_grad = after(out_grad, (dense, lists))
+    out_grad = after(out_grad, dense)
     dense = lax.psum_scatter(dense, both, scatter_dimension=0, tiled=True)
 
     d_middle, small_grads, keep_f, send_f = ffn_backward(z, weights_two, two, out_grad)
@@ -1031,7 +984,7 @@
     came_f, came_a = crossed(send_f, "dp", 1), crossed(send_a, "dp", 1)
     d_middle, small_grads, keep_one_f, send_one_f = ffn_backward(z, weights_one, one, in_low)
     keep_f, came_f, keep_a, came_a = after((keep_f, came_f, keep_a, came_a), d_middle)
-    split_two = add_cores_split((keep_a, keep_f), (came_a, came_f))
+    split_two = add_cores_split(z, (keep_a, keep_f), (came_a, came_f))
     d_middle = after(d_middle, split_two)
     terms_two = scatter_first(*split_two, "shard")
     came_one_f = crossed(send_one_f, "dp", 1)
@@ -1040,47 +993,50 @@
     send_one_a, d_embed = after((send_one_a, d_embed), terms_two)
     came_one_a = crossed(send_one_a, "dp", 1)
     columns = d_embed[None]
-    steps = [("dp", 1 << n) for n in range(dp.bit_length() - 1)] + [("section", 1)]
+    steps = [("dp", 1 << n) for n in range(dp.bit_length() - 1)]
     for n, (axis, bit) in enumerate(steps):
         middle = columns.shape[1] // 2
         columns = jnp.concatenate([columns[:, :middle], crossed(columns[:, middle:], axis, bit)], axis=0)
         if n == 0:
             came_one_a = after(came_one_a, columns)
-    columns = columns[:, 0]
-    stay_one, leave_one = add_core(z, keep_one_a, came_one_a, keep_one_f, came_one_f)
-    came_one = crossed(leave_one, "dp", 2)
-    terms_two = scatter_second(*terms_two, "shard")
-    terms_two, columns = after((terms_two, columns), (stay_one, columns))
-    stay_two, leave_two = halves_by_y(z, terms_two)
-    ring_columns = gather_first(after(columns, stay_two), "shard")
-    stay_one = after(stay_one, stay_two)
-    split_one = add_split(stay_one, came_one)
+    split_one = add_cores_split(z, (keep_one_a, keep_one_f), (came_one_a, came_one_f))
+    columns = after(columns, split_one)
+    columns = jnp.concatenate([columns[:, 0], crossed(columns[:, 1], "section", 1)], axis=0)
+    second_two = scatter_second(*terms_two, "shard")
     terms_one = scatter_first(*split_one, "shard")
-    sum_two = stay_two + crossed(leave_two, "dp", 2)
-    ring_columns = after(ring_columns, terms_one)
-    sum_one = sum(scatter_second(*terms_one, "shard"))
-    layer_one, extra = sum_one[: z.part], sum_one[z.part :]
-    keep = jnp.concatenate([jnp.where(first, layer_one, sum_two), extra], axis=0)
-    send = jnp.concatenate([jnp.where(first, sum_two, layer_one), extra], axis=0)
-    total = keep + crossed(send, "section", 1)
-    far_columns = gather_second(*after(ring_columns, sum_one), "shard")
-    bit = 4
+    own_in = jnp.where(first, in_one, in_two)
+    came_in = crossed(jnp.where(first, in_two, in_one).astype(BF16), "section", 1)
+    lists = after(lists, columns)
+    bit = 1
     while bit < dp:
-        total = total + crossed(total, "dp", bit)
+        lists = jnp.concatenate([lists, crossed(lists, "dp", bit)], axis=0)
         bit *= 2
-    total_y = crossed(total, "dp", 2)
-    unpacked = unpack_grads(z, (total, total_y, crossed(total, "dp", 1), crossed(total_y, "dp", 1)))
-
-    word_grad = table_grad([dense], (columns, *ring_columns, *far_columns), lists, vocab).T
-
-    def by_micro(layer_one, layer_two, moved, dtype):
-        own = jnp.where(first, layer_one, layer_two)
-        sent = jnp.where(first, layer_two, layer_one).astype(moved)
-        came = crossed(sent, "section", 1).astype(dtype)
+    lists = jnp.concatenate([lists, crossed(lists, "section", 1)], axis=0)
+    sum_two = sum(after(second_two, (columns, split_one)))
+    second_one = scatter_second(*after(terms_one, sum_two), "shard")
+    sum_one = sum(after(second_one, (sum_two, lists, came_in)))
+    columns = after(columns, sum_one)
+    ring_columns = gather_first(columns, "shard")
+    high = z.part + 2 * z.extra
+    extra = sum_one[z.part : high]
+    layer_one = jnp.concatenate([sum_one[: z.part], sum_one[high:]], axis=0)
+    total = jnp.concatenate([jnp.where(first, layer_one, sum_two), extra], axis=0)
+    total = total + crossed(jnp.concatenate([jnp.where(first, sum_two, layer_one), extra], axis=0), "section", 1)
+    total, ring_columns = after((total, ring_columns), ())
+    far_columns = gather_second(*ring_columns, "shard")
+    bit = 2
+    while bit < dp:
+        total = total + after(crossed(total, "dp", bit), far_columns)
+        bit *= 2
+    unpacked = unpack_grads(z, total, crossed(total, "dp", 1))
+
+    word_grad = table_grad(dense, (columns, ring_columns[1], ring_columns[0], *far_columns), lists, vocab).T
+
+    def by_micro(own, came):
         return jnp.stack([jnp.where(first, own, came), jnp.where(first, came, own)]).reshape(1, micro, 1, seq, d)
 
-    layer_outputs = by_micro(one["out"], two["out"], BF16, BF16)
-    input_grads = by_micro(in_one, in_two, BF16, F32)
+    layer_outputs = by_micro(own_out, came_out)
+    input_grads = by_micro(own_in, came_in.astype(F32))
     qkv_g, out_g, fin_g, fout_g, gain_g, bias_g, pos_g, eg_g, es_g = unpacked
     return (
         layer_outputs,

time: 475 us -> 446 us (0.939)
  waiting for transfers between devices: 126 us -> 115 us
  starting transfers between devices: 76.2 us -> 65.5 us
  Pallas kernels: 197 us -> 189 us
    ppermute x36 -> x30, waiting for transfers between devices: 84.8 us -> 48.9 us  [crossed(): lax.ppermute(block, axis, [(i, i ^ bit) for i in range(lax.axis_size(axis...]
    ppermute x30 -> x28, waiting for transfers between devices: 41.6 us -> 63.2 us  [turned(): lax.ppermute(block, axis, [(i, (i + by) % size) for i in range(size)])]
    pallas_call x19, Pallas kernels: 197 us -> 189 us  [call(): pl.pallas_call(kernel, out_shape=outs, in_specs=[vmem if s is None else s...]
    ppermute x36 -> x30, starting transfers between devices: 25.6 us -> 18.4 us  [crossed(): lax.ppermute(block, axis, [(i, i ^ bit) for i in range(lax.axis_size(axis...]
    ppermute x30 -> x28, starting transfers between devices: 50.6 us -> 47.1 us  [turned(): lax.ppermute(block, axis, [(i, (i + by) % size) for i in range(size)])]
    unnamed x119 -> x127, local copies, waits for them, and re-layouts: 14.9 us -> 13 us
  transfers between devices with their start and end apart: 68 -> 60, of which waited for: 30 -> 22; matrix products, arithmetic and copies ran while one was open for 8% -> 10% of each run, Pallas kernels for 26% -> 33%
where the time goes in v3:
time: 446 us; the launch traced here: 439 us
  Pallas kernels  189 us (42%)
  waiting for transfers between devices  115 us (26%)
  starting transfers between devices  65.5 us (15%)
  local copies, waits for them, and re-layouts  45.4 us (10%)
  between operations  15.3 us (3%)
  other arithmetic  9.38 us (2%)
    pallas_call x19, Pallas kernels, call(): pl.pallas_call(kernel, out_shape=outs, in_specs=[vmem if s is None else s...  189 us
    ppermute x28, waiting for transfers between devices, turned(): lax.ppermute(block, axis, [(i, (i + by) % size) for i in range(size)])  63.2 us
    ppermute x30, waiting for transfers between devices, crossed(): lax.ppermute(block, axis, [(i, i ^ bit) for i in range(lax.axis_size(axis...  48.9 us
    ppermute x28, starting transfers between devices, turned(): lax.ppermute(block, axis, [(i, (i + by) % size) for i in range(size)])  47.1 us
    gather x2, local copies, waits for them, and re-layouts, rows_of(): word_table.at[jnp.clip(ids.reshape(-1) - offset, 0, vocab - 1)]  22.8 us
    ppermute x30, starting transfers between devices, crossed(): lax.ppermute(block, axis, [(i, i ^ bit) for i in range(lax.axis_size(axis...  18.4 us
    unnamed x127, local copies, waits for them, and re-layouts  13 us
  transfers between devices with their start and end apart: 60, of which 22 were waited for; matrix products, arithmetic and copies ran while one was open for 10% of the time, Pallas kernels for 33%

profile of v3, /device:TPU:0, one launch (start us, length us, event | category | flops | bytes accessed | tf_op | source)
XLA Modules:
  0.0 438.9 jit_solution(13824951794900528381)
XLA Ops:
  24.6 11.4 %gather_fusion = bf16[1024,768]{1,0:T(8,128)(2,1)} fusion(bf16[7632,768]{1,0:T(8,128)(2,1)} %refs_5_.1, s32[1024]{0:T(1024)S(1)} %broadcast_clamp_fusion.1), kind=kCustom, calls=%fused_computation | custom fusion | bytes 3149824 | tf_op jit(solution)/shard_map/gather | solution.py:919
  45.9 11.4 %gather_fusion.1 = bf16[1024,768]{1,0:T(8,128)(2,1)} fusion(bf16[7632,768]{1,0:T(8,128)(2,1)} %refs_5_.1, s32[1024]{0:T(1024)S(1)} %broadcast_clamp_fusion), kind=kCustom, calls=%fused_computation.1 | custom fusion | bytes 3149824 | tf_op jit(solution)/shard_map/gather | solution.py:919
  71.5 5.8 %collective-permute-done.23.refs_22_ = bf16[256,768]{1,0:T(8,128)(2,1)S(1)} collective-permute-done((bf16[256,768]{1,0:T(8,128)(2,1)S(1)}, bf16[256,768]{1,0:T(8,128)(2,1)S(1)}, u32[]{:S(2)}, u32[]{:S(2)}) %collective-permute-start.23) | collective-permute-done | bytes 393248 | tf_op jit(solution)/shard_map/ppermute | solution.py:84
  77.3 7.0 %collective-permute-done.22.refs_21_ = bf16[256,768]{1,0:T(8,128)(2,1)S(1)} collective-permute-done((bf16[256,768]{1,0:T(8,128)(2,1)S(1)}, bf16[256,768]{1,0:T(8,128)(2,1)S(1)}, u32[]{:S(2)}, u32[]{:S(2)}) %collective-permute-start.22) | collective-permute-done | bytes 393248 | tf_op jit(solution)/shard_map/ppermute | solution.py:84
  93.5 11.1 %layer_first.1 = (bf16[256,768]{1,0:T(8,128)(2,1)}, bf16[256,768]{1,0:T(8,128)(2,1)}, bf16[256,768]{1,0:T(8,128)(2,1)}, bf16[12,256,256]{2,1,0:T(8,128)(2,1)}, b...) custom-call(bf16[2,2,192,768]{3,2,1,0:T(8,128)(2,1)} %get-tuple-elem, ...), custom_call_target="tpu_custom_call" | custom-call | tf_op jit(solution)/shard_map/layer_first/pallas_call | solution.py:65
  104.6 11.0 %layer_second.1 = (bf16[256,768]{1,0:T(8,128)(2,1)}, bf16[256,768]{1,0:T(8,128)(2,1)}, bf16[256,768]{1,0:T(8,128)(2,1)}, bf16[12,256,256]{2,1,0:T(8,128)(2,1)}, ...) custom-call(bf16[2,2,192,768]{3,2,1,0:T(8,128)(2,1)} %get-tuple-elem, ...), custom_call_target="tpu_custom_call" | custom-call | tf_op jit(solution)/shard_map/layer_second/pallas_call | solution.py:65
  115.7 3.8 collective-permute-start.25
  120.2 11.0 %head_forward.4 = (f32[256,768]{1,0:T(8,128)}, f32[8,256]{1,0:T(8,128)}) custom-call(bf16[256,768]{1,0:T(8,128)(2,1)} %get-tuple-element.158.refs_0_, bf16[7632,768]{1,0:T(8,128)(2,1)} %refs_5_.1), custom_call_target="tpu_custom_call" | custom-call | tf_op jit(solution)/shard_map/head_forward/pallas_call | solution.py:65
  133.9 10.9 %head_forward.5 = (f32[256,768]{1,0:T(8,128)}, f32[8,256]{1,0:T(8,128)}) custom-call(bf16[256,768]{1,0:T(8,128)(2,1)} %copy-done.20, bf16[7632,768]{1,0:T(8,128)(2,1)} %refs_5_.1), custom_call_target="tpu_custom_call" | custom-call | tf_op jit(solution)/shard_map/head_forward/pallas_call | solution.py:65
  152.2 10.9 %head_forward.6 = (f32[256,768]{1,0:T(8,128)}, f32[8,256]{1,0:T(8,128)}) custom-call(bf16[256,768]{1,0:T(8,128)(2,1)} %copy-done.21, bf16[7632,768]{1,0:T(8,128)(2,1)} %refs_5_.1), custom_call_target="tpu_custom_call" | custom-call | tf_op jit(solution)/shard_map/head_forward/pallas_call | solution.py:65
  165.3 10.9 %head_forward.7 = (f32[256,768]{1,0:T(8,128)}, f32[8,256]{1,0:T(8,128)}) custom-call(bf16[128,768]{1,0:T(8,128)(2,1)} %copy-done.29, bf16[128,768]{1,0:T(8,128)(2,1)} %copy-done.30, bf16[7632,768]{1,0:T(8,128)(2,1)} %refs_5_.1), custom_call_target="tpu_custom_call" | custom-call | tf_op jit(solution)/shard_map/head_forward/pallas_call | solution.py:65
  181.3 5.2 %list_tokens.1 = s32[1,1152]{1,0:T(1,128)} custom-call(s32[1,1024]{1,0:T(1,128)} %bitcast.79), custom_call_target="tpu_custom_call" | custom-call | tf_op jit(solution)/shard_map/list_tokens/pallas_call | solution.py:65
  187.2 4.6 %head_combine.1 = (bf16[1024,768]{1,0:T(8,128)(2,1)}, f32[1024,1]{1,0:T(8,128)}) custom-call(f32[256,768]{1,0:T(8,128)} %get-tuple-element.159.x0_ref, f32[256,768]{1,0:T(8,128)} %get-tuple-element.163.x1_ref, f32[256,768]{1,0:T(8,128)} %get-tuple-element.166.x2_ref, f32[256,768]{1,0:T(8,128)} %get-tuple-element.161.x3_ref, bf16[1024,768]{1,0:T(8,128)(2,1)} %gather_fusion.1, ...), custom_call_target="tpu_custom_call" | custom-call | tf_op jit(solution)/shard_map/head_combine/pallas_call | solution.py:65
  191.8 31.7 %head_table.1 = bf16[768,7632]{1,0:T(8,128)(2,1)} custom-call(bf16[256,768]{1,0:T(8,128)(2,1)} %get-tuple-element.158.refs_0_, bf16[256,768]{1,0:T(8,128)(2,1)} %copy-done.21, bf16[128,768]{1,0:T(8,128)(2,1)} %copy-done.29, bf16[128,768]{1,0:T(8,128)(2,1)} %copy-done.30, bf16[256,768]{1,0:T(8,128)(2,1)} %copy-done.20, bf16[7632,768]{1,0:T(8,128)(2,1)} %refs_5_.1, ...), custom_call_target="tpu_custom_call" | custom-call | tf_op jit(solution)/shard_map/head_table/pallas_call | solution.py:65
  225.9 8.3 %ffn_back.2 = (f32[256,768]{1,0:T(8,128)}, f32[16,768]{1,0:T(8,128)}, bf16[4,192,768]{2,1,0:T(8,128)(2,1)}, bf16[4,192,768]{2,1,0:T(8,128)(2,1)}) custom-call(bf16[2,2,192,768]{3,2,1,0:T(8,128)(2,1)} %get-tuple-element.141.refs_0_, bf16[384,768]{1,0:T(8,128)(2,1)} %copy-done.2, bf16[192,768]{1,0:T(8,128)(2,1)} %copy-done.9, bf16[384,768]{1,0:T(8,128)(2,1)} %copy-done.5, ...), custom_call_target="tpu_custom_call" | custom-call | tf_op jit(solution)/shard_map/ffn_back/pallas_call | solution.py:65
  234.2 14.3 %att_back.2 = (f32[256,768]{1,0:T(8,128)}, bf16[256,768]{1,0:T(8,128)(2,1)}, bf16[4,192,768]{2,1,0:T(8,128)(2,1)}, bf16[4,192,768]{2,1,0:T(8,128)(2,1)}) custom-call(bf16[2,2,192,768]{3,2,1,0:T(8,128)(2,1)} %get-tuple-element.141.refs_0_, bf16[384,768]{1,0:T(8,128)(2,1)} %copy-done.2, bf16[192,768]{1,0:T(8,128)(2,1)} %copy-done.9, ...), custom_call_target="tpu_custom_call" | custom-call | tf_op jit(solution)/shard_map/att_back/pallas_call | solution.py:65
  249.1 8.4 %ffn_back.3 = (f32[256,768]{1,0:T(8,128)}, f32[16,768]{1,0:T(8,128)}, bf16[4,192,768]{2,1,0:T(8,128)(2,1)}, bf16[4,192,768]{2,1,0:T(8,128)(2,1)}) custom-call(bf16[2,2,192,768]{3,2,1,0:T(8,128)(2,1)} %get-tuple-element.141.refs_0_, bf16[384,768]{1,0:T(8,128)(2,1)} %copy-done.2, bf16[192,768]{1,0:T(8,128)(2,1)} %copy-done.9, bf16[384,768]{1,0:T(8,128)(2,1)} %copy-done.5, ...), custom_call_target="tpu_custom_call" | custom-call | tf_op jit(solution)/shard_map/ffn_back/pallas_call | solution.py:65
  259.0 3.8 add_cores_split.2
  266.6 15.2 %att_back.3 = (f32[256,768]{1,0:T(8,128)}, bf16[256,768]{1,0:T(8,128)(2,1)}, bf16[4,288,768]{2,1,0:T(8,128)(2,1)}, bf16[4,288,768]{2,1,0:T(8,128)(2,1)}, bf16[8,96,256]{2,1,0:T(8,128)(2,1)}) custom-call(bf16[2,2,192,768]{3,2,1,0:T(8,128)(2,1)} %get-tuple-element.141.refs_0_, bf16[384,768]{1,0:T(8,128)(2,1)} %copy-done.2, bf16[192,768]{1,0:T(8,128)(2,1)} %copy-done.9, ...), custom_call_target="tpu_custom_call" | custom-call | tf_op jit(solution)/shard_map/att_back/pallas_call | solution.py:65
  285.1 5.0 %collective-permute-done.37 = bf16[1,4,96,256]{3,2,0,1:T(8,128)(2,1)S(1)} collective-permute-done((bf16[1,4,96,256]{3,2,0,1:T(8,128)(2,1)S(1)}, bf16[1,4,96,256]{3,2,0,1:T(8,128)(2,1)S(1)}, u32[]{:S(2)}, u32[]{:S(2)}) %collective-permute-start.37) | collective-permute-done | bytes 196640 | tf_op jit(solution)/shard_map/ppermute | solution.py:88
  298.6 4.4 add_cores_split.3
  308.1 6.4 %collective-permute-done.41 = bf16[4,96,256]{2,1,0:T(8,128)(2,1)S(1)} collective-permute-done((bf16[4,96,256]{2,1,0:T(8,128)(2,1)S(1)}, bf16[4,96,256]{2,1,0:T(8,128)(2,1)S(1)}, u32[]{:S(2)}, u32[]{:S(2)}) %collective-permute-start.41) | collective-permute-done | bytes 196640 | tf_op jit(solution)/shard_map/ppermute | solution.py:88
  314.6 14.3 %collective-permute-done.45 = bf16[384,768]{1,0:T(8,128)(2,1)S(1)} collective-permute-done((bf16[384,768]{1,0:T(8,128)(2,1)S(1)}, bf16[384,768]{1,0:T(8,128)(2,1)S(1)}, u32[]{:S(2)}, u32[]{:S(2)}) %collective-permute-start.45) | collective-permute-done | bytes 589856 | tf_op jit(solution)/shard_map/ppermute | solution.py:84
  330.1 5.5 %collective-permute-done.43 = bf16[240,768]{1,0:T(8,128)(2,1)S(1)} collective-permute-done((bf16[240,768]{1,0:T(8,128)(2,1)}, bf16[240,768]{1,0:T(8,128)(2,1)S(1)}, u32[]{:S(2)}, u32[]{:S(2)}) %collective-permute-start.43) | collective-permute-done | bytes 368672 | tf_op jit(solution)/shard_map/ppermute | solution.py:84
  336.0 3.8 collective-permute-start.47
  342.1 7.7 %collective-permute-done.50 = s32[4,1152]{1,0:T(4,128)S(1)} collective-permute-done((s32[4,1152]{1,0:T(4,128)S(1)}, s32[4,1152]{1,0:T(4,128)S(1)}, u32[]{:S(2)}, u32[]{:S(2)}) %collective-permute-start.50) | collective-permute-done | bytes 18464 | tf_op jit(solution)/shard_map/ppermute | solution.py:88
  350.4 6.8 %collective-permute-done.46 = bf16[480,768]{1,0:T(8,128)(2,1)S(1)} collective-permute-done((bf16[480,768]{1,0:T(8,128)(2,1)S(1)}, bf16[480,768]{1,0:T(8,128)(2,1)S(1)}, u32[]{:S(2)}, u32[]{:S(2)}) %collective-permute-start.46) | collective-permute-done | bytes 737312 | tf_op jit(solution)/shard_map/ppermute | solution.py:84
  357.2 12.4 %collective-permute-done.47 = bf16[480,768]{1,0:T(8,128)(2,1)S(1)} collective-permute-done((bf16[480,768]{1,0:T(8,128)(2,1)S(1)}, bf16[480,768]{1,0:T(8,128)(2,1)S(1)}, u32[]{:S(2)}, u32[]{:S(2)}) %collective-permute-start.47) | collective-permute-done | bytes 737312 | tf_op jit(solution)/shard_map/ppermute | solution.py:84
  373.3 13.9 %collective-permute-done.51 = bf16[480,768]{1,0:T(8,128)(2,1)S(1)} collective-permute-done((bf16[480,768]{1,0:T(8,128)(2,1)S(1)}, bf16[480,768]{1,0:T(8,128)(2,1)S(1)}, u32[]{:S(2)}, u32[]{:S(2)}) %collective-permute-start.51) | collective-permute-done | bytes 737312 | tf_op jit(solution)/shard_map/ppermute | solution.py:88
  396.1 4.3 collective-permute-done.54.far_a_ref
  401.4 4.9 %collective-permute-done.56 = bf16[480,768]{1,0:T(8,128)(2,1)S(1)} collective-permute-done((bf16[480,768]{1,0:T(8,128)(2,1)S(1)}, bf16[480,768]{1,0:T(8,128)(2,1)S(1)}, u32[]{:S(2)}, u32[]{:S(2)}) %collective-permute-start.56) | collective-permute-done | bytes 737312 | tf_op jit(solution)/shard_map/ppermute | solution.py:88
  414.6 17.3 %table_grad.1 = f32[96,7632]{1,0:T(8,128)} custom-call(bf16[96,7632]{1,0:T(8,128)(2,1)} %reduce-scatter.5.cloned.1.call-done.d_ref, bf16[8,96,256]{2,1,0:T(8,128)(2,1)} %copy-done.23, bf16[8,96,256]{2,1,0:T(8,128)(2,1)} %copy-done.27, bf16[8,96,256]{2,1,0:T(8,128)(2,1)} %copy-done.28, bf16[4,96,256]{2,1,0:T(8,128)(2,1)} %copy-done.44, ...), custom_call_target="tpu_custom_call" | custom-call | tf_op jit(solution)/shard_map/table_grad/pallas_call | solution.py:65
  (307 shorter events, 120.2 us)
Async XLA Ops:
  7.2 218.7 %reduce-scatter.3.cloned.1.call-start = ((), (), s32[]{:S(2)}) async-start(), calls=%async_computation.2 | async-start | bytes 1966080 | tf_op jit(solution)/shard_map/reduce_scatter | solution.py:976
  8.0 14.5 %collective-permute-start.4 = (s32[3,256]{1,0:T(4,128)S(1)}, s32[3,256]{1,0:T(4,128)S(1)}, u32[]{:S(2)}, u32[]{:S(2)}) collective-permute-start(s32[3,256]{1,0:T(4,128)S(1)} %bitcast.71), channel_id=1, source_target_pairs={{0,1},{1,2},{2,3},{3,0},{4,5},{5,6},{6,7},{7,4},{8,9},{9,10},{10,1... | collective-permute-start | bytes 9224 | tf_op jit(solution)/shard_map/ppermute | solution.py:84
  11.0 12.9 %collective-permute-start.3 = (s32[3,256]{1,0:T(4,128)S(1)}, s32[3,256]{1,0:T(4,128)S(1)}, u32[]{:S(2)}, u32[]{:S(2)}) collective-permute-start(s32[3,256]{1,0:T(4,128)S(1)} %bitcast.72), channel_id=1, source_target_pairs={{0,2},{1,3},{2,0},{3,1},{4,6},{5,7},{6,4},{7,5},{8,10},{9,11},{10,... | collective-permute-start | bytes 9224 | tf_op jit(solution)/shard_map/ppermute | solution.py:84
  20.4 15.6 %collective-permute-start.1 = (bf16[192,768]{1,0:T(8,128)(2,1)}, bf16[192,768]{1,0:T(8,128)(2,1)S(1)}, u32[]{:S(2)}, u32[]{:S(2)}) collective-permute-start(bf16[192,768]{1,0:T(8,128)(2,1)} %get-tuple-element.142), channel_id=1, source_target_pairs={{0,3},{1,0},{2,1},{3,2},{4,7},{5,4},{6,5},{7,6},{8,11},{9,8},{10,9... | collective-permute-start | bytes 884744 | tf_op jit(solution)/shard_map/ppermute | solution.py:84
  20.9 15.2 %collective-permute-start = (bf16[192,768]{1,0:T(8,128)(2,1)}, bf16[192,768]{1,0:T(8,128)(2,1)S(1)}, u32[]{:S(2)}, u32[]{:S(2)}) collective-permute-start(bf16[192,768]{1,0:T(8,128)(2,1)} %get-tuple-element.142), channel_id=1, source_target_pairs={{0,1},{1,2},{2,3},{3,0},{4,5},{5,6},{6,7},{7,4},{8,9},{9,10},{10,1... | collective-permute-start | bytes 884744 | tf_op jit(solution)/shard_map/ppermute | solution.py:84
  22.4 34.8 %collective-permute-start.14 = (bf16[2,192,768]{2,1,0:T(8,128)(2,1)}, bf16[2,192,768]{2,1,0:T(8,128)(2,1)S(1)}, u32[]{:S(2)}, u32[]{:S(2)}) collective-permute-start(bf16[2,192,768]{2,1,0:T(8,128)(2,1)} %get-tuple-element.156), channel_id=1, source_target_pairs={{0,16},{16,0},{1,17},{17,1},{2,18},{18,2},{3,19},{19,3},{4,20},{20... | collective-permute-start | bytes 1769480 | tf_op jit(solution)/shard_map/ppermute | solution.py:88
  39.9 23.8 %collective-permute-start.10 = (bf16[384,768]{1,0:T(8,128)(2,1)S(1)}, bf16[384,768]{1,0:T(8,128)(2,1)S(1)}, u32[]{:S(2)}, u32[]{:S(2)}) collective-permute-start(bf16[384,768]{1,0:T(8,128)(2,1)S(1)} %constant_dynamic-update-slice_fusion.refs_1_), channel_id=1, source_target_pairs={{0,16},{16,0},{1,17},{17,1},{2,18},{18,2},{3,19},{19,3},{4,20},{20... | collective-permute-start | bytes 1769480 | tf_op jit(solution)/shard_map/ppermute | solution.py:88
  40.5 25.3 %collective-permute-start.9 = (bf16[384,768]{1,0:T(8,128)(2,1)S(1)}, bf16[384,768]{1,0:T(8,128)(2,1)S(1)}, u32[]{:S(2)}, u32[]{:S(2)}) collective-permute-start(bf16[384,768]{1,0:T(8,128)(2,1)S(1)} %constant_dynamic-update-slice_fusion.refs_1_), channel_id=1, source_target_pairs={{0,8},{4,12},{8,0},{12,4},{1,9},{5,13},{9,1},{13,5},{2,10},{6,14},... | collective-permute-start | bytes 1769480 | tf_op jit(solution)/shard_map/ppermute | solution.py:88
  43.6 13.8 %collective-permute-start.6 = (bf16[224,768]{1,0:T(8,128)(2,1)}, bf16[224,768]{1,0:T(8,128)(2,1)}, u32[]{:S(2)}, u32[]{:S(2)}) collective-permute-start(bf16[224,768]{1,0:T(8,128)(2,1)} %pad_maximum_fusion.14), channel_id=1, source_target_pairs={{0,3},{1,0},{2,1},{3,2},{4,7},{5,4},{6,5},{7,6},{8,11},{9,8},{10,9... | collective-permute-start | bytes 1032200 | tf_op jit(solution)/shard_map/ppermute | solution.py:84
  45.8 15.4 %collective-permute-start.5 = (bf16[224,768]{1,0:T(8,128)(2,1)}, bf16[224,768]{1,0:T(8,128)(2,1)}, u32[]{:S(2)}, u32[]{:S(2)}) collective-permute-start(bf16[224,768]{1,0:T(8,128)(2,1)} %pad_maximum_fusion.13), channel_id=1, source_target_pairs={{0,1},{1,2},{2,3},{3,0},{4,5},{5,6},{6,7},{7,4},{8,9},{9,10},{10,1... | collective-permute-start | bytes 1032200 | tf_op jit(solution)/shard_map/ppermute | solution.py:84
  57.4 29.2 %collective-permute-start.15 = (bf16[2,192,768]{2,1,0:T(8,128)(2,1)S(1)}, bf16[2,192,768]{2,1,0:T(8,128)(2,1)S(1)}, u32[]{:S(2)}, u32[]{:S(2)}) collective-permute-start(bf16[2,192,768]{2,1,0:T(8,128)(2,1)S(1)} %collective-permute-done.14.refs_9_), channel_id=1, source_target_pairs={{0,4},{4,0},{8,12},{12,8},{1,5},{5,1},{9,13},{13,9},{2,6},{6,2},{1... | collective-permute-start | bytes 1769480 | tf_op jit(solution)/shard_map/ppermute | solution.py:88
  63.8 22.7 %collective-permute-start.11 = (bf16[576,768]{1,0:T(8,128)(2,1)S(1)}, bf16[576,768]{1,0:T(8,128)(2,1)S(1)}, u32[]{:S(2)}, u32[]{:S(2)}) collective-permute-start(bf16[576,768]{1,0:T(8,128)(2,1)S(1)} %pad_maximum_fusion.2), channel_id=1, source_target_pairs={{0,8},{4,12},{8,0},{12,4},{1,9},{5,13},{9,1},{13,5},{2,10},{6,14},... | collective-permute-start | bytes 2654216 | tf_op jit(solution)/shard_map/ppermute | solution.py:88
  70.7 13.6 %collective-permute-start.22 = (bf16[256,768]{1,0:T(8,128)(2,1)S(1)}, bf16[256,768]{1,0:T(8,128)(2,1)S(1)}, u32[]{:S(2)}, u32[]{:S(2)}) collective-permute-start(bf16[256,768]{1,0:T(8,128)(2,1)S(1)} %pad_maximum_fusion.9), channel_id=1, source_target_pairs={{0,1},{1,2},{2,3},{3,0},{4,5},{5,6},{6,7},{7,4},{8,9},{9,10},{10,1... | collective-permute-start | bytes 1179656 | tf_op jit(solution)/shard_map/ppermute | solution.py:84
  70.9 19.0 %collective-permute-start.19 = (bf16[192,768]{1,0:T(8,128)(2,1)S(1)}, bf16[192,768]{1,0:T(8,128)(2,1)}, u32[]{:S(2)}, u32[]{:S(2)}) collective-permute-start(bf16[192,768]{1,0:T(8,128)(2,1)S(1)} %collective-permute-done.16.refs_12_), channel_id=1, source_target_pairs={{0,8},{4,12},{8,0},{12,4},{1,9},{5,13},{9,1},{13,5},{2,10},{6,14},... | collective-permute-start | bytes 884744 | tf_op jit(solution)/shard_map/ppermute | solution.py:88
  115.6 17.5 %collective-permute-start.26 = (bf16[256,768]{1,0:T(8,128)(2,1)}, bf16[256,768]{1,0:T(8,128)(2,1)S(1)}, u32[]{:S(2)}, u32[]{:S(2)}) collective-permute-start(bf16[256,768]{1,0:T(8,128)(2,1)} %get-tuple-element.158.refs_0_), channel_id=1, source_target_pairs={{0,1},{1,2},{2,3},{3,0},{4,5},{5,6},{6,7},{7,4},{8,9},{9,10},{10,1... | collective-permute-start | bytes 1179656 | tf_op jit(solution)/shard_map/ppermute | solution.py:84
  115.7 31.5 %collective-permute-start.25 = (bf16[256,768]{1,0:T(8,128)(2,1)}, bf16[256,768]{1,0:T(8,128)(2,1)S(1)}, u32[]{:S(2)}, u32[]{:S(2)}) collective-permute-start(bf16[256,768]{1,0:T(8,128)(2,1)} %get-tuple-element.158.refs_0_), channel_id=1, source_target_pairs={{0,3},{1,0},{2,1},{3,2},{4,7},{5,4},{6,5},{7,6},{8,11},{9,8},{10,9... | collective-permute-start | bytes 1179656 | tf_op jit(solution)/shard_map/ppermute | solution.py:84
  131.3 55.2 %collective-permute-start.24 = (bf16[256,768]{1,0:T(8,128)(2,1)S(1)}, bf16[256,768]{1,0:T(8,128)(2,1)S(1)}, u32[]{:S(2)}, u32[]{:S(2)}) collective-permute-start(bf16[256,768]{1,0:T(8,128)(2,1)S(1)} %broadcast_select_fusion.3), channel_id=1, source_target_pairs={{0,16},{16,0},{1,17},{17,1},{2,18},{18,2},{3,19},{19,3},{4,20},{20... | collective-permute-start | bytes 1179656 | tf_op jit(solution)/shard_map/ppermute | solution.py:88
  144.8 19.7 %collective-permute-start.27 = (bf16[128,768]{1,0:T(8,128)(2,1)S(1)}, bf16[128,768]{1,0:T(8,128)(2,1)S(1)}, u32[]{:S(2)}, u32[]{:S(2)}) collective-permute-start(bf16[128,768]{1,0:T(8,128)(2,1)S(1)} %slice.151), channel_id=1, source_target_pairs={{0,1},{1,2},{2,3},{3,0},{4,5},{5,6},{6,7},{7,4},{8,9},{9,10},{10,1... | collective-permute-start | bytes 589832 | tf_op jit(solution)/shard_map/ppermute | solution.py:84
  147.2 17.3 %collective-permute-start.28 = (bf16[128,768]{1,0:T(8,128)(2,1)S(1)}, bf16[128,768]{1,0:T(8,128)(2,1)S(1)}, u32[]{:S(2)}, u32[]{:S(2)}) collective-permute-start(bf16[128,768]{1,0:T(8,128)(2,1)S(1)} %slice.152), channel_id=1, source_target_pairs={{0,3},{1,0},{2,1},{3,2},{4,7},{5,4},{6,5},{7,6},{8,11},{9,8},{10,9... | collective-permute-start | bytes 589832 | tf_op jit(solution)/shard_map/ppermute | solution.py:84
  191.8 222.8 %reduce-scatter.5.cloned.1.call-start = ((), (), s32[]{:S(2)}) async-start(), calls=%async_computation.3 | async-start | bytes 13271040 | tf_op jit(solution)/shard_map/reduce_scatter | solution.py:980
  262.8 19.0 %collective-permute-start.35 = (bf16[192,768]{1,0:T(8,128)(2,1)}, bf16[192,768]{1,0:T(8,128)(2,1)S(1)}, u32[]{:S(2)}, u32[]{:S(2)}) collective-permute-start(bf16[192,768]{1,0:T(8,128)(2,1)} %get-tuple-element.211), channel_id=1, source_target_pairs={{0,1},{1,2},{2,3},{3,0},{4,5},{5,6},{6,7},{7,4},{8,9},{9,10},{10,1... | collective-permute-start | bytes 884744 | tf_op jit(solution)/shard_map/ppermute | solution.py:84
  263.6 18.2 %collective-permute-start.36 = (bf16[192,768]{1,0:T(8,128)(2,1)}, bf16[192,768]{1,0:T(8,128)(2,1)S(1)}, u32[]{:S(2)}, u32[]{:S(2)}) collective-permute-start(bf16[192,768]{1,0:T(8,128)(2,1)} %get-tuple-element.212), channel_id=1, source_target_pairs={{0,3},{1,0},{2,1},{3,2},{4,7},{5,4},{6,5},{7,6},{8,11},{9,8},{10,9... | collective-permute-start | bytes 884744 | tf_op jit(solution)/shard_map/ppermute | solution.py:84
  292.1 36.8 %collective-permute-start.45 = (bf16[384,768]{1,0:T(8,128)(2,1)S(1)}, bf16[384,768]{1,0:T(8,128)(2,1)S(1)}, u32[]{:S(2)}, u32[]{:S(2)}) collective-permute-start(bf16[384,768]{1,0:T(8,128)(2,1)S(1)} %pad_maximum_fusion.6), channel_id=1, source_target_pairs={{0,3},{1,0},{2,1},{3,2},{4,7},{5,4},{6,5},{7,6},{8,11},{9,8},{10,9... | collective-permute-start | bytes 1769480 | tf_op jit(solution)/shard_map/ppermute | solution.py:84
  292.1 36.8 %collective-permute-start.44 = (bf16[384,768]{1,0:T(8,128)(2,1)S(1)}, bf16[384,768]{1,0:T(8,128)(2,1)S(1)}, u32[]{:S(2)}, u32[]{:S(2)}) collective-permute-start(bf16[384,768]{1,0:T(8,128)(2,1)S(1)} %pad_maximum_fusion.5), channel_id=1, source_target_pairs={{0,1},{1,2},{2,3},{3,0},{4,5},{5,6},{6,7},{7,4},{8,9},{9,10},{10,1... | collective-permute-start | bytes 1769480 | tf_op jit(solution)/shard_map/ppermute | solution.py:84
  304.2 25.9 %collective-permute-start.42 = (bf16[240,768]{1,0:T(8,128)(2,1)}, bf16[240,768]{1,0:T(8,128)(2,1)S(1)}, u32[]{:S(2)}, u32[]{:S(2)}) collective-permute-start(bf16[240,768]{1,0:T(8,128)(2,1)} %get-tuple-element.240), channel_id=1, source_target_pairs={{0,1},{1,2},{2,3},{3,0},{4,5},{5,6},{6,7},{7,4},{8,9},{9,10},{10,1... | collective-permute-start | bytes 1105928 | tf_op jit(solution)/shard_map/ppermute | solution.py:84
  304.5 31.1 %collective-permute-start.43 = (bf16[240,768]{1,0:T(8,128)(2,1)}, bf16[240,768]{1,0:T(8,128)(2,1)S(1)}, u32[]{:S(2)}, u32[]{:S(2)}) collective-permute-start(bf16[240,768]{1,0:T(8,128)(2,1)} %get-tuple-element.241), channel_id=1, source_target_pairs={{0,3},{1,0},{2,1},{3,2},{4,7},{5,4},{6,5},{7,6},{8,11},{9,8},{10,9... | collective-permute-start | bytes 1105928 | tf_op jit(solution)/shard_map/ppermute | solution.py:84
  335.9 21.3 %collective-permute-start.46 = (bf16[480,768]{1,0:T(8,128)(2,1)S(1)}, bf16[480,768]{1,0:T(8,128)(2,1)S(1)}, u32[]{:S(2)}, u32[]{:S(2)}) collective-permute-start(bf16[480,768]{1,0:T(8,128)(2,1)S(1)} %pad_maximum_fusion.3), channel_id=1, source_target_pairs={{0,1},{1,2},{2,3},{3,0},{4,5},{5,6},{6,7},{7,4},{8,9},{9,10},{10,1... | collective-permute-start | bytes 2211848 | tf_op jit(solution)/shard_map/ppermute | solution.py:84
  336.0 33.7 %collective-permute-start.47 = (bf16[480,768]{1,0:T(8,128)(2,1)S(1)}, bf16[480,768]{1,0:T(8,128)(2,1)S(1)}, u32[]{:S(2)}, u32[]{:S(2)}) collective-permute-start(bf16[480,768]{1,0:T(8,128)(2,1)S(1)} %pad_maximum_fusion.4), channel_id=1, source_target_pairs={{0,3},{1,0},{2,1},{3,2},{4,7},{5,4},{6,5},{7,6},{8,11},{9,8},{10,9... | collective-permute-start | bytes 2211848 | tf_op jit(solution)/shard_map/ppermute | solution.py:84
  370.1 17.1 %collective-permute-start.51 = (bf16[480,768]{1,0:T(8,128)(2,1)S(1)}, bf16[480,768]{1,0:T(8,128)(2,1)S(1)}, u32[]{:S(2)}, u32[]{:S(2)}) collective-permute-start(bf16[480,768]{1,0:T(8,128)(2,1)S(1)} %pad_maximum_fusion), channel_id=1, source_target_pairs={{0,16},{16,0},{1,17},{17,1},{2,18},{18,2},{3,19},{19,3},{4,20},{20... | collective-permute-start | bytes 2211848 | tf_op jit(solution)/shard_map/ppermute | solution.py:88
  371.0 16.5 %collective-permute-start.53 = (bf16[8,96,256]{2,1,0:T(8,128)(2,1)S(1)}, bf16[8,96,256]{2,1,0:T(8,128)(2,1)S(1)}, u32[]{:S(2)}, u32[]{:S(2)}) collective-permute-start(bf16[8,96,256]{2,1,0:T(8,128)(2,1)S(1)} %pad_maximum_fusion.12.own_ref), channel_id=1, source_target_pairs={{0,3},{1,0},{2,1},{3,2},{4,7},{5,4},{6,5},{7,6},{8,11},{9,8},{10,9... | collective-permute-start | bytes 1179656 | tf_op jit(solution)/shard_map/ppermute | solution.py:84
  373.3 16.8 %collective-permute-start.52 = (bf16[8,96,256]{2,1,0:T(8,128)(2,1)S(1)}, bf16[8,96,256]{2,1,0:T(8,128)(2,1)S(1)}, u32[]{:S(2)}, u32[]{:S(2)}) collective-permute-start(bf16[8,96,256]{2,1,0:T(8,128)(2,1)S(1)} %pad_maximum_fusion.12.own_ref), channel_id=1, source_target_pairs={{0,1},{1,2},{2,3},{3,0},{4,5},{5,6},{6,7},{7,4},{8,9},{9,10},{10,1... | collective-permute-start | bytes 1179656 | tf_op jit(solution)/shard_map/ppermute | solution.py:84
  390.1 16.2 %collective-permute-start.56 = (bf16[480,768]{1,0:T(8,128)(2,1)S(1)}, bf16[480,768]{1,0:T(8,128)(2,1)S(1)}, u32[]{:S(2)}, u32[]{:S(2)}) collective-permute-start(bf16[480,768]{1,0:T(8,128)(2,1)S(1)} %fusion.2), channel_id=1, source_target_pairs={{0,8},{4,12},{8,0},{12,4},{1,9},{5,13},{9,1},{13,5},{2,10},{6,14},... | collective-permute-start | bytes 2211848 | tf_op jit(solution)/shard_map/ppermute | solution.py:88
  (89 other events, 821.6 us)
Sparse Core Ops, SparseCore 0:
  191.9 33.9 reduce-scatter.2
  229.4 91.3 reduce-scatter.4

commit v4 on v3

--- a/solution.py
+++ b/solution.py
@@ -128,8 +128,8 @@
         self.part = out[1]
         self.at_small = 3 * part
         self.rows = 2 * self.part
-        self.pos = pos_rows // 4
-        self.extra = self.pos + 16
+        self.pos = self.part - self.at_small - 16
+        self.extra = (pos_rows - self.pos) // 2
 
 
 def pack_weights(z, qkv, out, fin, fout, small):
@@ -242,10 +242,14 @@
         self.copies = []
 
     def put(self, name, value, index=None):
+        source = self.buffers[name] if index is None else self.buffers[name].at[index]
+        source[...] = value.astype(source.dtype)
+        self.send(name, index)
+
+    def send(self, name, index=None):
         source, target = self.buffers[name], self.refs[name]
         if index is not None:
             source, target = source.at[index], target.at[index]
-        source[...] = value.astype(source.dtype)
         copy = pltpu.make_async_copy(source, target, self.sems.at[len(self.copies)])
         copy.start()
         self.copies.append(copy)
@@ -266,12 +270,18 @@
         z = self.z
         return sum(self.w[1, h, z.at_small : z.at_small + 16, :].astype(F32) for h in range(z.shards))
 
-    def proj(self, c):
+    def proj(self, c, p):
         z = self.z
-        dense = self.w[1, :, c * z.gi : (c + 1) * z.gi, :].reshape(z.gw, z.d)
-        tall = jnp.concatenate([dense] * z.groups, axis=0)
-        keep = group_of(iota(tall.shape, 0), z.gw, z.groups) == group_of(iota(tall.shape, 1), z.gw, z.groups)
-        return jnp.where(keep, tall, jnp.zeros_like(tall))
+        lanes = slice(2 * p * z.gw, 2 * (p + 1) * z.gw)
+        dense = self.w[1, :, c * z.gi : (c + 1) * z.gi, lanes].reshape(z.gw, 2 * z.gw)
+        high = iota(dense.shape, 1) >= z.gw
+        blank = jnp.zeros_like(dense)
+        return jnp.concatenate([jnp.where(high, blank, dense), jnp.where(high, dense, blank)], axis=0)
+
+    def project(self, value, c):
+        z = self.z
+        wide = 2 * z.gw
+        return jnp.concatenate([nn(value[:, p * wide : (p + 1) * wide], self.proj(c, p)) for p in range(z.groups // 2)], axis=1)
 
     def fin(self, g):
         z = self.z
@@ -321,12 +331,12 @@
 def layer_forward(z, pieces, seg_row, first, words=None, layer_in=None):
     seq = seg_row.shape[1]
     d = z.d
-    flat, whole = like((seq, d), BF16), like((seq, d), F32)
-    shapes = {"q": flat, "k": flat, "v": flat, "p": like((HEADS, seq, seq), BF16), "att": flat, "n1": whole, "mid": flat}
+    flat = like((seq, d), BF16)
+    shapes = {"q": flat, "k": flat, "v": flat, "p": like((HEADS, seq, seq), BF16), "att": flat, "n1": flat, "mid": flat}
     shapes.update({"act": like((z.groups, seq, d), BF16), "slope": like((z.groups, seq, d), BF16)})
-    shapes.update({"n2": whole, "stats": like((seq, 128), F32), "small": like((16, d), F32), "out": flat})
+    shapes.update({"n2": flat, "stats": like((seq, 128), F32), "small": like((16, d), F32), "out": flat})
     if first:
-        shapes.update({"x": flat, "n0": whole})
+        shapes.update({"x": flat, "n0": flat})
     stores = Stores(shapes, split=("p", "act", "slope"))
     head = d // HEADS
     inputs = list(words) if first else [layer_in]
@@ -339,7 +349,7 @@
         w_ref, sems, *buffers = refs
         waits = pieces.start(piece_refs, w_ref, sems, (0, 1))
         stores.bind(out_refs, buffers)
-        put = stores.put
+        put, send = stores.put, stores.send
         w = Weights(z, w_ref)
         if first:
             unit, r0 = normed(sum(ref[...].astype(F32) for ref in in_refs))
@@ -355,29 +365,34 @@
             r0 = jnp.zeros((seq, 1), F32)
             x_low = in_refs[0][...]
             x = x_low.astype(F32)
-        q = (nn(x_low, w.proj(0)).astype(BF16).astype(F32) * (1.0 / math.sqrt(head))).astype(BF16)
-        k = nn(x_low, w.proj(1)).astype(BF16)
-        v = (nn(x_low, w.proj(2)) + small[2:3]).astype(BF16)
+        q = (w.project(x_low, 0).astype(BF16).astype(F32) * (1.0 / math.sqrt(head))).astype(BF16)
+        k = w.project(x_low, 1).astype(BF16)
+        v = (w.project(x_low, 2) + small[2:3]).astype(BF16)
         put("q", q)
         put("k", k)
         put("v", v)
         same = upright(row_ref[...], seq) == row_ref[...].astype(F32)
         second = iota((seq, 128), 1) >= head
-        tiles = []
-        for t in range(d // 128):
-            lanes = slice(t * 128, (t + 1) * 128)
-            q_t, k_t, v_t = q[:, lanes], k[:, lanes], v[:, lanes]
+        q_ref, k_ref, v_ref, att_ref = (stores.buffers[name] for name in ("q", "k", "v", "att"))
+
+        def heads(t, carry):
+            lanes = pl.ds(pl.multiple_of(t * 128, 128), 128)
+            q_t, k_t, v_t = q_ref[:, lanes], k_ref[:, lanes], v_ref[:, lanes]
+            raw = [nt(jnp.where(second == (j == 1), q_t, jnp.zeros_like(q_t)), k_t) for j in range(2)]
             results = []
             for j in range(2):
-                picked = jnp.where(second == (j == 1), q_t, jnp.zeros_like(q_t))
-                scores = jnp.where(same, nt(picked, k_t), MASKED)
+                scores = jnp.where(same, raw[j], MASKED)
                 scores = jnp.exp(scores - jnp.max(scores, axis=-1, keepdims=True))
                 probs = (scores * (1.0 / jnp.sum(scores, axis=-1, keepdims=True))).astype(BF16)
-                put("p", probs, 2 * t + j)
+                stores.buffers["p"][2 * t + j] = probs
                 results.append(nn(probs, v_t))
-            tiles.append(jnp.where(second, results[1], results[0]).astype(BF16))
-        attended = jnp.concatenate(tiles, axis=1)
-        put("att", attended)
+            att_ref[:, lanes] = jnp.where(second, results[1], results[0]).astype(BF16)
+            return carry
+
+        lax.fori_loop(0, d // 128, heads, jnp.int32(0))
+        attended = att_ref[...]
+        send("p")
+        send("att")
         unit, r1 = normed(x + (nn(attended, w.out()) + small[3:4]))
         put("n1", unit)
         middle = unit * small[0:1] + small[4:5]
@@ -385,9 +400,15 @@
         put("mid", middle_low)
         wait_all(waits[1])
         back = [None] * (z.groups // 2)
+
+        def pre_of(g):
+            pair = slice((g // 2) * 2 * z.gw, (g // 2 + 1) * 2 * z.gw)
+            return nn(middle_low[:, pair], w.fin(g))
+
+        raw = pre_of(0)
         for g in range(z.groups):
-            pair = slice((g // 2) * 2 * z.gw, (g // 2 + 1) * 2 * z.gw)
-            pre = nn(middle_low[:, pair], w.fin(g)) + small[5 + g : 6 + g]
+            following = pre_of(g + 1) if g + 1 < z.groups else None
+            pre = raw + small[5 + g : 6 + g]
             half = 0.5 + 0.5 * lax.erf(pre * math.sqrt(0.5))
             slope = half + pre * (jnp.exp(-0.5 * pre * pre) * (1.0 / math.sqrt(2.0 * math.pi)))
             active = (pre * half).astype(BF16)
@@ -395,6 +416,7 @@
             put("slope", slope, g)
             added = nn(active, w.fout(g))
             back[g // 2] = added if back[g // 2] is None else back[g // 2] + added
+            raw = following
         unit, r2 = normed(middle + (jnp.concatenate(back, axis=1) + small[9:10]))
         put("n2", unit)
         put("out", unit * small[1:2] + small[10:11])
@@ -442,7 +464,7 @@
         waits = pieces.start(piece_refs, w_ref, sems, (1,))
         w = Weights(z, w_ref)
         dy = loads["dy"][...].astype(F32)
-        n2 = loads["n2"][...]
+        n2 = loads["n2"][...].astype(F32)
         scale = loads["stats"][:, 2:3]
         small = loads["small"][...]
         gain_two, shift_two = col_sum(dy * n2), col_sum(dy)
@@ -454,21 +476,30 @@
         wait_all(waits[1])
         pre_shift = []
         pair_back = [None] * (z.groups // 2)
+        wide = 2 * z.gw
+
+        def act_grad(g):
+            p = g // 2
+            return nt(d_ffn[:, p * wide : (p + 1) * wide], w.fout(g))
+
+        raw = act_grad(0)
         for p in range(z.groups // 2):
-            lanes = slice(p * 2 * z.gw, (p + 1) * 2 * z.gw)
+            lanes = slice(p * wide, (p + 1) * wide)
             out_pair = d_ffn[:, lanes]
             back_pair = []
             for g in (2 * p, 2 * p + 1):
-                d_pre = (nt(out_pair, w.fout(g)) * slope[g].astype(F32)).astype(BF16)
+                following = act_grad(g + 1) if g + 1 < z.groups else None
+                d_pre = (raw * slope[g].astype(F32)).astype(BF16)
                 pre_shift.append(col_sum(d_pre.astype(F32)))
                 back_pair.append(tn(act[g], out_pair))
                 grad_in = nn(middle_t[g * z.gw : (g + 1) * z.gw], d_pre)
                 g_ref[0, :, g * z.gi : (g + 1) * z.gi, :] = grad_in.astype(BF16).reshape(z.shards, z.gi, d)
                 added = nt(d_pre, w.fin(g))
                 pair_back[p] = added if pair_back[p] is None else pair_back[p] + added
+                raw = following
             odd = iota(back_pair[0].shape, 1) >= z.gw
             both = jnp.where(odd, back_pair[1], back_pair[0]).astype(BF16)
-            g_ref[1, :, :, lanes] = both.reshape(z.shards, z.part, 2 * z.gw)
+            g_ref[1, :, :, lanes] = both.reshape(z.shards, z.part, wide)
         copies = send_halves(z, g_ref, keep_ref, send_ref, out_sems)
         dm_ref[...] = d_final + jnp.concatenate(pair_back, axis=1)
         blank = jnp.zeros((1, d), F32)
@@ -496,7 +527,7 @@
     head = d // HEADS
     keys = ["n1", "stats", "small", "att", "q", "k", "v", "p", "x"] + (["n0"] if first else [])
     loads = Loads({"dm": d_middle, **{key: state[key] for key in keys}, "grads": small_in, **({"seg": seg_row} if first else {})})
-    rows = z.part + (2 * z.extra if first else 0)
+    rows = z.part + (z.extra if first else 0)
     outs = [like((seq, d), F32), like((seq, d), BF16)] + [like((z.shards, rows, d), BF16)] * 2
     blocks = 2 * lax.axis_size("dp")
     if first:
@@ -512,7 +543,7 @@
         waits = pieces.start(piece_refs, w_ref, sems, (0,))
         w = Weights(z, w_ref)
         d_middle = loads["dm"][...]
-        n1 = loads["n1"][...]
+        n1 = loads["n1"][...].astype(F32)
         stats = loads["stats"][...]
         r0, r1 = stats[:, 0:1], stats[:, 1:2]
         small = loads["small"][...]
@@ -526,44 +557,49 @@
         second = iota((seq, 128), 1) >= head
         scale = 1.0 / math.sqrt(head)
         q_ref, k_ref, v_ref, p_ref = (loads[key] for key in ("q", "k", "v", "p"))
+        units = [(t, j) for t in range(d // 128) for j in range(2)]
+
+        def probs_grad(unit):
+            t, j = unit
+            lanes = slice(t * 128, (t + 1) * 128)
+            a_j = jnp.where(second == (j == 1), d_att[:, lanes], jnp.zeros((seq, 128), BF16))
+            return nt(a_j, v_ref[:, lanes])
+
         dq, dk, dv = [], [], []
-        for t in range(d // 128):
+        raw = probs_grad(units[0])
+        for n, (t, j) in enumerate(units):
+            following = probs_grad(units[n + 1]) if n + 1 < len(units) else None
             lanes = slice(t * 128, (t + 1) * 128)
-            q_t, k_t, v_t, a_t = q_ref[:, lanes], k_ref[:, lanes], v_ref[:, lanes], d_att[:, lanes]
-            parts = []
-            for j in range(2):
-                a_j = jnp.where(second == (j == 1), a_t, jnp.zeros_like(a_t))
-                probs_low = p_ref[2 * t + j]
-                probs = probs_low.astype(F32)
-                d_probs = nt(a_j, v_t)
-                inner = jnp.sum(probs * d_probs, axis=-1, keepdims=True)
-                d_scores = (probs * (d_probs - inner)).astype(BF16)
-                parts.append((nn(d_scores, k_t), tn(d_scores, q_t), tn(probs_low, a_t)))
-            dq.append((jnp.where(second, parts[1][0], parts[0][0]) * scale).astype(BF16))
-            dk.append(jnp.where(second, parts[1][1], parts[0][1]).astype(BF16))
-            dv.append(jnp.where(second, parts[1][2], parts[0][2]).astype(BF16))
+            probs_low = p_ref[n]
+            probs = probs_low.astype(F32)
+            inner = jnp.sum(probs * raw, axis=-1, keepdims=True)
+            d_scores = (probs * (raw - inner)).astype(BF16)
+            result = (nn(d_scores, k_ref[:, lanes]), tn(d_scores, q_ref[:, lanes]), tn(probs_low, d_att[:, lanes]))
+            if j == 0:
+                kept = result
+            else:
+                dq.append((jnp.where(second, result[0], kept[0]) * scale).astype(BF16))
+                dk.append(jnp.where(second, result[1], kept[1]).astype(BF16))
+                dv.append(jnp.where(second, result[2], kept[2]).astype(BF16))
+            raw = following
         value_shift = col_sum(jnp.concatenate(dv, axis=1).astype(F32))
         x_t = loads["x"][...].T
-        d_in = d_mid
+        d_in = [d_mid[:, : 2 * z.gw], d_mid[:, 2 * z.gw :]]
+        high = iota((z.gw, 2 * z.gw), 1) >= z.gw
         for c, parts in enumerate((dq, dk, dv)):
             d_c = jnp.concatenate(parts, axis=1)
-            full = nn(x_t, d_c)
-            lane = group_of(iota((z.gw, d), 1), z.gw, z.groups)
-            grad = full[0 : z.gw]
-            for g in range(1, z.groups):
-                grad = jnp.where(lane == g, full[g * z.gw : (g + 1) * z.gw], grad)
-            g_ref[1, :, c * z.gi : (c + 1) * z.gi, :] = grad.astype(BF16).reshape(z.shards, z.gi, d)
-            d_in = d_in + nt(d_c, w.proj(c))
+            for p in range(z.groups // 2):
+                lanes = slice(2 * p * z.gw, 2 * (p + 1) * z.gw)
+                full = nn(x_t[lanes], d_c[:, lanes])
+                grad = jnp.where(high, full[z.gw :], full[: z.gw]).astype(BF16)
+                g_ref[1, :, c * z.gi : (c + 1) * z.gi, lanes] = grad.reshape(z.shards, z.gi, 2 * z.gw)
+                d_in[p] = d_in[p] + nt(d_c[:, lanes], w.proj(c, p))
+        d_in = jnp.concatenate(d_in, axis=1)
         blank = jnp.zeros((1, d), F32)
-        small_grads = jnp.concatenate([gain_one, blank, value_shift, branch_shift, shift_one, jnp.zeros((11, d), F32)], axis=0)
-        small_grads = (small_grads + loads["grads"][...]).astype(BF16)
-        spare = jnp.zeros((z.part - z.at_small - 16, d), BF16)
-        for h in range(z.shards):
-            g_ref[1, h, z.at_small : z.at_small + 16, :] = small_grads
-            g_ref[1, h, z.at_small + 16 : z.part, :] = spare
+        embed_grads = [blank, blank]
         if first:
-            n0 = loads["n0"][...]
-            embed_grads = jnp.concatenate([col_sum(d_in * n0), col_sum(d_in), jnp.zeros((14, d), F32)], axis=0).astype(BF16)
+            n0 = loads["n0"][...].astype(F32)
+            embed_grads = [col_sum(d_in * n0), col_sum(d_in)]
             d_embed = norm_back(d_in, n0, r0, small[11:12])
             d_embed_t = d_embed.T
             bits = blocks.bit_length() - 1
@@ -578,13 +614,19 @@
             place = jnp.sum(jnp.where(same & later, 1.0, 0.0), axis=0, keepdims=True).astype(jnp.int32)
             spot = (iota((pos_rows, seq), 0) == place).astype(BF16)
             pos_grad = nn(spot, d_embed.astype(BF16)).astype(BF16)
-            for side in range(2):
-                for h in range(z.shards):
-                    for y in range(2):
-                        row = z.part + y * z.extra
-                        part = pos_grad[(2 * side + y) * z.pos : (2 * side + y + 1) * z.pos]
-                        g_ref[side, h, row : row + z.pos, :] = part if h == 0 else jnp.zeros_like(part)
-                        g_ref[side, h, row + z.pos : row + z.extra, :] = embed_grads
+        small_grads = jnp.concatenate([gain_one, blank, value_shift, branch_shift, shift_one, jnp.zeros((6, d), F32), *embed_grads, jnp.zeros((3, d), F32)], axis=0)
+        small_grads = (small_grads + loads["grads"][...]).astype(BF16)
+        for h in range(z.shards):
+            g_ref[1, h, z.at_small : z.at_small + 16, :] = small_grads
+            if first and h == 0:
+                g_ref[1, h, z.at_small + 16 : z.part, :] = pos_grad[: z.pos]
+                for side in range(2):
+                    g_ref[side, h, z.part : rows, :] = pos_grad[z.pos + side * z.extra : z.pos + (side + 1) * z.extra]
+            else:
+                g_ref[1, h, z.at_small + 16 : z.part, :] = jnp.zeros((z.pos, d), BF16)
+                if first:
+                    for side in range(2):
+                        g_ref[side, h, z.part : rows, :] = jnp.zeros((z.extra, d), BF16)
         copies = send_halves(z, g_ref, keep_ref, send_ref, out_sems)
         dx_ref[...] = d_in
         low_ref[...] = d_in.astype(BF16)
@@ -795,10 +837,14 @@
     sources, _, seq = pieces[0].shape
     shards = 4
     listed = shards * seq
+    line = lists.shape[1]
     unit = 1 << (vocab - 1).bit_length()
-    ways = 4
-
-    def kernel(d_ref, own_ref, later_ref, before_ref, far_a_ref, far_b_ref, l_ref, o_ref, flat_ref, *acc):
+    ways, each = 4, 4
+    rows = (lists & (unit - 1)).reshape(-1)
+    tokens = ((lists >> (unit.bit_length() - 1)) + listed * jnp.arange(sources, dtype=jnp.int32)[:, None]).reshape(-1)
+    counts = lists[:, listed]
+
+    def kernel(d_ref, own_ref, later_ref, before_ref, far_a_ref, far_b_ref, r_ref, t_ref, n_ref, o_ref, flat_ref, *acc):
         half = sources // 2
         for j in range(sources):
             far = far_a_ref[j] if j < half else far_b_ref[j - half]
@@ -808,27 +854,26 @@
         for ref in acc:
             ref[...] = jnp.zeros(ref.shape, F32)
 
-        def add(ref, j, at):
-            packed = l_ref[j, at]
-            row = packed & (unit - 1)
-            token = lax.shift_right_logical(packed, unit.bit_length() - 1) + j * listed
-            ref[pl.ds(row, 1), :] += flat_ref[pl.ds(token, 1), :]
-
         def source(j, carry):
-            many = l_ref[j, listed]
-            rounds = many // ways
+            many = n_ref[j]
+            rounds = many // (ways * each)
 
             def step(i, carry):
-                for way, ref in enumerate(acc):
-                    add(ref, j, i * ways + way)
+                at = j * line + i * ways * each
+                place = [r_ref[at + n] for n in range(ways * each)]
+                value = [flat_ref[pl.ds(t_ref[at + n], 1), :] for n in range(ways * each)]
+                for n in range(each):
+                    old = [ref[pl.ds(place[n * ways + way], 1), :] for way, ref in enumerate(acc)]
+                    for way, ref in enumerate(acc):
+                        ref[pl.ds(place[n * ways + way], 1), :] = old[way] + value[n * ways + way]
                 return carry
 
             def rest(at, carry):
-                add(acc[0], j, at)
+                acc[0][pl.ds(r_ref[j * line + at], 1), :] += flat_ref[pl.ds(t_ref[j * line + at], 1), :]
                 return carry
 
             lax.fori_loop(0, rounds, step, jnp.int32(0))
-            lax.fori_loop(rounds * ways, many, rest, jnp.int32(0))
+            lax.fori_loop(rounds * ways * each, many, rest, jnp.int32(0))
             return carry
 
         lax.fori_loop(0, sources, source, jnp.int32(0))
@@ -838,8 +883,8 @@
     return call(
         kernel,
         [like((width, vocab), F32)],
-        (dense, *pieces, lists),
-        specs=[None] * 6 + [smem],
+        (dense, *pieces, rows, tokens, counts),
+        specs=[None] * 6 + [smem] * 3,
         scratch=[pltpu.VMEM((sources * listed, width), F32)] + [pltpu.VMEM((vocab, width), F32)] * ways,
         limit=60,
         name="table_grad",
@@ -847,7 +892,8 @@
 
 
 def unpack_grads(z, own, other):
-    rows = z.rows + 2 * z.extra
+    rows = z.rows + z.extra
+    pos_rows = z.pos + 2 * z.extra
 
     def kernel(own_ref, other_ref, qkv_ref, out_ref, fin_ref, fout_ref, gain_ref, bias_ref, pos_ref, eg_ref, es_ref, all_ref):
         core = side_of(1)
@@ -873,12 +919,11 @@
         small = own_lanes(all_ref[1, z.at_small : z.at_small + 16].astype(F32))
         gain_ref[...] = small[0:2]
         bias_ref[...] = small[2:11]
-        for n in range(4):
-            row = z.rows + (n % 2) * z.extra
-            pos_ref[n * z.pos : (n + 1) * z.pos] = all_ref[n // 2, row : row + z.pos].astype(F32)
-        small = own_lanes(all_ref[0, z.rows + z.pos : z.rows + z.extra].astype(F32))
-        eg_ref[...] = small[0:1]
-        es_ref[...] = small[1:2]
+        eg_ref[...] = small[11:12]
+        es_ref[...] = small[12:13]
+        pos_ref[: z.pos] = all_ref[1, z.at_small + 16 : z.part].astype(F32)
+        for side in range(2):
+            pos_ref[z.pos + side * z.extra : z.pos + (side + 1) * z.extra] = all_ref[side, z.rows :].astype(F32)
 
     return call(
         kernel,
@@ -889,7 +934,7 @@
             like((z.groups, z.part, z.gw), F32),
             like((2, z.part), F32),
             like((9, z.part), F32),
-            like((4 * z.pos, z.d), F32),
+            like((pos_rows, z.d), F32),
             like((1, z.part), F32),
             like((1, z.part), F32),
         ],
@@ -1017,20 +1062,24 @@
     sum_one = sum(after(second_one, (sum_two, lists, came_in)))
     columns = after(columns, sum_one)
     ring_columns = gather_first(columns, "shard")
-    high = z.part + 2 * z.extra
+    high = z.part + z.extra
     extra = sum_one[z.part : high]
     layer_one = jnp.concatenate([sum_one[: z.part], sum_one[high:]], axis=0)
-    total = jnp.concatenate([jnp.where(first, layer_one, sum_two), extra], axis=0)
-    total = total + crossed(jnp.concatenate([jnp.where(first, sum_two, layer_one), extra], axis=0), "section", 1)
+    row = jnp.arange(z.rows)[:, None]
+    embed_rows = (row >= z.at_small + 11) & (row < z.part) & (side_of(1) == 1)
+    layer_two = jnp.where(embed_rows, layer_one, sum_two)
+    total = jnp.concatenate([jnp.where(first, layer_one, layer_two), extra], axis=0)
+    total = total + crossed(jnp.concatenate([jnp.where(first, layer_two, layer_one), extra], axis=0), "section", 1)
     total, ring_columns = after((total, ring_columns), ())
     far_columns = gather_second(*ring_columns, "shard")
+    word_grad = table_grad(dense, (columns, ring_columns[1], ring_columns[0], *far_columns), lists, vocab)
     bit = 2
     while bit < dp:
-        total = total + after(crossed(total, "dp", bit), far_columns)
+        total = total + after(crossed(total, "dp", bit), word_grad)
         bit *= 2
     unpacked = unpack_grads(z, total, crossed(total, "dp", 1))
 
-    word_grad = table_grad(dense, (columns, ring_columns[1], ring_columns[0], *far_columns), lists, vocab).T
+    word_grad = word_grad.T
 
     def by_micro(own, came):
         return jnp.stack([jnp.where(first, own, came), jnp.where(first, came, own)]).reshape(1, micro, 1, seq, d)

time: 446 us -> 432 us (0.969)
  Pallas kernels: 189 us -> 179 us
  waiting for transfers between devices: 115 us -> 105 us
    ppermute x28, waiting for transfers between devices: 63.2 us -> 52.5 us  [turned(): lax.ppermute(block, axis, [(i, (i + by) % size) for i in range(size)])]
    pallas_call x19, Pallas kernels: 189 us -> 179 us  [call(): pl.pallas_call(kernel, out_shape=outs, in_specs=[vmem if s is None else s...]
  transfers between devices with their start and end apart: 60 -> 60, of which waited for: 22 -> 20; matrix products, arithmetic and copies ran while one was open for 10% -> 11% of each run, Pallas kernels for 33% -> 35%
where the time goes in v4:
time: 432 us; the launch traced here: 426 us
  Pallas kernels  179 us (41%)
  waiting for transfers between devices  105 us (24%)
  starting transfers between devices  64.2 us (15%)
  local copies, waits for them, and re-layouts  49.5 us (11%)
  between operations  15.5 us (4%)
  other arithmetic  12.2 us (3%)
    pallas_call x19, Pallas kernels, call(): pl.pallas_call(kernel, out_shape=outs, in_specs=[vmem if s is None else s...  179 us
    ppermute x28, waiting for transfers between devices, turned(): lax.ppermute(block, axis, [(i, (i + by) % size) for i in range(size)])  52.5 us
    ppermute x30, waiting for transfers between devices, crossed(): lax.ppermute(block, axis, [(i, i ^ bit) for i in range(lax.axis_size(axis...  49.7 us
    ppermute x28, starting transfers between devices, turned(): lax.ppermute(block, axis, [(i, (i + by) % size) for i in range(size)])  44.6 us
    gather x2, local copies, waits for them, and re-layouts, rows_of(): word_table.at[jnp.clip(ids.reshape(-1) - offset, 0, vocab - 1)]  22.8 us
    ppermute x30, starting transfers between devices, crossed(): lax.ppermute(block, axis, [(i, i ^ bit) for i in range(lax.axis_size(axis...  19.5 us
    unnamed x127, local copies, waits for them, and re-layouts  12.2 us
  transfers between devices with their start and end apart: 60, of which 20 were waited for; matrix products, arithmetic and copies ran while one was open for 11% of the time, Pallas kernels for 35%

profile of v4, /device:TPU:0, one launch (start us, length us, event | category | flops | bytes accessed | tf_op | source)
XLA Modules:
  0.0 426.1 jit_solution(4461313622987426358)
XLA Ops:
  8.0 5.1 %collective-permute-start.2 = (s32[3,256]{1,0:T(4,128)S(1)}, s32[3,256]{1,0:T(4,128)S(1)}, u32[]{:S(2)}, u32[]{:S(2)}) collective-permute-start(s32[3,256]{1,0:T(4,128)S(1)} %bitcast.71), channel_id=1, source_target_pairs={{0,3},{1,0},{2,1},{3,2},{4,7},{5,4},{6,5},{7,6},{8,11},{9,8},{10,9... | collective-permute-start | bytes 9224 | tf_op jit(solution)/shard_map/ppermute | solution.py:84
  25.5 11.4 %gather_fusion = bf16[1024,768]{1,0:T(8,128)(2,1)} fusion(bf16[7632,768]{1,0:T(8,128)(2,1)} %refs_5_.1, s32[1024]{0:T(1024)S(1)} %broadcast_clamp_fusion.1), kind=kCustom, calls=%fused_computation | custom fusion | bytes 3149824 | tf_op jit(solution)/shard_map/gather | solution.py:964
  36.9 3.8 embed_parts.1
  46.1 11.4 %gather_fusion.1 = bf16[1024,768]{1,0:T(8,128)(2,1)} fusion(bf16[7632,768]{1,0:T(8,128)(2,1)} %refs_5_.1, s32[1024]{0:T(1024)S(1)} %broadcast_clamp_fusion), kind=kCustom, calls=%fused_computation.1 | custom fusion | bytes 3149824 | tf_op jit(solution)/shard_map/gather | solution.py:964
  66.8 4.3 %collective-permute-done.16.refs_12_ = bf16[192,768]{1,0:T(8,128)(2,1)S(1)} collective-permute-done((bf16[192,768]{1,0:T(8,128)(2,1)S(1)}, bf16[192,768]{1,0:T(8,128)(2,1)S(1)}, u32[]{:S(2)}, u32[]{:S(2)}) %collective-permute-start.16) | collective-permute-done | bytes 294944 | tf_op jit(solution)/shard_map/ppermute | solution.py:88
  72.4 3.9 collective-permute-done.23.refs_22_
  76.3 7.8 %collective-permute-done.22.refs_21_ = bf16[256,768]{1,0:T(8,128)(2,1)S(1)} collective-permute-done((bf16[256,768]{1,0:T(8,128)(2,1)S(1)}, bf16[256,768]{1,0:T(8,128)(2,1)S(1)}, u32[]{:S(2)}, u32[]{:S(2)}) %collective-permute-start.22) | collective-permute-done | bytes 393248 | tf_op jit(solution)/shard_map/ppermute | solution.py:84
  94.2 12.2 %layer_first.1 = (bf16[256,768]{1,0:T(8,128)(2,1)}, bf16[256,768]{1,0:T(8,128)(2,1)}, bf16[256,768]{1,0:T(8,128)(2,1)}, bf16[12,256,256]{2,1,0:T(8,128)(2,1)}, b...) custom-call(bf16[2,2,192,768]{3,2,1,0:T(8,128)(2,1)} %get-tuple-elem, ...), custom_call_target="tpu_custom_call" | custom-call | tf_op jit(solution)/shard_map/layer_first/pallas_call | solution.py:65
  106.4 11.9 %layer_second.1 = (bf16[256,768]{1,0:T(8,128)(2,1)}, bf16[256,768]{1,0:T(8,128)(2,1)}, bf16[256,768]{1,0:T(8,128)(2,1)}, bf16[12,256,256]{2,1,0:T(8,128)(2,1)}, ...) custom-call(bf16[2,2,192,768]{3,2,1,0:T(8,128)(2,1)} %get-tuple-elem, ...), custom_call_target="tpu_custom_call" | custom-call | tf_op jit(solution)/shard_map/layer_second/pallas_call | solution.py:65
  123.3 11.0 %head_forward.4 = (f32[256,768]{1,0:T(8,128)}, f32[8,256]{1,0:T(8,128)}) custom-call(bf16[256,768]{1,0:T(8,128)(2,1)} %get-tuple-element.158.refs_0_, bf16[7632,768]{1,0:T(8,128)(2,1)} %refs_5_.1), custom_call_target="tpu_custom_call" | custom-call | tf_op jit(solution)/shard_map/head_forward/pallas_call | solution.py:65
  136.6 10.9 %head_forward.5 = (f32[256,768]{1,0:T(8,128)}, f32[8,256]{1,0:T(8,128)}) custom-call(bf16[256,768]{1,0:T(8,128)(2,1)} %copy-done.20, bf16[7632,768]{1,0:T(8,128)(2,1)} %refs_5_.1), custom_call_target="tpu_custom_call" | custom-call | tf_op jit(solution)/shard_map/head_forward/pallas_call | solution.py:65
  151.9 10.9 %head_forward.6 = (f32[256,768]{1,0:T(8,128)}, f32[8,256]{1,0:T(8,128)}) custom-call(bf16[256,768]{1,0:T(8,128)(2,1)} %copy-done.21, bf16[7632,768]{1,0:T(8,128)(2,1)} %refs_5_.1), custom_call_target="tpu_custom_call" | custom-call | tf_op jit(solution)/shard_map/head_forward/pallas_call | solution.py:65
  165.0 10.9 %head_forward.7 = (f32[256,768]{1,0:T(8,128)}, f32[8,256]{1,0:T(8,128)}) custom-call(bf16[128,768]{1,0:T(8,128)(2,1)} %copy-done.30, bf16[128,768]{1,0:T(8,128)(2,1)} %copy-done.29, bf16[7632,768]{1,0:T(8,128)(2,1)} %refs_5_.1), custom_call_target="tpu_custom_call" | custom-call | tf_op jit(solution)/shard_map/head_forward/pallas_call | solution.py:65
  179.8 5.2 %list_tokens.1 = s32[1,1152]{1,0:T(1,128)} custom-call(s32[1,1024]{1,0:T(1,128)} %bitcast.79), custom_call_target="tpu_custom_call" | custom-call | tf_op jit(solution)/shard_map/list_tokens/pallas_call | solution.py:65
  185.7 4.6 %head_combine.1 = (bf16[1024,768]{1,0:T(8,128)(2,1)}, f32[1024,1]{1,0:T(8,128)}) custom-call(f32[256,768]{1,0:T(8,128)} %get-tuple-element.159.x0_ref, f32[256,768]{1,0:T(8,128)} %get-tuple-element.163.x1_ref, f32[256,768]{1,0:T(8,128)} %get-tuple-element.166.x2_ref, f32[256,768]{1,0:T(8,128)} %get-tuple-element.161.x3_ref, bf16[1024,768]{1,0:T(8,128)(2,1)} %gather_fusion.1, ...), custom_call_target="tpu_custom_call" | custom-call | tf_op jit(solution)/shard_map/head_combine/pallas_call | solution.py:65
  190.4 31.3 %head_table.1 = bf16[768,7632]{1,0:T(8,128)(2,1)} custom-call(bf16[256,768]{1,0:T(8,128)(2,1)} %get-tuple-element.158.refs_0_, bf16[256,768]{1,0:T(8,128)(2,1)} %copy-done.21, bf16[128,768]{1,0:T(8,128)(2,1)} %copy-done.30, bf16[128,768]{1,0:T(8,128)(2,1)} %copy-done.29, bf16[256,768]{1,0:T(8,128)(2,1)} %copy-done.20, bf16[7632,768]{1,0:T(8,128)(2,1)} %refs_5_.1, ...), custom_call_target="tpu_custom_call" | custom-call | tf_op jit(solution)/shard_map/head_table/pallas_call | solution.py:65
  224.9 8.1 %ffn_back.2 = (f32[256,768]{1,0:T(8,128)}, f32[16,768]{1,0:T(8,128)}, bf16[4,192,768]{2,1,0:T(8,128)(2,1)}, bf16[4,192,768]{2,1,0:T(8,128)(2,1)}) custom-call(bf16[2,2,192,768]{3,2,1,0:T(8,128)(2,1)} %get-tuple-element.141.refs_0_, bf16[384,768]{1,0:T(8,128)(2,1)} %copy-done.2, bf16[192,768]{1,0:T(8,128)(2,1)} %copy-done.9, bf16[384,768]{1,0:T(8,128)(2,1)} %copy-done.5, ...), custom_call_target="tpu_custom_call" | custom-call | tf_op jit(solution)/shard_map/ffn_back/pallas_call | solution.py:65
  233.0 11.4 %att_back.2 = (f32[256,768]{1,0:T(8,128)}, bf16[256,768]{1,0:T(8,128)(2,1)}, bf16[4,192,768]{2,1,0:T(8,128)(2,1)}, bf16[4,192,768]{2,1,0:T(8,128)(2,1)}) custom-call(bf16[2,2,192,768]{3,2,1,0:T(8,128)(2,1)} %get-tuple-element.141.refs_0_, bf16[384,768]{1,0:T(8,128)(2,1)} %copy-done.2, bf16[192,768]{1,0:T(8,128)(2,1)} %copy-done.9, ...), custom_call_target="tpu_custom_call" | custom-call | tf_op jit(solution)/shard_map/att_back/pallas_call | solution.py:65
  245.0 8.8 %ffn_back.3 = (f32[256,768]{1,0:T(8,128)}, f32[16,768]{1,0:T(8,128)}, bf16[4,192,768]{2,1,0:T(8,128)(2,1)}, bf16[4,192,768]{2,1,0:T(8,128)(2,1)}) custom-call(bf16[2,2,192,768]{3,2,1,0:T(8,128)(2,1)} %get-tuple-element.141.refs_0_, bf16[384,768]{1,0:T(8,128)(2,1)} %copy-done.2, bf16[192,768]{1,0:T(8,128)(2,1)} %copy-done.9, bf16[384,768]{1,0:T(8,128)(2,1)} %copy-done.5, ...), custom_call_target="tpu_custom_call" | custom-call | tf_op jit(solution)/shard_map/ffn_back/pallas_call | solution.py:65
  255.2 4.8 %add_cores_split.2 = (bf16[384,768]{1,0:T(8,128)(2,1)}, bf16[384,768]{1,0:T(8,128)(2,1)}, bf16[192,768]{1,0:T(8,128)(2,1)}, bf16[192,768]{1,0:T(8,128)(2,1)}, bf16[384,768]{1,0:T(8,128)(2,1)}) custom-call(bf16[4,192,768]{2,1,0:T(8,128)(2,1)} %get-tuple-element.205.a_ref, bf16[4,192,768]{2,1,0:T(8,128)(2,1)} %get-tuple-element.206.f_ref, ...), custom_call_target="tpu_custom_call" | custom-call | tf_op jit(solution)/shard_map/add_cores_split/pallas_call | solution.py:65
  263.8 12.3 %att_back.3 = (f32[256,768]{1,0:T(8,128)}, bf16[256,768]{1,0:T(8,128)(2,1)}, bf16[4,240,768]{2,1,0:T(8,128)(2,1)}, bf16[4,240,768]{2,1,0:T(8,128)(2,1)}, bf16[8,96,256]{2,1,0:T(8,128)(2,1)}) custom-call(bf16[2,2,192,768]{3,2,1,0:T(8,128)(2,1)} %get-tuple-element.141.refs_0_, bf16[384,768]{1,0:T(8,128)(2,1)} %copy-done.2, bf16[192,768]{1,0:T(8,128)(2,1)} %copy-done.9, ...), custom_call_target="tpu_custom_call" | custom-call | tf_op jit(solution)/shard_map/att_back/pallas_call | solution.py:65
  279.5 4.6 %collective-permute-done.37 = bf16[1,4,96,256]{3,2,0,1:T(8,128)(2,1)S(1)} collective-permute-done((bf16[1,4,96,256]{3,2,0,1:T(8,128)(2,1)S(1)}, bf16[1,4,96,256]{3,2,0,1:T(8,128)(2,1)S(1)}, u32[]{:S(2)}, u32[]{:S(2)}) %collective-permute-start.37) | collective-permute-done | bytes 196640 | tf_op jit(solution)/shard_map/ppermute | solution.py:88
  287.9 6.4 %collective-permute-done.38 = bf16[2,2,96,256]{3,2,0,1:T(8,128)(2,1)S(1)} collective-permute-done((bf16[2,2,96,256]{3,2,0,1:T(8,128)(2,1)S(1)}, bf16[2,2,96,256]{3,2,0,1:T(8,128)(2,1)S(1)}, u32[]{:S(2)}, u32[]{:S(2)}) %collective-permute-start.38) | collective-permute-done | bytes 196640 | tf_op jit(solution)/shard_map/ppermute | solution.py:88
  295.5 4.1 add_cores_split.3
  301.8 9.8 %collective-permute-done.41 = bf16[4,96,256]{2,1,0:T(8,128)(2,1)} collective-permute-done((bf16[4,96,256]{2,1,0:T(8,128)(2,1)}, bf16[4,96,256]{2,1,0:T(8,128)(2,1)}, u32[]{:S(2)}, u32[]{:S(2)}) %collective-permute-start.41) | collective-permute-done | bytes 196640 | tf_op jit(solution)/shard_map/ppermute | solution.py:88
  320.8 10.9 %collective-permute-done.42 = bf16[208,768]{1,0:T(8,128)(2,1)S(1)} collective-permute-done((bf16[208,768]{1,0:T(8,128)(2,1)}, bf16[208,768]{1,0:T(8,128)(2,1)S(1)}, u32[]{:S(2)}, u32[]{:S(2)}) %collective-permute-start.42) | collective-permute-done | bytes 319520 | tf_op jit(solution)/shard_map/ppermute | solution.py:84
  338.0 8.3 %collective-permute-done.34 = bf16[256,768]{1,0:T(8,128)(2,1)S(1)} collective-permute-done((bf16[256,768]{1,0:T(8,128)(2,1)S(1)}, bf16[256,768]{1,0:T(8,128)(2,1)S(1)}, u32[]{:S(2)}, u32[]{:S(2)}) %collective-permute-start.34) | collective-permute-done | bytes 393248 | tf_op jit(solution)/shard_map/ppermute | solution.py:88
  346.3 5.4 %collective-permute-done.46 = bf16[432,768]{1,0:T(8,128)(2,1)S(1)} collective-permute-done((bf16[432,768]{1,0:T(8,128)(2,1)S(1)}, bf16[432,768]{1,0:T(8,128)(2,1)S(1)}, u32[]{:S(2)}, u32[]{:S(2)}) %collective-permute-start.46) | collective-permute-done | bytes 663584 | tf_op jit(solution)/shard_map/ppermute | solution.py:84
  351.7 11.9 %collective-permute-done.47 = bf16[432,768]{1,0:T(8,128)(2,1)S(1)} collective-permute-done((bf16[432,768]{1,0:T(8,128)(2,1)S(1)}, bf16[432,768]{1,0:T(8,128)(2,1)S(1)}, u32[]{:S(2)}, u32[]{:S(2)}) %collective-permute-start.47) | collective-permute-done | bytes 663584 | tf_op jit(solution)/shard_map/ppermute | solution.py:84
  369.6 10.3 %collective-permute-done.51 = bf16[432,768]{1,0:T(8,128)(2,1)S(1)} collective-permute-done((bf16[432,768]{1,0:T(8,128)(2,1)S(1)}, bf16[432,768]{1,0:T(8,128)(2,1)S(1)}, u32[]{:S(2)}, u32[]{:S(2)}) %collective-permute-start.51) | collective-permute-done | bytes 663584 | tf_op jit(solution)/shard_map/ppermute | solution.py:88
  380.1 5.0 %collective-permute-done.53.later_ref = bf16[8,96,256]{2,1,0:T(8,128)(2,1)S(1)} collective-permute-done((bf16[8,96,256]{2,1,0:T(8,128)(2,1)S(1)}, bf16[8,96,256]{2,1,0:T(8,128)(2,1)S(1)}, u32[]{:S(2)}, u32[]{:S(2)}) %collective-permute-start.53) | collective-permute-done | bytes 393248 | tf_op jit(solution)/shard_map/ppermute | solution.py:84
  398.2 11.2 %table_grad.1 = f32[96,7632]{1,0:T(8,128)} custom-call(bf16[96,7632]{1,0:T(8,128)(2,1)} %reduce-scatter.5.cloned.1.call-done.d_ref, bf16[8,96,256]{2,1,0:T(8,128)(2,1)} %copy-done.22, bf16[8,96,256]{2,1,0:T(8,128)(2,1)} %copy-done.28, bf16[8,96,256]{2,1,0:T(8,128)(2,1)} %copy-done.27, bf16[4,96,256]{2,1,0:T(8,128)(2,1)} %collective-permute-done.54.far_a_ref, ...), custom_call_target="tpu_custom_call" | custom-call | tf_op jit(solution)/shard_map/table_grad/pallas_call | solution.py:65
  (314 shorter events, 120.7 us)
Async XLA Ops:
  7.2 217.7 %reduce-scatter.3.cloned.1.call-start = ((), (), s32[]{:S(2)}) async-start(), calls=%async_computation.2 | async-start | bytes 1966080 | tf_op jit(solution)/shard_map/reduce_scatter | solution.py:1021
  8.0 15.4 %collective-permute-start.2 = (s32[3,256]{1,0:T(4,128)S(1)}, s32[3,256]{1,0:T(4,128)S(1)}, u32[]{:S(2)}, u32[]{:S(2)}) collective-permute-start(s32[3,256]{1,0:T(4,128)S(1)} %bitcast.71), channel_id=1, source_target_pairs={{0,3},{1,0},{2,1},{3,2},{4,7},{5,4},{6,5},{7,6},{8,11},{9,8},{10,9... | collective-permute-start | bytes 9224 | tf_op jit(solution)/shard_map/ppermute | solution.py:84
  19.5 17.4 %collective-permute-start = (bf16[192,768]{1,0:T(8,128)(2,1)}, bf16[192,768]{1,0:T(8,128)(2,1)S(1)}, u32[]{:S(2)}, u32[]{:S(2)}) collective-permute-start(bf16[192,768]{1,0:T(8,128)(2,1)} %get-tuple-element.142), channel_id=1, source_target_pairs={{0,1},{1,2},{2,3},{3,0},{4,5},{5,6},{6,7},{7,4},{8,9},{9,10},{10,1... | collective-permute-start | bytes 884744 | tf_op jit(solution)/shard_map/ppermute | solution.py:84
  22.0 14.9 %collective-permute-start.1 = (bf16[192,768]{1,0:T(8,128)(2,1)}, bf16[192,768]{1,0:T(8,128)(2,1)S(1)}, u32[]{:S(2)}, u32[]{:S(2)}) collective-permute-start(bf16[192,768]{1,0:T(8,128)(2,1)} %get-tuple-element.142), channel_id=1, source_target_pairs={{0,3},{1,0},{2,1},{3,2},{4,7},{5,4},{6,5},{7,6},{8,11},{9,8},{10,9... | collective-permute-start | bytes 884744 | tf_op jit(solution)/shard_map/ppermute | solution.py:84
  23.3 34.2 %collective-permute-start.14 = (bf16[2,192,768]{2,1,0:T(8,128)(2,1)}, bf16[2,192,768]{2,1,0:T(8,128)(2,1)S(1)}, u32[]{:S(2)}, u32[]{:S(2)}) collective-permute-start(bf16[2,192,768]{2,1,0:T(8,128)(2,1)} %get-tuple-element.156), channel_id=1, source_target_pairs={{0,16},{16,0},{1,17},{17,1},{2,18},{18,2},{3,19},{19,3},{4,20},{20... | collective-permute-start | bytes 1769480 | tf_op jit(solution)/shard_map/ppermute | solution.py:88
  40.8 21.4 %collective-permute-start.10 = (bf16[384,768]{1,0:T(8,128)(2,1)S(1)}, bf16[384,768]{1,0:T(8,128)(2,1)S(1)}, u32[]{:S(2)}, u32[]{:S(2)}) collective-permute-start(bf16[384,768]{1,0:T(8,128)(2,1)S(1)} %constant_dynamic-update-slice_fusion.refs_1_), channel_id=1, source_target_pairs={{0,16},{16,0},{1,17},{17,1},{2,18},{18,2},{3,19},{19,3},{4,20},{20... | collective-permute-start | bytes 1769480 | tf_op jit(solution)/shard_map/ppermute | solution.py:88
  41.4 22.9 %collective-permute-start.9 = (bf16[384,768]{1,0:T(8,128)(2,1)S(1)}, bf16[384,768]{1,0:T(8,128)(2,1)S(1)}, u32[]{:S(2)}, u32[]{:S(2)}) collective-permute-start(bf16[384,768]{1,0:T(8,128)(2,1)S(1)} %constant_dynamic-update-slice_fusion.refs_1_), channel_id=1, source_target_pairs={{0,8},{4,12},{8,0},{12,4},{1,9},{5,13},{9,1},{13,5},{2,10},{6,14},... | collective-permute-start | bytes 1769480 | tf_op jit(solution)/shard_map/ppermute | solution.py:88
  43.0 16.7 %collective-permute-start.6 = (bf16[224,768]{1,0:T(8,128)(2,1)S(1)}, bf16[224,768]{1,0:T(8,128)(2,1)}, u32[]{:S(2)}, u32[]{:S(2)}) collective-permute-start(bf16[224,768]{1,0:T(8,128)(2,1)S(1)} %pad_maximum_fusion.14), channel_id=1, source_target_pairs={{0,3},{1,0},{2,1},{3,2},{4,7},{5,4},{6,5},{7,6},{8,11},{9,8},{10,9... | collective-permute-start | bytes 1032200 | tf_op jit(solution)/shard_map/ppermute | solution.py:84
  59.7 25.3 %collective-permute-start.15 = (bf16[2,192,768]{2,1,0:T(8,128)(2,1)S(1)}, bf16[2,192,768]{2,1,0:T(8,128)(2,1)S(1)}, u32[]{:S(2)}, u32[]{:S(2)}) collective-permute-start(bf16[2,192,768]{2,1,0:T(8,128)(2,1)S(1)} %collective-permute-done.14.refs_9_), channel_id=1, source_target_pairs={{0,4},{4,0},{8,12},{12,8},{1,5},{5,1},{9,13},{13,9},{2,6},{6,2},{1... | collective-permute-start | bytes 1769480 | tf_op jit(solution)/shard_map/ppermute | solution.py:88
  62.3 22.5 %collective-permute-start.11 = (bf16[576,768]{1,0:T(8,128)(2,1)S(1)}, bf16[576,768]{1,0:T(8,128)(2,1)S(1)}, u32[]{:S(2)}, u32[]{:S(2)}) collective-permute-start(bf16[576,768]{1,0:T(8,128)(2,1)S(1)} %pad_maximum_fusion), channel_id=1, source_target_pairs={{0,8},{4,12},{8,0},{12,4},{1,9},{5,13},{9,1},{13,5},{2,10},{6,14},... | collective-permute-start | bytes 2654216 | tf_op jit(solution)/shard_map/ppermute | solution.py:88
  71.9 18.7 %collective-permute-start.19 = (bf16[192,768]{1,0:T(8,128)(2,1)S(1)}, bf16[192,768]{1,0:T(8,128)(2,1)}, u32[]{:S(2)}, u32[]{:S(2)}) collective-permute-start(bf16[192,768]{1,0:T(8,128)(2,1)S(1)} %collective-permute-done.16.refs_12_), channel_id=1, source_target_pairs={{0,8},{4,12},{8,0},{12,4},{1,9},{5,13},{9,1},{13,5},{2,10},{6,14},... | collective-permute-start | bytes 884744 | tf_op jit(solution)/shard_map/ppermute | solution.py:88
  76.3 14.3 %collective-permute-start.18 = (bf16[192,768]{1,0:T(8,128)(2,1)S(1)}, bf16[192,768]{1,0:T(8,128)(2,1)S(1)}, u32[]{:S(2)}, u32[]{:S(2)}) collective-permute-start(bf16[192,768]{1,0:T(8,128)(2,1)S(1)} %collective-permute-done.16.refs_12_), channel_id=1, source_target_pairs={{0,4},{4,0},{8,12},{12,8},{1,5},{5,1},{9,13},{13,9},{2,6},{6,2},{1... | collective-permute-start | bytes 884744 | tf_op jit(solution)/shard_map/ppermute | solution.py:88
  118.2 17.6 %collective-permute-start.26 = (bf16[256,768]{1,0:T(8,128)(2,1)}, bf16[256,768]{1,0:T(8,128)(2,1)S(1)}, u32[]{:S(2)}, u32[]{:S(2)}) collective-permute-start(bf16[256,768]{1,0:T(8,128)(2,1)} %get-tuple-element.158.refs_0_), channel_id=1, source_target_pairs={{0,1},{1,2},{2,3},{3,0},{4,5},{5,6},{6,7},{7,4},{8,9},{9,10},{10,1... | collective-permute-start | bytes 1179656 | tf_op jit(solution)/shard_map/ppermute | solution.py:84
  118.9 29.6 %collective-permute-start.25 = (bf16[256,768]{1,0:T(8,128)(2,1)}, bf16[256,768]{1,0:T(8,128)(2,1)S(1)}, u32[]{:S(2)}, u32[]{:S(2)}) collective-permute-start(bf16[256,768]{1,0:T(8,128)(2,1)} %get-tuple-element.158.refs_0_), channel_id=1, source_target_pairs={{0,3},{1,0},{2,1},{3,2},{4,7},{5,4},{6,5},{7,6},{8,11},{9,8},{10,9... | collective-permute-start | bytes 1179656 | tf_op jit(solution)/shard_map/ppermute | solution.py:84
  134.3 50.7 %collective-permute-start.24 = (bf16[256,768]{1,0:T(8,128)(2,1)S(1)}, bf16[256,768]{1,0:T(8,128)(2,1)S(1)}, u32[]{:S(2)}, u32[]{:S(2)}) collective-permute-start(bf16[256,768]{1,0:T(8,128)(2,1)S(1)} %broadcast_select_fusion.1), channel_id=1, source_target_pairs={{0,16},{16,0},{1,17},{17,1},{2,18},{18,2},{3,19},{19,3},{4,20},{20... | collective-permute-start | bytes 1179656 | tf_op jit(solution)/shard_map/ppermute | solution.py:88
  148.5 15.7 %collective-permute-start.28 = (bf16[128,768]{1,0:T(8,128)(2,1)S(1)}, bf16[128,768]{1,0:T(8,128)(2,1)S(1)}, u32[]{:S(2)}, u32[]{:S(2)}) collective-permute-start(bf16[128,768]{1,0:T(8,128)(2,1)S(1)} %slice.155), channel_id=1, source_target_pairs={{0,3},{1,0},{2,1},{3,2},{4,7},{5,4},{6,5},{7,6},{8,11},{9,8},{10,9... | collective-permute-start | bytes 589832 | tf_op jit(solution)/shard_map/ppermute | solution.py:84
  148.6 15.7 %collective-permute-start.27 = (bf16[128,768]{1,0:T(8,128)(2,1)S(1)}, bf16[128,768]{1,0:T(8,128)(2,1)S(1)}, u32[]{:S(2)}, u32[]{:S(2)}) collective-permute-start(bf16[128,768]{1,0:T(8,128)(2,1)S(1)} %slice.154), channel_id=1, source_target_pairs={{0,1},{1,2},{2,3},{3,0},{4,5},{5,6},{6,7},{7,4},{8,9},{9,10},{10,1... | collective-permute-start | bytes 589832 | tf_op jit(solution)/shard_map/ppermute | solution.py:84
  190.3 207.9 %reduce-scatter.5.cloned.1.call-start = ((), (), s32[]{:S(2)}) async-start(), calls=%async_computation.3 | async-start | bytes 13271040 | tf_op jit(solution)/shard_map/reduce_scatter | solution.py:1025
  260.0 16.2 %collective-permute-start.35 = (bf16[192,768]{1,0:T(8,128)(2,1)}, bf16[192,768]{1,0:T(8,128)(2,1)S(1)}, u32[]{:S(2)}, u32[]{:S(2)}) collective-permute-start(bf16[192,768]{1,0:T(8,128)(2,1)} %get-tuple-element.211), channel_id=1, source_target_pairs={{0,1},{1,2},{2,3},{3,0},{4,5},{5,6},{6,7},{7,4},{8,9},{9,10},{10,1... | collective-permute-start | bytes 884744 | tf_op jit(solution)/shard_map/ppermute | solution.py:84
  260.1 16.1 %collective-permute-start.36 = (bf16[192,768]{1,0:T(8,128)(2,1)}, bf16[192,768]{1,0:T(8,128)(2,1)S(1)}, u32[]{:S(2)}, u32[]{:S(2)}) collective-permute-start(bf16[192,768]{1,0:T(8,128)(2,1)} %get-tuple-element.212), channel_id=1, source_target_pairs={{0,3},{1,0},{2,1},{3,2},{4,7},{5,4},{6,5},{7,6},{8,11},{9,8},{10,9... | collective-permute-start | bytes 884744 | tf_op jit(solution)/shard_map/ppermute | solution.py:84
  278.9 15.5 %collective-permute-start.40 = (bf16[4,240,768]{2,1,0:T(8,128)(2,1)S(1)}, bf16[4,240,768]{2,1,0:T(8,128)(2,1)S(1)}, u32[]{:S(2)}, u32[]{:S(2)}) collective-permute-start(bf16[4,240,768]{2,1,0:T(8,128)(2,1)S(1)} %copy-done.58), channel_id=1, source_target_pairs={{0,4},{4,0},{8,12},{12,8},{1,5},{5,1},{9,13},{13,9},{2,6},{6,2},{1... | collective-permute-start | bytes 4423688 | tf_op jit(solution)/shard_map/ppermute | solution.py:88
  285.9 29.5 %collective-permute-start.45 = (bf16[384,768]{1,0:T(8,128)(2,1)S(1)}, bf16[384,768]{1,0:T(8,128)(2,1)S(1)}, u32[]{:S(2)}, u32[]{:S(2)}) collective-permute-start(bf16[384,768]{1,0:T(8,128)(2,1)S(1)} %pad_maximum_fusion.6), channel_id=1, source_target_pairs={{0,3},{1,0},{2,1},{3,2},{4,7},{5,4},{6,5},{7,6},{8,11},{9,8},{10,9... | collective-permute-start | bytes 1769480 | tf_op jit(solution)/shard_map/ppermute | solution.py:84
  287.3 28.1 %collective-permute-start.44 = (bf16[384,768]{1,0:T(8,128)(2,1)}, bf16[384,768]{1,0:T(8,128)(2,1)}, u32[]{:S(2)}, u32[]{:S(2)}) collective-permute-start(bf16[384,768]{1,0:T(8,128)(2,1)} %pad_maximum_fusion.5), channel_id=1, source_target_pairs={{0,1},{1,2},{2,3},{3,0},{4,5},{5,6},{6,7},{7,4},{8,9},{9,10},{10,1... | collective-permute-start | bytes 1769480 | tf_op jit(solution)/shard_map/ppermute | solution.py:84
  312.7 19.0 %collective-permute-start.43 = (bf16[224,768]{1,0:T(8,128)(2,1)}, bf16[224,768]{1,0:T(8,128)(2,1)S(1)}, u32[]{:S(2)}, u32[]{:S(2)}) collective-permute-start(bf16[224,768]{1,0:T(8,128)(2,1)} %get-tuple-element.241), channel_id=1, source_target_pairs={{0,3},{1,0},{2,1},{3,2},{4,7},{5,4},{6,5},{7,6},{8,11},{9,8},{10,9... | collective-permute-start | bytes 1032200 | tf_op jit(solution)/shard_map/ppermute | solution.py:84
  315.3 16.4 %collective-permute-start.42 = (bf16[208,768]{1,0:T(8,128)(2,1)}, bf16[208,768]{1,0:T(8,128)(2,1)S(1)}, u32[]{:S(2)}, u32[]{:S(2)}) collective-permute-start(bf16[208,768]{1,0:T(8,128)(2,1)} %get-tuple-element.240), channel_id=1, source_target_pairs={{0,1},{1,2},{2,3},{3,0},{4,5},{5,6},{6,7},{7,4},{8,9},{9,10},{10,1... | collective-permute-start | bytes 958472 | tf_op jit(solution)/shard_map/ppermute | solution.py:84
  319.3 18.7 %collective-permute-start.50 = (s32[4,1152]{1,0:T(4,128)S(1)}, s32[4,1152]{1,0:T(4,128)S(1)}, u32[]{:S(2)}, u32[]{:S(2)}) collective-permute-start(s32[4,1152]{1,0:T(4,128)S(1)} %pad_add_fusion.1), channel_id=1, source_target_pairs={{0,16},{16,0},{1,17},{17,1},{2,18},{18,2},{3,19},{19,3},{4,20},{20... | collective-permute-start | bytes 55304 | tf_op jit(solution)/shard_map/ppermute | solution.py:88
  332.0 19.7 %collective-permute-start.46 = (bf16[432,768]{1,0:T(8,128)(2,1)S(1)}, bf16[432,768]{1,0:T(8,128)(2,1)S(1)}, u32[]{:S(2)}, u32[]{:S(2)}) collective-permute-start(bf16[432,768]{1,0:T(8,128)(2,1)S(1)} %pad_maximum_fusion.3), channel_id=1, source_target_pairs={{0,1},{1,2},{2,3},{3,0},{4,5},{5,6},{6,7},{7,4},{8,9},{9,10},{10,1... | collective-permute-start | bytes 1990664 | tf_op jit(solution)/shard_map/ppermute | solution.py:84
  333.1 30.4 %collective-permute-start.47 = (bf16[432,768]{1,0:T(8,128)(2,1)S(1)}, bf16[432,768]{1,0:T(8,128)(2,1)S(1)}, u32[]{:S(2)}, u32[]{:S(2)}) collective-permute-start(bf16[432,768]{1,0:T(8,128)(2,1)S(1)} %pad_maximum_fusion.4), channel_id=1, source_target_pairs={{0,3},{1,0},{2,1},{3,2},{4,7},{5,4},{6,5},{7,6},{8,11},{9,8},{10,9... | collective-permute-start | bytes 1990664 | tf_op jit(solution)/shard_map/ppermute | solution.py:84
  364.1 15.8 %collective-permute-start.51 = (bf16[432,768]{1,0:T(8,128)(2,1)S(1)}, bf16[432,768]{1,0:T(8,128)(2,1)S(1)}, u32[]{:S(2)}, u32[]{:S(2)}) collective-permute-start(bf16[432,768]{1,0:T(8,128)(2,1)S(1)} %pad_maximum_fusion.1), channel_id=1, source_target_pairs={{0,16},{16,0},{1,17},{17,1},{2,18},{18,2},{3,19},{19,3},{4,20},{20... | collective-permute-start | bytes 1990664 | tf_op jit(solution)/shard_map/ppermute | solution.py:88
  365.5 14.5 %collective-permute-start.52 = (bf16[8,96,256]{2,1,0:T(8,128)(2,1)S(1)}, bf16[8,96,256]{2,1,0:T(8,128)(2,1)S(1)}, u32[]{:S(2)}, u32[]{:S(2)}) collective-permute-start(bf16[8,96,256]{2,1,0:T(8,128)(2,1)S(1)} %pad_maximum_fusion.12.own_ref), channel_id=1, source_target_pairs={{0,1},{1,2},{2,3},{3,0},{4,5},{5,6},{6,7},{7,4},{8,9},{9,10},{10,1... | collective-permute-start | bytes 1179656 | tf_op jit(solution)/shard_map/ppermute | solution.py:84
  367.0 18.0 %collective-permute-start.53 = (bf16[8,96,256]{2,1,0:T(8,128)(2,1)S(1)}, bf16[8,96,256]{2,1,0:T(8,128)(2,1)S(1)}, u32[]{:S(2)}, u32[]{:S(2)}) collective-permute-start(bf16[8,96,256]{2,1,0:T(8,128)(2,1)S(1)} %pad_maximum_fusion.12.own_ref), channel_id=1, source_target_pairs={{0,3},{1,0},{2,1},{3,2},{4,7},{5,4},{6,5},{7,6},{8,11},{9,8},{10,9... | collective-permute-start | bytes 1179656 | tf_op jit(solution)/shard_map/ppermute | solution.py:84
  385.0 24.4 %collective-permute-start.56 = (bf16[432,768]{1,0:T(8,128)(2,1)S(1)}, bf16[432,768]{1,0:T(8,128)(2,1)}, u32[]{:S(2)}, u32[]{:S(2)}) collective-permute-start(bf16[432,768]{1,0:T(8,128)(2,1)S(1)} %fusion.2), channel_id=1, source_target_pairs={{0,8},{4,12},{8,0},{12,4},{1,9},{5,13},{9,1},{13,5},{2,10},{6,14},... | collective-permute-start | bytes 1990664 | tf_op jit(solution)/shard_map/ppermute | solution.py:88
  (89 other events, 753.4 us)
Sparse Core Ops, SparseCore 0:
  190.4 34.4 reduce-scatter.2
  228.4 96.5 reduce-scatter.4

commit v5 on v4

--- a/solution.py
+++ b/solution.py
@@ -69,7 +69,7 @@
         out_specs=out_specs if out_specs is not None else [vmem] * len(outs),
         scratch_shapes=list(scratch),
         compiler_params=pltpu.CompilerParams(vmem_limit_bytes=limit * MIB),
-        cost_estimate=pl.CostEstimate(flops=0, bytes_accessed=0, transcendentals=0),
+        cost_estimate=pl.CostEstimate(flops=flops, bytes_accessed=0, transcendentals=0),
         name=name,
         **extra,
     )(*ins)
@@ -104,6 +104,10 @@
 
 def side_of(bit):
     return (lax.axis_index("dp") // bit) % 2
+
+
+def direct_scatter(parts, axis):
+    return parts[0], turned(parts[1], axis, 1), turned(parts[3], axis, -1), turned(parts[2], axis, 2)
 
 
 def gather_first(block, axis):
@@ -129,7 +133,8 @@
         self.at_small = 3 * part
         self.rows = 2 * self.part
         self.pos = self.part - self.at_small - 16
-        self.extra = (pos_rows - self.pos) // 2
+        self.quarter = (pos_rows - self.pos) // 4
+        self.extra = -(-self.quarter // 16) * 16
 
 
 def pack_weights(z, qkv, out, fin, fout, small):
@@ -325,7 +330,7 @@
                 (c0, c1, None, c3)[k][...] = total
 
     full, part = like((seq, width), BF16), like((half, width), BF16)
-    return call(kernel, [full, full, part, part, full], (picked, ids_by, pos_table), moved=4 * MIB, name="embed_parts")
+    return call(kernel, [full, full, part, part, full], (picked, ids_by, pos_table), name="embed_parts")
 
 
 def layer_forward(z, pieces, seg_row, first, words=None, layer_in=None):
@@ -431,8 +436,7 @@
         specs=pieces.specs + [None] * (1 + len(inputs)),
         out_specs=stores.specs,
         scratch=pieces.scratch + stores.scratch,
-        flops=3 * 10**9,
-        moved=16 * MIB,
+        flops=12 * 10**9,
         name="layer_first" if first else "layer_second",
     )
     return dict(zip(stores.names, outs))
@@ -452,8 +456,8 @@
 
 
 def ffn_backward(z, pieces, state, out_grad):
-    seq, d = out_grad.shape
-    loads = Loads({"dy": out_grad, **{key: state[key] for key in ("n2", "stats", "small", "mid", "act", "slope")}})
+    seq, d = out_grad[0].shape
+    loads = Loads({**{f"dy{n}": term for n, term in enumerate(out_grad)}, **{key: state[key] for key in ("n2", "stats", "small", "mid", "act", "slope")}})
     outs = [like((seq, d), F32), like((16, d), F32)] + [like((z.shards, z.part, d), BF16)] * 2
 
     def kernel(*refs):
@@ -463,7 +467,7 @@
         loads.start(load_refs, buffers)
         waits = pieces.start(piece_refs, w_ref, sems, (1,))
         w = Weights(z, w_ref)
-        dy = loads["dy"][...].astype(F32)
+        dy = sum(loads[f"dy{n}"][...].astype(F32) for n in range(len(out_grad)))
         n2 = loads["n2"][...].astype(F32)
         scale = loads["stats"][:, 2:3]
         small = loads["small"][...]
@@ -516,8 +520,7 @@
         specs=pieces.specs + loads.specs,
         out_specs=[pl.BlockSpec(memory_space=pltpu.VMEM)] * 2 + [anywhere] * 2,
         scratch=pieces.scratch + [pltpu.VMEM((2, z.shards, z.part, d), BF16), pltpu.SemaphoreType.DMA((2 * z.shards,))] + loads.scratch,
-        flops=8 * 10**9,
-        moved=16 * MIB,
+        flops=9 * 10**9,
         name="ffn_back",
     )
 
@@ -527,7 +530,7 @@
     head = d // HEADS
     keys = ["n1", "stats", "small", "att", "q", "k", "v", "p", "x"] + (["n0"] if first else [])
     loads = Loads({"dm": d_middle, **{key: state[key] for key in keys}, "grads": small_in, **({"seg": seg_row} if first else {})})
-    rows = z.part + (z.extra if first else 0)
+    rows = z.part + (2 * z.extra if first else 0)
     outs = [like((seq, d), F32), like((seq, d), BF16)] + [like((z.shards, rows, d), BF16)] * 2
     blocks = 2 * lax.axis_size("dp")
     if first:
@@ -616,17 +619,19 @@
             pos_grad = nn(spot, d_embed.astype(BF16)).astype(BF16)
         small_grads = jnp.concatenate([gain_one, blank, value_shift, branch_shift, shift_one, jnp.zeros((6, d), F32), *embed_grads, jnp.zeros((3, d), F32)], axis=0)
         small_grads = (small_grads + loads["grads"][...]).astype(BF16)
+        if first:
+            blank = jnp.zeros((z.extra - z.quarter, d), BF16)
+            others = [pos_grad[z.pos + n * z.quarter : z.pos + (n + 1) * z.quarter] for n in range(4)]
         for h in range(z.shards):
             g_ref[1, h, z.at_small : z.at_small + 16, :] = small_grads
-            if first and h == 0:
-                g_ref[1, h, z.at_small + 16 : z.part, :] = pos_grad[: z.pos]
+            spare = pos_grad[: z.pos] if first and h == 0 else jnp.zeros((z.pos, d), BF16)
+            g_ref[1, h, z.at_small + 16 : z.part, :] = spare
+            if first:
                 for side in range(2):
-                    g_ref[side, h, z.part : rows, :] = pos_grad[z.pos + side * z.extra : z.pos + (side + 1) * z.extra]
-            else:
-                g_ref[1, h, z.at_small + 16 : z.part, :] = jnp.zeros((z.pos, d), BF16)
-                if first:
-                    for side in range(2):
-                        g_ref[side, h, z.part : rows, :] = jnp.zeros((z.extra, d), BF16)
+                    for y in range(2):
+                        row = z.part + y * z.extra
+                        part = jnp.concatenate([others[2 * side + y].astype(F32), blank.astype(F32)], axis=0).astype(BF16) if h == 0 else jnp.zeros((z.extra, d), BF16)
+                        g_ref[side, h, row : row + z.extra, :] = part
         copies = send_halves(z, g_ref, keep_ref, send_ref, out_sems)
         dx_ref[...] = d_in
         low_ref[...] = d_in.astype(BF16)
@@ -641,29 +646,75 @@
         specs=pieces.specs + loads.specs,
         out_specs=[vmem, vmem, anywhere, anywhere] + [vmem] * (len(outs) - 4),
         scratch=pieces.scratch + [pltpu.VMEM((2, z.shards, rows, d), BF16), pltpu.SemaphoreType.DMA((2 * z.shards,))] + loads.scratch,
-        flops=8 * 10**9,
-        moved=16 * MIB,
+        flops=13 * 10**9,
         name="att_back",
     )
 
 
 def add_cores_split(z, keep, came):
-    shards, high, d = keep[0].shape
-    rows = high + z.part
-    half = rows // 32 * 16
+    shards, part, d = keep[0].shape
 
     def kernel(a_ref, f_ref, b_ref, e_ref, c0, c1, c2a, c2b, c3):
         for k, ref in ((0, c0), (1, c1), (3, c3)):
-            ref[:high] = a_ref[k] + b_ref[k]
-            ref[high:] = f_ref[k] + e_ref[k]
+            ref[:part] = a_ref[k] + b_ref[k]
+            ref[part:] = f_ref[k] + e_ref[k]
+        c2a[...] = a_ref[2] + b_ref[2]
+        c2b[...] = f_ref[2] + e_ref[2]
+
+    full, half = like((2 * part, d), BF16), like((part, d), BF16)
+    return call(kernel, [full, full, half, half, full], (*keep, *came), name="add_cores_split")
+
+
+def halves_by_y(z, terms):
+    def kernel(a_ref, b_ref, c_ref, keep_ref, send_ref):
+        y = side_of(2)
+        for ref, part in ((keep_ref, y), (send_ref, 1 - y)):
+            span = pl.ds(pl.multiple_of(part * z.part, z.part), z.part)
+            ref[...] = (a_ref[span].astype(F32) + b_ref[span].astype(F32) + c_ref[span].astype(F32)).astype(BF16)
+
+    return call(kernel, [like((z.part, z.d), BF16)] * 2, terms, name="halves_by_y")
+
+
+def add_core(z, keep_a, came_a, keep_f, came_f):
+    rows = z.part + z.extra
+
+    def kernel(a_ref, b_ref, c_ref, e_ref, keep_ref, send_ref):
+        y = side_of(2)
+
+        def place(ref, part):
+            if part == 0:
+                ref[:, : z.part] = a_ref[:, : z.part] + b_ref[:, : z.part]
+            else:
+                ref[:, : z.part] = c_ref[...] + e_ref[...]
+            span = slice(z.part + part * z.extra, z.part + (part + 1) * z.extra)
+            ref[:, z.part :] = a_ref[:, span] + b_ref[:, span]
+
+        @pl.when(y == 0)
+        def _():
+            place(keep_ref, 0)
+            place(send_ref, 1)
+
+        @pl.when(y == 1)
+        def _():
+            place(keep_ref, 1)
+            place(send_ref, 0)
+
+    return call(kernel, [like((z.shards, rows, z.d), BF16)] * 2, (keep_a, came_a, keep_f, came_f), name="add_core")
+
+
+def add_split(kept, came):
+    _, rows, d = kept.shape
+    half = rows // 32 * 16
+
+    def kernel(a_ref, b_ref, c0, c1, c2a, c2b, c3):
+        for k, ref in ((0, c0), (1, c1), (3, c3)):
+            ref[...] = a_ref[k] + b_ref[k]
         c2a[...] = a_ref[2, :half] + b_ref[2, :half]
-        if half < high:
-            c2b[: high - half] = a_ref[2, half:] + b_ref[2, half:]
-        c2b[high - half :] = f_ref[2] + e_ref[2]
+        c2b[...] = a_ref[2, half:] + b_ref[2, half:]
 
     full = like((rows, d), BF16)
     outs = [full, full, like((half, d), BF16), like((rows - half, d), BF16), full]
-    return call(kernel, outs, (*keep, *came), name="add_cores_split")
+    return call(kernel, outs, (kept, came), name="add_split")
 
 
 def head_forward(pieces, table):
@@ -724,8 +775,7 @@
         out_specs=[pl.BlockSpec((count, d), fixed), pl.BlockSpec((8, count), fixed)],
         scratch=[pltpu.VMEM((count, d), BF16), pltpu.VMEM((count, 1), F32), pltpu.VMEM((count, 1), F32), pltpu.VMEM((count, d), F32)],
         grid=(tiles,),
-        flops=8 * count * vocab * d,
-        moved=14 * MIB,
+        flops=11 * 10**9,
         name="head_forward",
     )
 
@@ -734,7 +784,8 @@
     shards = ids_by.shape[0]
     d = picked.shape[1]
 
-    def kernel(x0_ref, x1_ref, x2_ref, x3_ref, p_ref, i_ref, a_ref, b_ref, c_ref, e_ref, out_ref, lse_ref):
+    def kernel(x0_ref, x1_ref, x2_ref, x3_ref, p_ref, i_ref, a_ref, b_ref, c_ref, e_ref, *outs):
+        lse_ref = outs[shards]
         shard = lax.axis_index("shard")
         parts = (a_ref, b_ref, c_ref, e_ref)
         for k in range(shards):
@@ -751,29 +802,38 @@
             inside = upright(jnp.where((local >= 0) & (local < vocab), 1.0, 0.0), seq)
             hit = jnp.where(inside > 0.5, p_ref[span].astype(F32), 0.0)
             ctx = (x0_ref, x1_ref, x2_ref, x3_ref)[k][...]
-            target = pl.multiple_of(((shard + k) % shards) * seq, seq)
-            out_ref[pl.ds(target, seq), :] = (ctx * weight - hit).astype(BF16)
+            outs[k][...] = (ctx * weight - hit).astype(BF16)
 
     return call(
         kernel,
-        [like((shards * seq, d), BF16), like((shards * seq, 1), F32)],
+        [like((seq, d), BF16)] * shards + [like((shards * seq, 1), F32)],
         (*ctxs, picked, ids_by, *lses),
-        moved=7 * MIB,
         name="head_combine",
     )
 
 
-def head_table(pieces, table, lse, ids_by, first_tile, tiles, block):
+def head_table(pieces, table, lse, ids_by, core=None):
     count = sum(piece.shape[0] for piece in pieces)
-    shards, _, seq = ids_by.shape
+    shards, _, seq = ids_by[0].shape
     vocab, d = table.shape
-    width = min(vocab - first_tile * block, tiles * block)
+    block = 1280
+    tiles = pl.cdiv(vocab, block)
+    shared = core is not None
+    if shared:
+        tiles = (tiles + 1) // 2
+    else:
+        core = jnp.zeros((1,), jnp.int32)
     chunk = 256
-    many = len(pieces)
-
-    def kernel(*refs):
-        piece_refs, (w_ref, lse_ref, i_ref, o_ref, x_ref, xt_ref, t_ref, p_ref) = refs[:many], refs[many:]
+    many, groups = len(pieces), len(ids_by)
+    wide = d // 8
+
+    def kernel(core_ref, *refs):
+        piece_refs, refs = refs[:many], refs[many:]
+        w_ref, refs = refs[0], refs[1:]
+        lse_refs, i_refs, refs = refs[:groups], refs[groups : 2 * groups], refs[2 * groups :]
+        out_refs, (x_ref, xt_ref, t_ref, l_ref, p_ref) = refs[:-5], refs[-5:]
         step = pl.program_id(0)
+        first_tile = core_ref[0] * tiles
 
         @pl.when(step == 0)
         def _():
@@ -783,35 +843,83 @@
                 at += ref.shape[0]
             xt_ref[...] = x_ref[...].T
             start = lax.axis_index("shard") * vocab + first_tile * block
-            for k in range(shards):
-                t_ref[k * seq : (k + 1) * seq] = upright(i_ref[k, 1:2] - start, seq).astype(jnp.int32)
+            for n in range(groups):
+                for k in range(shards):
+                    at = (n * shards + k) * seq
+                    t_ref[at : at + seq] = upright(i_refs[n][k, 1:2] - start, seq).astype(jnp.int32)
+                at = n * shards * seq
+                l_ref[at : at + shards * seq] = lse_refs[n][...]
 
         w = w_ref[...]
         for r in range(count // chunk):
             span = slice(r * chunk, (r + 1) * chunk)
             logits = nt(x_ref[span], w)
             hit = iota(logits.shape, 1) == t_ref[span] - step * block
-            p_ref[span] = (jnp.exp(logits - lse_ref[span]) - jnp.where(hit, 1.0, 0.0)).astype(BF16)
-        o_ref[...] = nn(xt_ref[...], p_ref[...]).astype(BF16)
-
-    fixed = lambda i: (0, 0)
-    return call(
+            p_ref[span] = (jnp.exp(logits - l_ref[span]) - jnp.where(hit, 1.0, 0.0)).astype(BF16)
+        result = nn(xt_ref[...], p_ref[...]).astype(BF16)
+        if not shared:
+            out_refs[0][...] = result
+            return
+        zero = jnp.zeros((wide, block), jnp.int32)
+        first = zero + lax.axis_index("section") == 0
+        front = zero + side_of(2) == 0
+        blocks = [result[n * wide : (n + 1) * wide] for n in range(8)]
+        for n in range(2):
+            low, high = blocks[2 * n], blocks[4 + 2 * n]
+            out_refs[0][n], out_refs[1][n] = jnp.where(first, low, high), jnp.where(first, high, low)
+            low, high = blocks[4 * n + 1], blocks[4 * n + 3]
+            out_refs[2][n], out_refs[3][n] = jnp.where(front, low, high), jnp.where(front, high, low)
+
+    if shared:
+        outs = [like((2, wide, tiles * block), BF16)] * 4
+        out_specs = [pl.BlockSpec((2, wide, block), lambda i, c: (0, 0, i))] * 4
+    else:
+        outs, out_specs = [like((d, vocab), BF16)], [pl.BlockSpec((d, block), lambda i, c: (0, i))]
+    fixed = lambda i, c: (0, 0)
+    return pl.pallas_call(
         kernel,
-        [like((d, width), BF16)],
-        (*pieces, table, lse, ids_by),
-        specs=[pl.BlockSpec(piece.shape, fixed) for piece in pieces]
-        + [
-            pl.BlockSpec((block, d), lambda i: (i + first_tile, 0)),
-            pl.BlockSpec((count, 1), fixed),
-            pl.BlockSpec(ids_by.shape, lambda i: (0, 0, 0)),
-        ],
-        out_specs=[pl.BlockSpec((d, block), lambda i: (0, i))],
-        scratch=[pltpu.VMEM((count, d), BF16), pltpu.VMEM((d, count), BF16), pltpu.VMEM((count, 1), jnp.int32), pltpu.VMEM((count, block), BF16)],
-        grid=(tiles,),
-        flops=6 * count * width * d,
-        moved=8 * MIB,
+        out_shape=outs,
+        grid_spec=pltpu.PrefetchScalarGridSpec(
+            num_scalar_prefetch=1,
+            grid=(tiles,),
+            in_specs=[pl.BlockSpec(piece.shape, fixed) for piece in pieces]
+            + [pl.BlockSpec((block, d), lambda i, c: (i + c[0] * tiles, 0))]
+            + [pl.BlockSpec((shards * seq, 1), fixed)] * groups
+            + [pl.BlockSpec(ids_by[0].shape, lambda i, c: (0, 0, 0))] * groups,
+            out_specs=out_specs,
+            scratch_shapes=[
+                pltpu.VMEM((count, d), BF16),
+                pltpu.VMEM((d, count), BF16),
+                pltpu.VMEM((count, 1), jnp.int32),
+                pltpu.VMEM((count, 1), F32),
+                pltpu.VMEM((count, block), BF16),
+            ],
+        ),
+        compiler_params=pltpu.CompilerParams(vmem_limit_bytes=58 * MIB),
+        cost_estimate=pl.CostEstimate(flops=32 * 10**9, bytes_accessed=0, transcendentals=0),
         name="head_table",
-    )[0]
+    )(core, *pieces, table, *lse, *ids_by)
+
+
+def add_halves(even, odd):
+    shape = even[0].shape[1:]
+
+    def kernel(a_ref, b_ref, c_ref, e_ref, *outs):
+        for n, (one, two, side) in enumerate(((a_ref, b_ref, side_of(2)), (c_ref, e_ref, lax.axis_index("section")))):
+            outs[2 * n][...] = one[side] + two[side]
+            outs[2 * n + 1][...] = one[1 - side] + two[1 - side]
+
+    return call(kernel, [like(shape, BF16)] * 4, (*even, *odd), name="add_halves")
+
+
+def add_last(even, odd):
+    def kernel(a_ref, b_ref, c_ref, e_ref, own_ref, send_ref):
+        first = (jnp.zeros(a_ref.shape, jnp.int32) + side_of(1)) == 0
+        low, high = a_ref[...] + b_ref[...], c_ref[...] + e_ref[...]
+        own_ref[...] = jnp.where(first, low, high)
+        send_ref[...] = jnp.where(first, high, low)
+
+    return call(kernel, [like(even[0].shape, BF16)] * 2, (*even, *odd), name="add_last")
 
 
 def list_tokens(ids, vocab):
@@ -833,7 +941,8 @@
 
 
 def table_grad(dense, pieces, lists, vocab):
-    width = dense.shape[0]
+    width = pieces[0].shape[1]
+    arrays = dense
     sources, _, seq = pieces[0].shape
     shards = 4
     listed = shards * seq
@@ -844,7 +953,9 @@
     tokens = ((lists >> (unit.bit_length() - 1)) + listed * jnp.arange(sources, dtype=jnp.int32)[:, None]).reshape(-1)
     counts = lists[:, listed]
 
-    def kernel(d_ref, own_ref, later_ref, before_ref, far_a_ref, far_b_ref, r_ref, t_ref, n_ref, o_ref, flat_ref, *acc):
+    def kernel(*refs):
+        d_refs, refs = refs[: len(arrays)], refs[len(arrays) :]
+        own_ref, later_ref, before_ref, far_a_ref, far_b_ref, r_ref, t_ref, n_ref, o_ref, flat_ref, *acc = refs
         half = sources // 2
         for j in range(sources):
             far = far_a_ref[j] if j < half else far_b_ref[j - half]
@@ -877,29 +988,39 @@
             return carry
 
         lax.fori_loop(0, sources, source, jnp.int32(0))
-        o_ref[...] = d_ref[...].astype(F32) + sum(ref[...] for ref in acc).T
+        if len(d_refs) == 1:
+            o_ref[...] = d_refs[0][...].astype(F32) + sum(ref[...] for ref in acc).T
+            return
+        half = d_refs[0].shape[1]
+        first = (jnp.zeros((width, half), jnp.int32) + side_of(1)) == 0
+        own, other = d_refs[0][...], d_refs[1][...]
+        o_ref[:, :half] = jnp.where(first, own, other).astype(F32) + sum(ref[:half] for ref in acc).T
+        last = jnp.where(first, other, own)[:, : vocab - half]
+        o_ref[:, half:] = last.astype(F32) + sum(ref[half:] for ref in acc).T
 
     smem = pl.BlockSpec(memory_space=pltpu.SMEM)
     return call(
         kernel,
         [like((width, vocab), F32)],
-        (dense, *pieces, rows, tokens, counts),
-        specs=[None] * 6 + [smem] * 3,
+        (*arrays, *pieces, rows, tokens, counts),
+        specs=[None] * (len(arrays) + 5) + [smem] * 3,
         scratch=[pltpu.VMEM((sources * listed, width), F32)] + [pltpu.VMEM((vocab, width), F32)] * ways,
         limit=60,
         name="table_grad",
     )[0]
 
 
-def unpack_grads(z, own, other):
-    rows = z.rows + z.extra
-    pos_rows = z.pos + 2 * z.extra
-
-    def kernel(own_ref, other_ref, qkv_ref, out_ref, fin_ref, fout_ref, gain_ref, bias_ref, pos_ref, eg_ref, es_ref, all_ref):
-        core = side_of(1)
+def unpack_grads(z, blocks):
+    rows = z.part + z.extra
+    pos_rows = z.pos + 4 * z.quarter
+
+    def kernel(own_ref, y_ref, core_ref, both_ref, qkv_ref, out_ref, fin_ref, fout_ref, gain_ref, bias_ref, pos_ref, eg_ref, es_ref, all_ref):
+        core, y = side_of(1), side_of(2)
         shard = lax.axis_index("shard")
-        all_ref[core] = own_ref[...]
-        all_ref[1 - core] = other_ref[...]
+        all_ref[core, y] = own_ref[...]
+        all_ref[core, 1 - y] = y_ref[...]
+        all_ref[1 - core, y] = core_ref[...]
+        all_ref[1 - core, 1 - y] = both_ref[...]
 
         def own_lanes(value):
             total = jnp.zeros((value.shape[0], z.part), F32)
@@ -907,23 +1028,24 @@
                 total = total + jnp.where(shard == h, value[:, h * z.part : (h + 1) * z.part], 0.0)
             return total
 
-        out_ref[...] = all_ref[0, : z.part].astype(F32)
-        fin_ref[...] = all_ref[0, z.part : z.rows].astype(F32).reshape(z.groups, z.gi, z.d)
+        out_ref[...] = all_ref[0, 0, : z.part].astype(F32)
+        fin_ref[...] = all_ref[0, 1, : z.part].astype(F32).reshape(z.groups, z.gi, z.d)
         for c in range(3):
-            part = all_ref[1, c * z.gi : (c + 1) * z.gi].astype(F32)
+            part = all_ref[1, 0, c * z.gi : (c + 1) * z.gi].astype(F32)
             for g in range(z.groups):
                 qkv_ref[c, g] = part[:, g * z.gw : (g + 1) * z.gw]
-        part = all_ref[1, z.part : z.rows].astype(F32)
+        part = all_ref[1, 1, : z.part].astype(F32)
         for g in range(z.groups):
             fout_ref[g] = part[:, g * z.gw : (g + 1) * z.gw]
-        small = own_lanes(all_ref[1, z.at_small : z.at_small + 16].astype(F32))
+        small = own_lanes(all_ref[1, 0, z.at_small : z.at_small + 16].astype(F32))
         gain_ref[...] = small[0:2]
         bias_ref[...] = small[2:11]
         eg_ref[...] = small[11:12]
         es_ref[...] = small[12:13]
-        pos_ref[: z.pos] = all_ref[1, z.at_small + 16 : z.part].astype(F32)
-        for side in range(2):
-            pos_ref[z.pos + side * z.extra : z.pos + (side + 1) * z.extra] = all_ref[side, z.rows :].astype(F32)
+        pos_ref[: z.pos] = all_ref[1, 0, z.at_small + 16 : z.part].astype(F32)
+        for n in range(4):
+            row = z.pos + n * z.quarter
+            pos_ref[row : row + z.quarter] = all_ref[n // 2, n % 2, z.part :].astype(F32)[: z.quarter]
 
     return call(
         kernel,
@@ -938,8 +1060,8 @@
             like((1, z.part), F32),
             like((1, z.part), F32),
         ],
-        (own, other),
-        scratch=[pltpu.VMEM((2, rows, z.d), BF16)],
+        blocks,
+        scratch=[pltpu.VMEM((2, 2, rows, z.d), BF16)],
         name="unpack",
     )
 
@@ -983,6 +1105,7 @@
     c1 = jnp.concatenate([c1[:half] + right[:half], c1[half:]], axis=0)
     c3 = jnp.concatenate([c3[:half], c3[half:] + left[:half]], axis=0)
     words = scatter_second(c0, c1, c3, "shard")
+    near_y = after(near_y, words)
     far = jnp.concatenate([right[half:], left[half:]], axis=0)
     cross_far = crossed(far, "section", 1)
     both_y = crossed(jnp.concatenate([far, cross_near], axis=0), "dp", 2)
@@ -1014,24 +1137,31 @@
     ctx_far, lse_far = head_forward([far_a, far_b], word_table)
     lse = jnp.concatenate([lse_own[0:1], lse_later[0:1], lse_far[0:1], lse_before[0:1]], axis=1)
     listed = jnp.stack([ids_by[0, 0], ids_by[1, 0], ids_by[3, 0], ids_by[2, 0]]).reshape(1, -1)
-    lists = list_tokens(after(listed, lse), vocab)
     lses = (lse, turned(lse, "shard", -1), turned(lse, "shard", 2), turned(lse, "shard", 1))
-    lses = after(lses, (lists, came_out))
-    parts, whole_lse = head_combine(seq, (ctx_own, ctx_later, ctx_far, ctx_before), target_rows, ids_by, lses, vocab)
-    out_grad = lax.psum_scatter(parts, "shard", scatter_dimension=0, tiled=True)
-    dense = head_table([two["out"], later, far_a, far_b, before], word_table, whole_lse, ids_by, 0, 6, 1280)
-
-    out_grad = after(out_grad, dense)
-    dense = lax.psum_scatter(dense, both, scatter_dimension=0, tiled=True)
-
-    d_middle, small_grads, keep_f, send_f = ffn_backward(z, weights_two, two, out_grad)
+    lses = after(lses, came_out)
+    *parts, whole_lse = head_combine(seq, (ctx_own, ctx_later, ctx_far, ctx_before), target_rows, ids_by, lses, vocab)
+    head_rows = [two["out"], later, far_a, far_b, before]
+    dy_terms = direct_scatter(parts, "shard")
+    if dp == 4:
+        rows_other, ids_other, lse_other = [crossed(row, "dp", 1) for row in head_rows], crossed(ids_by, "dp", 1), crossed(whole_lse, "dp", 1)
+        core = side_of(1).astype(jnp.int32).reshape(1)
+        stay_x, leave_x, stay_y, leave_y = head_table([*head_rows, *rows_other], word_table, [whole_lse, lse_other], [ids_by, ids_other], core)
+        came_x, came_y = crossed(leave_x, "section", 1), crossed(leave_y, "dp", 2)
+        dy_terms = after(dy_terms, stay_x)
+    else:
+        dense = head_table(head_rows, word_table, [whole_lse], [ids_by])[0]
+        dense = [lax.psum_scatter(dense, both, scatter_dimension=0, tiled=True)]
+    d_middle, small_grads, keep_f, send_f = ffn_backward(z, weights_two, two, dy_terms)
+
     in_two, in_low, keep_a, send_a = attention_backward(z, weights_two, two, d_middle, small_grads, False)
     came_f, came_a = crossed(send_f, "dp", 1), crossed(send_a, "dp", 1)
-    d_middle, small_grads, keep_one_f, send_one_f = ffn_backward(z, weights_one, one, in_low)
+    d_middle, small_grads, keep_one_f, send_one_f = ffn_backward(z, weights_one, one, [in_low])
     keep_f, came_f, keep_a, came_a = after((keep_f, came_f, keep_a, came_a), d_middle)
     split_two = add_cores_split(z, (keep_a, keep_f), (came_a, came_f))
     d_middle = after(d_middle, split_two)
     terms_two = scatter_first(*split_two, "shard")
+    if dp == 4:
+        d_middle, came_x, came_y = after((d_middle, came_x, came_y), ())
     came_one_f = crossed(send_one_f, "dp", 1)
     in_one, in_one_low, keep_one_a, send_one_a, d_embed = attention_backward(z, weights_one, one, d_middle, small_grads, True, seg_row, pos_rows)
     keep_one_f, came_one_f = after((keep_one_f, came_one_f), d_embed)
@@ -1044,40 +1174,48 @@
         columns = jnp.concatenate([columns[:, :middle], crossed(columns[:, middle:], axis, bit)], axis=0)
         if n == 0:
             came_one_a = after(came_one_a, columns)
-    split_one = add_cores_split(z, (keep_one_a, keep_one_f), (came_one_a, came_one_f))
-    columns = after(columns, split_one)
+    second_two = scatter_second(*terms_two, "shard")
+    stay_one, leave_one = add_core(z, keep_one_a, came_one_a, keep_one_f, came_one_f)
+    came_one = crossed(after(leave_one, columns), "dp", 2)
+    columns = after(columns, (stay_one, second_two))
     columns = jnp.concatenate([columns[:, 0], crossed(columns[:, 1], "section", 1)], axis=0)
-    second_two = scatter_second(*terms_two, "shard")
-    terms_one = scatter_first(*split_one, "shard")
+    ring_columns = gather_first(columns, "shard")
     own_in = jnp.where(first, in_one, in_two)
     came_in = crossed(jnp.where(first, in_two, in_one).astype(BF16), "section", 1)
-    lists = after(lists, columns)
+    stay_two, leave_two = halves_by_y(z, after(second_two, (columns, stay_one)))
+    came_two = crossed(leave_two, "dp", 2)
+    if dp == 4:
+        stay_x, leave_x, stay_y, leave_y = add_halves(*after(((stay_x, came_x), (stay_y, came_y)), stay_two))
+        last_x, last_y = crossed(leave_x, "dp", 2), crossed(leave_y, "section", 1)
+    lists = list_tokens(after(listed, columns), vocab)
     bit = 1
     while bit < dp:
         lists = jnp.concatenate([lists, crossed(lists, "dp", bit)], axis=0)
         bit *= 2
     lists = jnp.concatenate([lists, crossed(lists, "section", 1)], axis=0)
-    sum_two = sum(after(second_two, (columns, split_one)))
-    second_one = scatter_second(*after(terms_one, sum_two), "shard")
-    sum_one = sum(after(second_one, (sum_two, lists, came_in)))
-    columns = after(columns, sum_one)
-    ring_columns = gather_first(columns, "shard")
-    high = z.part + z.extra
-    extra = sum_one[z.part : high]
-    layer_one = jnp.concatenate([sum_one[: z.part], sum_one[high:]], axis=0)
-    row = jnp.arange(z.rows)[:, None]
-    embed_rows = (row >= z.at_small + 11) & (row < z.part) & (side_of(1) == 1)
+    ring_columns = after(ring_columns, stay_two)
+    far_columns = gather_second(*ring_columns, "shard")
+    terms_one = scatter_first(*add_split(stay_one, after(came_one, (ring_columns, came_in))), "shard")
+    second_one = scatter_second(*terms_one, "shard")
+    if dp == 4:
+        own_dense, send_dense = add_last(*after(((stay_x, last_x), (stay_y, last_y)), second_one))
+        dense = [own_dense, crossed(send_dense, "dp", 1)]
+    word_grad = table_grad(dense, (columns, ring_columns[1], ring_columns[0], *far_columns), lists, vocab)
+    sum_two = stay_two + came_two
+    sum_one = sum(after(second_one, sum_two))
+    layer_one, extra = sum_one[: z.part], sum_one[z.part :]
+    row = jnp.arange(z.part)[:, None]
+    embed_rows = (row >= z.at_small + 11) & (side_of(1) == 1) & (side_of(2) == 0)
     layer_two = jnp.where(embed_rows, layer_one, sum_two)
     total = jnp.concatenate([jnp.where(first, layer_one, layer_two), extra], axis=0)
-    total = total + crossed(jnp.concatenate([jnp.where(first, layer_two, layer_one), extra], axis=0), "section", 1)
-    total, ring_columns = after((total, ring_columns), ())
-    far_columns = gather_second(*ring_columns, "shard")
-    word_grad = table_grad(dense, (columns, ring_columns[1], ring_columns[0], *far_columns), lists, vocab)
-    bit = 2
+    came = crossed(jnp.concatenate([jnp.where(first, layer_two, layer_one), extra], axis=0), "section", 1)
+    total = total + after(came, word_grad)
+    bit = 4
     while bit < dp:
-        total = total + after(crossed(total, "dp", bit), word_grad)
+        total = total + crossed(total, "dp", bit)
         bit *= 2
-    unpacked = unpack_grads(z, total, crossed(total, "dp", 1))
+    total_y = crossed(total, "dp", 2)
+    unpacked = unpack_grads(z, (total, total_y, crossed(total, "dp", 1), crossed(total_y, "dp", 1)))
 
     word_grad = word_grad.T
 

time: 432 us -> 415 us (0.961)
  waiting for transfers between devices: 105 us -> 83.8 us
  Pallas kernels: 179 us -> 193 us
  between operations: 15.5 us -> 2.33 us
  starting transfers between devices: 64.2 us -> 69.6 us
    pallas_call x0 -> x1, Pallas kernels: none -> 32 us  [head_table(): pl.pallas_call(kernel, out_shape=outs, grid_spec=pltpu.PrefetchScalarGrid...]
    pallas_call x19 -> x22, Pallas kernels: 179 us -> 161 us  [call(): pl.pallas_call(kernel, out_shape=outs, in_specs=[vmem if s is None else s...]
    ppermute x30 -> x45, waiting for transfers between devices: 49.7 us -> 38.1 us  [crossed(): lax.ppermute(block, axis, [(i, i ^ bit) for i in range(lax.axis_size(axis...]
    ppermute x28 -> x31, waiting for transfers between devices: 52.5 us -> 45.7 us  [turned(): lax.ppermute(block, axis, [(i, (i + by) % size) for i in range(size)])]
    ppermute x30 -> x45, starting transfers between devices: 19.5 us -> 26.3 us  [crossed(): lax.ppermute(block, axis, [(i, i ^ bit) for i in range(lax.axis_size(axis...]
    unnamed x127 -> x157, local copies, waits for them, and re-layouts: 12.2 us -> 15 us
    ppermute x28 -> x31, starting transfers between devices: 44.6 us -> 43.3 us  [turned(): lax.ppermute(block, axis, [(i, (i + by) % size) for i in range(size)])]
  transfers between devices with their start and end apart: 60 -> 76, of which waited for: 20 -> 19; matrix products, arithmetic and copies ran while one was open for 11% -> 11% of each run, Pallas kernels for 35% -> 47%
where the time goes in v5:
time: 415 us; the launch traced here: 409 us
  Pallas kernels  193 us (47%)
  waiting for transfers between devices  83.8 us (20%)
  starting transfers between devices  69.6 us (17%)
  local copies, waits for them, and re-layouts  49 us (12%)
  other arithmetic  10.9 us (3%)
    pallas_call x22, Pallas kernels, call(): pl.pallas_call(kernel, out_shape=outs, in_specs=[vmem if s is None else s...  161 us
    ppermute x31, waiting for transfers between devices, turned(): lax.ppermute(block, axis, [(i, (i + by) % size) for i in range(size)])  45.7 us
    ppermute x31, starting transfers between devices, turned(): lax.ppermute(block, axis, [(i, (i + by) % size) for i in range(size)])  43.3 us
    ppermute x45, waiting for transfers between devices, crossed(): lax.ppermute(block, axis, [(i, i ^ bit) for i in range(lax.axis_size(axis...  38.1 us
    pallas_call x1, Pallas kernels, head_table(): pl.pallas_call(kernel, out_shape=outs, grid_spec=pltpu.PrefetchScalarGrid...  32 us
    ppermute x45, starting transfers between devices, crossed(): lax.ppermute(block, axis, [(i, i ^ bit) for i in range(lax.axis_size(axis...  26.3 us
    gather x2, local copies, waits for them, and re-layouts, rows_of(): word_table.at[jnp.clip(ids.reshape(-1) - offset, 0, vocab - 1)]  22.9 us
    unnamed x157, local copies, waits for them, and re-layouts  15 us
  transfers between devices with their start and end apart: 76, of which 19 were waited for; matrix products, arithmetic and copies ran while one was open for 11% of the time, Pallas kernels for 47%

profile of v5, /device:TPU:0, one launch (start us, length us, event | category | flops | bytes accessed | tf_op | source)
XLA Modules:
  0.0 408.9 jit_solution(16410809929144413543)
XLA Ops:
  1.4 5.0 %collective-permute-start.2 = (s32[3,256]{1,0:T(4,128)S(1)}, s32[3,256]{1,0:T(4,128)S(1)}, u32[]{:S(2)}, u32[]{:S(2)}) collective-permute-start(s32[3,256]{1,0:T(4,128)S(1)} %bitcast.72), channel_id=1, source_target_pairs={{0,3},{1,0},{2,1},{3,2},{4,7},{5,4},{6,5},{7,6},{8,11},{9,8},{10,9... | collective-permute-start | bytes 9224 | tf_op jit(solution)/shard_map/ppermute | solution.py:84
  18.3 11.4 %gather_fusion = bf16[1024,768]{1,0:T(8,128)(2,1)} fusion(bf16[7632,768]{1,0:T(8,128)(2,1)} %refs_10_.1, s32[1024]{0:T(1024)S(1)} %broadcast_clamp_fusion.1), kind=kCustom, calls=%fused_computation | custom fusion | bytes 3149824 | tf_op jit(solution)/shard_map/gather | solution.py:1086
  29.8 3.8 embed_parts.1
  38.8 11.5 %gather_fusion.1 = bf16[1024,768]{1,0:T(8,128)(2,1)} fusion(bf16[7632,768]{1,0:T(8,128)(2,1)} %refs_10_.1, s32[1024]{0:T(1024)S(1)} %broadcast_clamp_fusion), kind=kCustom, calls=%fused_computation.1 | custom fusion | bytes 3149824 | tf_op jit(solution)/shard_map/gather | solution.py:1086
  56.8 8.3 %collective-permute-done.11.refs_22_ = bf16[256,768]{1,0:T(8,128)(2,1)S(1)} collective-permute-done((bf16[256,768]{1,0:T(8,128)(2,1)S(1)}, bf16[256,768]{1,0:T(8,128)(2,1)S(1)}, u32[]{:S(2)}, u32[]{:S(2)}) %collective-permute-start.11) | collective-permute-done | bytes 393248 | tf_op jit(solution)/shard_map/ppermute | solution.py:84
  65.9 8.0 %collective-permute-done.10.refs_21_ = bf16[256,768]{1,0:T(8,128)(2,1)S(1)} collective-permute-done((bf16[256,768]{1,0:T(8,128)(2,1)S(1)}, bf16[256,768]{1,0:T(8,128)(2,1)S(1)}, u32[]{:S(2)}, u32[]{:S(2)}) %collective-permute-start.10) | collective-permute-done | bytes 393248 | tf_op jit(solution)/shard_map/ppermute | solution.py:84
  77.6 6.0 %collective-permute-done.21.refs_16_ = bf16[192,768]{1,0:T(8,128)(2,1)} collective-permute-done((bf16[192,768]{1,0:T(8,128)(2,1)S(1)}, bf16[192,768]{1,0:T(8,128)(2,1)}, u32[]{:S(2)}, u32[]{:S(2)}) %collective-permute-start.21) | collective-permute-done | bytes 294944 | tf_op jit(solution)/shard_map/ppermute | solution.py:88
  86.4 12.2 %layer_first.1 = (bf16[256,768]{1,0:T(8,128)(2,1)}, bf16[256,768]{1,0:T(8,128)(2,1)}, bf16[256,768]{1,0:T(8,128)(2,1)}, bf16[12,256,256]{2,1,0:T(8,128)(2,1)}, b...) custom-call(bf16[2,2,192,768]{3,2,1,0:T(8,128)(2,1)} %get-tuple-elem, ...), custom_call_target="tpu_custom_call" | custom-call | flops 12000000000 | tf_op jit(solution)/shard_map/layer_first/pallas_call | solution.py:65
  98.6 11.8 %layer_second.1 = (bf16[256,768]{1,0:T(8,128)(2,1)}, bf16[256,768]{1,0:T(8,128)(2,1)}, bf16[256,768]{1,0:T(8,128)(2,1)}, bf16[12,256,256]{2,1,0:T(8,128)(2,1)}, ...) custom-call(bf16[2,2,192,768]{3,2,1,0:T(8,128)(2,1)} %get-tuple-elem, ...), custom_call_target="tpu_custom_call" | custom-call | flops 12000000000 | tf_op jit(solution)/shard_map/layer_second/pallas_call | solution.py:65
  110.8 11.8 %head_forward.4 = (f32[256,768]{1,0:T(8,128)}, f32[8,256]{1,0:T(8,128)}) custom-call(bf16[256,768]{1,0:T(8,128)(2,1)} %get-tuple-element.187.refs_0_, bf16[7632,768]{1,0:T(8,128)(2,1)} %refs_10_.1), custom_call_target="tpu_custom_call" | custom-call | flops 11000000512 | tf_op jit(solution)/shard_map/head_forward/pallas_call | solution.py:65
  127.0 10.9 %head_forward.5 = (f32[256,768]{1,0:T(8,128)}, f32[8,256]{1,0:T(8,128)}) custom-call(bf16[256,768]{1,0:T(8,128)(2,1)} %collective-permute-done.26.refs_0_.refs_4_, bf16[7632,768]{1,0:T(8,128)(2,1)} %refs_10_.1), custom_call_target="tpu_custom_call" | custom-call | flops 11000000512 | tf_op jit(solution)/shard_map/head_forward/pallas_call | solution.py:65
  140.9 10.9 %head_forward.6 = (f32[256,768]{1,0:T(8,128)}, f32[8,256]{1,0:T(8,128)}) custom-call(bf16[256,768]{1,0:T(8,128)(2,1)} %copy-done.43, bf16[7632,768]{1,0:T(8,128)(2,1)} %refs_10_.1), custom_call_target="tpu_custom_call" | custom-call | flops 11000000512 | tf_op jit(solution)/shard_map/head_forward/pallas_call | solution.py:65
  154.0 10.9 %head_forward.7 = (f32[256,768]{1,0:T(8,128)}, f32[8,256]{1,0:T(8,128)}) custom-call(bf16[128,768]{1,0:T(8,128)(2,1)} %copy-done.72, bf16[128,768]{1,0:T(8,128)(2,1)} %copy-done.71, bf16[7632,768]{1,0:T(8,128)(2,1)} %refs_10_.1), custom_call_target="tpu_custom_call" | custom-call | flops 11000000512 | tf_op jit(solution)/shard_map/head_forward/pallas_call | solution.py:65
  175.4 4.4 %head_combine.1 = (bf16[256,768]{1,0:T(8,128)(2,1)}, bf16[256,768]{1,0:T(8,128)(2,1)}, bf16[256,768]{1,0:T(8,128)(2,1)}, bf16[256,768]{1,0:T(8,128)(2,1)}, f32[1024,1]{1,0:T(8,128)}) custom-call(f32[256,768]{1,0:T(8,128)} %get-tuple-element.188.x0_ref, f32[256,768]{1,0:T(8,128)} %get-tuple-element.192.x1_ref, f32[256,768]{1,0:T(8,128)} %get-tuple-element.195.x2_ref, ...), custom_call_target="tpu_custom_call" | custom-call | tf_op jit(solution)/shard_map/head_combine/pallas_call | solution.py:65
  187.1 32.0 %head_table.1 = (bf16[2,96,3840]{2,1,0:T(8,128)(2,1)}, bf16[2,96,3840]{2,1,0:T(8,128)(2,1)}, bf16[2,96,3840]{2,1,0:T(8,128)(2,1)}, bf16[2,96,3840]{2,1,0:T(8,128)(2,1)}) custom-call(s32[1]{0:T(128)} %bitcast.18.core_ref, bf16[256,768]{1,0:T(8,128)(2,1)} %get-tuple-element.187.refs_0_, bf16[256,768]{1,0:T(8,128)(2,1)} %copy-done.43, ...), custom_call_target="tpu_custom_call" | custom-call | flops 32000000000 | tf_op jit(solution)/shard_map/head_table/pallas_call | solution.py:879
  223.0 8.4 %ffn_back.2 = (f32[256,768]{1,0:T(8,128)}, f32[16,768]{1,0:T(8,128)}, bf16[4,192,768]{2,1,0:T(8,128)(2,1)}, bf16[4,192,768]{2,1,0:T(8,128)(2,1)}) custom-call(bf16[2,2,192,768]{3,2,1,0:T(8,128)(2,1)} %get-tuple-element.169.refs_0_, bf16[384,768]{1,0:T(8,128)(2,1)} %copy-done.42, bf16[192,768]{1,0:T(8,128)(2,1)} %copy-done.36, bf16[384,768]{1,0:T(8,128)(2,1)} %copy-done.56, ...), custom_call_target="tpu_custom_call" | custom-call | flops 8999999488 | tf_op jit(solution)/shard_map/ffn_back/pallas_call | solution.py:65
  231.5 10.8 %att_back.2 = (f32[256,768]{1,0:T(8,128)}, bf16[256,768]{1,0:T(8,128)(2,1)}, bf16[4,192,768]{2,1,0:T(8,128)(2,1)}, bf16[4,192,768]{2,1,0:T(8,128)(2,1)}) custom-call(bf16[2,2,192,768]{3,2,1,0:T(8,128)(2,1)} %get-tuple-element.169.refs_0_, bf16[384,768]{1,0:T(8,128)(2,1)} %copy-done.42, bf16[192,768]{1,0:T(8,128)(2,1)} %copy-done.36, ...), custom_call_target="tpu_custom_call" | custom-call | flops 12999999488 | tf_op jit(solution)/shard_map/att_back/pallas_call | solution.py:65
  242.9 8.5 %ffn_back.3 = (f32[256,768]{1,0:T(8,128)}, f32[16,768]{1,0:T(8,128)}, bf16[4,192,768]{2,1,0:T(8,128)(2,1)}, bf16[4,192,768]{2,1,0:T(8,128)(2,1)}) custom-call(bf16[2,2,192,768]{3,2,1,0:T(8,128)(2,1)} %get-tuple-element.169.refs_0_, bf16[384,768]{1,0:T(8,128)(2,1)} %copy-done.42, bf16[192,768]{1,0:T(8,128)(2,1)} %copy-done.36, bf16[384,768]{1,0:T(8,128)(2,1)} %copy-done.56, ...), custom_call_target="tpu_custom_call" | custom-call | flops 8999999488 | tf_op jit(solution)/shard_map/ffn_back/pallas_call | solution.py:65
  252.8 3.9 add_cores_split.1
  260.5 13.3 %att_back.3 = (f32[256,768]{1,0:T(8,128)}, bf16[256,768]{1,0:T(8,128)(2,1)}, bf16[4,256,768]{2,1,0:T(8,128)(2,1)}, bf16[4,256,768]{2,1,0:T(8,128)(2,1)}, bf16[8,96,256]{2,1,0:T(8,128)(2,1)}) custom-call(bf16[2,2,192,768]{3,2,1,0:T(8,128)(2,1)} %get-tuple-element.169.refs_0_, bf16[384,768]{1,0:T(8,128)(2,1)} %copy-done.42, bf16[192,768]{1,0:T(8,128)(2,1)} %copy-done.36, ...), custom_call_target="tpu_custom_call" | custom-call | flops 12999999488 | tf_op jit(solution)/shard_map/att_back/pallas_call | solution.py:65
  282.6 6.2 %collective-permute-done.52 = bf16[2,2,96,256]{3,2,0,1:T(8,128)(2,1)S(1)} collective-permute-done((bf16[2,2,96,256]{3,2,0,1:T(8,128)(2,1)S(1)}, bf16[2,2,96,256]{3,2,0,1:T(8,128)(2,1)S(1)}, u32[]{:S(2)}, u32[]{:S(2)}) %collective-permute-start.52) | collective-permute-done | bytes 196640 | tf_op jit(solution)/shard_map/ppermute | solution.py:88
  290.0 4.6 %add_core.1 = (bf16[4,224,768]{2,1,0:T(8,128)(2,1)}, bf16[4,224,768]{2,1,0:T(8,128)(2,1)}) custom-call(bf16[4,256,768]{2,1,0:T(8,128)(2,1)} %get-tuple-element.272.a_ref, bf16[4,256,768]{2,1,0:T(8,128)(2,1)} %copy-done.3, bf16[4,192,768]{2,1,0:T(8,128)(2,1)} %get-tuple-element.277.c_ref, bf16[4,192,768]{2,1,0:T(8,128)(2,1)} %copy-done.12), custom_call_target="tpu_custom_call" | custom-call | tf_op jit(solution)/shard_map/add_core/pallas_call | solution.py:65
  296.0 9.8 %collective-permute-done.49.b_ref = bf16[384,768]{1,0:T(8,128)(2,1)S(1)} collective-permute-done((bf16[384,768]{1,0:T(8,128)(2,1)S(1)}, bf16[384,768]{1,0:T(8,128)(2,1)S(1)}, u32[]{:S(2)}, u32[]{:S(2)}) %collective-permute-start.49) | collective-permute-done | bytes 589856 | tf_op jit(solution)/shard_map/ppermute | solution.py:84
  308.1 5.6 %collective-permute-done.55 = bf16[4,96,256]{2,1,0:T(8,128)(2,1)S(1)} collective-permute-done((bf16[4,96,256]{2,1,0:T(8,128)(2,1)S(1)}, bf16[4,96,256]{2,1,0:T(8,128)(2,1)S(1)}, u32[]{:S(2)}, u32[]{:S(2)}) %collective-permute-start.55) | collective-permute-done | bytes 196640 | tf_op jit(solution)/shard_map/ppermute | solution.py:88
  319.6 5.4 %list_tokens.1 = s32[1,1152]{1,0:T(1,128)} custom-call(s32[1,1024]{1,0:T(1,128)} %bitcast.80), custom_call_target="tpu_custom_call" | custom-call | tf_op jit(solution)/shard_map/list_tokens/pallas_call | solution.py:65
  327.5 4.6 %add_halves.1 = (bf16[96,3840]{1,0:T(8,128)(2,1)}, bf16[96,3840]{1,0:T(8,128)(2,1)}, bf16[96,3840]{1,0:T(8,128)(2,1)}, bf16[96,3840]{1,0:T(8,128)(2,1)}) custom-call(bf16[2,96,3840]{2,1,0:T(8,128)(2,1)} %get-tuple-element.285.a_ref, bf16[2,96,3840]{2,1,0:T(8,128)(2,1)} %copy-done.8, bf16[2,96,3840]{2,1,0:T(8,128)(2,1)} %get-tuple-element.287.c_ref, ...), custom_call_target="tpu_custom_call" | custom-call | tf_op jit(solution)/shard_map/add_halves/pallas_call | solution.py:65
  337.8 3.8 collective-permute-start.62
  342.8 4.2 %collective-permute-done.61 = bf16[112,768]{1,0:T(8,128)(2,1)S(1)} collective-permute-done((bf16[112,768]{1,0:T(8,128)(2,1)}, bf16[112,768]{1,0:T(8,128)(2,1)S(1)}, u32[]{:S(2)}, u32[]{:S(2)}) %collective-permute-start.61) | collective-permute-done | bytes 172064 | tf_op jit(solution)/shard_map/ppermute | solution.py:84
  353.9 6.9 %collective-permute-done.71 = bf16[192,768]{1,0:T(8,128)(2,1)S(1)} collective-permute-done((bf16[192,768]{1,0:T(8,128)(2,1)}, bf16[192,768]{1,0:T(8,128)(2,1)S(1)}, u32[]{:S(2)}, u32[]{:S(2)}) %collective-permute-start.71) | collective-permute-done | bytes 294944 | tf_op jit(solution)/shard_map/ppermute | solution.py:88
  365.2 4.7 %collective-permute-done.63 = bf16[224,768]{1,0:T(8,128)(2,1)S(1)} collective-permute-done((bf16[224,768]{1,0:T(8,128)(2,1)}, bf16[224,768]{1,0:T(8,128)(2,1)S(1)}, u32[]{:S(2)}, u32[]{:S(2)}) %collective-permute-start.63) | collective-permute-done | bytes 344096 | tf_op jit(solution)/shard_map/ppermute | solution.py:84
  378.6 10.7 %table_grad.1 = f32[96,7632]{1,0:T(8,128)} custom-call(bf16[96,3840]{1,0:T(8,128)(2,1)} %get-tuple-element.309.refs_0_, bf16[96,3840]{1,0:T(8,128)(2,1)} %copy-done.17, bf16[8,96,256]{2,1,0:T(8,128)(2,1)} %copy-done.2, bf16[8,96,256]{2,1,0:T(8,128)(2,1)} %copy-done.16, bf16[8,96,256]{2,1,0:T(8,128)(2,1)} %copy-done.15, ...), custom_call_target="tpu_custom_call" | custom-call | tf_op jit(solution)/shard_map/table_grad/pallas_call | solution.py:65
  392.7 7.9 %collective-permute-done.73.y_ref = bf16[224,768]{1,0:T(8,128)(2,1)S(1)} collective-permute-done((bf16[224,768]{1,0:T(8,128)(2,1)S(1)}, bf16[224,768]{1,0:T(8,128)(2,1)S(1)}, u32[]{:S(2)}, u32[]{:S(2)}) %collective-permute-start.73) | collective-permute-done | bytes 344096 | tf_op jit(solution)/shard_map/ppermute | solution.py:88
  (374 shorter events, 128.3 us)
Async XLA Ops:
  12.9 16.9 %collective-permute-start = (bf16[192,768]{1,0:T(8,128)(2,1)}, bf16[192,768]{1,0:T(8,128)(2,1)S(1)}, u32[]{:S(2)}, u32[]{:S(2)}) collective-permute-start(bf16[192,768]{1,0:T(8,128)(2,1)} %get-tuple-element.170), channel_id=1, source_target_pairs={{0,1},{1,2},{2,3},{3,0},{4,5},{5,6},{6,7},{7,4},{8,9},{9,10},{10,1... | collective-permute-start | bytes 884744 | tf_op jit(solution)/shard_map/ppermute | solution.py:84
  16.7 39.6 %collective-permute-start.16 = (bf16[2,192,768]{2,1,0:T(8,128)(2,1)}, bf16[2,192,768]{2,1,0:T(8,128)(2,1)}, u32[]{:S(2)}, u32[]{:S(2)}) collective-permute-start(bf16[2,192,768]{2,1,0:T(8,128)(2,1)} %get-tuple-element.185), channel_id=1, source_target_pairs={{0,16},{16,0},{1,17},{17,1},{2,18},{18,2},{3,19},{19,3},{4,20},{20... | collective-permute-start | bytes 1769480 | tf_op jit(solution)/shard_map/ppermute | solution.py:88
  33.7 19.6 %collective-permute-start.12 = (bf16[384,768]{1,0:T(8,128)(2,1)S(1)}, bf16[384,768]{1,0:T(8,128)(2,1)S(1)}, u32[]{:S(2)}, u32[]{:S(2)}) collective-permute-start(bf16[384,768]{1,0:T(8,128)(2,1)S(1)} %constant_dynamic-update-slice_fusion.refs_1_), channel_id=1, source_target_pairs={{0,16},{16,0},{1,17},{17,1},{2,18},{18,2},{3,19},{19,3},{4,20},{20... | collective-permute-start | bytes 1769480 | tf_op jit(solution)/shard_map/ppermute | solution.py:88
  34.6 21.7 %collective-permute-start.9 = (bf16[384,768]{1,0:T(8,128)(2,1)S(1)}, bf16[384,768]{1,0:T(8,128)(2,1)}, u32[]{:S(2)}, u32[]{:S(2)}) collective-permute-start(bf16[384,768]{1,0:T(8,128)(2,1)S(1)} %constant_dynamic-update-slice_fusion.refs_1_), channel_id=1, source_target_pairs={{0,8},{4,12},{8,0},{12,4},{1,9},{5,13},{9,1},{13,5},{2,10},{6,14},... | collective-permute-start | bytes 1769480 | tf_op jit(solution)/shard_map/ppermute | solution.py:88
  36.2 16.9 %collective-permute-start.6 = (bf16[224,768]{1,0:T(8,128)(2,1)S(1)}, bf16[224,768]{1,0:T(8,128)(2,1)S(1)}, u32[]{:S(2)}, u32[]{:S(2)}) collective-permute-start(bf16[224,768]{1,0:T(8,128)(2,1)S(1)} %pad_maximum_fusion.11), channel_id=1, source_target_pairs={{0,3},{1,0},{2,1},{3,2},{4,7},{5,4},{6,5},{7,6},{8,11},{9,8},{10,9... | collective-permute-start | bytes 1032200 | tf_op jit(solution)/shard_map/ppermute | solution.py:84
  53.3 21.2 %collective-permute-start.13 = (bf16[576,768]{1,0:T(8,128)(2,1)S(1)}, bf16[576,768]{1,0:T(8,128)(2,1)S(1)}, u32[]{:S(2)}, u32[]{:S(2)}) collective-permute-start(bf16[576,768]{1,0:T(8,128)(2,1)S(1)} %pad_maximum_fusion), channel_id=1, source_target_pairs={{0,8},{4,12},{8,0},{12,4},{1,9},{5,13},{9,1},{13,5},{2,10},{6,14},... | collective-permute-start | bytes 2654216 | tf_op jit(solution)/shard_map/ppermute | solution.py:88
  55.6 18.4 %collective-permute-start.10 = (bf16[256,768]{1,0:T(8,128)(2,1)S(1)}, bf16[256,768]{1,0:T(8,128)(2,1)S(1)}, u32[]{:S(2)}, u32[]{:S(2)}) collective-permute-start(bf16[256,768]{1,0:T(8,128)(2,1)S(1)} %pad_maximum_fusion.6), channel_id=1, source_target_pairs={{0,1},{1,2},{2,3},{3,0},{4,5},{5,6},{6,7},{7,4},{8,9},{9,10},{10,1... | collective-permute-start | bytes 1179656 | tf_op jit(solution)/shard_map/ppermute | solution.py:84
  56.3 20.0 %collective-permute-start.7 = (bf16[384,768]{1,0:T(8,128)(2,1)S(1)}, bf16[384,768]{1,0:T(8,128)(2,1)S(1)}, u32[]{:S(2)}, u32[]{:S(2)}) collective-permute-start(bf16[384,768]{1,0:T(8,128)(2,1)S(1)} %constant_dynamic-update-slice_fusion.refs_1_), channel_id=1, source_target_pairs={{0,4},{4,0},{8,12},{12,8},{1,5},{5,1},{9,13},{13,9},{2,6},{6,2},{1... | collective-permute-start | bytes 1769480 | tf_op jit(solution)/shard_map/ppermute | solution.py:88
  56.3 20.6 %collective-permute-start.17 = (bf16[2,192,768]{2,1,0:T(8,128)(2,1)}, bf16[2,192,768]{2,1,0:T(8,128)(2,1)S(1)}, u32[]{:S(2)}, u32[]{:S(2)}) collective-permute-start(bf16[2,192,768]{2,1,0:T(8,128)(2,1)} %collective-permute-done.16.refs_9_), channel_id=1, source_target_pairs={{0,4},{4,0},{8,12},{12,8},{1,5},{5,1},{9,13},{13,9},{2,6},{6,2},{1... | collective-permute-start | bytes 1769480 | tf_op jit(solution)/shard_map/ppermute | solution.py:88
  84.8 80.8 %collective-permute-start.41 = (s32[4,3,256]{2,1,0:T(4,128)S(1)}, s32[4,3,256]{2,1,0:T(4,128)S(1)}, u32[]{:S(2)}, u32[]{:S(2)}) collective-permute-start(s32[4,3,256]{2,1,0:T(4,128)S(1)} %copy-done.39), channel_id=1, source_target_pairs={{0,4},{4,0},{8,12},{12,8},{1,5},{5,1},{9,13},{13,9},{2,6},{6,2},{1... | collective-permute-start | bytes 36872 | tf_op jit(solution)/shard_map/ppermute | solution.py:88
  110.4 16.6 %collective-permute-start.26 = (bf16[256,768]{1,0:T(8,128)(2,1)}, bf16[256,768]{1,0:T(8,128)(2,1)}, u32[]{:S(2)}, u32[]{:S(2)}) collective-permute-start(bf16[256,768]{1,0:T(8,128)(2,1)} %get-tuple-element.187.refs_0_), channel_id=1, source_target_pairs={{0,1},{1,2},{2,3},{3,0},{4,5},{5,6},{6,7},{7,4},{8,9},{9,10},{10,1... | collective-permute-start | bytes 1179656 | tf_op jit(solution)/shard_map/ppermute | solution.py:84
  125.4 54.4 %collective-permute-start.35 = (bf16[256,768]{1,0:T(8,128)(2,1)S(1)}, bf16[256,768]{1,0:T(8,128)(2,1)S(1)}, u32[]{:S(2)}, u32[]{:S(2)}) collective-permute-start(bf16[256,768]{1,0:T(8,128)(2,1)S(1)} %copy-done.6), channel_id=1, source_target_pairs={{0,4},{4,0},{8,12},{12,8},{1,5},{5,1},{9,13},{13,9},{2,6},{6,2},{1... | collective-permute-start | bytes 1179656 | tf_op jit(solution)/shard_map/ppermute | solution.py:88
  126.1 41.6 %collective-permute-start.24 = (bf16[256,768]{1,0:T(8,128)(2,1)S(1)}, bf16[256,768]{1,0:T(8,128)(2,1)S(1)}, u32[]{:S(2)}, u32[]{:S(2)}) collective-permute-start(bf16[256,768]{1,0:T(8,128)(2,1)S(1)} %broadcast_select_fusion.1), channel_id=1, source_target_pairs={{0,16},{16,0},{1,17},{17,1},{2,18},{18,2},{3,19},{19,3},{4,20},{20... | collective-permute-start | bytes 1179656 | tf_op jit(solution)/shard_map/ppermute | solution.py:88
  153.2 29.1 %collective-permute-start.36 = (bf16[256,768]{1,0:T(8,128)(2,1)}, bf16[256,768]{1,0:T(8,128)(2,1)S(1)}, u32[]{:S(2)}, u32[]{:S(2)}) collective-permute-start(bf16[256,768]{1,0:T(8,128)(2,1)} %copy-done.43), channel_id=1, source_target_pairs={{0,4},{4,0},{8,12},{12,8},{1,5},{5,1},{9,13},{13,9},{2,6},{6,2},{1... | collective-permute-start | bytes 1179656 | tf_op jit(solution)/shard_map/ppermute | solution.py:88
  153.3 32.9 %collective-permute-start.39 = (bf16[256,768]{1,0:T(8,128)(2,1)}, bf16[256,768]{1,0:T(8,128)(2,1)S(1)}, u32[]{:S(2)}, u32[]{:S(2)}) collective-permute-start(bf16[256,768]{1,0:T(8,128)(2,1)} %collective-permute-done.26.refs_0_.refs_4_), channel_id=1, source_target_pairs={{0,4},{4,0},{8,12},{12,8},{1,5},{5,1},{9,13},{13,9},{2,6},{6,2},{1... | collective-permute-start | bytes 1179656 | tf_op jit(solution)/shard_map/ppermute | solution.py:88
  182.0 40.0 %collective-permute-start.32 = (bf16[256,768]{1,0:T(8,128)(2,1)}, bf16[256,768]{1,0:T(8,128)(2,1)S(1)}, u32[]{:S(2)}, u32[]{:S(2)}) collective-permute-start(bf16[256,768]{1,0:T(8,128)(2,1)} %get-tuple-element.205), channel_id=1, source_target_pairs={{0,1},{1,2},{2,3},{3,0},{4,5},{5,6},{6,7},{7,4},{8,9},{9,10},{10,1... | collective-permute-start | bytes 1179656 | tf_op jit(solution)/shard_map/ppermute | solution.py:84
  182.4 39.6 %collective-permute-start.33 = (bf16[256,768]{1,0:T(8,128)(2,1)}, bf16[256,768]{1,0:T(8,128)(2,1)S(1)}, u32[]{:S(2)}, u32[]{:S(2)}) collective-permute-start(bf16[256,768]{1,0:T(8,128)(2,1)} %get-tuple-element.206), channel_id=1, source_target_pairs={{0,3},{1,0},{2,1},{3,2},{4,7},{5,4},{6,5},{7,6},{8,11},{9,8},{10,9... | collective-permute-start | bytes 1179656 | tf_op jit(solution)/shard_map/ppermute | solution.py:84
  186.2 35.8 %collective-permute-start.34 = (bf16[256,768]{1,0:T(8,128)(2,1)}, bf16[256,768]{1,0:T(8,128)(2,1)S(1)}, u32[]{:S(2)}, u32[]{:S(2)}) collective-permute-start(bf16[256,768]{1,0:T(8,128)(2,1)} %get-tuple-element.207), channel_id=1, source_target_pairs={{0,2},{1,3},{2,0},{3,1},{4,6},{5,7},{6,4},{7,5},{8,10},{9,11},{10,... | collective-permute-start | bytes 1179656 | tf_op jit(solution)/shard_map/ppermute | solution.py:84
  219.1 41.4 %collective-permute-start.44 = (bf16[2,96,3840]{2,1,0:T(8,128)(2,1)}, bf16[2,96,3840]{2,1,0:T(8,128)(2,1)S(1)}, u32[]{:S(2)}, u32[]{:S(2)}) collective-permute-start(bf16[2,96,3840]{2,1,0:T(8,128)(2,1)} %get-tuple-element.250), channel_id=1, source_target_pairs={{0,16},{16,0},{1,17},{17,1},{2,18},{18,2},{3,19},{19,3},{4,20},{20... | collective-permute-start | bytes 4423688 | tf_op jit(solution)/shard_map/ppermute | solution.py:88
  220.4 40.1 %collective-permute-start.45 = (bf16[2,96,3840]{2,1,0:T(8,128)(2,1)}, bf16[2,96,3840]{2,1,0:T(8,128)(2,1)S(1)}, u32[]{:S(2)}, u32[]{:S(2)}) collective-permute-start(bf16[2,96,3840]{2,1,0:T(8,128)(2,1)} %get-tuple-element.251), channel_id=1, source_target_pairs={{0,8},{4,12},{8,0},{12,4},{1,9},{5,13},{9,1},{13,5},{2,10},{6,14},... | collective-permute-start | bytes 4423688 | tf_op jit(solution)/shard_map/ppermute | solution.py:88
  256.7 17.2 %collective-permute-start.47 = (bf16[192,768]{1,0:T(8,128)(2,1)}, bf16[192,768]{1,0:T(8,128)(2,1)S(1)}, u32[]{:S(2)}, u32[]{:S(2)}) collective-permute-start(bf16[192,768]{1,0:T(8,128)(2,1)} %get-tuple-element.246), channel_id=1, source_target_pairs={{0,1},{1,2},{2,3},{3,0},{4,5},{5,6},{6,7},{7,4},{8,9},{9,10},{10,1... | collective-permute-start | bytes 884744 | tf_op jit(solution)/shard_map/ppermute | solution.py:84
  257.3 16.6 %collective-permute-start.48 = (bf16[192,768]{1,0:T(8,128)(2,1)}, bf16[192,768]{1,0:T(8,128)(2,1)S(1)}, u32[]{:S(2)}, u32[]{:S(2)}) collective-permute-start(bf16[192,768]{1,0:T(8,128)(2,1)} %get-tuple-element.247), channel_id=1, source_target_pairs={{0,3},{1,0},{2,1},{3,2},{4,7},{5,4},{6,5},{7,6},{8,11},{9,8},{10,9... | collective-permute-start | bytes 884744 | tf_op jit(solution)/shard_map/ppermute | solution.py:84
  277.3 18.7 %collective-permute-start.50 = (bf16[384,768]{1,0:T(8,128)(2,1)S(1)}, bf16[384,768]{1,0:T(8,128)(2,1)S(1)}, u32[]{:S(2)}, u32[]{:S(2)}) collective-permute-start(bf16[384,768]{1,0:T(8,128)(2,1)S(1)} %pad_maximum_fusion.2), channel_id=1, source_target_pairs={{0,3},{1,0},{2,1},{3,2},{4,7},{5,4},{6,5},{7,6},{8,11},{9,8},{10,9... | collective-permute-start | bytes 1769480 | tf_op jit(solution)/shard_map/ppermute | solution.py:84
  277.7 28.1 %collective-permute-start.49 = (bf16[384,768]{1,0:T(8,128)(2,1)S(1)}, bf16[384,768]{1,0:T(8,128)(2,1)S(1)}, u32[]{:S(2)}, u32[]{:S(2)}) collective-permute-start(bf16[384,768]{1,0:T(8,128)(2,1)S(1)} %pad_maximum_fusion.1), channel_id=1, source_target_pairs={{0,1},{1,2},{2,3},{3,0},{4,5},{5,6},{6,7},{7,4},{8,9},{9,10},{10,1... | collective-permute-start | bytes 1769480 | tf_op jit(solution)/shard_map/ppermute | solution.py:84
  294.6 39.2 %collective-permute-start.58 = (bf16[4,224,768]{2,1,0:T(8,128)(2,1)}, bf16[4,224,768]{2,1,0:T(8,128)(2,1)S(1)}, u32[]{:S(2)}, u32[]{:S(2)}) collective-permute-start(bf16[4,224,768]{2,1,0:T(8,128)(2,1)} %get-tuple-element.294), channel_id=1, source_target_pairs={{0,8},{4,12},{8,0},{12,4},{1,9},{5,13},{9,1},{13,5},{2,10},{6,14},... | collective-permute-start | bytes 4128776 | tf_op jit(solution)/shard_map/ppermute | solution.py:88
  306.6 27.1 %collective-permute-start.46 = (bf16[256,768]{1,0:T(8,128)(2,1)S(1)}, bf16[256,768]{1,0:T(8,128)(2,1)S(1)}, u32[]{:S(2)}, u32[]{:S(2)}) collective-permute-start(bf16[256,768]{1,0:T(8,128)(2,1)S(1)} %select_convert_fusion), channel_id=1, source_target_pairs={{0,16},{16,0},{1,17},{17,1},{2,18},{18,2},{3,19},{19,3},{4,20},{20... | collective-permute-start | bytes 1179656 | tf_op jit(solution)/shard_map/ppermute | solution.py:88
  313.8 18.4 %collective-permute-start.59 = (bf16[8,96,256]{2,1,0:T(8,128)(2,1)S(1)}, bf16[8,96,256]{2,1,0:T(8,128)(2,1)S(1)}, u32[]{:S(2)}, u32[]{:S(2)}) collective-permute-start(bf16[8,96,256]{2,1,0:T(8,128)(2,1)S(1)} %pad_maximum_fusion.9.refs_2_), channel_id=1, source_target_pairs={{0,1},{1,2},{2,3},{3,0},{4,5},{5,6},{6,7},{7,4},{8,9},{9,10},{10,1... | collective-permute-start | bytes 1179656 | tf_op jit(solution)/shard_map/ppermute | solution.py:84
  313.9 19.1 %collective-permute-start.60 = (bf16[8,96,256]{2,1,0:T(8,128)(2,1)S(1)}, bf16[8,96,256]{2,1,0:T(8,128)(2,1)S(1)}, u32[]{:S(2)}, u32[]{:S(2)}) collective-permute-start(bf16[8,96,256]{2,1,0:T(8,128)(2,1)S(1)} %pad_maximum_fusion.9.refs_2_), channel_id=1, source_target_pairs={{0,3},{1,0},{2,1},{3,2},{4,7},{5,4},{6,5},{7,6},{8,11},{9,8},{10,9... | collective-permute-start | bytes 1179656 | tf_op jit(solution)/shard_map/ppermute | solution.py:84
  325.1 16.6 %collective-permute-start.68 = (s32[1,1152]{1,0:T(1,128)}, s32[1,1152]{1,0:T(1,128)S(1)}, u32[]{:S(2)}, u32[]{:S(2)}) collective-permute-start(s32[1,1152]{1,0:T(1,128)} %list_tokens.1), channel_id=1, source_target_pairs={{0,4},{4,0},{8,12},{12,8},{1,5},{5,1},{9,13},{13,9},{2,6},{6,2},{1... | collective-permute-start | bytes 13832 | tf_op jit(solution)/shard_map/ppermute | solution.py:88
  332.1 38.3 %collective-permute-start.56 = (bf16[96,3840]{1,0:T(8,128)(2,1)}, bf16[96,3840]{1,0:T(8,128)(2,1)}, u32[]{:S(2)}, u32[]{:S(2)}) collective-permute-start(bf16[96,3840]{1,0:T(8,128)(2,1)} %get-tuple-element.290), channel_id=1, source_target_pairs={{0,8},{4,12},{8,0},{12,4},{1,9},{5,13},{9,1},{13,5},{2,10},{6,14},... | collective-permute-start | bytes 2211848 | tf_op jit(solution)/shard_map/ppermute | solution.py:88
  333.0 37.5 %collective-permute-start.57 = (bf16[96,3840]{1,0:T(8,128)(2,1)}, bf16[96,3840]{1,0:T(8,128)(2,1)}, u32[]{:S(2)}, u32[]{:S(2)}) collective-permute-start(bf16[96,3840]{1,0:T(8,128)(2,1)} %get-tuple-element.292), channel_id=1, source_target_pairs={{0,16},{16,0},{1,17},{17,1},{2,18},{18,2},{3,19},{19,3},{4,20},{20... | collective-permute-start | bytes 2211848 | tf_op jit(solution)/shard_map/ppermute | solution.py:88
  352.6 17.3 %collective-permute-start.63 = (bf16[224,768]{1,0:T(8,128)(2,1)}, bf16[224,768]{1,0:T(8,128)(2,1)S(1)}, u32[]{:S(2)}, u32[]{:S(2)}) collective-permute-start(bf16[224,768]{1,0:T(8,128)(2,1)} %pad_maximum_fusion.12), channel_id=1, source_target_pairs={{0,1},{1,2},{2,3},{3,0},{4,5},{5,6},{6,7},{7,4},{8,9},{9,10},{10,1... | collective-permute-start | bytes 1032200 | tf_op jit(solution)/shard_map/ppermute | solution.py:84
  (120 other events, 1091.2 us)

commit v6 on v5

--- a/solution.py
+++ b/solution.py
@@ -137,8 +137,8 @@
         self.extra = -(-self.quarter // 16) * 16
 
 
-def pack_weights(z, qkv, out, fin, fout, small):
-    def kernel(qkv_ref, out_ref, fin_ref, fout_ref, small_ref, o_ref, pair_ref, own_ref):
+def pack_weights(z, qkv, out, fin, fout, gains, biases, egain, eshift):
+    def kernel(qkv_ref, out_ref, fin_ref, fout_ref, gain_ref, bias_ref, eg_ref, es_ref, o_ref, pair_ref, own_ref):
         shard = lax.axis_index("shard")
 
         def spread(pieces):
@@ -148,7 +148,8 @@
         o_ref[0, 1] = fin_ref[...].reshape(z.part, z.d)
         for c in range(3):
             o_ref[1, 0, c * z.gi : (c + 1) * z.gi] = spread([qkv_ref[c, g] for g in range(z.groups)])
-        tall = jnp.concatenate([small_ref[...].astype(F32), jnp.zeros((16 - small_ref.shape[0], z.part), F32)], axis=0)
+        embed = [ref[...].astype(F32).reshape(1, z.part) for ref in (eg_ref, es_ref)]
+        tall = jnp.concatenate([gain_ref[...].astype(F32), bias_ref[...].astype(F32), *embed, jnp.zeros((3, z.part), F32)], axis=0)
         wide = jnp.concatenate([tall] * z.shards, axis=1)
         lane = group_of(iota(wide.shape, 1), z.part, z.shards)
         o_ref[1, 0, z.at_small : z.at_small + 16] = jnp.where(lane == shard, wide, 0.0).astype(BF16)
@@ -158,7 +159,7 @@
         own_ref[...] = o_ref[side_of(1), side_of(2)]
 
     outs = [like((2, 2, z.part, z.d), BF16), like((2, z.part, z.d), BF16), like((z.part, z.d), BF16)]
-    return call(kernel, outs, (qkv, out, fin, fout, small), name="pack")
+    return call(kernel, outs, (qkv, out, fin, fout, gains, biases, egain, eshift), name="pack")
 
 
 class Pieces:
@@ -330,7 +331,7 @@
                 (c0, c1, None, c3)[k][...] = total
 
     full, part = like((seq, width), BF16), like((half, width), BF16)
-    return call(kernel, [full, full, part, part, full], (picked, ids_by, pos_table), name="embed_parts")
+    return call(kernel, [full, full, part, part, full], (picked, ids_by, pos_table), limit=24, name="embed_parts")
 
 
 def layer_forward(z, pieces, seg_row, first, words=None, layer_in=None):
@@ -354,7 +355,7 @@
         w_ref, sems, *buffers = refs
         waits = pieces.start(piece_refs, w_ref, sems, (0, 1))
         stores.bind(out_refs, buffers)
-        put, send = stores.put, stores.send
+        put = stores.put
         w = Weights(z, w_ref)
         if first:
             unit, r0 = normed(sum(ref[...].astype(F32) for ref in in_refs))
@@ -378,26 +379,30 @@
         put("v", v)
         same = upright(row_ref[...], seq) == row_ref[...].astype(F32)
         second = iota((seq, 128), 1) >= head
-        q_ref, k_ref, v_ref, att_ref = (stores.buffers[name] for name in ("q", "k", "v", "att"))
-
-        def heads(t, carry):
-            lanes = pl.ds(pl.multiple_of(t * 128, 128), 128)
-            q_t, k_t, v_t = q_ref[:, lanes], k_ref[:, lanes], v_ref[:, lanes]
-            raw = [nt(jnp.where(second == (j == 1), q_t, jnp.zeros_like(q_t)), k_t) for j in range(2)]
-            results = []
-            for j in range(2):
-                scores = jnp.where(same, raw[j], MASKED)
-                scores = jnp.exp(scores - jnp.max(scores, axis=-1, keepdims=True))
-                probs = (scores * (1.0 / jnp.sum(scores, axis=-1, keepdims=True))).astype(BF16)
-                stores.buffers["p"][2 * t + j] = probs
-                results.append(nn(probs, v_t))
-            att_ref[:, lanes] = jnp.where(second, results[1], results[0]).astype(BF16)
-            return carry
-
-        lax.fori_loop(0, d // 128, heads, jnp.int32(0))
-        attended = att_ref[...]
-        send("p")
-        send("att")
+        units = [(t, j) for t in range(d // 128) for j in range(2)]
+
+        def scores_of(unit):
+            t, j = unit
+            lanes = slice(t * 128, (t + 1) * 128)
+            picked = jnp.where(second == (j == 1), q[:, lanes], jnp.zeros((seq, 128), BF16))
+            return nt(picked, k[:, lanes])
+
+        tiles = []
+        raw = scores_of(units[0])
+        for n, (t, j) in enumerate(units):
+            following = scores_of(units[n + 1]) if n + 1 < len(units) else None
+            scores = jnp.where(same, raw, MASKED)
+            scores = jnp.exp(scores - jnp.max(scores, axis=-1, keepdims=True))
+            probs = (scores * (1.0 / jnp.sum(scores, axis=-1, keepdims=True))).astype(BF16)
+            put("p", probs, n)
+            result = nn(probs, v[:, t * 128 : (t + 1) * 128])
+            if j == 0:
+                kept = result
+            else:
+                tiles.append(jnp.where(second, result, kept).astype(BF16))
+            raw = following
+        attended = jnp.concatenate(tiles, axis=1)
+        put("att", attended)
         unit, r1 = normed(x + (nn(attended, w.out()) + small[3:4]))
         put("n1", unit)
         middle = unit * small[0:1] + small[4:5]
@@ -662,7 +667,7 @@
         c2b[...] = f_ref[2] + e_ref[2]
 
     full, half = like((2 * part, d), BF16), like((part, d), BF16)
-    return call(kernel, [full, full, half, half, full], (*keep, *came), name="add_cores_split")
+    return call(kernel, [full, full, half, half, full], (*keep, *came), limit=24, name="add_cores_split")
 
 
 def halves_by_y(z, terms):
@@ -672,7 +677,7 @@
             span = pl.ds(pl.multiple_of(part * z.part, z.part), z.part)
             ref[...] = (a_ref[span].astype(F32) + b_ref[span].astype(F32) + c_ref[span].astype(F32)).astype(BF16)
 
-    return call(kernel, [like((z.part, z.d), BF16)] * 2, terms, name="halves_by_y")
+    return call(kernel, [like((z.part, z.d), BF16)] * 2, terms, limit=8, name="halves_by_y")
 
 
 def add_core(z, keep_a, came_a, keep_f, came_f):
@@ -699,7 +704,7 @@
             place(keep_ref, 1)
             place(send_ref, 0)
 
-    return call(kernel, [like((z.shards, rows, z.d), BF16)] * 2, (keep_a, came_a, keep_f, came_f), name="add_core")
+    return call(kernel, [like((z.shards, rows, z.d), BF16)] * 2, (keep_a, came_a, keep_f, came_f), limit=24, name="add_core")
 
 
 def add_split(kept, came):
@@ -714,7 +719,7 @@
 
     full = like((rows, d), BF16)
     outs = [full, full, like((half, d), BF16), like((rows - half, d), BF16), full]
-    return call(kernel, outs, (kept, came), name="add_split")
+    return call(kernel, outs, (kept, came), limit=16, name="add_split")
 
 
 def head_forward(pieces, table):
@@ -776,6 +781,7 @@
         scratch=[pltpu.VMEM((count, d), BF16), pltpu.VMEM((count, 1), F32), pltpu.VMEM((count, 1), F32), pltpu.VMEM((count, d), F32)],
         grid=(tiles,),
         flops=11 * 10**9,
+        limit=36,
         name="head_forward",
     )
 
@@ -808,7 +814,7 @@
         kernel,
         [like((seq, d), BF16)] * shards + [like((shards * seq, 1), F32)],
         (*ctxs, picked, ids_by, *lses),
-        name="head_combine",
+        limit=20, name="head_combine",
     )
 
 
@@ -909,7 +915,7 @@
             outs[2 * n][...] = one[side] + two[side]
             outs[2 * n + 1][...] = one[1 - side] + two[1 - side]
 
-    return call(kernel, [like(shape, BF16)] * 4, (*even, *odd), name="add_halves")
+    return call(kernel, [like(shape, BF16)] * 4, (*even, *odd), limit=32, name="add_halves")
 
 
 def add_last(even, odd):
@@ -919,7 +925,7 @@
         own_ref[...] = jnp.where(first, low, high)
         send_ref[...] = jnp.where(first, high, low)
 
-    return call(kernel, [like(even[0].shape, BF16)] * 2, (*even, *odd), name="add_last")
+    return call(kernel, [like(even[0].shape, BF16)] * 2, (*even, *odd), limit=16, name="add_last")
 
 
 def list_tokens(ids, vocab):
@@ -937,7 +943,7 @@
         list_ref[0, count] = lax.fori_loop(0, count, step, jnp.int32(0), unroll=8)
 
     smem = pl.BlockSpec(memory_space=pltpu.SMEM)
-    return call(kernel, [like((1, count + 128), jnp.int32)], (ids,), specs=[smem], out_specs=[smem], name="list_tokens")[0]
+    return call(kernel, [like((1, count + 128), jnp.int32)], (ids,), specs=[smem], out_specs=[smem], limit=4, name="list_tokens")[0]
 
 
 def table_grad(dense, pieces, lists, vocab):
@@ -1038,8 +1044,9 @@
         for g in range(z.groups):
             fout_ref[g] = part[:, g * z.gw : (g + 1) * z.gw]
         small = own_lanes(all_ref[1, 0, z.at_small : z.at_small + 16].astype(F32))
+        for n in range(9):
+            bias_ref[n] = small[2 + n : 3 + n]
         gain_ref[...] = small[0:2]
-        bias_ref[...] = small[2:11]
         eg_ref[...] = small[11:12]
         es_ref[...] = small[12:13]
         pos_ref[: z.pos] = all_ref[1, 0, z.at_small + 16 : z.part].astype(F32)
@@ -1055,14 +1062,14 @@
             like((z.groups, z.gi, z.d), F32),
             like((z.groups, z.part, z.gw), F32),
             like((2, z.part), F32),
-            like((9, z.part), F32),
+            like((9, 1, z.part), F32),
             like((pos_rows, z.d), F32),
             like((1, z.part), F32),
             like((1, z.part), F32),
         ],
         blocks,
         scratch=[pltpu.VMEM((2, 2, rows, z.d), BF16)],
-        name="unpack",
+        limit=16, name="unpack",
     )
 
 
@@ -1078,15 +1085,18 @@
     z = Sizes(qkv_weight.shape, out_weight.shape, shards, pos_rows)
     offset = lax.axis_index("shard") * vocab
 
+    local, pair, packed = pack_weights(
+        z, qkv_weight[0], out_weight[0], ffn_in[0], ffn_out[0], layer_gains[0], layer_biases[0], embed_gain, embed_shift
+    )
+
     mine = lax.dynamic_index_in_dim(jnp.stack([token_ids[:, 0], targets[:, 0], segment_ids[:, 0]], axis=1), section, 0, keepdims=False)
+    mine = after(mine, packed)
     ids_by = jnp.stack([mine, turned(mine, "shard", -1), turned(mine, "shard", 2), turned(mine, "shard", 1)])
     seg_row = mine[2:3]
 
     def rows_of(ids):
         return word_table.at[jnp.clip(ids.reshape(-1) - offset, 0, vocab - 1)].get(mode="promise_in_bounds")
 
-    small = jnp.concatenate([layer_gains[0], layer_biases[0], embed_gain[None], embed_shift[None]], axis=0)
-    local, pair, packed = pack_weights(z, qkv_weight[0], out_weight[0], ffn_in[0], ffn_out[0], small)
     cross_pair = crossed(pair, "section", 1)
     near = gather_first(packed, "shard")
     picked = rows_of(ids_by[:, 0])
@@ -1215,15 +1225,16 @@
         total = total + crossed(total, "dp", bit)
         bit *= 2
     total_y = crossed(total, "dp", 2)
-    unpacked = unpack_grads(z, (total, total_y, crossed(total, "dp", 1), crossed(total_y, "dp", 1)))
-
-    word_grad = word_grad.T
-
     def by_micro(own, came):
         return jnp.stack([jnp.where(first, own, came), jnp.where(first, came, own)]).reshape(1, micro, 1, seq, d)
 
     layer_outputs = by_micro(own_out, came_out)
     input_grads = by_micro(own_in, came_in.astype(F32))
+    total_y = after(total_y, (layer_outputs, input_grads))
+    unpacked = unpack_grads(z, (total, total_y, crossed(total, "dp", 1), crossed(total_y, "dp", 1)))
+
+    word_grad = word_grad.T
+
     qkv_g, out_g, fin_g, fout_g, gain_g, bias_g, pos_g, eg_g, es_g = unpacked
     return (
         layer_outputs,
@@ -1237,7 +1248,7 @@
         fin_g[None],
         fout_g[None],
         gain_g[None],
-        bias_g[None],
+        bias_g.transpose(1, 0, 2),
     )
 
 

time: 415 us -> 387 us (0.933)
  Pallas kernels: 193 us -> 154 us
  waiting for transfers between devices: 83.8 us -> 91.2 us
    pallas_call x22, Pallas kernels: 161 us -> 122 us  [call(): pl.pallas_call(kernel, out_shape=outs, in_specs=[vmem if s is None else s...]
    ppermute x31, waiting for transfers between devices: 45.7 us -> 53.9 us  [turned(): lax.ppermute(block, axis, [(i, (i + by) % size) for i in range(size)])]
    ppermute x31, starting transfers between devices: 43.3 us -> 49.9 us  [turned(): lax.ppermute(block, axis, [(i, (i + by) % size) for i in range(size)])]
    unnamed x157 -> x128, local copies, waits for them, and re-layouts: 15 us -> 16.7 us
  transfers between devices with their start and end apart: 76 -> 76, of which waited for: 19 -> 23; matrix products, arithmetic and copies ran while one was open for 11% -> 11% of each run, Pallas kernels for 47% -> 39%
where the time goes in v6:
time: 387 us; the launch traced here: 381 us
  Pallas kernels  154 us (40%)
  waiting for transfers between devices  91.2 us (24%)
  starting transfers between devices  73.2 us (19%)
  local copies, waits for them, and re-layouts  49.3 us (13%)
  other arithmetic  11 us (3%)
    pallas_call x22, Pallas kernels, call(): pl.pallas_call(kernel, out_shape=outs, in_specs=[vmem if s is None else s...  122 us
    ppermute x31, waiting for transfers between devices, turned(): lax.ppermute(block, axis, [(i, (i + by) % size) for i in range(size)])  53.9 us
    ppermute x31, starting transfers between devices, turned(): lax.ppermute(block, axis, [(i, (i + by) % size) for i in range(size)])  49.9 us
    ppermute x45, waiting for transfers between devices, crossed(): lax.ppermute(block, axis, [(i, i ^ bit) for i in range(lax.axis_size(axis...  37.3 us
    pallas_call x1, Pallas kernels, head_table(): pl.pallas_call(kernel, out_shape=outs, grid_spec=pltpu.PrefetchScalarGrid...  32 us
    ppermute x45, starting transfers between devices, crossed(): lax.ppermute(block, axis, [(i, i ^ bit) for i in range(lax.axis_size(axis...  23.3 us
    gather x2, local copies, waits for them, and re-layouts, rows_of(): word_table.at[jnp.clip(ids.reshape(-1) - offset, 0, vocab - 1)]  20.7 us
    unnamed x128, local copies, waits for them, and re-layouts  16.7 us
  transfers between devices with their start and end apart: 76, of which 23 were waited for; matrix products, arithmetic and copies ran while one was open for 11% of the time, Pallas kernels for 39%

profile of v6, /device:TPU:0, one launch (start us, length us, event | category | flops | bytes accessed | tf_op | source)
XLA Modules:
  0.0 380.6 jit_solution(10017350416009758271)
XLA Ops:
  16.3 10.4 %gather_fusion = bf16[1024,768]{1,0:T(8,128)(2,1)S(1)} fusion(bf16[7632,768]{1,0:T(8,128)(2,1)} %refs_10_.1, s32[1024]{0:T(1024)S(1)} %broadcast_clamp_fusion.1), kind=kCustom, calls=%fused_computation | custom fusion | bytes 3149824 | tf_op jit(solution)/shard_map/gather | solution.py:1098
  35.1 10.3 %gather_fusion.1 = bf16[1024,768]{1,0:T(8,128)(2,1)S(1)} fusion(bf16[7632,768]{1,0:T(8,128)(2,1)} %refs_10_.1, s32[1024]{0:T(1024)S(1)} %broadcast_clamp_fusion), kind=kCustom, calls=%fused_computation.1 | custom fusion | bytes 3149824 | tf_op jit(solution)/shard_map/gather | solution.py:1098
  45.4 3.4 collective-permute-done.5
  55.7 8.6 %collective-permute-done.11.refs_22_ = bf16[256,768]{1,0:T(8,128)(2,1)S(1)} collective-permute-done((bf16[256,768]{1,0:T(8,128)(2,1)S(1)}, bf16[256,768]{1,0:T(8,128)(2,1)S(1)}, u32[]{:S(2)}, u32[]{:S(2)}) %collective-permute-start.11) | collective-permute-done | bytes 393248 | tf_op jit(solution)/shard_map/ppermute | solution.py:84
  64.9 7.6 %collective-permute-done.10.refs_21_ = bf16[256,768]{1,0:T(8,128)(2,1)S(1)} collective-permute-done((bf16[256,768]{1,0:T(8,128)(2,1)S(1)}, bf16[256,768]{1,0:T(8,128)(2,1)S(1)}, u32[]{:S(2)}, u32[]{:S(2)}) %collective-permute-start.10) | collective-permute-done | bytes 393248 | tf_op jit(solution)/shard_map/ppermute | solution.py:84
  75.6 6.7 %collective-permute-done.21.refs_16_ = bf16[192,768]{1,0:T(8,128)(2,1)} collective-permute-done((bf16[192,768]{1,0:T(8,128)(2,1)S(1)}, bf16[192,768]{1,0:T(8,128)(2,1)}, u32[]{:S(2)}, u32[]{:S(2)}) %collective-permute-start.21) | collective-permute-done | bytes 294944 | tf_op jit(solution)/shard_map/ppermute | solution.py:88
  84.8 10.5 %layer_first.1 = (bf16[256,768]{1,0:T(8,128)(2,1)}, bf16[256,768]{1,0:T(8,128)(2,1)}, bf16[256,768]{1,0:T(8,128)(2,1)}, bf16[12,256,256]{2,1,0:T(8,128)(2,1)}, b...) custom-call(bf16[2,2,192,768]{3,2,1,0:T(8,128)(2,1)} %get-tuple-elem, ...), custom_call_target="tpu_custom_call" | custom-call | flops 12000000000 | tf_op jit(solution)/shard_map/layer_first/pallas_call | solution.py:65
  95.3 10.2 %layer_second.1 = (bf16[256,768]{1,0:T(8,128)(2,1)}, bf16[256,768]{1,0:T(8,128)(2,1)}, bf16[256,768]{1,0:T(8,128)(2,1)}, bf16[12,256,256]{2,1,0:T(8,128)(2,1)}, ...) custom-call(bf16[2,2,192,768]{3,2,1,0:T(8,128)(2,1)} %get-tuple-elem, ...), custom_call_target="tpu_custom_call" | custom-call | flops 12000000000 | tf_op jit(solution)/shard_map/layer_second/pallas_call | solution.py:65
  107.0 4.3 %copy-done = bf16[7632,768]{1,0:T(8,128)(2,1)S(1)} copy-done((bf16[7632,768]{1,0:T(8,128)(2,1)S(1)}, bf16[7632,768]{1,0:T(8,128)(2,1)}, u32[]{:S(2)}) %copy-start) | copy-done | bytes 11722776
  111.4 9.0 %head_forward.4 = (f32[256,768]{1,0:T(8,128)S(1)}, f32[8,256]{1,0:T(8,128)S(1)}) custom-call(bf16[256,768]{1,0:T(8,128)(2,1)} %get-tuple-element.190.refs_0_, bf16[7632,768]{1,0:T(8,128)(2,1)S(1)} %copy-done), custom_call_target="tpu_custom_call" | custom-call | flops 11000000512 | tf_op jit(solution)/shard_map/head_forward/pallas_call | solution.py:65
  124.0 8.0 %head_forward.5 = (f32[256,768]{1,0:T(8,128)S(1)}, f32[8,256]{1,0:T(8,128)S(1)}) custom-call(bf16[256,768]{1,0:T(8,128)(2,1)S(1)} %collective-permute-done.26.refs_0_.refs_4_, bf16[7632,768]{1,0:T(8,128)(2,1)S(1)} %copy-done), custom_call_target="tpu_custom_call" | custom-call | flops 11000000512 | tf_op jit(solution)/shard_map/head_forward/pallas_call | solution.py:65
  132.1 3.6 collective-permute-start.28
  135.9 8.0 %head_forward.6 = (f32[256,768]{1,0:T(8,128)S(1)}, f32[8,256]{1,0:T(8,128)S(1)}) custom-call(bf16[256,768]{1,0:T(8,128)(2,1)S(1)} %collective-permute-done.25.refs_0_.refs_1_, bf16[7632,768]{1,0:T(8,128)(2,1)S(1)} %copy-done), custom_call_target="tpu_custom_call" | custom-call | flops 11000000512 | tf_op jit(solution)/shard_map/head_forward/pallas_call | solution.py:65
  144.5 8.9 %head_forward.7 = (f32[256,768]{1,0:T(8,128)S(1)}, f32[8,256]{1,0:T(8,128)S(1)}) custom-call(bf16[128,768]{1,0:T(8,128)(2,1)} %collective-permute-done.27.refs_0_.refs_2_, bf16[128,768]{1,0:T(8,128)(2,1)S(1)} %collective-permute-done.28.refs_1_.refs_3_, bf16[7632,768]{1,0:T(8,128)(2,1)S(1)} %copy-done), custom_call_target="tpu_custom_call" | custom-call | flops 11000000512 | tf_op jit(solution)/shard_map/head_forward/pallas_call | solution.py:65
  153.5 3.8 %collective-permute-start.29 = (f32[1,1024]{1,0:T(1,128)S(1)}, f32[1,1024]{1,0:T(1,128)S(1)}, u32[]{:S(2)}, u32[]{:S(2)}) collective-permute-start(f32[1,1024]{1,0:T(1,128)S(1)} %pad_maximum_fusion.15.a_ref), channel_id=1, source_target_pairs={{0,3},{1,0},{2,1},{3,2},{4,7},{5,4},{6,5},{7,6},{8,11},{9,8},{10,9... | collective-permute-start | bytes 12296 | tf_op jit(solution)/shard_map/ppermute | solution.py:84
  158.7 3.2 collective-permute-done.30.c_ref
  170.6 4.3 %collective-permute-start.33 = (bf16[256,768]{1,0:T(8,128)(2,1)}, bf16[256,768]{1,0:T(8,128)(2,1)S(1)}, u32[]{:S(2)}, u32[]{:S(2)}) collective-permute-start(bf16[256,768]{1,0:T(8,128)(2,1)} %copy-done.20), channel_id=1, source_target_pairs={{0,3},{1,0},{2,1},{3,2},{4,7},{5,4},{6,5},{7,6},{8,11},{9,8},{10,9... | collective-permute-start | bytes 1179656 | tf_op jit(solution)/shard_map/ppermute | solution.py:84
  174.9 32.0 %head_table.1 = (bf16[2,96,3840]{2,1,0:T(8,128)(2,1)}, bf16[2,96,3840]{2,1,0:T(8,128)(2,1)}, bf16[2,96,3840]{2,1,0:T(8,128)(2,1)}, bf16[2,96,3840]{2,1,0:T(8,128)(2,1)}) custom-call(s32[1]{0:T(128)} %bitcast.18.core_ref, bf16[256,768]{1,0:T(8,128)(2,1)} %get-tuple-element.190.refs_0_, bf16[256,768]{1,0:T(8,128)(2,1)} %copy-done.16, ...), custom_call_target="tpu_custom_call" | custom-call | flops 32000000000 | tf_op jit(solution)/shard_map/head_table/pallas_call | solution.py:885
  210.1 8.5 %ffn_back.2 = (f32[256,768]{1,0:T(8,128)}, f32[16,768]{1,0:T(8,128)}, bf16[4,192,768]{2,1,0:T(8,128)(2,1)}, bf16[4,192,768]{2,1,0:T(8,128)(2,1)}) custom-call(bf16[2,2,192,768]{3,2,1,0:T(8,128)(2,1)} %get-tuple-element.171.refs_0_, bf16[384,768]{1,0:T(8,128)(2,1)} %constant_dynamic-update-slice_fusion.refs_1_, bf16[192,768]{1,0:T(8,128)(2,1)} %copy-done.40, ...), custom_call_target="tpu_custom_call" | custom-call | flops 8999999488 | tf_op jit(solution)/shard_map/ffn_back/pallas_call | solution.py:65
  218.6 10.8 %att_back.2 = (f32[256,768]{1,0:T(8,128)}, bf16[256,768]{1,0:T(8,128)(2,1)}, bf16[4,192,768]{2,1,0:T(8,128)(2,1)}, bf16[4,192,768]{2,1,0:T(8,128)(2,1)}) custom-call(bf16[2,2,192,768]{3,2,1,0:T(8,128)(2,1)} %get-tuple-element.171.refs_0_, bf16[384,768]{1,0:T(8,128)(2,1)} %constant_dynamic-update-slice_fusion.refs_1_, bf16[192,768]{1,0:T(8,128)(2,1)} %copy-done.40, ...), custom_call_target="tpu_custom_call" | custom-call | flops 12999999488 | tf_op jit(solution)/shard_map/att_back/pallas_call | solution.py:65
  230.0 8.6 %ffn_back.3 = (f32[256,768]{1,0:T(8,128)}, f32[16,768]{1,0:T(8,128)}, bf16[4,192,768]{2,1,0:T(8,128)(2,1)}, bf16[4,192,768]{2,1,0:T(8,128)(2,1)}) custom-call(bf16[2,2,192,768]{3,2,1,0:T(8,128)(2,1)} %get-tuple-element.171.refs_0_, bf16[384,768]{1,0:T(8,128)(2,1)} %constant_dynamic-update-slice_fusion.refs_1_, bf16[192,768]{1,0:T(8,128)(2,1)} %copy-done.40, ...), custom_call_target="tpu_custom_call" | custom-call | flops 8999999488 | tf_op jit(solution)/shard_map/ffn_back/pallas_call | solution.py:65
  245.2 12.3 %att_back.3 = (f32[256,768]{1,0:T(8,128)}, bf16[256,768]{1,0:T(8,128)(2,1)}, bf16[4,256,768]{2,1,0:T(8,128)(2,1)}, bf16[4,256,768]{2,1,0:T(8,128)(2,1)}, bf16[8,96,256]{2,1,0:T(8,128)(2,1)}) custom-call(bf16[2,2,192,768]{3,2,1,0:T(8,128)(2,1)} %get-tuple-element.171.refs_0_, bf16[384,768]{1,0:T(8,128)(2,1)} %constant_dynamic-update-slice_fusion.refs_1_, ...), custom_call_target="tpu_custom_call" | custom-call | flops 12999999488 | tf_op jit(solution)/shard_map/att_back/pallas_call | solution.py:65
  267.0 5.4 %collective-permute-done.52 = bf16[2,2,96,256]{3,2,0,1:T(8,128)(2,1)S(1)} collective-permute-done((bf16[2,2,96,256]{3,2,0,1:T(8,128)(2,1)S(1)}, bf16[2,2,96,256]{3,2,0,1:T(8,128)(2,1)S(1)}, u32[]{:S(2)}, u32[]{:S(2)}) %collective-permute-start.52) | collective-permute-done | bytes 196640 | tf_op jit(solution)/shard_map/ppermute | solution.py:88
  276.3 13.4 %collective-permute-done.49.b_ref = bf16[384,768]{1,0:T(8,128)(2,1)S(1)} collective-permute-done((bf16[384,768]{1,0:T(8,128)(2,1)S(1)}, bf16[384,768]{1,0:T(8,128)(2,1)S(1)}, u32[]{:S(2)}, u32[]{:S(2)}) %collective-permute-start.49) | collective-permute-done | bytes 589856 | tf_op jit(solution)/shard_map/ppermute | solution.py:84
  292.0 5.6 %collective-permute-done.55 = bf16[4,96,256]{2,1,0:T(8,128)(2,1)S(1)} collective-permute-done((bf16[4,96,256]{2,1,0:T(8,128)(2,1)S(1)}, bf16[4,96,256]{2,1,0:T(8,128)(2,1)S(1)}, u32[]{:S(2)}, u32[]{:S(2)}) %collective-permute-start.55) | collective-permute-done | bytes 196640 | tf_op jit(solution)/shard_map/ppermute | solution.py:88
  298.1 3.5 collective-permute-start.60
  302.9 5.4 %list_tokens.1 = s32[1,1152]{1,0:T(1,128)S(1)} custom-call(s32[1,1024]{1,0:T(1,128)S(1)} %bitcast.66), custom_call_target="tpu_custom_call" | custom-call | tf_op jit(solution)/shard_map/list_tokens/pallas_call | solution.py:65
  322.0 4.3 %collective-permute-done.61 = bf16[112,768]{1,0:T(8,128)(2,1)S(1)} collective-permute-done((bf16[112,768]{1,0:T(8,128)(2,1)S(1)}, bf16[112,768]{1,0:T(8,128)(2,1)S(1)}, u32[]{:S(2)}, u32[]{:S(2)}) %collective-permute-start.61) | collective-permute-done | bytes 172064 | tf_op jit(solution)/shard_map/ppermute | solution.py:84
  332.7 7.6 %collective-permute-done.71 = bf16[192,768]{1,0:T(8,128)(2,1)S(1)} collective-permute-done((bf16[192,768]{1,0:T(8,128)(2,1)}, bf16[192,768]{1,0:T(8,128)(2,1)S(1)}, u32[]{:S(2)}, u32[]{:S(2)}) %collective-permute-start.71) | collective-permute-done | bytes 294944 | tf_op jit(solution)/shard_map/ppermute | solution.py:88
  346.6 3.8 %collective-permute-start.67 = (bf16[4,96,256]{2,1,0:T(8,128)(2,1)}, bf16[4,96,256]{2,1,0:T(8,128)(2,1)}, u32[]{:S(2)}, u32[]{:S(2)}) collective-permute-start(bf16[4,96,256]{2,1,0:T(8,128)(2,1)} %slice.168), channel_id=1, source_target_pairs={{0,3},{1,0},{2,1},{3,2},{4,7},{5,4},{6,5},{7,6},{8,11},{9,8},{10,9... | collective-permute-start | bytes 589832 | tf_op jit(solution)/shard_map/ppermute | solution.py:84
  357.0 10.0 %table_grad.1 = f32[96,7632]{1,0:T(8,128)} custom-call(bf16[96,3840]{1,0:T(8,128)(2,1)} %copy-done.7, bf16[96,3840]{1,0:T(8,128)(2,1)} %copy-done.32, bf16[8,96,256]{2,1,0:T(8,128)(2,1)} %copy-done.28, bf16[8,96,256]{2,1,0:T(8,128)(2,1)} %copy-done.31, bf16[8,96,256]{2,1,0:T(8,128)(2,1)} %collective-permute-done.59.refs_4_, bf16[4,96,256]{2,1,0:T(8,128)(2,1)} %copy-done.42, ...), custom_call_target="tpu_custom_call" | custom-call | tf_op jit(solution)/shard_map/table_grad/pallas_call | solution.py:65
  368.9 7.7 %collective-permute-done.73.y_ref = bf16[224,768]{1,0:T(8,128)(2,1)S(1)} collective-permute-done((bf16[224,768]{1,0:T(8,128)(2,1)S(1)}, bf16[224,768]{1,0:T(8,128)(2,1)S(1)}, u32[]{:S(2)}, u32[]{:S(2)}) %collective-permute-start.73) | collective-permute-done | bytes 344096 | tf_op jit(solution)/shard_map/ppermute | solution.py:88
  (343 shorter events, 118.6 us)
Async XLA Ops:
  10.3 16.4 %collective-permute-start = (bf16[192,768]{1,0:T(8,128)(2,1)}, bf16[192,768]{1,0:T(8,128)(2,1)S(1)}, u32[]{:S(2)}, u32[]{:S(2)}) collective-permute-start(bf16[192,768]{1,0:T(8,128)(2,1)} %get-tuple-element.172), channel_id=1, source_target_pairs={{0,1},{1,2},{2,3},{3,0},{4,5},{5,6},{6,7},{7,4},{8,9},{9,10},{10,1... | collective-permute-start | bytes 884744 | tf_op jit(solution)/shard_map/ppermute | solution.py:84
  11.9 14.8 %collective-permute-start.1 = (bf16[192,768]{1,0:T(8,128)(2,1)}, bf16[192,768]{1,0:T(8,128)(2,1)S(1)}, u32[]{:S(2)}, u32[]{:S(2)}) collective-permute-start(bf16[192,768]{1,0:T(8,128)(2,1)} %get-tuple-element.172), channel_id=1, source_target_pairs={{0,3},{1,0},{2,1},{3,2},{4,7},{5,4},{6,5},{7,6},{8,11},{9,8},{10,9... | collective-permute-start | bytes 884744 | tf_op jit(solution)/shard_map/ppermute | solution.py:84
  14.1 41.0 %collective-permute-start.16 = (bf16[2,192,768]{2,1,0:T(8,128)(2,1)}, bf16[2,192,768]{2,1,0:T(8,128)(2,1)}, u32[]{:S(2)}, u32[]{:S(2)}) collective-permute-start(bf16[2,192,768]{2,1,0:T(8,128)(2,1)} %get-tuple-element.188), channel_id=1, source_target_pairs={{0,16},{16,0},{1,17},{17,1},{2,18},{18,2},{3,19},{19,3},{4,20},{20... | collective-permute-start | bytes 1769480 | tf_op jit(solution)/shard_map/ppermute | solution.py:88
  29.7 22.1 %collective-permute-start.12 = (bf16[384,768]{1,0:T(8,128)(2,1)}, bf16[384,768]{1,0:T(8,128)(2,1)S(1)}, u32[]{:S(2)}, u32[]{:S(2)}) collective-permute-start(bf16[384,768]{1,0:T(8,128)(2,1)} %constant_dynamic-update-slice_fusion.refs_1_), channel_id=1, source_target_pairs={{0,16},{16,0},{1,17},{17,1},{2,18},{18,2},{3,19},{19,3},{4,20},{20... | collective-permute-start | bytes 1769480 | tf_op jit(solution)/shard_map/ppermute | solution.py:88
  30.6 24.5 %collective-permute-start.9 = (bf16[384,768]{1,0:T(8,128)(2,1)}, bf16[384,768]{1,0:T(8,128)(2,1)}, u32[]{:S(2)}, u32[]{:S(2)}) collective-permute-start(bf16[384,768]{1,0:T(8,128)(2,1)} %constant_dynamic-update-slice_fusion.refs_1_), channel_id=1, source_target_pairs={{0,8},{4,12},{8,0},{12,4},{1,9},{5,13},{9,1},{13,5},{2,10},{6,14},... | collective-permute-start | bytes 1769480 | tf_op jit(solution)/shard_map/ppermute | solution.py:88
  51.9 21.2 %collective-permute-start.13 = (bf16[576,768]{1,0:T(8,128)(2,1)S(1)}, bf16[576,768]{1,0:T(8,128)(2,1)S(1)}, u32[]{:S(2)}, u32[]{:S(2)}) collective-permute-start(bf16[576,768]{1,0:T(8,128)(2,1)S(1)} %pad_maximum_fusion), channel_id=1, source_target_pairs={{0,8},{4,12},{8,0},{12,4},{1,9},{5,13},{9,1},{13,5},{2,10},{6,14},... | collective-permute-start | bytes 2654216 | tf_op jit(solution)/shard_map/ppermute | solution.py:88
  54.8 17.7 %collective-permute-start.10 = (bf16[256,768]{1,0:T(8,128)(2,1)S(1)}, bf16[256,768]{1,0:T(8,128)(2,1)S(1)}, u32[]{:S(2)}, u32[]{:S(2)}) collective-permute-start(bf16[256,768]{1,0:T(8,128)(2,1)S(1)} %pad_maximum_fusion.6), channel_id=1, source_target_pairs={{0,1},{1,2},{2,3},{3,0},{4,5},{5,6},{6,7},{7,4},{8,9},{9,10},{10,1... | collective-permute-start | bytes 1179656 | tf_op jit(solution)/shard_map/ppermute | solution.py:84
  55.1 19.8 %collective-permute-start.7 = (bf16[384,768]{1,0:T(8,128)(2,1)}, bf16[384,768]{1,0:T(8,128)(2,1)S(1)}, u32[]{:S(2)}, u32[]{:S(2)}) collective-permute-start(bf16[384,768]{1,0:T(8,128)(2,1)} %constant_dynamic-update-slice_fusion.refs_1_), channel_id=1, source_target_pairs={{0,4},{4,0},{8,12},{12,8},{1,5},{5,1},{9,13},{13,9},{2,6},{6,2},{1... | collective-permute-start | bytes 1769480 | tf_op jit(solution)/shard_map/ppermute | solution.py:88
  55.2 20.3 %collective-permute-start.17 = (bf16[2,192,768]{2,1,0:T(8,128)(2,1)}, bf16[2,192,768]{2,1,0:T(8,128)(2,1)S(1)}, u32[]{:S(2)}, u32[]{:S(2)}) collective-permute-start(bf16[2,192,768]{2,1,0:T(8,128)(2,1)} %collective-permute-done.16.refs_9_), channel_id=1, source_target_pairs={{0,4},{4,0},{8,12},{12,8},{1,5},{5,1},{9,13},{13,9},{2,6},{6,2},{1... | collective-permute-start | bytes 1769480 | tf_op jit(solution)/shard_map/ppermute | solution.py:88
  84.2 69.3 %collective-permute-start.41 = (s32[4,3,256]{2,1,0:T(4,128)S(1)}, s32[4,3,256]{2,1,0:T(4,128)S(1)}, u32[]{:S(2)}, u32[]{:S(2)}) collective-permute-start(s32[4,3,256]{2,1,0:T(4,128)S(1)} %pad_add_fusion.2.i_ref.refs_13_), channel_id=1, source_target_pairs={{0,4},{4,0},{8,12},{12,8},{1,5},{5,1},{9,13},{13,9},{2,6},{6,2},{1... | collective-permute-start | bytes 36872 | tf_op jit(solution)/shard_map/ppermute | solution.py:88
  105.5 18.5 %collective-permute-start.26 = (bf16[256,768]{1,0:T(8,128)(2,1)}, bf16[256,768]{1,0:T(8,128)(2,1)S(1)}, u32[]{:S(2)}, u32[]{:S(2)}) collective-permute-start(bf16[256,768]{1,0:T(8,128)(2,1)} %get-tuple-element.190.refs_0_), channel_id=1, source_target_pairs={{0,1},{1,2},{2,3},{3,0},{4,5},{5,6},{6,7},{7,4},{8,9},{9,10},{10,1... | collective-permute-start | bytes 1179656 | tf_op jit(solution)/shard_map/ppermute | solution.py:84
  122.8 45.0 %collective-permute-start.35 = (bf16[256,768]{1,0:T(8,128)(2,1)}, bf16[256,768]{1,0:T(8,128)(2,1)S(1)}, u32[]{:S(2)}, u32[]{:S(2)}) collective-permute-start(bf16[256,768]{1,0:T(8,128)(2,1)} %get-tuple-element.190.refs_0_), channel_id=1, source_target_pairs={{0,4},{4,0},{8,12},{12,8},{1,5},{5,1},{9,13},{13,9},{2,6},{6,2},{1... | collective-permute-start | bytes 1179656 | tf_op jit(solution)/shard_map/ppermute | solution.py:88
  123.9 33.5 %collective-permute-start.24 = (bf16[256,768]{1,0:T(8,128)(2,1)S(1)}, bf16[256,768]{1,0:T(8,128)(2,1)S(1)}, u32[]{:S(2)}, u32[]{:S(2)}) collective-permute-start(bf16[256,768]{1,0:T(8,128)(2,1)S(1)} %broadcast_select_fusion.1), channel_id=1, source_target_pairs={{0,16},{16,0},{1,17},{17,1},{2,18},{18,2},{3,19},{19,3},{4,20},{20... | collective-permute-start | bytes 1179656 | tf_op jit(solution)/shard_map/ppermute | solution.py:88
  143.9 26.6 %collective-permute-start.36 = (bf16[256,768]{1,0:T(8,128)(2,1)S(1)}, bf16[256,768]{1,0:T(8,128)(2,1)}, u32[]{:S(2)}, u32[]{:S(2)}) collective-permute-start(bf16[256,768]{1,0:T(8,128)(2,1)S(1)} %collective-permute-done.25.refs_0_.refs_1_), channel_id=1, source_target_pairs={{0,4},{4,0},{8,12},{12,8},{1,5},{5,1},{9,13},{13,9},{2,6},{6,2},{1... | collective-permute-start | bytes 1179656 | tf_op jit(solution)/shard_map/ppermute | solution.py:88
  144.0 30.8 %collective-permute-start.39 = (bf16[256,768]{1,0:T(8,128)(2,1)S(1)}, bf16[256,768]{1,0:T(8,128)(2,1)}, u32[]{:S(2)}, u32[]{:S(2)}) collective-permute-start(bf16[256,768]{1,0:T(8,128)(2,1)S(1)} %collective-permute-done.26.refs_0_.refs_4_), channel_id=1, source_target_pairs={{0,4},{4,0},{8,12},{12,8},{1,5},{5,1},{9,13},{13,9},{2,6},{6,2},{1... | collective-permute-start | bytes 1179656 | tf_op jit(solution)/shard_map/ppermute | solution.py:88
  170.6 38.5 %collective-permute-start.32 = (bf16[256,768]{1,0:T(8,128)(2,1)}, bf16[256,768]{1,0:T(8,128)(2,1)S(1)}, u32[]{:S(2)}, u32[]{:S(2)}) collective-permute-start(bf16[256,768]{1,0:T(8,128)(2,1)} %copy-done.21), channel_id=1, source_target_pairs={{0,1},{1,2},{2,3},{3,0},{4,5},{5,6},{6,7},{7,4},{8,9},{9,10},{10,1... | collective-permute-start | bytes 1179656 | tf_op jit(solution)/shard_map/ppermute | solution.py:84
  170.6 38.5 %collective-permute-start.33 = (bf16[256,768]{1,0:T(8,128)(2,1)}, bf16[256,768]{1,0:T(8,128)(2,1)S(1)}, u32[]{:S(2)}, u32[]{:S(2)}) collective-permute-start(bf16[256,768]{1,0:T(8,128)(2,1)} %copy-done.20), channel_id=1, source_target_pairs={{0,3},{1,0},{2,1},{3,2},{4,7},{5,4},{6,5},{7,6},{8,11},{9,8},{10,9... | collective-permute-start | bytes 1179656 | tf_op jit(solution)/shard_map/ppermute | solution.py:84
  174.9 34.2 %collective-permute-start.34 = (bf16[256,768]{1,0:T(8,128)(2,1)S(1)}, bf16[256,768]{1,0:T(8,128)(2,1)S(1)}, u32[]{:S(2)}, u32[]{:S(2)}) collective-permute-start(bf16[256,768]{1,0:T(8,128)(2,1)S(1)} %get-tuple-element.210), channel_id=1, source_target_pairs={{0,2},{1,3},{2,0},{3,1},{4,6},{5,7},{6,4},{7,5},{8,10},{9,11},{10,... | collective-permute-start | bytes 1179656 | tf_op jit(solution)/shard_map/ppermute | solution.py:84
  206.9 38.2 %collective-permute-start.44 = (bf16[2,96,3840]{2,1,0:T(8,128)(2,1)}, bf16[2,96,3840]{2,1,0:T(8,128)(2,1)S(1)}, u32[]{:S(2)}, u32[]{:S(2)}) collective-permute-start(bf16[2,96,3840]{2,1,0:T(8,128)(2,1)} %get-tuple-element.253), channel_id=1, source_target_pairs={{0,16},{16,0},{1,17},{17,1},{2,18},{18,2},{3,19},{19,3},{4,20},{20... | collective-permute-start | bytes 4423688 | tf_op jit(solution)/shard_map/ppermute | solution.py:88
  207.5 37.7 %collective-permute-start.45 = (bf16[2,96,3840]{2,1,0:T(8,128)(2,1)}, bf16[2,96,3840]{2,1,0:T(8,128)(2,1)S(1)}, u32[]{:S(2)}, u32[]{:S(2)}) collective-permute-start(bf16[2,96,3840]{2,1,0:T(8,128)(2,1)} %get-tuple-element.254), channel_id=1, source_target_pairs={{0,8},{4,12},{8,0},{12,4},{1,9},{5,13},{9,1},{13,5},{2,10},{6,14},... | collective-permute-start | bytes 4423688 | tf_op jit(solution)/shard_map/ppermute | solution.py:88
  241.3 16.1 %collective-permute-start.47 = (bf16[192,768]{1,0:T(8,128)(2,1)}, bf16[192,768]{1,0:T(8,128)(2,1)S(1)}, u32[]{:S(2)}, u32[]{:S(2)}) collective-permute-start(bf16[192,768]{1,0:T(8,128)(2,1)} %get-tuple-element.249), channel_id=1, source_target_pairs={{0,1},{1,2},{2,3},{3,0},{4,5},{5,6},{6,7},{7,4},{8,9},{9,10},{10,1... | collective-permute-start | bytes 884744 | tf_op jit(solution)/shard_map/ppermute | solution.py:84
  242.1 16.2 %collective-permute-start.48 = (bf16[192,768]{1,0:T(8,128)(2,1)}, bf16[192,768]{1,0:T(8,128)(2,1)S(1)}, u32[]{:S(2)}, u32[]{:S(2)}) collective-permute-start(bf16[192,768]{1,0:T(8,128)(2,1)} %get-tuple-element.250), channel_id=1, source_target_pairs={{0,3},{1,0},{2,1},{3,2},{4,7},{5,4},{6,5},{7,6},{8,11},{9,8},{10,9... | collective-permute-start | bytes 884744 | tf_op jit(solution)/shard_map/ppermute | solution.py:84
  260.9 15.4 %collective-permute-start.50 = (bf16[384,768]{1,0:T(8,128)(2,1)S(1)}, bf16[384,768]{1,0:T(8,128)(2,1)S(1)}, u32[]{:S(2)}, u32[]{:S(2)}) collective-permute-start(bf16[384,768]{1,0:T(8,128)(2,1)S(1)} %pad_maximum_fusion.2), channel_id=1, source_target_pairs={{0,3},{1,0},{2,1},{3,2},{4,7},{5,4},{6,5},{7,6},{8,11},{9,8},{10,9... | collective-permute-start | bytes 1769480 | tf_op jit(solution)/shard_map/ppermute | solution.py:84
  262.0 27.7 %collective-permute-start.49 = (bf16[384,768]{1,0:T(8,128)(2,1)S(1)}, bf16[384,768]{1,0:T(8,128)(2,1)S(1)}, u32[]{:S(2)}, u32[]{:S(2)}) collective-permute-start(bf16[384,768]{1,0:T(8,128)(2,1)S(1)} %pad_maximum_fusion.1), channel_id=1, source_target_pairs={{0,1},{1,2},{2,3},{3,0},{4,5},{5,6},{6,7},{7,4},{8,9},{9,10},{10,1... | collective-permute-start | bytes 1769480 | tf_op jit(solution)/shard_map/ppermute | solution.py:84
  272.8 44.5 %collective-permute-start.58 = (bf16[4,224,768]{2,1,0:T(8,128)(2,1)S(1)}, bf16[4,224,768]{2,1,0:T(8,128)(2,1)S(1)}, u32[]{:S(2)}, u32[]{:S(2)}) collective-permute-start(bf16[4,224,768]{2,1,0:T(8,128)(2,1)S(1)} %get-tuple-element.297), channel_id=1, source_target_pairs={{0,8},{4,12},{8,0},{12,4},{1,9},{5,13},{9,1},{13,5},{2,10},{6,14},... | collective-permute-start | bytes 4128776 | tf_op jit(solution)/shard_map/ppermute | solution.py:88
  291.4 25.8 %collective-permute-start.46 = (bf16[256,768]{1,0:T(8,128)(2,1)S(1)}, bf16[256,768]{1,0:T(8,128)(2,1)S(1)}, u32[]{:S(2)}, u32[]{:S(2)}) collective-permute-start(bf16[256,768]{1,0:T(8,128)(2,1)S(1)} %select_convert_fusion), channel_id=1, source_target_pairs={{0,16},{16,0},{1,17},{17,1},{2,18},{18,2},{3,19},{19,3},{4,20},{20... | collective-permute-start | bytes 1179656 | tf_op jit(solution)/shard_map/ppermute | solution.py:88
  297.7 14.0 %collective-permute-start.59 = (bf16[8,96,256]{2,1,0:T(8,128)(2,1)S(1)}, bf16[8,96,256]{2,1,0:T(8,128)(2,1)}, u32[]{:S(2)}, u32[]{:S(2)}) collective-permute-start(bf16[8,96,256]{2,1,0:T(8,128)(2,1)S(1)} %pad_maximum_fusion.9.refs_2_), channel_id=1, source_target_pairs={{0,1},{1,2},{2,3},{3,0},{4,5},{5,6},{6,7},{7,4},{8,9},{9,10},{10,1... | collective-permute-start | bytes 1179656 | tf_op jit(solution)/shard_map/ppermute | solution.py:84
  298.1 16.9 %collective-permute-start.60 = (bf16[8,96,256]{2,1,0:T(8,128)(2,1)S(1)}, bf16[8,96,256]{2,1,0:T(8,128)(2,1)S(1)}, u32[]{:S(2)}, u32[]{:S(2)}) collective-permute-start(bf16[8,96,256]{2,1,0:T(8,128)(2,1)S(1)} %pad_maximum_fusion.9.refs_2_), channel_id=1, source_target_pairs={{0,3},{1,0},{2,1},{3,2},{4,7},{5,4},{6,5},{7,6},{8,11},{9,8},{10,9... | collective-permute-start | bytes 1179656 | tf_op jit(solution)/shard_map/ppermute | solution.py:84
  311.7 38.7 %collective-permute-start.56 = (bf16[96,3840]{1,0:T(8,128)(2,1)}, bf16[96,3840]{1,0:T(8,128)(2,1)S(1)}, u32[]{:S(2)}, u32[]{:S(2)}) collective-permute-start(bf16[96,3840]{1,0:T(8,128)(2,1)} %get-tuple-element.293), channel_id=1, source_target_pairs={{0,8},{4,12},{8,0},{12,4},{1,9},{5,13},{9,1},{13,5},{2,10},{6,14},... | collective-permute-start | bytes 2211848 | tf_op jit(solution)/shard_map/ppermute | solution.py:88
  315.7 34.7 %collective-permute-start.57 = (bf16[96,3840]{1,0:T(8,128)(2,1)}, bf16[96,3840]{1,0:T(8,128)(2,1)S(1)}, u32[]{:S(2)}, u32[]{:S(2)}) collective-permute-start(bf16[96,3840]{1,0:T(8,128)(2,1)} %get-tuple-element.295), channel_id=1, source_target_pairs={{0,16},{16,0},{1,17},{17,1},{2,18},{18,2},{3,19},{19,3},{4,20},{20... | collective-permute-start | bytes 2211848 | tf_op jit(solution)/shard_map/ppermute | solution.py:88
  328.9 17.6 %collective-permute-start.64 = (bf16[224,768]{1,0:T(8,128)(2,1)}, bf16[224,768]{1,0:T(8,128)(2,1)}, u32[]{:S(2)}, u32[]{:S(2)}) collective-permute-start(bf16[224,768]{1,0:T(8,128)(2,1)} %pad_maximum_fusion.13), channel_id=1, source_target_pairs={{0,3},{1,0},{2,1},{3,2},{4,7},{5,4},{6,5},{7,6},{8,11},{9,8},{10,9... | collective-permute-start | bytes 1032200 | tf_op jit(solution)/shard_map/ppermute | solution.py:84
  331.8 14.7 %collective-permute-start.63 = (bf16[224,768]{1,0:T(8,128)(2,1)}, bf16[224,768]{1,0:T(8,128)(2,1)}, u32[]{:S(2)}, u32[]{:S(2)}) collective-permute-start(bf16[224,768]{1,0:T(8,128)(2,1)} %pad_maximum_fusion.12), channel_id=1, source_target_pairs={{0,1},{1,2},{2,3},{3,0},{4,5},{5,6},{6,7},{7,4},{8,9},{9,10},{10,1... | collective-permute-start | bytes 1032200 | tf_op jit(solution)/shard_map/ppermute | solution.py:84
  (106 other events, 1001.3 us)

commit v7 on v6

--- a/solution.py
+++ b/solution.py
@@ -1103,14 +1103,15 @@
     near, pos_table = after((near, pos_table), near)
     word_parts = embed_parts(picked, ids_by, pos_table, vocab)
     near = after(near, word_parts)
-    near_rows = jnp.concatenate(near, axis=0)
+    c0, c1, c2a, c2b, c3 = word_parts
+    half, quarter = seq // 2, z.part // 2
+    right = jnp.concatenate([c2a, near[0][:quarter]], axis=0)
+    left = jnp.concatenate([c2b, near[1][quarter:]], axis=0)
+    near_rows = jnp.concatenate(after(near, (right, left)), axis=0)
+    right, left = turned(right, "shard", 1), turned(left, "shard", -1)
     near_y = crossed(near_rows, "dp", 2)
     cross_near = crossed(near_rows, "section", 1)
     target_rows = rows_of(after(ids_by[:, 1], near_rows))
-    c0, c1, c2a, c2b, c3 = word_parts
-    half, quarter = seq // 2, z.part // 2
-    right = turned(jnp.concatenate([c2a, near[0][:quarter]], axis=0), "shard", 1)
-    left = turned(jnp.concatenate([c2b, near[1][quarter:]], axis=0), "shard", -1)
     right, left = after((right, left), target_rows)
     c1 = jnp.concatenate([c1[:half] + right[:half], c1[half:]], axis=0)
     c3 = jnp.concatenate([c3[:half], c3[half:] + left[:half]], axis=0)
@@ -1208,7 +1209,7 @@
     terms_one = scatter_first(*add_split(stay_one, after(came_one, (ring_columns, came_in))), "shard")
     second_one = scatter_second(*terms_one, "shard")
     if dp == 4:
-        own_dense, send_dense = add_last(*after(((stay_x, last_x), (stay_y, last_y)), second_one))
+        own_dense, send_dense = add_last(*after(((stay_x, last_x), (stay_y, last_y)), second_one[1]))
         dense = [own_dense, crossed(send_dense, "dp", 1)]
     word_grad = table_grad(dense, (columns, ring_columns[1], ring_columns[0], *far_columns), lists, vocab)
     sum_two = stay_two + came_two

time: 387 us -> 385 us (level)
  waiting for transfers between devices: 91.2 us -> 83.3 us
  starting transfers between devices: 73.2 us -> 79 us
    ppermute x31, waiting for transfers between devices: 53.9 us -> 46.5 us  [turned(): lax.ppermute(block, axis, [(i, (i + by) % size) for i in range(size)])]
    ppermute x45, starting transfers between devices: 23.3 us -> 29.4 us  [crossed(): lax.ppermute(block, axis, [(i, i ^ bit) for i in range(lax.axis_size(axis...]
  transfers between devices with their start and end apart: 76 -> 76, of which waited for: 23 -> 24; matrix products, arithmetic and copies ran while one was open for 11% -> 11% of each run, Pallas kernels for 39% -> 39%
where the time goes in v7:
time: 385 us; the launch traced here: 378 us
  Pallas kernels  154 us (40%)
  waiting for transfers between devices  83.3 us (22%)
  starting transfers between devices  79 us (21%)
  local copies, waits for them, and re-layouts  49.2 us (13%)
  other arithmetic  11 us (3%)
    pallas_call x22, Pallas kernels, call(): pl.pallas_call(kernel, out_shape=outs, in_specs=[vmem if s is None else s...  122 us
    ppermute x31, starting transfers between devices, turned(): lax.ppermute(block, axis, [(i, (i + by) % size) for i in range(size)])  49.7 us
    ppermute x31, waiting for transfers between devices, turned(): lax.ppermute(block, axis, [(i, (i + by) % size) for i in range(size)])  46.5 us
    ppermute x45, waiting for transfers between devices, crossed(): lax.ppermute(block, axis, [(i, i ^ bit) for i in range(lax.axis_size(axis...  36.7 us
    pallas_call x1, Pallas kernels, head_table(): pl.pallas_call(kernel, out_shape=outs, grid_spec=pltpu.PrefetchScalarGrid...  32 us
    ppermute x45, starting transfers between devices, crossed(): lax.ppermute(block, axis, [(i, i ^ bit) for i in range(lax.axis_size(axis...  29.4 us
    gather x2, local copies, waits for them, and re-layouts, rows_of(): word_table.at[jnp.clip(ids.reshape(-1) - offset, 0, vocab - 1)]  20.7 us
    unnamed x128, local copies, waits for them, and re-layouts  16.7 us
  transfers between devices with their start and end apart: 76, of which 24 were waited for; matrix products, arithmetic and copies ran while one was open for 11% of the time, Pallas kernels for 39%

profile of v7, /device:TPU:0, one launch (start us, length us, event | category | flops | bytes accessed | tf_op | source)
XLA Modules:
  0.0 378.3 jit_solution(6506116493437093772)
XLA Ops:
  16.3 10.4 %gather_fusion = bf16[1024,768]{1,0:T(8,128)(2,1)S(1)} fusion(bf16[7632,768]{1,0:T(8,128)(2,1)} %refs_10_.1, s32[1024]{0:T(1024)S(1)} %broadcast_clamp_fusion.1), kind=kCustom, calls=%fused_computation | custom fusion | bytes 3149824 | tf_op jit(solution)/shard_map/gather | solution.py:1098
  35.0 10.3 %gather_fusion.1 = bf16[1024,768]{1,0:T(8,128)(2,1)S(1)} fusion(bf16[7632,768]{1,0:T(8,128)(2,1)} %refs_10_.1, s32[1024]{0:T(1024)S(1)} %broadcast_clamp_fusion), kind=kCustom, calls=%fused_computation.1 | custom fusion | bytes 3149824 | tf_op jit(solution)/shard_map/gather | solution.py:1098
  53.8 8.7 %collective-permute-done.11.refs_22_ = bf16[256,768]{1,0:T(8,128)(2,1)S(1)} collective-permute-done((bf16[256,768]{1,0:T(8,128)(2,1)S(1)}, bf16[256,768]{1,0:T(8,128)(2,1)S(1)}, u32[]{:S(2)}, u32[]{:S(2)}) %collective-permute-start.11) | collective-permute-done | bytes 393248 | tf_op jit(solution)/shard_map/ppermute | solution.py:84
  63.6 6.7 %collective-permute-done.10.refs_21_ = bf16[256,768]{1,0:T(8,128)(2,1)S(1)} collective-permute-done((bf16[256,768]{1,0:T(8,128)(2,1)S(1)}, bf16[256,768]{1,0:T(8,128)(2,1)S(1)}, u32[]{:S(2)}, u32[]{:S(2)}) %collective-permute-start.10) | collective-permute-done | bytes 393248 | tf_op jit(solution)/shard_map/ppermute | solution.py:84
  72.4 7.6 %collective-permute-done.21.refs_16_ = bf16[192,768]{1,0:T(8,128)(2,1)} collective-permute-done((bf16[192,768]{1,0:T(8,128)(2,1)S(1)}, bf16[192,768]{1,0:T(8,128)(2,1)}, u32[]{:S(2)}, u32[]{:S(2)}) %collective-permute-start.21) | collective-permute-done | bytes 294944 | tf_op jit(solution)/shard_map/ppermute | solution.py:88
  82.5 10.5 %layer_first.1 = (bf16[256,768]{1,0:T(8,128)(2,1)}, bf16[256,768]{1,0:T(8,128)(2,1)}, bf16[256,768]{1,0:T(8,128)(2,1)}, bf16[12,256,256]{2,1,0:T(8,128)(2,1)}, b...) custom-call(bf16[2,2,192,768]{3,2,1,0:T(8,128)(2,1)} %get-tuple-elem, ...), custom_call_target="tpu_custom_call" | custom-call | flops 12000000000 | tf_op jit(solution)/shard_map/layer_first/pallas_call | solution.py:65
  93.0 10.2 %layer_second.1 = (bf16[256,768]{1,0:T(8,128)(2,1)}, bf16[256,768]{1,0:T(8,128)(2,1)}, bf16[256,768]{1,0:T(8,128)(2,1)}, bf16[12,256,256]{2,1,0:T(8,128)(2,1)}, ...) custom-call(bf16[2,2,192,768]{3,2,1,0:T(8,128)(2,1)} %get-tuple-elem, ...), custom_call_target="tpu_custom_call" | custom-call | flops 12000000000 | tf_op jit(solution)/shard_map/layer_second/pallas_call | solution.py:65
  104.8 4.3 %copy-done = bf16[7632,768]{1,0:T(8,128)(2,1)S(1)} copy-done((bf16[7632,768]{1,0:T(8,128)(2,1)S(1)}, bf16[7632,768]{1,0:T(8,128)(2,1)}, u32[]{:S(2)}) %copy-start) | copy-done | bytes 11722776
  109.1 9.0 %head_forward.4 = (f32[256,768]{1,0:T(8,128)S(1)}, f32[8,256]{1,0:T(8,128)S(1)}) custom-call(bf16[256,768]{1,0:T(8,128)(2,1)} %get-tuple-element.194.refs_0_, bf16[7632,768]{1,0:T(8,128)(2,1)S(1)} %copy-done), custom_call_target="tpu_custom_call" | custom-call | flops 11000000512 | tf_op jit(solution)/shard_map/head_forward/pallas_call | solution.py:65
  122.2 8.0 %head_forward.5 = (f32[256,768]{1,0:T(8,128)S(1)}, f32[8,256]{1,0:T(8,128)S(1)}) custom-call(bf16[256,768]{1,0:T(8,128)(2,1)S(1)} %collective-permute-done.26.refs_0_.refs_4_, bf16[7632,768]{1,0:T(8,128)(2,1)S(1)} %copy-done), custom_call_target="tpu_custom_call" | custom-call | flops 11000000512 | tf_op jit(solution)/shard_map/head_forward/pallas_call | solution.py:65
  130.3 3.1 collective-permute-start.28
  133.6 8.0 %head_forward.6 = (f32[256,768]{1,0:T(8,128)S(1)}, f32[8,256]{1,0:T(8,128)S(1)}) custom-call(bf16[256,768]{1,0:T(8,128)(2,1)S(1)} %collective-permute-done.25.refs_0_.refs_1_, bf16[7632,768]{1,0:T(8,128)(2,1)S(1)} %copy-done), custom_call_target="tpu_custom_call" | custom-call | flops 11000000512 | tf_op jit(solution)/shard_map/head_forward/pallas_call | solution.py:65
  142.3 8.9 %head_forward.7 = (f32[256,768]{1,0:T(8,128)S(1)}, f32[8,256]{1,0:T(8,128)S(1)}) custom-call(bf16[128,768]{1,0:T(8,128)(2,1)} %collective-permute-done.27.refs_0_.refs_2_, bf16[128,768]{1,0:T(8,128)(2,1)S(1)} %collective-permute-done.28.refs_1_.refs_3_, bf16[7632,768]{1,0:T(8,128)(2,1)S(1)} %copy-done), custom_call_target="tpu_custom_call" | custom-call | flops 11000000512 | tf_op jit(solution)/shard_map/head_forward/pallas_call | solution.py:65
  151.3 3.8 %collective-permute-start.29 = (f32[1,1024]{1,0:T(1,128)S(1)}, f32[1,1024]{1,0:T(1,128)S(1)}, u32[]{:S(2)}, u32[]{:S(2)}) collective-permute-start(f32[1,1024]{1,0:T(1,128)S(1)} %pad_maximum_fusion.15.a_ref), channel_id=1, source_target_pairs={{0,3},{1,0},{2,1},{3,2},{4,7},{5,4},{6,5},{7,6},{8,11},{9,8},{10,9... | collective-permute-start | bytes 12296 | tf_op jit(solution)/shard_map/ppermute | solution.py:84
  156.4 3.2 collective-permute-done.30.c_ref
  168.3 4.3 %collective-permute-start.33 = (bf16[256,768]{1,0:T(8,128)(2,1)}, bf16[256,768]{1,0:T(8,128)(2,1)S(1)}, u32[]{:S(2)}, u32[]{:S(2)}) collective-permute-start(bf16[256,768]{1,0:T(8,128)(2,1)} %copy-done.20), channel_id=1, source_target_pairs={{0,3},{1,0},{2,1},{3,2},{4,7},{5,4},{6,5},{7,6},{8,11},{9,8},{10,9... | collective-permute-start | bytes 1179656 | tf_op jit(solution)/shard_map/ppermute | solution.py:84
  172.7 32.0 %head_table.1 = (bf16[2,96,3840]{2,1,0:T(8,128)(2,1)}, bf16[2,96,3840]{2,1,0:T(8,128)(2,1)}, bf16[2,96,3840]{2,1,0:T(8,128)(2,1)}, bf16[2,96,3840]{2,1,0:T(8,128)(2,1)}) custom-call(s32[1]{0:T(128)} %bitcast.18.core_ref, bf16[256,768]{1,0:T(8,128)(2,1)} %get-tuple-element.194.refs_0_, bf16[256,768]{1,0:T(8,128)(2,1)} %copy-done.16, ...), custom_call_target="tpu_custom_call" | custom-call | flops 32000000000 | tf_op jit(solution)/shard_map/head_table/pallas_call | solution.py:885
  207.9 8.5 %ffn_back.2 = (f32[256,768]{1,0:T(8,128)}, f32[16,768]{1,0:T(8,128)}, bf16[4,192,768]{2,1,0:T(8,128)(2,1)}, bf16[4,192,768]{2,1,0:T(8,128)(2,1)}) custom-call(bf16[2,2,192,768]{3,2,1,0:T(8,128)(2,1)} %get-tuple-element.173.refs_0_, bf16[384,768]{1,0:T(8,128)(2,1)} %constant_dynamic-update-slice_fusion.refs_1_, bf16[192,768]{1,0:T(8,128)(2,1)} %copy-done.40, ...), custom_call_target="tpu_custom_call" | custom-call | flops 8999999488 | tf_op jit(solution)/shard_map/ffn_back/pallas_call | solution.py:65
  216.4 10.8 %att_back.2 = (f32[256,768]{1,0:T(8,128)}, bf16[256,768]{1,0:T(8,128)(2,1)}, bf16[4,192,768]{2,1,0:T(8,128)(2,1)}, bf16[4,192,768]{2,1,0:T(8,128)(2,1)}) custom-call(bf16[2,2,192,768]{3,2,1,0:T(8,128)(2,1)} %get-tuple-element.173.refs_0_, bf16[384,768]{1,0:T(8,128)(2,1)} %constant_dynamic-update-slice_fusion.refs_1_, bf16[192,768]{1,0:T(8,128)(2,1)} %copy-done.40, ...), custom_call_target="tpu_custom_call" | custom-call | flops 12999999488 | tf_op jit(solution)/shard_map/att_back/pallas_call | solution.py:65
  227.7 8.6 %ffn_back.3 = (f32[256,768]{1,0:T(8,128)}, f32[16,768]{1,0:T(8,128)}, bf16[4,192,768]{2,1,0:T(8,128)(2,1)}, bf16[4,192,768]{2,1,0:T(8,128)(2,1)}) custom-call(bf16[2,2,192,768]{3,2,1,0:T(8,128)(2,1)} %get-tuple-element.173.refs_0_, bf16[384,768]{1,0:T(8,128)(2,1)} %constant_dynamic-update-slice_fusion.refs_1_, bf16[192,768]{1,0:T(8,128)(2,1)} %copy-done.40, ...), custom_call_target="tpu_custom_call" | custom-call | flops 8999999488 | tf_op jit(solution)/shard_map/ffn_back/pallas_call | solution.py:65
  239.9 3.0 collective-permute-start.48
  242.9 12.3 %att_back.3 = (f32[256,768]{1,0:T(8,128)}, bf16[256,768]{1,0:T(8,128)(2,1)}, bf16[4,256,768]{2,1,0:T(8,128)(2,1)}, bf16[4,256,768]{2,1,0:T(8,128)(2,1)}, bf16[8,96,256]{2,1,0:T(8,128)(2,1)}) custom-call(bf16[2,2,192,768]{3,2,1,0:T(8,128)(2,1)} %get-tuple-element.173.refs_0_, bf16[384,768]{1,0:T(8,128)(2,1)} %constant_dynamic-update-slice_fusion.refs_1_, ...), custom_call_target="tpu_custom_call" | custom-call | flops 12999999488 | tf_op jit(solution)/shard_map/att_back/pallas_call | solution.py:65
  265.6 4.5 %collective-permute-done.52 = bf16[2,2,96,256]{3,2,0,1:T(8,128)(2,1)S(1)} collective-permute-done((bf16[2,2,96,256]{3,2,0,1:T(8,128)(2,1)S(1)}, bf16[2,2,96,256]{3,2,0,1:T(8,128)(2,1)S(1)}, u32[]{:S(2)}, u32[]{:S(2)}) %collective-permute-start.52) | collective-permute-done | bytes 196640 | tf_op jit(solution)/shard_map/ppermute | solution.py:88
  274.0 13.4 %collective-permute-done.49.b_ref = bf16[384,768]{1,0:T(8,128)(2,1)S(1)} collective-permute-done((bf16[384,768]{1,0:T(8,128)(2,1)S(1)}, bf16[384,768]{1,0:T(8,128)(2,1)S(1)}, u32[]{:S(2)}, u32[]{:S(2)}) %collective-permute-start.49) | collective-permute-done | bytes 589856 | tf_op jit(solution)/shard_map/ppermute | solution.py:84
  289.7 5.6 %collective-permute-done.55 = bf16[4,96,256]{2,1,0:T(8,128)(2,1)S(1)} collective-permute-done((bf16[4,96,256]{2,1,0:T(8,128)(2,1)S(1)}, bf16[4,96,256]{2,1,0:T(8,128)(2,1)S(1)}, u32[]{:S(2)}, u32[]{:S(2)}) %collective-permute-start.55) | collective-permute-done | bytes 196640 | tf_op jit(solution)/shard_map/ppermute | solution.py:88
  295.9 3.4 collective-permute-start.60
  300.7 5.4 %list_tokens.1 = s32[1,1152]{1,0:T(1,128)S(1)} custom-call(s32[1,1024]{1,0:T(1,128)S(1)} %bitcast.66), custom_call_target="tpu_custom_call" | custom-call | tf_op jit(solution)/shard_map/list_tokens/pallas_call | solution.py:65
  319.7 3.9 %collective-permute-done.61 = bf16[112,768]{1,0:T(8,128)(2,1)S(1)} collective-permute-done((bf16[112,768]{1,0:T(8,128)(2,1)S(1)}, bf16[112,768]{1,0:T(8,128)(2,1)S(1)}, u32[]{:S(2)}, u32[]{:S(2)}) %collective-permute-start.61) | collective-permute-done | bytes 172064 | tf_op jit(solution)/shard_map/ppermute | solution.py:84
  330.3 7.3 %collective-permute-done.71 = bf16[192,768]{1,0:T(8,128)(2,1)S(1)} collective-permute-done((bf16[192,768]{1,0:T(8,128)(2,1)}, bf16[192,768]{1,0:T(8,128)(2,1)S(1)}, u32[]{:S(2)}, u32[]{:S(2)}) %collective-permute-start.71) | collective-permute-done | bytes 294944 | tf_op jit(solution)/shard_map/ppermute | solution.py:88
  343.9 3.8 %collective-permute-start.66 = (bf16[4,96,256]{2,1,0:T(8,128)(2,1)}, bf16[4,96,256]{2,1,0:T(8,128)(2,1)}, u32[]{:S(2)}, u32[]{:S(2)}) collective-permute-start(bf16[4,96,256]{2,1,0:T(8,128)(2,1)} %slice.166), channel_id=1, source_target_pairs={{0,3},{1,0},{2,1},{3,2},{4,7},{5,4},{6,5},{7,6},{8,11},{9,8},{10,9... | collective-permute-start | bytes 589832 | tf_op jit(solution)/shard_map/ppermute | solution.py:84
  354.3 10.0 %table_grad.1 = f32[96,7632]{1,0:T(8,128)} custom-call(bf16[96,3840]{1,0:T(8,128)(2,1)} %copy-done.7, bf16[96,3840]{1,0:T(8,128)(2,1)} %copy-done.32, bf16[8,96,256]{2,1,0:T(8,128)(2,1)} %copy-done.28, bf16[8,96,256]{2,1,0:T(8,128)(2,1)} %copy-done.31, bf16[8,96,256]{2,1,0:T(8,128)(2,1)} %collective-permute-done.59.refs_4_, bf16[4,96,256]{2,1,0:T(8,128)(2,1)} %copy-done.42, ...), custom_call_target="tpu_custom_call" | custom-call | tf_op jit(solution)/shard_map/table_grad/pallas_call | solution.py:65
  367.1 7.3 %collective-permute-done.73.y_ref = bf16[224,768]{1,0:T(8,128)(2,1)S(1)} collective-permute-done((bf16[224,768]{1,0:T(8,128)(2,1)S(1)}, bf16[224,768]{1,0:T(8,128)(2,1)S(1)}, u32[]{:S(2)}, u32[]{:S(2)}) %collective-permute-start.73) | collective-permute-done | bytes 344096 | tf_op jit(solution)/shard_map/ppermute | solution.py:88
  (343 shorter events, 119.4 us)
Async XLA Ops:
  10.3 16.4 %collective-permute-start = (bf16[192,768]{1,0:T(8,128)(2,1)}, bf16[192,768]{1,0:T(8,128)(2,1)S(1)}, u32[]{:S(2)}, u32[]{:S(2)}) collective-permute-start(bf16[192,768]{1,0:T(8,128)(2,1)} %get-tuple-element.174), channel_id=1, source_target_pairs={{0,1},{1,2},{2,3},{3,0},{4,5},{5,6},{6,7},{7,4},{8,9},{9,10},{10,1... | collective-permute-start | bytes 884744 | tf_op jit(solution)/shard_map/ppermute | solution.py:84
  11.9 14.8 %collective-permute-start.1 = (bf16[192,768]{1,0:T(8,128)(2,1)}, bf16[192,768]{1,0:T(8,128)(2,1)S(1)}, u32[]{:S(2)}, u32[]{:S(2)}) collective-permute-start(bf16[192,768]{1,0:T(8,128)(2,1)} %get-tuple-element.174), channel_id=1, source_target_pairs={{0,3},{1,0},{2,1},{3,2},{4,7},{5,4},{6,5},{7,6},{8,11},{9,8},{10,9... | collective-permute-start | bytes 884744 | tf_op jit(solution)/shard_map/ppermute | solution.py:84
  14.1 39.0 %collective-permute-start.16 = (bf16[2,192,768]{2,1,0:T(8,128)(2,1)}, bf16[2,192,768]{2,1,0:T(8,128)(2,1)}, u32[]{:S(2)}, u32[]{:S(2)}) collective-permute-start(bf16[2,192,768]{2,1,0:T(8,128)(2,1)} %get-tuple-element.192), channel_id=1, source_target_pairs={{0,16},{16,0},{1,17},{17,1},{2,18},{18,2},{3,19},{19,3},{4,20},{20... | collective-permute-start | bytes 1769480 | tf_op jit(solution)/shard_map/ppermute | solution.py:88
  29.0 16.3 %collective-permute-start.6 = (bf16[224,768]{1,0:T(8,128)(2,1)S(1)}, bf16[224,768]{1,0:T(8,128)(2,1)}, u32[]{:S(2)}, u32[]{:S(2)}) collective-permute-start(bf16[224,768]{1,0:T(8,128)(2,1)S(1)} %pad_maximum_fusion.11), channel_id=1, source_target_pairs={{0,3},{1,0},{2,1},{3,2},{4,7},{5,4},{6,5},{7,6},{8,11},{9,8},{10,9... | collective-permute-start | bytes 1032200 | tf_op jit(solution)/shard_map/ppermute | solution.py:84
  30.5 15.0 %collective-permute-start.5 = (bf16[224,768]{1,0:T(8,128)(2,1)}, bf16[224,768]{1,0:T(8,128)(2,1)}, u32[]{:S(2)}, u32[]{:S(2)}) collective-permute-start(bf16[224,768]{1,0:T(8,128)(2,1)} %pad_maximum_fusion.10), channel_id=1, source_target_pairs={{0,1},{1,2},{2,3},{3,0},{4,5},{5,6},{6,7},{7,4},{8,9},{9,10},{10,1... | collective-permute-start | bytes 1032200 | tf_op jit(solution)/shard_map/ppermute | solution.py:84
  32.5 15.9 %collective-permute-start.12 = (bf16[384,768]{1,0:T(8,128)(2,1)}, bf16[384,768]{1,0:T(8,128)(2,1)S(1)}, u32[]{:S(2)}, u32[]{:S(2)}) collective-permute-start(bf16[384,768]{1,0:T(8,128)(2,1)} %constant_dynamic-update-slice_fusion.refs_1_), channel_id=1, source_target_pairs={{0,16},{16,0},{1,17},{17,1},{2,18},{18,2},{3,19},{19,3},{4,20},{20... | collective-permute-start | bytes 1769480 | tf_op jit(solution)/shard_map/ppermute | solution.py:88
  33.5 19.8 %collective-permute-start.9 = (bf16[384,768]{1,0:T(8,128)(2,1)}, bf16[384,768]{1,0:T(8,128)(2,1)}, u32[]{:S(2)}, u32[]{:S(2)}) collective-permute-start(bf16[384,768]{1,0:T(8,128)(2,1)} %constant_dynamic-update-slice_fusion.refs_1_), channel_id=1, source_target_pairs={{0,8},{4,12},{8,0},{12,4},{1,9},{5,13},{9,1},{13,5},{2,10},{6,14},... | collective-permute-start | bytes 1769480 | tf_op jit(solution)/shard_map/ppermute | solution.py:88
  48.6 22.3 %collective-permute-start.13 = (bf16[576,768]{1,0:T(8,128)(2,1)S(1)}, bf16[576,768]{1,0:T(8,128)(2,1)S(1)}, u32[]{:S(2)}, u32[]{:S(2)}) collective-permute-start(bf16[576,768]{1,0:T(8,128)(2,1)S(1)} %pad_maximum_fusion), channel_id=1, source_target_pairs={{0,8},{4,12},{8,0},{12,4},{1,9},{5,13},{9,1},{13,5},{2,10},{6,14},... | collective-permute-start | bytes 2654216 | tf_op jit(solution)/shard_map/ppermute | solution.py:88
  52.9 17.4 %collective-permute-start.10 = (bf16[256,768]{1,0:T(8,128)(2,1)S(1)}, bf16[256,768]{1,0:T(8,128)(2,1)S(1)}, u32[]{:S(2)}, u32[]{:S(2)}) collective-permute-start(bf16[256,768]{1,0:T(8,128)(2,1)S(1)} %pad_maximum_fusion.6), channel_id=1, source_target_pairs={{0,1},{1,2},{2,3},{3,0},{4,5},{5,6},{6,7},{7,4},{8,9},{9,10},{10,1... | collective-permute-start | bytes 1179656 | tf_op jit(solution)/shard_map/ppermute | solution.py:84
  53.2 18.4 %collective-permute-start.7 = (bf16[384,768]{1,0:T(8,128)(2,1)}, bf16[384,768]{1,0:T(8,128)(2,1)S(1)}, u32[]{:S(2)}, u32[]{:S(2)}) collective-permute-start(bf16[384,768]{1,0:T(8,128)(2,1)} %constant_dynamic-update-slice_fusion.refs_1_), channel_id=1, source_target_pairs={{0,4},{4,0},{8,12},{12,8},{1,5},{5,1},{9,13},{13,9},{2,6},{6,2},{1... | collective-permute-start | bytes 1769480 | tf_op jit(solution)/shard_map/ppermute | solution.py:88
  53.2 18.9 %collective-permute-start.17 = (bf16[2,192,768]{2,1,0:T(8,128)(2,1)}, bf16[2,192,768]{2,1,0:T(8,128)(2,1)S(1)}, u32[]{:S(2)}, u32[]{:S(2)}) collective-permute-start(bf16[2,192,768]{2,1,0:T(8,128)(2,1)} %collective-permute-done.16.refs_9_), channel_id=1, source_target_pairs={{0,4},{4,0},{8,12},{12,8},{1,5},{5,1},{9,13},{13,9},{2,6},{6,2},{1... | collective-permute-start | bytes 1769480 | tf_op jit(solution)/shard_map/ppermute | solution.py:88
  82.0 69.3 %collective-permute-start.41 = (s32[4,3,256]{2,1,0:T(4,128)S(1)}, s32[4,3,256]{2,1,0:T(4,128)S(1)}, u32[]{:S(2)}, u32[]{:S(2)}) collective-permute-start(s32[4,3,256]{2,1,0:T(4,128)S(1)} %pad_add_fusion.2.i_ref.refs_13_), channel_id=1, source_target_pairs={{0,4},{4,0},{8,12},{12,8},{1,5},{5,1},{9,13},{13,9},{2,6},{6,2},{1... | collective-permute-start | bytes 36872 | tf_op jit(solution)/shard_map/ppermute | solution.py:88
  103.3 18.9 %collective-permute-start.26 = (bf16[256,768]{1,0:T(8,128)(2,1)}, bf16[256,768]{1,0:T(8,128)(2,1)S(1)}, u32[]{:S(2)}, u32[]{:S(2)}) collective-permute-start(bf16[256,768]{1,0:T(8,128)(2,1)} %get-tuple-element.194.refs_0_), channel_id=1, source_target_pairs={{0,1},{1,2},{2,3},{3,0},{4,5},{5,6},{6,7},{7,4},{8,9},{9,10},{10,1... | collective-permute-start | bytes 1179656 | tf_op jit(solution)/shard_map/ppermute | solution.py:84
  120.6 44.9 %collective-permute-start.35 = (bf16[256,768]{1,0:T(8,128)(2,1)}, bf16[256,768]{1,0:T(8,128)(2,1)S(1)}, u32[]{:S(2)}, u32[]{:S(2)}) collective-permute-start(bf16[256,768]{1,0:T(8,128)(2,1)} %get-tuple-element.194.refs_0_), channel_id=1, source_target_pairs={{0,4},{4,0},{8,12},{12,8},{1,5},{5,1},{9,13},{13,9},{2,6},{6,2},{1... | collective-permute-start | bytes 1179656 | tf_op jit(solution)/shard_map/ppermute | solution.py:88
  121.6 33.4 %collective-permute-start.24 = (bf16[256,768]{1,0:T(8,128)(2,1)S(1)}, bf16[256,768]{1,0:T(8,128)(2,1)S(1)}, u32[]{:S(2)}, u32[]{:S(2)}) collective-permute-start(bf16[256,768]{1,0:T(8,128)(2,1)S(1)} %broadcast_select_fusion.1), channel_id=1, source_target_pairs={{0,16},{16,0},{1,17},{17,1},{2,18},{18,2},{3,19},{19,3},{4,20},{20... | collective-permute-start | bytes 1179656 | tf_op jit(solution)/shard_map/ppermute | solution.py:88
  141.7 26.6 %collective-permute-start.36 = (bf16[256,768]{1,0:T(8,128)(2,1)S(1)}, bf16[256,768]{1,0:T(8,128)(2,1)}, u32[]{:S(2)}, u32[]{:S(2)}) collective-permute-start(bf16[256,768]{1,0:T(8,128)(2,1)S(1)} %collective-permute-done.25.refs_0_.refs_1_), channel_id=1, source_target_pairs={{0,4},{4,0},{8,12},{12,8},{1,5},{5,1},{9,13},{13,9},{2,6},{6,2},{1... | collective-permute-start | bytes 1179656 | tf_op jit(solution)/shard_map/ppermute | solution.py:88
  141.8 30.8 %collective-permute-start.39 = (bf16[256,768]{1,0:T(8,128)(2,1)S(1)}, bf16[256,768]{1,0:T(8,128)(2,1)}, u32[]{:S(2)}, u32[]{:S(2)}) collective-permute-start(bf16[256,768]{1,0:T(8,128)(2,1)S(1)} %collective-permute-done.26.refs_0_.refs_4_), channel_id=1, source_target_pairs={{0,4},{4,0},{8,12},{12,8},{1,5},{5,1},{9,13},{13,9},{2,6},{6,2},{1... | collective-permute-start | bytes 1179656 | tf_op jit(solution)/shard_map/ppermute | solution.py:88
  168.3 38.5 %collective-permute-start.32 = (bf16[256,768]{1,0:T(8,128)(2,1)}, bf16[256,768]{1,0:T(8,128)(2,1)S(1)}, u32[]{:S(2)}, u32[]{:S(2)}) collective-permute-start(bf16[256,768]{1,0:T(8,128)(2,1)} %copy-done.21), channel_id=1, source_target_pairs={{0,1},{1,2},{2,3},{3,0},{4,5},{5,6},{6,7},{7,4},{8,9},{9,10},{10,1... | collective-permute-start | bytes 1179656 | tf_op jit(solution)/shard_map/ppermute | solution.py:84
  168.3 38.5 %collective-permute-start.33 = (bf16[256,768]{1,0:T(8,128)(2,1)}, bf16[256,768]{1,0:T(8,128)(2,1)S(1)}, u32[]{:S(2)}, u32[]{:S(2)}) collective-permute-start(bf16[256,768]{1,0:T(8,128)(2,1)} %copy-done.20), channel_id=1, source_target_pairs={{0,3},{1,0},{2,1},{3,2},{4,7},{5,4},{6,5},{7,6},{8,11},{9,8},{10,9... | collective-permute-start | bytes 1179656 | tf_op jit(solution)/shard_map/ppermute | solution.py:84
  172.6 34.2 %collective-permute-start.34 = (bf16[256,768]{1,0:T(8,128)(2,1)S(1)}, bf16[256,768]{1,0:T(8,128)(2,1)S(1)}, u32[]{:S(2)}, u32[]{:S(2)}) collective-permute-start(bf16[256,768]{1,0:T(8,128)(2,1)S(1)} %get-tuple-element.214), channel_id=1, source_target_pairs={{0,2},{1,3},{2,0},{3,1},{4,6},{5,7},{6,4},{7,5},{8,10},{9,11},{10,... | collective-permute-start | bytes 1179656 | tf_op jit(solution)/shard_map/ppermute | solution.py:84
  204.7 38.2 %collective-permute-start.44 = (bf16[2,96,3840]{2,1,0:T(8,128)(2,1)}, bf16[2,96,3840]{2,1,0:T(8,128)(2,1)S(1)}, u32[]{:S(2)}, u32[]{:S(2)}) collective-permute-start(bf16[2,96,3840]{2,1,0:T(8,128)(2,1)} %get-tuple-element.257), channel_id=1, source_target_pairs={{0,16},{16,0},{1,17},{17,1},{2,18},{18,2},{3,19},{19,3},{4,20},{20... | collective-permute-start | bytes 4423688 | tf_op jit(solution)/shard_map/ppermute | solution.py:88
  206.2 36.7 %collective-permute-start.45 = (bf16[2,96,3840]{2,1,0:T(8,128)(2,1)}, bf16[2,96,3840]{2,1,0:T(8,128)(2,1)S(1)}, u32[]{:S(2)}, u32[]{:S(2)}) collective-permute-start(bf16[2,96,3840]{2,1,0:T(8,128)(2,1)} %get-tuple-element.258), channel_id=1, source_target_pairs={{0,8},{4,12},{8,0},{12,4},{1,9},{5,13},{9,1},{13,5},{2,10},{6,14},... | collective-permute-start | bytes 4423688 | tf_op jit(solution)/shard_map/ppermute | solution.py:88
  239.1 16.1 %collective-permute-start.47 = (bf16[192,768]{1,0:T(8,128)(2,1)}, bf16[192,768]{1,0:T(8,128)(2,1)S(1)}, u32[]{:S(2)}, u32[]{:S(2)}) collective-permute-start(bf16[192,768]{1,0:T(8,128)(2,1)} %get-tuple-element.253), channel_id=1, source_target_pairs={{0,1},{1,2},{2,3},{3,0},{4,5},{5,6},{6,7},{7,4},{8,9},{9,10},{10,1... | collective-permute-start | bytes 884744 | tf_op jit(solution)/shard_map/ppermute | solution.py:84
  239.9 16.2 %collective-permute-start.48 = (bf16[192,768]{1,0:T(8,128)(2,1)}, bf16[192,768]{1,0:T(8,128)(2,1)S(1)}, u32[]{:S(2)}, u32[]{:S(2)}) collective-permute-start(bf16[192,768]{1,0:T(8,128)(2,1)} %get-tuple-element.254), channel_id=1, source_target_pairs={{0,3},{1,0},{2,1},{3,2},{4,7},{5,4},{6,5},{7,6},{8,11},{9,8},{10,9... | collective-permute-start | bytes 884744 | tf_op jit(solution)/shard_map/ppermute | solution.py:84
  258.6 15.4 %collective-permute-start.50 = (bf16[384,768]{1,0:T(8,128)(2,1)S(1)}, bf16[384,768]{1,0:T(8,128)(2,1)S(1)}, u32[]{:S(2)}, u32[]{:S(2)}) collective-permute-start(bf16[384,768]{1,0:T(8,128)(2,1)S(1)} %pad_maximum_fusion.2), channel_id=1, source_target_pairs={{0,3},{1,0},{2,1},{3,2},{4,7},{5,4},{6,5},{7,6},{8,11},{9,8},{10,9... | collective-permute-start | bytes 1769480 | tf_op jit(solution)/shard_map/ppermute | solution.py:84
  259.7 27.7 %collective-permute-start.49 = (bf16[384,768]{1,0:T(8,128)(2,1)S(1)}, bf16[384,768]{1,0:T(8,128)(2,1)S(1)}, u32[]{:S(2)}, u32[]{:S(2)}) collective-permute-start(bf16[384,768]{1,0:T(8,128)(2,1)S(1)} %pad_maximum_fusion.1), channel_id=1, source_target_pairs={{0,1},{1,2},{2,3},{3,0},{4,5},{5,6},{6,7},{7,4},{8,9},{9,10},{10,1... | collective-permute-start | bytes 1769480 | tf_op jit(solution)/shard_map/ppermute | solution.py:84
  270.5 44.0 %collective-permute-start.58 = (bf16[4,224,768]{2,1,0:T(8,128)(2,1)S(1)}, bf16[4,224,768]{2,1,0:T(8,128)(2,1)S(1)}, u32[]{:S(2)}, u32[]{:S(2)}) collective-permute-start(bf16[4,224,768]{2,1,0:T(8,128)(2,1)S(1)} %get-tuple-element.301), channel_id=1, source_target_pairs={{0,8},{4,12},{8,0},{12,4},{1,9},{5,13},{9,1},{13,5},{2,10},{6,14},... | collective-permute-start | bytes 4128776 | tf_op jit(solution)/shard_map/ppermute | solution.py:88
  288.7 25.8 %collective-permute-start.46 = (bf16[256,768]{1,0:T(8,128)(2,1)S(1)}, bf16[256,768]{1,0:T(8,128)(2,1)S(1)}, u32[]{:S(2)}, u32[]{:S(2)}) collective-permute-start(bf16[256,768]{1,0:T(8,128)(2,1)S(1)} %select_convert_fusion), channel_id=1, source_target_pairs={{0,16},{16,0},{1,17},{17,1},{2,18},{18,2},{3,19},{19,3},{4,20},{20... | collective-permute-start | bytes 1179656 | tf_op jit(solution)/shard_map/ppermute | solution.py:88
  295.9 16.9 %collective-permute-start.60 = (bf16[8,96,256]{2,1,0:T(8,128)(2,1)S(1)}, bf16[8,96,256]{2,1,0:T(8,128)(2,1)S(1)}, u32[]{:S(2)}, u32[]{:S(2)}) collective-permute-start(bf16[8,96,256]{2,1,0:T(8,128)(2,1)S(1)} %pad_maximum_fusion.9.refs_2_), channel_id=1, source_target_pairs={{0,3},{1,0},{2,1},{3,2},{4,7},{5,4},{6,5},{7,6},{8,11},{9,8},{10,9... | collective-permute-start | bytes 1179656 | tf_op jit(solution)/shard_map/ppermute | solution.py:84
  309.4 38.3 %collective-permute-start.56 = (bf16[96,3840]{1,0:T(8,128)(2,1)}, bf16[96,3840]{1,0:T(8,128)(2,1)S(1)}, u32[]{:S(2)}, u32[]{:S(2)}) collective-permute-start(bf16[96,3840]{1,0:T(8,128)(2,1)} %get-tuple-element.297), channel_id=1, source_target_pairs={{0,8},{4,12},{8,0},{12,4},{1,9},{5,13},{9,1},{13,5},{2,10},{6,14},... | collective-permute-start | bytes 2211848 | tf_op jit(solution)/shard_map/ppermute | solution.py:88
  313.5 34.2 %collective-permute-start.57 = (bf16[96,3840]{1,0:T(8,128)(2,1)}, bf16[96,3840]{1,0:T(8,128)(2,1)S(1)}, u32[]{:S(2)}, u32[]{:S(2)}) collective-permute-start(bf16[96,3840]{1,0:T(8,128)(2,1)} %get-tuple-element.299), channel_id=1, source_target_pairs={{0,16},{16,0},{1,17},{17,1},{2,18},{18,2},{3,19},{19,3},{4,20},{20... | collective-permute-start | bytes 2211848 | tf_op jit(solution)/shard_map/ppermute | solution.py:88
  326.3 17.6 %collective-permute-start.70 = (bf16[224,768]{1,0:T(8,128)(2,1)}, bf16[224,768]{1,0:T(8,128)(2,1)}, u32[]{:S(2)}, u32[]{:S(2)}) collective-permute-start(bf16[224,768]{1,0:T(8,128)(2,1)} %pad_maximum_fusion.13), channel_id=1, source_target_pairs={{0,3},{1,0},{2,1},{3,2},{4,7},{5,4},{6,5},{7,6},{8,11},{9,8},{10,9... | collective-permute-start | bytes 1032200 | tf_op jit(solution)/shard_map/ppermute | solution.py:84
  (106 other events, 1008.8 us)

commit v8 on v7

--- a/solution.py
+++ b/solution.py
@@ -536,16 +536,18 @@
     keys = ["n1", "stats", "small", "att", "q", "k", "v", "p", "x"] + (["n0"] if first else [])
     loads = Loads({"dm": d_middle, **{key: state[key] for key in keys}, "grads": small_in, **({"seg": seg_row} if first else {})})
     rows = z.part + (2 * z.extra if first else 0)
-    outs = [like((seq, d), F32), like((seq, d), BF16)] + [like((z.shards, rows, d), BF16)] * 2
+    outs = [like((seq, d), F32)] + [like((z.shards, rows, d), BF16)] * 2
     blocks = 2 * lax.axis_size("dp")
     if first:
         outs.append(like((blocks, d // blocks, seq), BF16))
+    else:
+        outs.append(like((seq, d), BF16))
 
     def kernel(*refs):
         piece_refs, refs = refs[: len(pieces.arrays)], refs[len(pieces.arrays) :]
         load_refs, refs = refs[: len(loads.names)], refs[len(loads.names) :]
-        dx_ref, low_ref, keep_ref, send_ref = refs[:4]
-        de_ref = refs[4] if first else None
+        dx_ref, keep_ref, send_ref, last_ref = refs[:4]
+        de_ref = last_ref if first else None
         w_ref, sems, g_ref, out_sems, *buffers = refs[len(outs) :]
         loads.start(load_refs, buffers)
         waits = pieces.start(piece_refs, w_ref, sems, (0,))
@@ -639,7 +641,8 @@
                         g_ref[side, h, row : row + z.extra, :] = part
         copies = send_halves(z, g_ref, keep_ref, send_ref, out_sems)
         dx_ref[...] = d_in
-        low_ref[...] = d_in.astype(BF16)
+        if not first:
+            last_ref[...] = d_in.astype(BF16)
         wait_all(copies)
 
     anywhere = pl.BlockSpec(memory_space=pl.ANY)
@@ -649,7 +652,7 @@
         outs,
         (*pieces.arrays, *loads.arrays),
         specs=pieces.specs + loads.specs,
-        out_specs=[vmem, vmem, anywhere, anywhere] + [vmem] * (len(outs) - 4),
+        out_specs=[vmem, anywhere, anywhere, vmem],
         scratch=pieces.scratch + [pltpu.VMEM((2, z.shards, rows, d), BF16), pltpu.SemaphoreType.DMA((2 * z.shards,))] + loads.scratch,
         flops=13 * 10**9,
         name="att_back",
@@ -1164,7 +1167,7 @@
         dense = [lax.psum_scatter(dense, both, scatter_dimension=0, tiled=True)]
     d_middle, small_grads, keep_f, send_f = ffn_backward(z, weights_two, two, dy_terms)
 
-    in_two, in_low, keep_a, send_a = attention_backward(z, weights_two, two, d_middle, small_grads, False)
+    in_two, keep_a, send_a, in_low = attention_backward(z, weights_two, two, d_middle, small_grads, False)
     came_f, came_a = crossed(send_f, "dp", 1), crossed(send_a, "dp", 1)
     d_middle, small_grads, keep_one_f, send_one_f = ffn_backward(z, weights_one, one, [in_low])
     keep_f, came_f, keep_a, came_a = after((keep_f, came_f, keep_a, came_a), d_middle)
@@ -1174,7 +1177,7 @@
     if dp == 4:
         d_middle, came_x, came_y = after((d_middle, came_x, came_y), ())
     came_one_f = crossed(send_one_f, "dp", 1)
-    in_one, in_one_low, keep_one_a, send_one_a, d_embed = attention_backward(z, weights_one, one, d_middle, small_grads, True, seg_row, pos_rows)
+    in_one, keep_one_a, send_one_a, d_embed = attention_backward(z, weights_one, one, d_middle, small_grads, True, seg_row, pos_rows)
     keep_one_f, came_one_f = after((keep_one_f, came_one_f), d_embed)
     send_one_a, d_embed = after((send_one_a, d_embed), terms_two)
     came_one_a = crossed(send_one_a, "dp", 1)

time: 385 us -> 385 us (level)
  no operation moved by 1% of the time
where the time goes in v8:
time: 385 us; the launch traced here: 378 us
  Pallas kernels  153 us (40%)
  waiting for transfers between devices  83.6 us (22%)
  starting transfers between devices  79 us (21%)
  local copies, waits for them, and re-layouts  49.1 us (13%)
  other arithmetic  11 us (3%)
    pallas_call x22, Pallas kernels, call(): pl.pallas_call(kernel, out_shape=outs, in_specs=[vmem if s is None else s...  121 us
    ppermute x31, starting transfers between devices, turned(): lax.ppermute(block, axis, [(i, (i + by) % size) for i in range(size)])  49.7 us
    ppermute x31, waiting for transfers between devices, turned(): lax.ppermute(block, axis, [(i, (i + by) % size) for i in range(size)])  46.8 us
    ppermute x45, waiting for transfers between devices, crossed(): lax.ppermute(block, axis, [(i, i ^ bit) for i in range(lax.axis_size(axis...  36.7 us
    pallas_call x1, Pallas kernels, head_table(): pl.pallas_call(kernel, out_shape=outs, grid_spec=pltpu.PrefetchScalarGrid...  32 us
    ppermute x45, starting transfers between devices, crossed(): lax.ppermute(block, axis, [(i, i ^ bit) for i in range(lax.axis_size(axis...  29.3 us
    gather x2, local copies, waits for them, and re-layouts, rows_of(): word_table.at[jnp.clip(ids.reshape(-1) - offset, 0, vocab - 1)]  20.7 us
    unnamed x128, local copies, waits for them, and re-layouts  16.5 us
  transfers between devices with their start and end apart: 76, of which 24 were waited for; matrix products, arithmetic and copies ran while one was open for 11% of the time, Pallas kernels for 39%

profile of v8, /device:TPU:0, one launch (start us, length us, event | category | flops | bytes accessed | tf_op | source)
XLA Modules:
  0.0 378.2 jit_solution(4313161355526921312)
XLA Ops:
  16.3 10.4 %gather_fusion = bf16[1024,768]{1,0:T(8,128)(2,1)S(1)} fusion(bf16[7632,768]{1,0:T(8,128)(2,1)} %refs_10_.1, s32[1024]{0:T(1024)S(1)} %broadcast_clamp_fusion.1), kind=kCustom, calls=%fused_computation | custom fusion | bytes 3149824 | tf_op jit(solution)/shard_map/gather | solution.py:1101
  35.0 10.3 %gather_fusion.1 = bf16[1024,768]{1,0:T(8,128)(2,1)S(1)} fusion(bf16[7632,768]{1,0:T(8,128)(2,1)} %refs_10_.1, s32[1024]{0:T(1024)S(1)} %broadcast_clamp_fusion), kind=kCustom, calls=%fused_computation.1 | custom fusion | bytes 3149824 | tf_op jit(solution)/shard_map/gather | solution.py:1101
  53.8 8.7 %collective-permute-done.11.refs_22_ = bf16[256,768]{1,0:T(8,128)(2,1)S(1)} collective-permute-done((bf16[256,768]{1,0:T(8,128)(2,1)S(1)}, bf16[256,768]{1,0:T(8,128)(2,1)S(1)}, u32[]{:S(2)}, u32[]{:S(2)}) %collective-permute-start.11) | collective-permute-done | bytes 393248 | tf_op jit(solution)/shard_map/ppermute | solution.py:84
  63.6 6.7 %collective-permute-done.10.refs_21_ = bf16[256,768]{1,0:T(8,128)(2,1)S(1)} collective-permute-done((bf16[256,768]{1,0:T(8,128)(2,1)S(1)}, bf16[256,768]{1,0:T(8,128)(2,1)S(1)}, u32[]{:S(2)}, u32[]{:S(2)}) %collective-permute-start.10) | collective-permute-done | bytes 393248 | tf_op jit(solution)/shard_map/ppermute | solution.py:84
  72.4 7.6 %collective-permute-done.21.refs_16_ = bf16[192,768]{1,0:T(8,128)(2,1)} collective-permute-done((bf16[192,768]{1,0:T(8,128)(2,1)S(1)}, bf16[192,768]{1,0:T(8,128)(2,1)}, u32[]{:S(2)}, u32[]{:S(2)}) %collective-permute-start.21) | collective-permute-done | bytes 294944 | tf_op jit(solution)/shard_map/ppermute | solution.py:88
  82.5 10.5 %layer_first.1 = (bf16[256,768]{1,0:T(8,128)(2,1)}, bf16[256,768]{1,0:T(8,128)(2,1)}, bf16[256,768]{1,0:T(8,128)(2,1)}, bf16[12,256,256]{2,1,0:T(8,128)(2,1)}, b...) custom-call(bf16[2,2,192,768]{3,2,1,0:T(8,128)(2,1)} %get-tuple-elem, ...), custom_call_target="tpu_custom_call" | custom-call | flops 12000000000 | tf_op jit(solution)/shard_map/layer_first/pallas_call | solution.py:65
  93.0 10.2 %layer_second.1 = (bf16[256,768]{1,0:T(8,128)(2,1)}, bf16[256,768]{1,0:T(8,128)(2,1)}, bf16[256,768]{1,0:T(8,128)(2,1)}, bf16[12,256,256]{2,1,0:T(8,128)(2,1)}, ...) custom-call(bf16[2,2,192,768]{3,2,1,0:T(8,128)(2,1)} %get-tuple-elem, ...), custom_call_target="tpu_custom_call" | custom-call | flops 12000000000 | tf_op jit(solution)/shard_map/layer_second/pallas_call | solution.py:65
  104.8 4.3 %copy-done = bf16[7632,768]{1,0:T(8,128)(2,1)S(1)} copy-done((bf16[7632,768]{1,0:T(8,128)(2,1)S(1)}, bf16[7632,768]{1,0:T(8,128)(2,1)}, u32[]{:S(2)}) %copy-start) | copy-done | bytes 11722776
  109.1 9.0 %head_forward.4 = (f32[256,768]{1,0:T(8,128)S(1)}, f32[8,256]{1,0:T(8,128)S(1)}) custom-call(bf16[256,768]{1,0:T(8,128)(2,1)} %get-tuple-element.194.refs_0_, bf16[7632,768]{1,0:T(8,128)(2,1)S(1)} %copy-done), custom_call_target="tpu_custom_call" | custom-call | flops 11000000512 | tf_op jit(solution)/shard_map/head_forward/pallas_call | solution.py:65
  122.2 8.0 %head_forward.5 = (f32[256,768]{1,0:T(8,128)S(1)}, f32[8,256]{1,0:T(8,128)S(1)}) custom-call(bf16[256,768]{1,0:T(8,128)(2,1)S(1)} %collective-permute-done.26.refs_0_.refs_4_, bf16[7632,768]{1,0:T(8,128)(2,1)S(1)} %copy-done), custom_call_target="tpu_custom_call" | custom-call | flops 11000000512 | tf_op jit(solution)/shard_map/head_forward/pallas_call | solution.py:65
  130.3 3.1 collective-permute-start.28
  133.6 8.0 %head_forward.6 = (f32[256,768]{1,0:T(8,128)S(1)}, f32[8,256]{1,0:T(8,128)S(1)}) custom-call(bf16[256,768]{1,0:T(8,128)(2,1)S(1)} %collective-permute-done.25.refs_0_.refs_1_, bf16[7632,768]{1,0:T(8,128)(2,1)S(1)} %copy-done), custom_call_target="tpu_custom_call" | custom-call | flops 11000000512 | tf_op jit(solution)/shard_map/head_forward/pallas_call | solution.py:65
  142.3 8.9 %head_forward.7 = (f32[256,768]{1,0:T(8,128)S(1)}, f32[8,256]{1,0:T(8,128)S(1)}) custom-call(bf16[128,768]{1,0:T(8,128)(2,1)} %collective-permute-done.27.refs_0_.refs_2_, bf16[128,768]{1,0:T(8,128)(2,1)S(1)} %collective-permute-done.28.refs_1_.refs_3_, bf16[7632,768]{1,0:T(8,128)(2,1)S(1)} %copy-done), custom_call_target="tpu_custom_call" | custom-call | flops 11000000512 | tf_op jit(solution)/shard_map/head_forward/pallas_call | solution.py:65
  151.3 3.8 %collective-permute-start.29 = (f32[1,1024]{1,0:T(1,128)S(1)}, f32[1,1024]{1,0:T(1,128)S(1)}, u32[]{:S(2)}, u32[]{:S(2)}) collective-permute-start(f32[1,1024]{1,0:T(1,128)S(1)} %pad_maximum_fusion.15.a_ref), channel_id=1, source_target_pairs={{0,3},{1,0},{2,1},{3,2},{4,7},{5,4},{6,5},{7,6},{8,11},{9,8},{10,9... | collective-permute-start | bytes 12296 | tf_op jit(solution)/shard_map/ppermute | solution.py:84
  156.4 3.2 collective-permute-done.30.c_ref
  168.3 4.3 %collective-permute-start.33 = (bf16[256,768]{1,0:T(8,128)(2,1)}, bf16[256,768]{1,0:T(8,128)(2,1)S(1)}, u32[]{:S(2)}, u32[]{:S(2)}) collective-permute-start(bf16[256,768]{1,0:T(8,128)(2,1)} %copy-done.20), channel_id=1, source_target_pairs={{0,3},{1,0},{2,1},{3,2},{4,7},{5,4},{6,5},{7,6},{8,11},{9,8},{10,9... | collective-permute-start | bytes 1179656 | tf_op jit(solution)/shard_map/ppermute | solution.py:84
  172.7 32.0 %head_table.1 = (bf16[2,96,3840]{2,1,0:T(8,128)(2,1)}, bf16[2,96,3840]{2,1,0:T(8,128)(2,1)}, bf16[2,96,3840]{2,1,0:T(8,128)(2,1)}, bf16[2,96,3840]{2,1,0:T(8,128)(2,1)}) custom-call(s32[1]{0:T(128)} %bitcast.18.core_ref, bf16[256,768]{1,0:T(8,128)(2,1)} %get-tuple-element.194.refs_0_, bf16[256,768]{1,0:T(8,128)(2,1)} %copy-done.16, ...), custom_call_target="tpu_custom_call" | custom-call | flops 32000000000 | tf_op jit(solution)/shard_map/head_table/pallas_call | solution.py:888
  207.9 8.5 %ffn_back.2 = (f32[256,768]{1,0:T(8,128)}, f32[16,768]{1,0:T(8,128)}, bf16[4,192,768]{2,1,0:T(8,128)(2,1)}, bf16[4,192,768]{2,1,0:T(8,128)(2,1)}) custom-call(bf16[2,2,192,768]{3,2,1,0:T(8,128)(2,1)} %get-tuple-element.173.refs_0_, bf16[384,768]{1,0:T(8,128)(2,1)} %constant_dynamic-update-slice_fusion.refs_1_, bf16[192,768]{1,0:T(8,128)(2,1)} %copy-done.40, ...), custom_call_target="tpu_custom_call" | custom-call | flops 8999999488 | tf_op jit(solution)/shard_map/ffn_back/pallas_call | solution.py:65
  216.4 10.8 %att_back.2 = (f32[256,768]{1,0:T(8,128)}, bf16[4,192,768]{2,1,0:T(8,128)(2,1)}, bf16[4,192,768]{2,1,0:T(8,128)(2,1)}, bf16[256,768]{1,0:T(8,128)(2,1)}) custom-call(bf16[2,2,192,768]{3,2,1,0:T(8,128)(2,1)} %get-tuple-element.173.refs_0_, bf16[384,768]{1,0:T(8,128)(2,1)} %constant_dynamic-update-slice_fusion.refs_1_, bf16[192,768]{1,0:T(8,128)(2,1)} %copy-done.40, ...), custom_call_target="tpu_custom_call" | custom-call | flops 12999999488 | tf_op jit(solution)/shard_map/att_back/pallas_call | solution.py:65
  227.7 8.6 %ffn_back.3 = (f32[256,768]{1,0:T(8,128)}, f32[16,768]{1,0:T(8,128)}, bf16[4,192,768]{2,1,0:T(8,128)(2,1)}, bf16[4,192,768]{2,1,0:T(8,128)(2,1)}) custom-call(bf16[2,2,192,768]{3,2,1,0:T(8,128)(2,1)} %get-tuple-element.173.refs_0_, bf16[384,768]{1,0:T(8,128)(2,1)} %constant_dynamic-update-slice_fusion.refs_1_, bf16[192,768]{1,0:T(8,128)(2,1)} %copy-done.40, ...), custom_call_target="tpu_custom_call" | custom-call | flops 8999999488 | tf_op jit(solution)/shard_map/ffn_back/pallas_call | solution.py:65
  239.9 3.0 collective-permute-start.48
  242.9 12.1 %att_back.3 = (f32[256,768]{1,0:T(8,128)}, bf16[4,256,768]{2,1,0:T(8,128)(2,1)}, bf16[4,256,768]{2,1,0:T(8,128)(2,1)}, bf16[8,96,256]{2,1,0:T(8,128)(2,1)}) custom-call(bf16[2,2,192,768]{3,2,1,0:T(8,128)(2,1)} %get-tuple-element.173.refs_0_, bf16[384,768]{1,0:T(8,128)(2,1)} %constant_dynamic-update-slice_fusion.refs_1_, bf16[192,768]{1,0:T(8,128)(2,1)} %copy-done.40, ...), custom_call_target="tpu_custom_call" | custom-call | flops 12999999488 | tf_op jit(solution)/shard_map/att_back/pallas_call | solution.py:65
  265.4 4.5 %collective-permute-done.52 = bf16[2,2,96,256]{3,2,0,1:T(8,128)(2,1)S(1)} collective-permute-done((bf16[2,2,96,256]{3,2,0,1:T(8,128)(2,1)S(1)}, bf16[2,2,96,256]{3,2,0,1:T(8,128)(2,1)S(1)}, u32[]{:S(2)}, u32[]{:S(2)}) %collective-permute-start.52) | collective-permute-done | bytes 196640 | tf_op jit(solution)/shard_map/ppermute | solution.py:88
  273.9 13.5 %collective-permute-done.49.b_ref = bf16[384,768]{1,0:T(8,128)(2,1)S(1)} collective-permute-done((bf16[384,768]{1,0:T(8,128)(2,1)S(1)}, bf16[384,768]{1,0:T(8,128)(2,1)S(1)}, u32[]{:S(2)}, u32[]{:S(2)}) %collective-permute-start.49) | collective-permute-done | bytes 589856 | tf_op jit(solution)/shard_map/ppermute | solution.py:84
  289.7 5.6 %collective-permute-done.55 = bf16[4,96,256]{2,1,0:T(8,128)(2,1)S(1)} collective-permute-done((bf16[4,96,256]{2,1,0:T(8,128)(2,1)S(1)}, bf16[4,96,256]{2,1,0:T(8,128)(2,1)S(1)}, u32[]{:S(2)}, u32[]{:S(2)}) %collective-permute-start.55) | collective-permute-done | bytes 196640 | tf_op jit(solution)/shard_map/ppermute | solution.py:88
  295.9 3.4 collective-permute-start.60
  300.7 5.4 %list_tokens.1 = s32[1,1152]{1,0:T(1,128)S(1)} custom-call(s32[1,1024]{1,0:T(1,128)S(1)} %bitcast.66), custom_call_target="tpu_custom_call" | custom-call | tf_op jit(solution)/shard_map/list_tokens/pallas_call | solution.py:65
  319.7 3.9 %collective-permute-done.61 = bf16[112,768]{1,0:T(8,128)(2,1)S(1)} collective-permute-done((bf16[112,768]{1,0:T(8,128)(2,1)S(1)}, bf16[112,768]{1,0:T(8,128)(2,1)S(1)}, u32[]{:S(2)}, u32[]{:S(2)}) %collective-permute-start.61) | collective-permute-done | bytes 172064 | tf_op jit(solution)/shard_map/ppermute | solution.py:84
  330.3 7.3 %collective-permute-done.71 = bf16[192,768]{1,0:T(8,128)(2,1)S(1)} collective-permute-done((bf16[192,768]{1,0:T(8,128)(2,1)}, bf16[192,768]{1,0:T(8,128)(2,1)S(1)}, u32[]{:S(2)}, u32[]{:S(2)}) %collective-permute-start.71) | collective-permute-done | bytes 294944 | tf_op jit(solution)/shard_map/ppermute | solution.py:88
  343.9 3.8 %collective-permute-start.66 = (bf16[4,96,256]{2,1,0:T(8,128)(2,1)}, bf16[4,96,256]{2,1,0:T(8,128)(2,1)}, u32[]{:S(2)}, u32[]{:S(2)}) collective-permute-start(bf16[4,96,256]{2,1,0:T(8,128)(2,1)} %slice.166), channel_id=1, source_target_pairs={{0,3},{1,0},{2,1},{3,2},{4,7},{5,4},{6,5},{7,6},{8,11},{9,8},{10,9... | collective-permute-start | bytes 589832 | tf_op jit(solution)/shard_map/ppermute | solution.py:84
  354.3 9.9 %table_grad.1 = f32[96,7632]{1,0:T(8,128)} custom-call(bf16[96,3840]{1,0:T(8,128)(2,1)} %copy-done.7, bf16[96,3840]{1,0:T(8,128)(2,1)} %copy-done.32, bf16[8,96,256]{2,1,0:T(8,128)(2,1)} %copy-done.28, bf16[8,96,256]{2,1,0:T(8,128)(2,1)} %copy-done.31, bf16[8,96,256]{2,1,0:T(8,128)(2,1)} %collective-permute-done.59.refs_4_, bf16[4,96,256]{2,1,0:T(8,128)(2,1)} %copy-done.42, ...), custom_call_target="tpu_custom_call" | custom-call | tf_op jit(solution)/shard_map/table_grad/pallas_call | solution.py:65
  367.0 7.3 %collective-permute-done.73.y_ref = bf16[224,768]{1,0:T(8,128)(2,1)S(1)} collective-permute-done((bf16[224,768]{1,0:T(8,128)(2,1)S(1)}, bf16[224,768]{1,0:T(8,128)(2,1)S(1)}, u32[]{:S(2)}, u32[]{:S(2)}) %collective-permute-start.73) | collective-permute-done | bytes 344096 | tf_op jit(solution)/shard_map/ppermute | solution.py:88
  (343 shorter events, 119.4 us)
Async XLA Ops:
  10.3 16.4 %collective-permute-start = (bf16[192,768]{1,0:T(8,128)(2,1)}, bf16[192,768]{1,0:T(8,128)(2,1)S(1)}, u32[]{:S(2)}, u32[]{:S(2)}) collective-permute-start(bf16[192,768]{1,0:T(8,128)(2,1)} %get-tuple-element.174), channel_id=1, source_target_pairs={{0,1},{1,2},{2,3},{3,0},{4,5},{5,6},{6,7},{7,4},{8,9},{9,10},{10,1... | collective-permute-start | bytes 884744 | tf_op jit(solution)/shard_map/ppermute | solution.py:84
  11.9 14.8 %collective-permute-start.1 = (bf16[192,768]{1,0:T(8,128)(2,1)}, bf16[192,768]{1,0:T(8,128)(2,1)S(1)}, u32[]{:S(2)}, u32[]{:S(2)}) collective-permute-start(bf16[192,768]{1,0:T(8,128)(2,1)} %get-tuple-element.174), channel_id=1, source_target_pairs={{0,3},{1,0},{2,1},{3,2},{4,7},{5,4},{6,5},{7,6},{8,11},{9,8},{10,9... | collective-permute-start | bytes 884744 | tf_op jit(solution)/shard_map/ppermute | solution.py:84
  14.1 39.0 %collective-permute-start.16 = (bf16[2,192,768]{2,1,0:T(8,128)(2,1)}, bf16[2,192,768]{2,1,0:T(8,128)(2,1)}, u32[]{:S(2)}, u32[]{:S(2)}) collective-permute-start(bf16[2,192,768]{2,1,0:T(8,128)(2,1)} %get-tuple-element.192), channel_id=1, source_target_pairs={{0,16},{16,0},{1,17},{17,1},{2,18},{18,2},{3,19},{19,3},{4,20},{20... | collective-permute-start | bytes 1769480 | tf_op jit(solution)/shard_map/ppermute | solution.py:88
  29.0 16.3 %collective-permute-start.6 = (bf16[224,768]{1,0:T(8,128)(2,1)S(1)}, bf16[224,768]{1,0:T(8,128)(2,1)}, u32[]{:S(2)}, u32[]{:S(2)}) collective-permute-start(bf16[224,768]{1,0:T(8,128)(2,1)S(1)} %pad_maximum_fusion.11), channel_id=1, source_target_pairs={{0,3},{1,0},{2,1},{3,2},{4,7},{5,4},{6,5},{7,6},{8,11},{9,8},{10,9... | collective-permute-start | bytes 1032200 | tf_op jit(solution)/shard_map/ppermute | solution.py:84
  30.5 15.0 %collective-permute-start.5 = (bf16[224,768]{1,0:T(8,128)(2,1)}, bf16[224,768]{1,0:T(8,128)(2,1)}, u32[]{:S(2)}, u32[]{:S(2)}) collective-permute-start(bf16[224,768]{1,0:T(8,128)(2,1)} %pad_maximum_fusion.10), channel_id=1, source_target_pairs={{0,1},{1,2},{2,3},{3,0},{4,5},{5,6},{6,7},{7,4},{8,9},{9,10},{10,1... | collective-permute-start | bytes 1032200 | tf_op jit(solution)/shard_map/ppermute | solution.py:84
  32.5 15.9 %collective-permute-start.12 = (bf16[384,768]{1,0:T(8,128)(2,1)}, bf16[384,768]{1,0:T(8,128)(2,1)S(1)}, u32[]{:S(2)}, u32[]{:S(2)}) collective-permute-start(bf16[384,768]{1,0:T(8,128)(2,1)} %constant_dynamic-update-slice_fusion.refs_1_), channel_id=1, source_target_pairs={{0,16},{16,0},{1,17},{17,1},{2,18},{18,2},{3,19},{19,3},{4,20},{20... | collective-permute-start | bytes 1769480 | tf_op jit(solution)/shard_map/ppermute | solution.py:88
  33.5 19.8 %collective-permute-start.9 = (bf16[384,768]{1,0:T(8,128)(2,1)}, bf16[384,768]{1,0:T(8,128)(2,1)}, u32[]{:S(2)}, u32[]{:S(2)}) collective-permute-start(bf16[384,768]{1,0:T(8,128)(2,1)} %constant_dynamic-update-slice_fusion.refs_1_), channel_id=1, source_target_pairs={{0,8},{4,12},{8,0},{12,4},{1,9},{5,13},{9,1},{13,5},{2,10},{6,14},... | collective-permute-start | bytes 1769480 | tf_op jit(solution)/shard_map/ppermute | solution.py:88
  48.6 22.3 %collective-permute-start.13 = (bf16[576,768]{1,0:T(8,128)(2,1)S(1)}, bf16[576,768]{1,0:T(8,128)(2,1)S(1)}, u32[]{:S(2)}, u32[]{:S(2)}) collective-permute-start(bf16[576,768]{1,0:T(8,128)(2,1)S(1)} %pad_maximum_fusion), channel_id=1, source_target_pairs={{0,8},{4,12},{8,0},{12,4},{1,9},{5,13},{9,1},{13,5},{2,10},{6,14},... | collective-permute-start | bytes 2654216 | tf_op jit(solution)/shard_map/ppermute | solution.py:88
  52.9 17.4 %collective-permute-start.10 = (bf16[256,768]{1,0:T(8,128)(2,1)S(1)}, bf16[256,768]{1,0:T(8,128)(2,1)S(1)}, u32[]{:S(2)}, u32[]{:S(2)}) collective-permute-start(bf16[256,768]{1,0:T(8,128)(2,1)S(1)} %pad_maximum_fusion.6), channel_id=1, source_target_pairs={{0,1},{1,2},{2,3},{3,0},{4,5},{5,6},{6,7},{7,4},{8,9},{9,10},{10,1... | collective-permute-start | bytes 1179656 | tf_op jit(solution)/shard_map/ppermute | solution.py:84
  53.2 18.4 %collective-permute-start.7 = (bf16[384,768]{1,0:T(8,128)(2,1)}, bf16[384,768]{1,0:T(8,128)(2,1)S(1)}, u32[]{:S(2)}, u32[]{:S(2)}) collective-permute-start(bf16[384,768]{1,0:T(8,128)(2,1)} %constant_dynamic-update-slice_fusion.refs_1_), channel_id=1, source_target_pairs={{0,4},{4,0},{8,12},{12,8},{1,5},{5,1},{9,13},{13,9},{2,6},{6,2},{1... | collective-permute-start | bytes 1769480 | tf_op jit(solution)/shard_map/ppermute | solution.py:88
  53.2 18.9 %collective-permute-start.17 = (bf16[2,192,768]{2,1,0:T(8,128)(2,1)}, bf16[2,192,768]{2,1,0:T(8,128)(2,1)S(1)}, u32[]{:S(2)}, u32[]{:S(2)}) collective-permute-start(bf16[2,192,768]{2,1,0:T(8,128)(2,1)} %collective-permute-done.16.refs_9_), channel_id=1, source_target_pairs={{0,4},{4,0},{8,12},{12,8},{1,5},{5,1},{9,13},{13,9},{2,6},{6,2},{1... | collective-permute-start | bytes 1769480 | tf_op jit(solution)/shard_map/ppermute | solution.py:88
  82.0 69.3 %collective-permute-start.41 = (s32[4,3,256]{2,1,0:T(4,128)S(1)}, s32[4,3,256]{2,1,0:T(4,128)S(1)}, u32[]{:S(2)}, u32[]{:S(2)}) collective-permute-start(s32[4,3,256]{2,1,0:T(4,128)S(1)} %pad_add_fusion.2.i_ref.refs_13_), channel_id=1, source_target_pairs={{0,4},{4,0},{8,12},{12,8},{1,5},{5,1},{9,13},{13,9},{2,6},{6,2},{1... | collective-permute-start | bytes 36872 | tf_op jit(solution)/shard_map/ppermute | solution.py:88
  103.3 18.9 %collective-permute-start.26 = (bf16[256,768]{1,0:T(8,128)(2,1)}, bf16[256,768]{1,0:T(8,128)(2,1)S(1)}, u32[]{:S(2)}, u32[]{:S(2)}) collective-permute-start(bf16[256,768]{1,0:T(8,128)(2,1)} %get-tuple-element.194.refs_0_), channel_id=1, source_target_pairs={{0,1},{1,2},{2,3},{3,0},{4,5},{5,6},{6,7},{7,4},{8,9},{9,10},{10,1... | collective-permute-start | bytes 1179656 | tf_op jit(solution)/shard_map/ppermute | solution.py:84
  120.6 44.9 %collective-permute-start.35 = (bf16[256,768]{1,0:T(8,128)(2,1)}, bf16[256,768]{1,0:T(8,128)(2,1)S(1)}, u32[]{:S(2)}, u32[]{:S(2)}) collective-permute-start(bf16[256,768]{1,0:T(8,128)(2,1)} %get-tuple-element.194.refs_0_), channel_id=1, source_target_pairs={{0,4},{4,0},{8,12},{12,8},{1,5},{5,1},{9,13},{13,9},{2,6},{6,2},{1... | collective-permute-start | bytes 1179656 | tf_op jit(solution)/shard_map/ppermute | solution.py:88
  121.6 33.4 %collective-permute-start.24 = (bf16[256,768]{1,0:T(8,128)(2,1)S(1)}, bf16[256,768]{1,0:T(8,128)(2,1)S(1)}, u32[]{:S(2)}, u32[]{:S(2)}) collective-permute-start(bf16[256,768]{1,0:T(8,128)(2,1)S(1)} %broadcast_select_fusion.1), channel_id=1, source_target_pairs={{0,16},{16,0},{1,17},{17,1},{2,18},{18,2},{3,19},{19,3},{4,20},{20... | collective-permute-start | bytes 1179656 | tf_op jit(solution)/shard_map/ppermute | solution.py:88
  141.7 26.6 %collective-permute-start.36 = (bf16[256,768]{1,0:T(8,128)(2,1)S(1)}, bf16[256,768]{1,0:T(8,128)(2,1)}, u32[]{:S(2)}, u32[]{:S(2)}) collective-permute-start(bf16[256,768]{1,0:T(8,128)(2,1)S(1)} %collective-permute-done.25.refs_0_.refs_1_), channel_id=1, source_target_pairs={{0,4},{4,0},{8,12},{12,8},{1,5},{5,1},{9,13},{13,9},{2,6},{6,2},{1... | collective-permute-start | bytes 1179656 | tf_op jit(solution)/shard_map/ppermute | solution.py:88
  141.8 30.8 %collective-permute-start.39 = (bf16[256,768]{1,0:T(8,128)(2,1)S(1)}, bf16[256,768]{1,0:T(8,128)(2,1)}, u32[]{:S(2)}, u32[]{:S(2)}) collective-permute-start(bf16[256,768]{1,0:T(8,128)(2,1)S(1)} %collective-permute-done.26.refs_0_.refs_4_), channel_id=1, source_target_pairs={{0,4},{4,0},{8,12},{12,8},{1,5},{5,1},{9,13},{13,9},{2,6},{6,2},{1... | collective-permute-start | bytes 1179656 | tf_op jit(solution)/shard_map/ppermute | solution.py:88
  168.3 38.5 %collective-permute-start.32 = (bf16[256,768]{1,0:T(8,128)(2,1)}, bf16[256,768]{1,0:T(8,128)(2,1)S(1)}, u32[]{:S(2)}, u32[]{:S(2)}) collective-permute-start(bf16[256,768]{1,0:T(8,128)(2,1)} %copy-done.21), channel_id=1, source_target_pairs={{0,1},{1,2},{2,3},{3,0},{4,5},{5,6},{6,7},{7,4},{8,9},{9,10},{10,1... | collective-permute-start | bytes 1179656 | tf_op jit(solution)/shard_map/ppermute | solution.py:84
  168.3 38.5 %collective-permute-start.33 = (bf16[256,768]{1,0:T(8,128)(2,1)}, bf16[256,768]{1,0:T(8,128)(2,1)S(1)}, u32[]{:S(2)}, u32[]{:S(2)}) collective-permute-start(bf16[256,768]{1,0:T(8,128)(2,1)} %copy-done.20), channel_id=1, source_target_pairs={{0,3},{1,0},{2,1},{3,2},{4,7},{5,4},{6,5},{7,6},{8,11},{9,8},{10,9... | collective-permute-start | bytes 1179656 | tf_op jit(solution)/shard_map/ppermute | solution.py:84
  172.6 34.2 %collective-permute-start.34 = (bf16[256,768]{1,0:T(8,128)(2,1)S(1)}, bf16[256,768]{1,0:T(8,128)(2,1)S(1)}, u32[]{:S(2)}, u32[]{:S(2)}) collective-permute-start(bf16[256,768]{1,0:T(8,128)(2,1)S(1)} %get-tuple-element.214), channel_id=1, source_target_pairs={{0,2},{1,3},{2,0},{3,1},{4,6},{5,7},{6,4},{7,5},{8,10},{9,11},{10,... | collective-permute-start | bytes 1179656 | tf_op jit(solution)/shard_map/ppermute | solution.py:84
  204.7 38.2 %collective-permute-start.44 = (bf16[2,96,3840]{2,1,0:T(8,128)(2,1)}, bf16[2,96,3840]{2,1,0:T(8,128)(2,1)S(1)}, u32[]{:S(2)}, u32[]{:S(2)}) collective-permute-start(bf16[2,96,3840]{2,1,0:T(8,128)(2,1)} %get-tuple-element.257), channel_id=1, source_target_pairs={{0,16},{16,0},{1,17},{17,1},{2,18},{18,2},{3,19},{19,3},{4,20},{20... | collective-permute-start | bytes 4423688 | tf_op jit(solution)/shard_map/ppermute | solution.py:88
  206.2 36.7 %collective-permute-start.45 = (bf16[2,96,3840]{2,1,0:T(8,128)(2,1)}, bf16[2,96,3840]{2,1,0:T(8,128)(2,1)S(1)}, u32[]{:S(2)}, u32[]{:S(2)}) collective-permute-start(bf16[2,96,3840]{2,1,0:T(8,128)(2,1)} %get-tuple-element.258), channel_id=1, source_target_pairs={{0,8},{4,12},{8,0},{12,4},{1,9},{5,13},{9,1},{13,5},{2,10},{6,14},... | collective-permute-start | bytes 4423688 | tf_op jit(solution)/shard_map/ppermute | solution.py:88
  239.1 16.0 %collective-permute-start.47 = (bf16[192,768]{1,0:T(8,128)(2,1)}, bf16[192,768]{1,0:T(8,128)(2,1)S(1)}, u32[]{:S(2)}, u32[]{:S(2)}) collective-permute-start(bf16[192,768]{1,0:T(8,128)(2,1)} %get-tuple-element.253), channel_id=1, source_target_pairs={{0,1},{1,2},{2,3},{3,0},{4,5},{5,6},{6,7},{7,4},{8,9},{9,10},{10,1... | collective-permute-start | bytes 884744 | tf_op jit(solution)/shard_map/ppermute | solution.py:84
  239.9 16.2 %collective-permute-start.48 = (bf16[192,768]{1,0:T(8,128)(2,1)}, bf16[192,768]{1,0:T(8,128)(2,1)S(1)}, u32[]{:S(2)}, u32[]{:S(2)}) collective-permute-start(bf16[192,768]{1,0:T(8,128)(2,1)} %get-tuple-element.254), channel_id=1, source_target_pairs={{0,3},{1,0},{2,1},{3,2},{4,7},{5,4},{6,5},{7,6},{8,11},{9,8},{10,9... | collective-permute-start | bytes 884744 | tf_op jit(solution)/shard_map/ppermute | solution.py:84
  258.5 15.4 %collective-permute-start.50 = (bf16[384,768]{1,0:T(8,128)(2,1)S(1)}, bf16[384,768]{1,0:T(8,128)(2,1)S(1)}, u32[]{:S(2)}, u32[]{:S(2)}) collective-permute-start(bf16[384,768]{1,0:T(8,128)(2,1)S(1)} %pad_maximum_fusion.2), channel_id=1, source_target_pairs={{0,3},{1,0},{2,1},{3,2},{4,7},{5,4},{6,5},{7,6},{8,11},{9,8},{10,9... | collective-permute-start | bytes 1769480 | tf_op jit(solution)/shard_map/ppermute | solution.py:84
  259.7 27.7 %collective-permute-start.49 = (bf16[384,768]{1,0:T(8,128)(2,1)S(1)}, bf16[384,768]{1,0:T(8,128)(2,1)S(1)}, u32[]{:S(2)}, u32[]{:S(2)}) collective-permute-start(bf16[384,768]{1,0:T(8,128)(2,1)S(1)} %pad_maximum_fusion.1), channel_id=1, source_target_pairs={{0,1},{1,2},{2,3},{3,0},{4,5},{5,6},{6,7},{7,4},{8,9},{9,10},{10,1... | collective-permute-start | bytes 1769480 | tf_op jit(solution)/shard_map/ppermute | solution.py:84
  270.4 44.2 %collective-permute-start.58 = (bf16[4,224,768]{2,1,0:T(8,128)(2,1)S(1)}, bf16[4,224,768]{2,1,0:T(8,128)(2,1)S(1)}, u32[]{:S(2)}, u32[]{:S(2)}) collective-permute-start(bf16[4,224,768]{2,1,0:T(8,128)(2,1)S(1)} %get-tuple-element.301), channel_id=1, source_target_pairs={{0,8},{4,12},{8,0},{12,4},{1,9},{5,13},{9,1},{13,5},{2,10},{6,14},... | collective-permute-start | bytes 4128776 | tf_op jit(solution)/shard_map/ppermute | solution.py:88
  288.7 25.8 %collective-permute-start.46 = (bf16[256,768]{1,0:T(8,128)(2,1)S(1)}, bf16[256,768]{1,0:T(8,128)(2,1)S(1)}, u32[]{:S(2)}, u32[]{:S(2)}) collective-permute-start(bf16[256,768]{1,0:T(8,128)(2,1)S(1)} %select_convert_fusion), channel_id=1, source_target_pairs={{0,16},{16,0},{1,17},{17,1},{2,18},{18,2},{3,19},{19,3},{4,20},{20... | collective-permute-start | bytes 1179656 | tf_op jit(solution)/shard_map/ppermute | solution.py:88
  295.9 16.9 %collective-permute-start.60 = (bf16[8,96,256]{2,1,0:T(8,128)(2,1)S(1)}, bf16[8,96,256]{2,1,0:T(8,128)(2,1)S(1)}, u32[]{:S(2)}, u32[]{:S(2)}) collective-permute-start(bf16[8,96,256]{2,1,0:T(8,128)(2,1)S(1)} %pad_maximum_fusion.9.refs_2_), channel_id=1, source_target_pairs={{0,3},{1,0},{2,1},{3,2},{4,7},{5,4},{6,5},{7,6},{8,11},{9,8},{10,9... | collective-permute-start | bytes 1179656 | tf_op jit(solution)/shard_map/ppermute | solution.py:84
  309.4 38.3 %collective-permute-start.56 = (bf16[96,3840]{1,0:T(8,128)(2,1)}, bf16[96,3840]{1,0:T(8,128)(2,1)S(1)}, u32[]{:S(2)}, u32[]{:S(2)}) collective-permute-start(bf16[96,3840]{1,0:T(8,128)(2,1)} %get-tuple-element.297), channel_id=1, source_target_pairs={{0,8},{4,12},{8,0},{12,4},{1,9},{5,13},{9,1},{13,5},{2,10},{6,14},... | collective-permute-start | bytes 2211848 | tf_op jit(solution)/shard_map/ppermute | solution.py:88
  313.5 34.2 %collective-permute-start.57 = (bf16[96,3840]{1,0:T(8,128)(2,1)}, bf16[96,3840]{1,0:T(8,128)(2,1)S(1)}, u32[]{:S(2)}, u32[]{:S(2)}) collective-permute-start(bf16[96,3840]{1,0:T(8,128)(2,1)} %get-tuple-element.299), channel_id=1, source_target_pairs={{0,16},{16,0},{1,17},{17,1},{2,18},{18,2},{3,19},{19,3},{4,20},{20... | collective-permute-start | bytes 2211848 | tf_op jit(solution)/shard_map/ppermute | solution.py:88
  326.3 17.6 %collective-permute-start.70 = (bf16[224,768]{1,0:T(8,128)(2,1)}, bf16[224,768]{1,0:T(8,128)(2,1)}, u32[]{:S(2)}, u32[]{:S(2)}) collective-permute-start(bf16[224,768]{1,0:T(8,128)(2,1)} %pad_maximum_fusion.13), channel_id=1, source_target_pairs={{0,3},{1,0},{2,1},{3,2},{4,7},{5,4},{6,5},{7,6},{8,11},{9,8},{10,9... | collective-permute-start | bytes 1032200 | tf_op jit(solution)/shard_map/ppermute | solution.py:84
  (106 other events, 1008.7 us)
